TPU v7x, 32 devices: a whole 2x2x4 slice. The times are simulated.
32 devices in a mesh: gx: 8 (over z, y), gy: 4 (over x, core).
Axes of the slice: x: 2, y: 2, z: 4, core: 2. Of those that a mesh axis runs over, the one named last changes fastest.
Arguments:
- right_side: float32 [3, 32, 64, 256], P(None, 'gx', 'gy'), may hold values from -45 to 45
- diag_blocks: float32 [9, 32, 64, 256], P(None, 'gx', 'gy'), may hold values from -1.2 to 1.8
- off_blocks: float32 [6, 9, 32, 64, 256], P(None, None, 'gx', 'gy'), may hold values from -0.25 to 0.16
- cell_inverse: float32 [9, 32, 64, 256], P(None, 'gx', 'gy'), may hold values from -0.4 to 0.85
- send_cells: int32 [32, 3200], P(('gx', 'gy')), may hold values from 0 to 16383, as said below
- recv_index: int32 [256, 400], P(('gx', 'gy')), may hold values from 0 to 28799, as said below
- seg_count: int32 [256], P(('gx', 'gy')), may hold values from 50 to 400, as said below
- span_inverse: float32 [25, 48, 12288], P(None, None, ('gx', 'gy')), may hold values from -0.24 to 1.2
- span_couple: float32 [25, 9, 256], P(None, None, ('gx', 'gy')), may hold values from -3 to 3
Outputs:
- solution: float32 [3, 32, 64, 256], P(None, 'gx', 'gy')
- residual: float32 [3, 32, 64, 256], P(None, 'gx', 'gy')
Inputs may be any that keep to these rules, and one draw needn't show every extreme that they name: `send_cells`: each row holds distinct local cells of its device. `recv_index`: over the live segments of one owner's wells the positions are distinct and name tiles inside the grid; entries of segments that are not live are arbitrary. `seg_count`: on one device in every draw all wells have 400 segments.
All inputs are finite; a program needn't handle non-finite values.
Results may differ from a plain program's by a relative error of at most 0.0001.
Values sent between devices are 32-bit elements; how exact they have to be, the bound alone decides.
No kernel may reach another device: no remote copies, remote signals or barrier semaphores. Data moves between devices by JAX's collectives and lax.ppermute only.
A program may use at most 128 MiB of HBM per device.

v0:
```python
import jax
import jax.numpy as jnp
from jax import lax
from jax.sharding import PartitionSpec as P

MAXSEG = 400
SPAN = 16
NCHUNK = 25


def with_halo(cells, sides, width):
    for axis, dim in sides:
        count = lax.axis_size(axis)
        ends = count - 1
        head = lax.slice_in_dim(cells, 0, width, axis=dim)
        tail = lax.slice_in_dim(cells, cells.shape[dim] - width, cells.shape[dim], axis=dim)
        cells = jnp.concatenate(
            [
                lax.ppermute(tail, axis, [(i, (i + 1) % count) for i in range(ends)]),
                cells,
                lax.ppermute(head, axis, [((i + 1) % count, i) for i in range(ends)]),
            ],
            axis=dim,
        )
    return cells


def block_apply(matrix, vector):
    return jnp.stack(
        [
            matrix[3 * a] * vector[0]
            + matrix[3 * a + 1] * vector[1]
            + matrix[3 * a + 2] * vector[2]
            for a in range(3)
        ]
    )


def apply_jacobian(field, diag_blocks, off_blocks):
    padded = with_halo(field, (("gx", 1), ("gy", 2)), 1)
    padded = jnp.pad(padded, ((0, 0), (0, 0), (0, 0), (1, 1)))
    beside = [
        padded[:, :-2, 1:-1, 1:-1],
        padded[:, 2:, 1:-1, 1:-1],
        padded[:, 1:-1, :-2, 1:-1],
        padded[:, 1:-1, 2:, 1:-1],
        padded[:, 1:-1, 1:-1, :-2],
        padded[:, 1:-1, 1:-1, 2:],
    ]
    total = block_apply(diag_blocks, field)
    for face in range(6):
        total = total + block_apply(off_blocks[face], beside[face])
    return total


def chain_solve(segments, span_inverse, span_couple):
    well_count = span_couple.shape[2]
    width = 3 * SPAN
    blocks = (
        segments.reshape(3, well_count, NCHUNK, SPAN)
        .transpose(2, 3, 0, 1)
        .reshape(NCHUNK, width, well_count)
    )
    inverse = span_inverse.reshape(NCHUNK, width, well_count, width)

    def advance(carry, packed):
        block_rhs, block_inverse, couple = packed
        first = block_rhs[:3] - block_apply(couple, carry)
        block_rhs = jnp.concatenate([first, block_rhs[3:]], axis=0)
        solved = jnp.sum(block_inverse * block_rhs[:, :, None], axis=0).T
        return (solved[width - 3 :], solved)

    start = jnp.zeros((3, well_count), jnp.float32)
    _, solved = lax.scan(advance, start, (blocks, inverse, span_couple))
    return (
        solved.reshape(NCHUNK, SPAN, 3, well_count)
        .transpose(2, 3, 0, 1)
        .reshape(3, well_count * MAXSEG)
    )


def gather_blocks(perforated):
    count = perforated.shape[0]
    beside_all = with_halo(perforated.reshape(count, 1, 1, -1), (("gx", 1), ("gy", 2)), 1)
    return beside_all.reshape(count, -1)


def gather_values(picked):
    count = picked.shape[0]
    beside_all = with_halo(picked.reshape(count, 1, 1, -1), (("gx", 1), ("gy", 2)), 1)
    return beside_all.reshape(count, -1)


def return_values(slots):
    count = slots.shape[0]
    spread = with_halo(slots.reshape(count, 3, 3, -1), (("gx", 1), ("gy", 2)), 1)
    return jnp.sum(spread[:, 0::2, 0::2], axis=(1, 2))


def orthogonalize(image, basis):
    sums = lax.psum(jnp.stack([jnp.sum(image * vector) for vector in basis]), ("gx", "gy"))
    coeffs = [sums[place] for place in range(len(basis))]
    for place in range(len(basis)):
        image = image - coeffs[place] * basis[place]
    return (image, coeffs)


def least_squares(top_first, sub_first, top_second, mid_second, sub_second, beta):
    gram_first = top_first * top_first + sub_first * sub_first
    gram_cross = top_first * top_second + sub_first * mid_second
    gram_second = top_second * top_second + mid_second * mid_second + sub_second * sub_second
    determinant = gram_first * gram_second - gram_cross * gram_cross
    weight_one = (gram_second * beta * top_first - gram_cross * beta * top_second) / determinant
    weight_two = (gram_first * beta * top_second - gram_cross * beta * top_first) / determinant
    return (weight_one, weight_two)


def body(
    right_side,
    diag_blocks,
    off_blocks,
    cell_inverse,
    send_cells,
    recv_index,
    seg_count,
    span_inverse,
    span_couple,
):
    cell_shape = right_side.shape
    send_list = send_cells[0]
    recv_list = recv_index.reshape(-1)
    alive = (jnp.arange(MAXSEG)[None, :] < seg_count[:, None]).reshape(1, -1)
    inverse_flat = cell_inverse.reshape(9, -1)
    perforated = jnp.take(diag_blocks.reshape(9, -1), send_list, axis=1)
    owner_blocks = jnp.take(gather_blocks(perforated), recv_list, axis=1)
    beta = jnp.sqrt(lax.psum(jnp.sum(right_side * right_side), ("gx", "gy")))
    basis = [right_side / beta]
    search = []
    entries = []
    for column in range(2):
        flat = basis[column].reshape(3, -1)
        result = block_apply(inverse_flat, flat)
        picked = jnp.take(flat, send_list, axis=1)
        arrived = jnp.take(gather_values(picked), recv_list, axis=1)
        arrived = block_apply(owner_blocks, arrived)
        segments = jnp.where(alive, arrived, 0.0)
        solved = jnp.where(alive, chain_solve(segments, span_inverse, span_couple), 0.0)
        slots = jnp.zeros((3, 9 * picked.shape[1]), jnp.float32).at[:, recv_list].add(solved)
        returned = return_values(slots)
        direction = result.at[:, send_list].add(returned).reshape(cell_shape)
        search.append(direction)
        image = apply_jacobian(direction, diag_blocks, off_blocks)
        image, coeffs = orthogonalize(image, basis)
        size = jnp.sqrt(lax.psum(jnp.sum(image * image), ("gx", "gy")))
        entries.append((coeffs, size))
        basis.append(image / size)
    top_first, sub_first = (entries[0][0][0], entries[0][1])
    top_second, mid_second, sub_second = (entries[1][0][0], entries[1][0][1], entries[1][1])
    weight_one, weight_two = least_squares(
        top_first, sub_first, top_second, mid_second, sub_second, beta
    )
    solution = weight_one * search[0] + weight_two * search[1]
    residual = (
        (beta - top_first * weight_one - top_second * weight_two) * basis[0]
        - (sub_first * weight_one + mid_second * weight_two) * basis[1]
        - sub_second * weight_two * basis[2]
    )
    return (solution, residual)


def solution(mesh):
    return jax.shard_map(
        body,
        mesh=mesh,
        in_specs=(
            P(None, "gx", "gy", None),
            P(None, "gx", "gy", None),
            P(None, None, "gx", "gy", None),
            P(None, "gx", "gy", None),
            P(("gx", "gy"), None),
            P(("gx", "gy"), None),
            P(("gx", "gy")),
            P(None, None, ("gx", "gy")),
            P(None, None, ("gx", "gy")),
        ),
        out_specs=(P(None, "gx", "gy", None), P(None, "gx", "gy", None)),
        check_vma=False,
    )
```

profile of v0, /device:TPU:0, one launch (start us, length us, event | category | flops | bytes accessed | tf_op | source)
XLA Modules:
  0.0 800.6 jit_solution(14820500451723711989)
XLA Ops:
  3.0 42.3 %psum.35 = f32[]{:T(128)} all-reduce(f32[]{:T(128)} %multiply_reduce_fusion.5), channel_id=1, replica_groups=mesh['gx'=8,'gy'=4] {'gx','gy'}, use_global_device_ids=true, to_apply=%region_1.2 | all-reduce | flops 1 | bytes 8 | tf_op jit(solution)/shard_map/psum | solution.py:136
  52.2 9.0 %gather_fusion.2 = f32[3200,3]{1,0:T(8,128)S(1)} fusion(f32[3,16384]{0,1:T(8,128)} %bitcast.710, s32[4096]{0:T(1024)S(1)} %pad_clamp_fusion.1), kind=kCustom, calls=%fused_computation.clone | custom fusion | bytes 89600 | tf_op jit(solution)/shard_map/jit(_take)/gather | solution.py:143
  74.4 9.0 %gather_fusion = f32[3200,9]{1,0:T(8,128)S(1)} fusion(f32[9,16384]{0,1:T(8,128)} %bitcast.709, s32[4096]{0:T(1024)S(1)} %pad_clamp_fusion.3), kind=kCustom, calls=%fused_computation.4 | custom fusion | bytes 243200 | tf_op jit(solution)/shard_map/jit(_take)/gather | solution.py:134
  119.8 10.8 %gather_fusion.3 = f32[3200,3]{1,0:T(8,128)S(1)} fusion(f32[3,28800]{0,1:T(8,128)} %bitcast.708, s32[4096]{0:T(1024)S(1)} %copy-done.30), kind=kCustom, calls=%fused_computation.1.clone | custom fusion | bytes 89600 | tf_op jit(solution)/shard_map/jit(_take)/gather | solution.py:144
  142.1 12.2 %gather_fusion.1 = f32[3200,9]{1,0:T(8,128)} fusion(f32[9,28800]{0,1:T(8,128)} %bitcast.706, s32[4096]{0:T(1024)S(1)} %copy-done.37), kind=kCustom, calls=%fused_computation.5 | custom fusion | bytes 243200 | tf_op jit(solution)/shard_map/jit(_take)/gather | solution.py:135
  165.3 33.0 %while.24 = (s32[]{:T(128)}, f32[3,8]{0,1:T(8,128)S(1)}, f32[25,48,8]{1,2,0:T(8,128)S(1)}, f32[25,48,8,48]{3,2,1,0:T(8,128)}, f32[25,48,8]{2,1,0:T(8,128)S(1)}, ...) while((s32[]{:T(128)}, f32[3,8]{0,1:T(8,128)S(1)}, ...), condition=%wide.region_4.7_spmd, body=%wide.region_2.0_spmd.sunk | while | flops 37066 | bytes 92397 | solution.py:74
  200.9 26.2 %scatter_custom_fusion = f32[3,28800]{0,1:T(8,128)} fusion(s32[3200]{0:T(1024)} %copy-done.39, f32[3200,3]{1,0:T(8,128)S(1)} %copy.332, f32[]{:T(128)} %constant.68.clone.1), kind=kCustom, calls=%fused_computation.100 | custom fusion | flops 9600 | bytes 346112 | tf_op jit(solution)/shard_map/scatter-add | solution.py:148
  227.1 8.2 %fusion.148 = (f32[3,1,3,3200]{0,3,2,1:T(8,128)}, f32[3,1,3,3200]{0,3,2,1:T(8,128)}) fusion(f32[3,3,3,3200]{0,3,2,1:T(8,128)} %bitcast.704), kind=kLoop, calls=%fused_computation.415 | loop fusion | bytes 460800 | tf_op jit(solution)/shard_map/slice | solution.py:16
  250.6 9.7 %copy.336 = f32[3,3,3,3200]{3,2,1,0:T(4,128)} copy(f32[3,3,3,3200]{0,3,2,1:T(8,128)} %bitcast.705) | data formatting | bytes 691200 | tf_op jit(solution)/shard_map/reshape | solution.py:96
  277.4 24.7 %scatter_fusion = f32[3,16384]{0,1:T(8,128)} fusion(f32[3,16384]{0,1:T(8,128)} %copy.341, s32[3200]{0:T(1024)S(1)} %copy-done.26, f32[3200,3]{1,0:T(8,128)} %copy.342), kind=kCustom, calls=%fused_computation.7 | custom fusion | flops 9600 | bytes 128000 | tf_op jit(solution)/shard_map/scatter-add | solution.py:150
  302.1 19.4 %slice_reduce_fusion.5 = (f32[16384]{0:T(1024)S(1)}, f32[16384]{0:T(1024)S(1)}, f32[16384]{0:T(1024)S(1)}) fusion(f32[3,16384]{0,1:T(8,128)} %scatter_fusion), kind=kLoop, calls=%fused_computation.97 | loop fusion | bytes 393216 | tf_op jit(solution)/shard_map/slice | solution.py:31
  350.2 42.7 %psum.36 = f32[]{:T(128)} all-reduce(f32[]{:T(128)} %get-tuple-element.209), channel_id=1, replica_groups=mesh['gx'=8,'gy'=4] {'gx','gy'}, use_global_device_ids=true, to_apply=%region_9.12 | all-reduce | flops 1 | bytes 8 | tf_op jit(solution)/shard_map/psum | solution.py:101
  394.1 39.1 %psum.37 = f32[]{:T(128)} all-reduce(f32[]{:T(128)} %multiply_reduce_fusion.3), channel_id=1, replica_groups=mesh['gx'=8,'gy'=4] {'gx','gy'}, use_global_device_ids=true, to_apply=%region_11.14 | all-reduce | flops 1 | bytes 8 | tf_op jit(solution)/shard_map/psum | solution.py:154
  439.2 10.4 %gather_fusion.4 = f32[3200,3]{1,0:T(8,128)} fusion(f32[3,16384]{0,1:T(8,128)} %bitcast.711, s32[4096]{0:T(1024)S(1)} %copy-done.32), kind=kCustom, calls=%fused_computation.2.clone | custom fusion | bytes 89600 | tf_op jit(solution)/shard_map/jit(_take)/gather | solution.py:143
  472.6 8.0 %copy.352 = f32[3,3,3,3200]{0,3,2,1:T(8,128)} copy(f32[3,3,3,3200]{3,2,1,0:T(4,128)S(1)} %pad_maximum_fusion.8) | data formatting | bytes 691200 | tf_op jit(solution)/shard_map/concatenate | solution.py:17
  480.6 12.2 %gather_fusion.5 = f32[3200,3]{1,0:T(8,128)} fusion(f32[3,28800]{0,1:T(8,128)} %bitcast.707, s32[4096]{0:T(1024)S(1)} %copy-done.30), kind=kCustom, calls=%fused_computation.3.clone | custom fusion | bytes 89600 | tf_op jit(solution)/shard_map/jit(_take)/gather | solution.py:144
  502.1 56.9 %while.25 = (s32[]{:T(128)}, f32[3,8]{0,1:T(8,128)S(1)}, f32[25,48,8]{1,2,0:T(8,128)S(1)}, f32[25,48,8,48]{3,2,1,0:T(8,128)}, f32[25,48,8]{2,1,0:T(8,128)S(1)}, ...) while((s32[]{:T(128)}, f32[3,8]{0,1:T(8,128)S(1)}, ...), condition=%wide.region_14.17_spmd, body=%wide.region_12.16_spmd.sunk | while | flops 37066 | bytes 92397 | solution.py:74
  560.1 26.2 %scatter_custom_fusion.2 = f32[3,28800]{0,1:T(8,128)} fusion(s32[3200]{0:T(1024)} %copy-done.39, f32[3200,3]{1,0:T(8,128)S(1)} %copy.358, f32[]{:T(128)} %constant.68.clone.1), kind=kCustom, calls=%fused_computation.98 | custom fusion | flops 9600 | bytes 346112 | tf_op jit(solution)/shard_map/scatter-add | solution.py:148
  586.3 8.2 %fusion.147 = (f32[3,1,3,3200]{0,3,2,1:T(8,128)}, f32[3,1,3,3200]{0,3,2,1:T(8,128)}) fusion(f32[3,3,3,3200]{0,3,2,1:T(8,128)} %bitcast.702), kind=kLoop, calls=%fused_computation.414 | loop fusion | bytes 460800 | tf_op jit(solution)/shard_map/slice | solution.py:16
  606.2 9.0 %copy.362 = f32[3,3,3,3200]{3,2,1,0:T(4,128)S(1)} copy(f32[3,3,3,3200]{0,3,2,1:T(8,128)} %bitcast.703) | data formatting | bytes 691200 | tf_op jit(solution)/shard_map/reshape | solution.py:96
  629.8 24.7 %scatter_fusion.1 = f32[3,16384]{0,1:T(8,128)} fusion(f32[3,16384]{0,1:T(8,128)} %copy.367, s32[3200]{0:T(1024)S(1)} %copy-done.26, f32[3200,3]{1,0:T(8,128)S(1)} %copy.368), kind=kCustom, calls=%fused_computation.9 | custom fusion | flops 9600 | bytes 128000 | tf_op jit(solution)/shard_map/scatter-add | solution.py:150
  654.5 19.2 %slice_reduce_fusion.2 = (f32[16384]{0:T(1024)S(1)}, f32[16384]{0:T(1024)S(1)}, f32[16384]{0:T(1024)S(1)}) fusion(f32[3,16384]{0,1:T(8,128)} %scatter_fusion.1), kind=kLoop, calls=%fused_computation.94 | loop fusion | bytes 393216 | tf_op jit(solution)/shard_map/slice | solution.py:31
  705.2 41.7 %psum.38 = f32[2]{0:T(128)S(1)} all-reduce(f32[2]{0:T(128)S(1)} %pad_maximum_fusion.52), channel_id=1, replica_groups=mesh['gx'=8,'gy'=4] {'gx','gy'}, use_global_device_ids=true, to_apply=%region_20.23 | all-reduce | flops 2 | bytes 16 | tf_op jit(solution)/shard_map/psum | solution.py:101
  754.8 39.7 %psum.39 = f32[]{:T(128)} all-reduce(f32[]{:T(128)} %multiply_reduce_fusion), channel_id=1, replica_groups=mesh['gx'=8,'gy'=4] {'gx','gy'}, use_global_device_ids=true, to_apply=%region_22.25 | all-reduce | flops 1 | bytes 8 | tf_op jit(solution)/shard_map/psum | solution.py:154
  (686 shorter events, 332.2 us)
Async XLA Ops:
  63.3 36.8 %collective-permute-start.4 = (f32[3,1,1,3200]{3,2,1,0:T(1,128)S(1)}, f32[3,1,1,3200]{3,2,1,0:T(1,128)}, u32[]{:S(2)}, u32[]{:S(2)}) collective-permute-start(f32[3,1,1,3200]{3,2,1,0:T(1,128)S(1)} %copy.323), channel_id=1, source_target_pairs={{0,4},{4,8},{8,12},{12,16},{16,20},{20,24},{24,28},{1,5},{5,9},{9,... | collective-permute-start | bytes 115208 | tf_op jit(solution)/shard_map/ppermute | solution.py:19
  68.3 31.8 %collective-permute-start.5 = (f32[3,1,1,3200]{3,2,1,0:T(1,128)S(1)}, f32[3,1,1,3200]{3,2,1,0:T(1,128)}, u32[]{:S(2)}, u32[]{:S(2)}) collective-permute-start(f32[3,1,1,3200]{3,2,1,0:T(1,128)S(1)} %copy.323), channel_id=1, source_target_pairs={{4,0},{8,4},{12,8},{16,12},{20,16},{24,20},{28,24},{5,1},{9,5},{13... | collective-permute-start | bytes 115208 | tf_op jit(solution)/shard_map/ppermute | solution.py:21
  86.2 17.4 %collective-permute-start = (f32[9,1,1,3200]{3,2,1,0:T(1,128)}, f32[9,1,1,3200]{3,2,1,0:T(1,128)S(1)}, u32[]{:S(2)}, u32[]{:S(2)}) collective-permute-start(f32[9,1,1,3200]{3,2,1,0:T(1,128)} %copy.318), channel_id=1, source_target_pairs={{0,4},{4,8},{8,12},{12,16},{16,20},{20,24},{24,28},{1,5},{5,9},{9,... | collective-permute-start | bytes 345608 | tf_op jit(solution)/shard_map/ppermute | solution.py:19
  90.7 12.9 %collective-permute-start.1 = (f32[9,1,1,3200]{3,2,1,0:T(1,128)}, f32[9,1,1,3200]{3,2,1,0:T(1,128)S(1)}, u32[]{:S(2)}, u32[]{:S(2)}) collective-permute-start(f32[9,1,1,3200]{3,2,1,0:T(1,128)} %copy.318), channel_id=1, source_target_pairs={{4,0},{8,4},{12,8},{16,12},{20,16},{24,20},{28,24},{5,1},{9,5},{13... | collective-permute-start | bytes 345608 | tf_op jit(solution)/shard_map/ppermute | solution.py:21
  101.0 10.0 %collective-permute-start.6 = (f32[3,3,1,3200]{3,2,1,0:T(1,128)S(1)}, f32[3,3,1,3200]{3,2,1,0:T(1,128)S(1)}, u32[]{:S(2)}, u32[]{:S(2)}) collective-permute-start(f32[3,3,1,3200]{3,2,1,0:T(1,128)S(1)} %pad_maximum_fusion.12), channel_id=1, source_target_pairs={{0,1},{1,2},{2,3},{4,5},{5,6},{6,7},{8,9},{9,10},{10,11},{12,13},{... | collective-permute-start | bytes 345608 | tf_op jit(solution)/shard_map/ppermute | solution.py:19
  102.3 8.8 %collective-permute-start.7 = (f32[3,3,1,3200]{3,2,1,0:T(1,128)S(1)}, f32[3,3,1,3200]{3,2,1,0:T(1,128)S(1)}, u32[]{:S(2)}, u32[]{:S(2)}) collective-permute-start(f32[3,3,1,3200]{3,2,1,0:T(1,128)S(1)} %pad_maximum_fusion.12), channel_id=1, source_target_pairs={{1,0},{2,1},{3,2},{5,4},{6,5},{7,6},{9,8},{10,9},{11,10},{13,12},{... | collective-permute-start | bytes 345608 | tf_op jit(solution)/shard_map/ppermute | solution.py:21
  104.7 27.6 %collective-permute-start.2 = (f32[9,3,1,3200]{3,2,1,0:T(1,128)}, f32[9,3,1,3200]{3,2,1,0:T(1,128)}, u32[]{:S(2)}, u32[]{:S(2)}) collective-permute-start(f32[9,3,1,3200]{3,2,1,0:T(1,128)} %pad_maximum_fusion.9), channel_id=1, source_target_pairs={{0,1},{1,2},{2,3},{4,5},{5,6},{6,7},{8,9},{9,10},{10,11},{12,13},{... | collective-permute-start | bytes 1036808 | tf_op jit(solution)/shard_map/ppermute | solution.py:19
  109.2 23.1 %collective-permute-start.3 = (f32[9,3,1,3200]{3,2,1,0:T(1,128)}, f32[9,3,1,3200]{3,2,1,0:T(1,128)}, u32[]{:S(2)}, u32[]{:S(2)}) collective-permute-start(f32[9,3,1,3200]{3,2,1,0:T(1,128)} %pad_maximum_fusion.9), channel_id=1, source_target_pairs={{1,0},{2,1},{3,2},{5,4},{6,5},{7,6},{9,8},{10,9},{11,10},{13,12},{... | collective-permute-start | bytes 1036808 | tf_op jit(solution)/shard_map/ppermute | solution.py:21
  238.6 21.7 %collective-permute-start.8 = (f32[3,1,3,3200]{3,1,2,0:T(1,128)S(1)}, f32[3,1,3,3200]{3,1,2,0:T(1,128)S(1)}, u32[]{:S(2)}, u32[]{:S(2)}) collective-permute-start(f32[3,1,3,3200]{3,1,2,0:T(1,128)S(1)} %copy.376), channel_id=1, source_target_pairs={{0,4},{4,8},{8,12},{12,16},{16,20},{20,24},{24,28},{1,5},{5,9},{9,... | collective-permute-start | bytes 345608 | tf_op jit(solution)/shard_map/ppermute | solution.py:19
  247.1 13.2 %collective-permute-start.9 = (f32[3,1,3,3200]{3,1,2,0:T(1,128)S(1)}, f32[3,1,3,3200]{3,1,2,0:T(1,128)S(1)}, u32[]{:S(2)}, u32[]{:S(2)}) collective-permute-start(f32[3,1,3,3200]{3,1,2,0:T(1,128)S(1)} %copy.377), channel_id=1, source_target_pairs={{4,0},{8,4},{12,8},{16,12},{20,16},{24,20},{28,24},{5,1},{9,5},{13... | collective-permute-start | bytes 345608 | tf_op jit(solution)/shard_map/ppermute | solution.py:21
  262.6 10.7 %collective-permute-start.10 = (f32[3,5,1,3200]{3,2,1,0:T(1,128)}, f32[3,5,1,3200]{3,2,1,0:T(1,128)}, u32[]{:S(2)}, u32[]{:S(2)}) collective-permute-start(f32[3,5,1,3200]{3,2,1,0:T(1,128)} %get-tuple-element.295), channel_id=1, source_target_pairs={{0,1},{1,2},{2,3},{4,5},{5,6},{6,7},{8,9},{9,10},{10,11},{12,13},{... | collective-permute-start | bytes 576008 | tf_op jit(solution)/shard_map/ppermute | solution.py:19
  266.5 7.8 collective-permute-start.11
  327.0 7.4 collective-permute-start.12
  332.7 6.6 collective-permute-start.13
  339.3 5.4 collective-permute-start.14
  342.4 5.5 collective-permute-start.15
  455.2 6.0 collective-permute-start.16
  459.6 5.9 collective-permute-start.17
  597.8 17.4 %collective-permute-start.20 = (f32[3,1,3,3200]{3,1,2,0:T(1,128)S(1)}, f32[3,1,3,3200]{3,1,2,0:T(1,128)S(1)}, u32[]{:S(2)}, u32[]{:S(2)}) collective-permute-start(f32[3,1,3,3200]{3,1,2,0:T(1,128)S(1)} %copy.378), channel_id=1, source_target_pairs={{0,4},{4,8},{8,12},{12,16},{16,20},{20,24},{24,28},{1,5},{5,9},{9,... | collective-permute-start | bytes 345608 | tf_op jit(solution)/shard_map/ppermute | solution.py:19
  604.6 10.7 %collective-permute-start.21 = (f32[3,1,3,3200]{3,1,2,0:T(1,128)S(1)}, f32[3,1,3,3200]{3,1,2,0:T(1,128)S(1)}, u32[]{:S(2)}, u32[]{:S(2)}) collective-permute-start(f32[3,1,3,3200]{3,1,2,0:T(1,128)S(1)} %copy.379), channel_id=1, source_target_pairs={{4,0},{8,4},{12,8},{16,12},{20,16},{24,20},{28,24},{5,1},{9,5},{13... | collective-permute-start | bytes 345608 | tf_op jit(solution)/shard_map/ppermute | solution.py:21
  615.8 12.9 %collective-permute-start.22 = (f32[3,5,1,3200]{3,2,1,0:T(1,128)S(1)}, f32[3,5,1,3200]{3,2,1,0:T(1,128)S(1)}, u32[]{:S(2)}, u32[]{:S(2)}) collective-permute-start(f32[3,5,1,3200]{3,2,1,0:T(1,128)S(1)} %get-tuple-element.293), channel_id=1, source_target_pairs={{0,1},{1,2},{2,3},{4,5},{5,6},{6,7},{8,9},{9,10},{10,11},{12,13},{... | collective-permute-start | bytes 576008 | tf_op jit(solution)/shard_map/ppermute | solution.py:19
  620.9 8.0 collective-permute-start.23
  682.6 6.8 collective-permute-start.24
  686.9 6.5 collective-permute-start.25
  (48 other events, 961.4 us)
where the time goes:
time: 811 us; the launch traced here: 801 us
  local copies, waits for them, and re-layouts  247 us (30%)
  other arithmetic  236 us (29%)
  blocking collectives  205 us (25%)
  starting transfers between devices  72.2 us (9%)
  waiting for transfers between devices  24.5 us (3%)
  between operations  14.1 us (2%)
    psum x2, blocking collectives, orthogonalize(): lax.psum(jnp.stack([jnp.sum(image * vector) for vector in basis]), ('gx',...  84.4 us
    psum x2, blocking collectives, body(): size = jnp.sqrt(lax.psum(jnp.sum(image * image), ('gx', 'gy')))  78.7 us
    ppermute x14, starting transfers between devices, with_halo(): lax.ppermute(tail, axis, [(i, (i + 1) % count) for i in range(ends)])  53.6 us
    reduce_sum x50, other arithmetic, advance(): solved = jnp.sum(block_inverse * block_rhs[:, :, None], axis=0).T  52.6 us
    scatter-add x2, other arithmetic, body(): jnp.zeros((3, 9 * picked.shape[1]), jnp.float32).at[:, recv_list]  52.4 us
    scatter-add x2, other arithmetic, body(): direction = result.at[:, send_list].add(returned).reshape(cell_shape)  49.4 us
    psum x1, blocking collectives, body(): beta = jnp.sqrt(lax.psum(jnp.sum(right_side * right_side), ('gx', 'gy')))  42.3 us
    add x70, other arithmetic, block_apply(): matrix[3 * a] * vector[0] + matrix[3 * a + 1] * vector[1]  40.2 us
  transfers between devices with their start and end apart: 28, of which 8 were waited for; matrix products, arithmetic and copies ran while one was open for 11% of the time, Pallas kernels for 0%

commit v1 on v0

v1 whole, which is shorter than its diff:
```python
import functools

import jax
import jax.numpy as jnp
from jax import lax
from jax.experimental import pallas as pl
from jax.experimental.pallas import tpu as pltpu
from jax.sharding import PartitionSpec as P

LANES = 128
F32 = jnp.float32
BF16 = jnp.bfloat16


def round_up(value, unit):
    return -(-value // unit) * unit


def iota(shape, dim):
    return lax.broadcasted_iota(jnp.int32, shape, dim)


def split(value, pieces):
    out = []
    for _ in range(pieces - 1):
        piece = value.astype(BF16)
        out.append(piece)
        value = value - piece.astype(F32)
    out.append(value.astype(BF16))
    return out


def mm(left, right, trans=False):
    dims = (((1,), (1 if trans else 0,)), ((), ()))
    return lax.dot_general(left, right, dims, preferred_element_type=F32)


def mm_exact(value, choice):
    total = None
    for piece in split(value, 3):
        part = mm(piece, choice)
        total = part if total is None else total + part
    return total


def ones_where(mask):
    return jnp.where(mask, 1.0, 0.0).astype(BF16)


def call(kernel, outs, scratch=(), flops=0):
    def run(*args):
        moved = sum(a.size * 4 for a in args) + sum(
            4 * functools.reduce(lambda p, q: p * q, o) for o in outs
        )
        return pl.pallas_call(
            kernel,
            out_shape=[jax.ShapeDtypeStruct(o, F32) for o in outs],
            in_specs=[pl.BlockSpec(memory_space=pltpu.VMEM)] * len(args),
            out_specs=[pl.BlockSpec(memory_space=pltpu.VMEM)] * len(outs),
            scratch_shapes=[pltpu.VMEM(s, t) for s, t in scratch],
            cost_estimate=pl.CostEstimate(
                flops=flops, bytes_accessed=moved, transcendentals=0
            ),
            compiler_params=pltpu.CompilerParams(vmem_limit_bytes=40 * 2**20),
        )(*args)

    return run


def chunk_of(slots):
    for groups in (5, 4, 3, 2, 1):
        if slots % (groups * LANES) == 0:
            return groups * LANES


def pick(field, idx_ref, out_ref):
    _, rows, depth = field.shape
    slots = idx_ref.shape[1]
    blocks = slots // LANES
    chunk = chunk_of(slots)
    flat = field.reshape(3 * rows, depth)
    left = jnp.concatenate(split(flat, 2), axis=0)
    for start in range(0, slots, chunk):
        row = idx_ref[0:1, start : start + chunk]
        deep = idx_ref[1:2, start : start + chunk]
        right = ones_where(iota((depth, chunk), 0) == deep)
        found = mm(left, right)
        found = found[: 3 * rows] + found[3 * rows :]
        here = iota((rows, chunk), 0) == row
        for comp in range(3):
            part = jnp.where(here, found[comp * rows : (comp + 1) * rows], 0.0)
            line = jnp.sum(part, axis=0, keepdims=True)
            for piece in range(chunk // LANES):
                at = comp * blocks + start // LANES + piece
                out_ref[at : at + 1, :] = line[:, piece * LANES : (piece + 1) * LANES]
    pad = out_ref.shape[0] - 3 * blocks
    if pad:
        out_ref[3 * blocks :, :] = jnp.zeros((pad, LANES), F32)


def times_diag(d_ref, field):
    nx, ny, nz = d_ref.shape[1:]
    return jnp.stack(
        [
            sum(d_ref[3 * a + b] * field[b] for b in range(3)).reshape(nx * ny, nz)
            for a in range(3)
        ]
    )


def first_kernel(idx_ref, v_ref, d_ref, out_ref):
    pick(times_diag(d_ref, [v_ref[b] for b in range(3)]), idx_ref, out_ref)


def spread_matrix(wells, width):
    shape = (wells, wells * width)
    gap = iota(shape, 1) - width * iota(shape, 0)
    return ones_where((gap >= 0) & (gap < width))


def last_matrix(wells, width, comp):
    shape = (wells * width, wells)
    return ones_where(iota(shape, 0) == width * iota(shape, 1) + (width - 3 + comp))


def prep_kernel(g_ref, couple_ref, h_ref, e_ref, apart_ref, part_ref):
    chunks, width, span_all = g_ref.shape
    wells = couple_ref.shape[2]
    span = width // 3
    for lane in range(0, span_all, LANES):
        part_ref[...] = g_ref[:, :, lane : lane + LANES]
        for comp in range(3):
            apart_ref[comp, :, :, lane : lane + LANES] = part_ref[
                :, pl.ds(comp, span, stride=3), :
            ]
    spread = spread_matrix(wells, width)
    heads = [g_ref[:, d, :] for d in range(3)]
    for b in range(3):
        total = sum(
            heads[d] * mm_exact(couple_ref[3 * d + b], spread)[:chunks] for d in range(3)
        )
        h_ref[b] = jnp.zeros(h_ref.shape[1:], F32)
        h_ref[b, :chunks, :] = total
        full = h_ref[b]
        for a in range(3):
            e_ref[3 * a + b] = mm_exact(full, last_matrix(wells, width, a))


def solve_kernel(
    idx_ref, low_ref, mid_ref, high_ref, g_ref, h_ref, e_ref,
    down_ref, keep_ref, up_ref,
    pool_ref, r_ref, q_ref, tail_ref, p_ref, y_ref, ohr_ref, w_ref,
):
    _, chunks, span, span_all = g_ref.shape
    width = 3 * span
    wells = span_all // width
    slots = idx_ref.shape[1]
    blocks = slots // LANES
    rows = pool_ref.shape[1]
    tile = low_ref.shape[0] // 3
    group = wells * span
    pool_ref[:, 9 * blocks :, :] = jnp.zeros((3, rows - 9 * blocks, LANES), F32)
    for a in range(3):
        for b, src in enumerate((low_ref, mid_ref, high_ref)):
            for comp in range(3):
                at = (a * 3 + b) * blocks
                pool_ref[comp, at : at + blocks, :] = src[
                    a * tile + comp * blocks : a * tile + (comp + 1) * blocks, :
                ]
    pooled = pool_ref[...].reshape(3 * rows, LANES)
    left = jnp.concatenate(split(pooled, 2), axis=1)
    size = chunk_of(slots)
    r_ref[...] = jnp.zeros(r_ref.shape, F32)
    for start in range(0, slots, size):
        high = idx_ref[2:3, start : start + size]
        low = idx_ref[3:4, start : start + size]
        right = ones_where((iota((2 * LANES, size), 0) & (LANES - 1)) == low)
        found = mm(left, right)
        here = iota((rows, size), 0) == high
        ohr_ref[:, start : start + size] = ones_where(here)
        for comp in range(3):
            part = jnp.where(here, found[comp * rows : (comp + 1) * rows], 0.0)
            line = jnp.sum(part, axis=0, keepdims=True)
            for piece in range(size // group):
                at = start // group + piece
                r_ref[comp, at : at + 1, :] = line[:, piece * group : (piece + 1) * group]
    two = (2 * group, span_all)
    well_of = lax.shift_right_logical(iota(two, 0) & (group - 1), (span - 1).bit_length())
    gap = iota(two, 1) - width * well_of
    spread = ones_where((gap >= 0) & (gap < width))
    own = (iota((span, group), 1) & (span - 1)) == iota((span, group), 0)
    total = None
    for comp in range(3):
        values = r_ref[comp][:chunks]
        wide = jnp.where(own[None], values[:, None, :], 0.0).reshape(chunks * span, group)
        lifted = mm(jnp.concatenate(split(wide, 2), axis=1), spread)
        lifted = lifted.reshape(chunks, span, span_all)
        part = g_ref[comp] * lifted
        total = part if total is None else total + part
    q_ref[...] = jnp.zeros(q_ref.shape, F32)
    q_ref[:chunks, :] = jnp.sum(total, axis=1)
    plain = q_ref[...]
    for a in range(3):
        tail_ref[a] = mm_exact(plain, last_matrix(wells, width, a))
    p_ref[...] = jnp.zeros(p_ref.shape, F32)
    state = [jnp.zeros((1, wells), F32)] * 3
    for c in range(chunks - 1):
        state = [
            tail_ref[a, c : c + 1, :]
            - (
                e_ref[3 * a, c : c + 1, :] * state[0]
                + e_ref[3 * a + 1, c : c + 1, :] * state[1]
                + e_ref[3 * a + 2, c : c + 1, :] * state[2]
            )
            for a in range(3)
        ]
        for a in range(3):
            p_ref[a, c + 1 : c + 2, :] = state[a]
    wide_well = spread_matrix(wells, width)
    for b in range(3):
        plain = plain - h_ref[b] * mm_exact(p_ref[b], wide_well)
    square = (span_all, span_all)
    lane = iota((1, span_all), 1)
    comp_of = lax.div(lane, jnp.int32(group))
    rest = lax.rem(lane, jnp.int32(group))
    source = width * lax.div(rest, jnp.int32(span)) + 3 * lax.rem(rest, jnp.int32(span)) + comp_of
    y_ref[...] = mm_exact(plain, ones_where(iota(square, 0) == source))
    for c in range(chunks):
        low = idx_ref[3:4, c * group : (c + 1) * group]
        match = iota((LANES, group), 0) == low
        for comp in range(3):
            value = y_ref[c : c + 1, comp * group : (comp + 1) * group]
            for place, piece in enumerate(split(value, 2)):
                at = (place * 3 + comp) * LANES
                w_ref[at : at + LANES, c * group : (c + 1) * group] = jnp.where(
                    match, piece.astype(F32), 0.0
                ).astype(BF16)
    spread_out = mm(ohr_ref[...], w_ref[...], trans=True)
    spread_out = spread_out[:, : 3 * LANES] + spread_out[:, 3 * LANES :]
    pool_ref[0] = spread_out[:, :LANES]
    pool_ref[1] = spread_out[:, LANES : 2 * LANES]
    pool_ref[2] = spread_out[:, 2 * LANES :]
    for a, dst in enumerate((down_ref, keep_ref, up_ref)):
        dst[...] = jnp.zeros(dst.shape, F32)
        for b in range(3):
            for comp in range(3):
                at = (a * 3 + b) * blocks
                dst[b * tile + comp * blocks : b * tile + (comp + 1) * blocks, :] = pool_ref[
                    comp, at : at + blocks, :
                ]


def add_kernel(x_ref, y_ref, z_ref, low_ref, mid_ref, high_ref):
    tile = low_ref.shape[0]
    for place, dst in enumerate((low_ref, mid_ref, high_ref)):
        part = slice(place * tile, (place + 1) * tile)
        dst[...] = x_ref[part, :] + y_ref[part, :] + z_ref[part, :]


def place_kernel(
    idx_ref, v_ref, inv_ref, x_ref, y_ref, z_ref,
    out_ref, xl_ref, xh_ref, yl_ref, yh_ref,
    left_ref, right_ref,
):
    nx, ny, nz = v_ref.shape[1:]
    rows = nx * ny
    slots = idx_ref.shape[1]
    blocks = slots // LANES
    back = x_ref[...] + y_ref[...] + z_ref[...]
    pieces = [piece.astype(F32) for piece in split(back, 2)]
    for block in range(blocks):
        lanes = slice(block * LANES, (block + 1) * LANES)
        here = iota((rows, LANES), 0) == idx_ref[0:1, lanes]
        right_ref[:, lanes] = ones_where(iota((nz, LANES), 0) == idx_ref[1:2, lanes])
        for place, piece in enumerate(pieces):
            for comp in range(3):
                at = comp * blocks + block
                group = (place * 3 + comp) * rows
                left_ref[group : group + rows, lanes] = jnp.where(
                    here, piece[at : at + 1, :], 0.0
                ).astype(BF16)
    placed = mm(left_ref[...], right_ref[...], trans=True)
    placed = placed[: 3 * rows] + placed[3 * rows :]
    for a in range(3):
        own = sum(inv_ref[3 * a + b] * v_ref[b] for b in range(3))
        out_ref[a] = own + placed[a * rows : (a + 1) * rows].reshape(nx, ny, nz)
        xl_ref[a] = out_ref[a, 0]
        xh_ref[a] = out_ref[a, nx - 1]
        yl_ref[a] = out_ref[a, :, 0, :]
        yh_ref[a] = out_ref[a, :, ny - 1, :]


def jacobian(z_ref, xl_ref, xh_ref, yl_ref, yh_ref, d_ref, off_ref, store):
    nx, ny, nz = z_ref.shape[1:]
    row = iota((ny, nz), 0)
    lane = iota((ny, nz), 1)
    for x in range(nx):
        beside = []
        for b in range(3):
            own = z_ref[b, x]
            beside.append(
                [
                    z_ref[b, x - 1] if x else xl_ref[b],
                    z_ref[b, x + 1] if x < nx - 1 else xh_ref[b],
                    jnp.where(row == 0, yl_ref[b, x : x + 1, :], pltpu.roll(own, 1, 0)),
                    jnp.where(row == ny - 1, yh_ref[b, x : x + 1, :], pltpu.roll(own, ny - 1, 0)),
                    jnp.where(lane == 0, 0.0, pltpu.roll(own, 1, 1)),
                    jnp.where(lane == nz - 1, 0.0, pltpu.roll(own, nz - 1, 1)),
                ]
            )
        for a in range(3):
            total = sum(d_ref[3 * a + b, x] * z_ref[b, x] for b in range(3))
            for face in range(6):
                for b in range(3):
                    total = total + off_ref[face, 3 * a + b, x] * beside[b][face]
            store(a, x, total)


def next_kernel(
    idx_ref, z_ref, xl_ref, xh_ref, yl_ref, yh_ref, d_ref, off_ref, v_ref,
    w_ref, t_ref, out_ref,
):
    def store(a, x, value):
        w_ref[a, x] = value
        t_ref[a, x] = value - v_ref[a, x]

    jacobian(z_ref, xl_ref, xh_ref, yl_ref, yh_ref, d_ref, off_ref, store)
    pick(times_diag(d_ref, [t_ref[b] for b in range(3)]), idx_ref, out_ref)


def gram_kernel(
    z_ref, xl_ref, xh_ref, yl_ref, yh_ref, d_ref, off_ref, v_ref, w1_ref,
    w_ref, sums_ref,
):
    def store(a, x, value):
        w_ref[a, x] = value

    jacobian(z_ref, xl_ref, xh_ref, yl_ref, yh_ref, d_ref, off_ref, store)
    one, two, rhs = w1_ref[...], w_ref[...], v_ref[...]
    top_one = jnp.maximum(jnp.max(jnp.abs(one)), 1e-30)
    top_two = jnp.maximum(jnp.max(jnp.abs(two)), 1e-30)
    one = one * (1.0 / jnp.full((1, 1), top_one))
    two = two * (1.0 / jnp.full((1, 1), top_two))
    sums = [
        jnp.sum(one * one), jnp.sum(one * two), jnp.sum(two * two),
        jnp.sum(one * rhs), jnp.sum(two * rhs), top_one, top_two,
    ]
    line = iota(sums_ref.shape, 0)
    total = jnp.zeros(sums_ref.shape, F32)
    for place, value in enumerate(sums):
        total = jnp.where(line == place, value, total)
    sums_ref[...] = total


def final_kernel(
    all_ref, v_ref, z1_ref, z2_ref, w1_ref, w2_ref, sol_ref, res_ref
):
    every = [all_ref[:, place, :] for place in range(7)]
    top_one = jnp.max(every[5], axis=0, keepdims=True)
    top_two = jnp.max(every[6], axis=0, keepdims=True)
    one = every[5] / top_one
    two = every[6] / top_two

    def add(value):
        return jnp.sum(value, axis=0, keepdims=True)

    g11 = add(every[0] * one * one)
    g12 = add(every[1] * one * two)
    g22 = add(every[2] * two * two)
    r1 = add(every[3] * one)
    r2 = add(every[4] * two)
    det = g11 * g22 - g12 * g12
    y1 = ((g22 * r1 - g12 * r2) / det / top_one)[:, :1]
    y2 = ((g11 * r2 - g12 * r1) / det / top_two)[:, :1]
    sol_ref[...] = y1 * z1_ref[...] + y2 * z2_ref[...]
    res_ref[...] = v_ref[...] - y1 * w1_ref[...] - y2 * w2_ref[...]


def shift(value, axis, step):
    count = lax.axis_size(axis)
    pairs = [(i, i + step) for i in range(count) if 0 <= i + step < count]
    return lax.ppermute(value, axis, pairs)


def body(
    right_side,
    diag_blocks,
    off_blocks,
    cell_inverse,
    send_cells,
    recv_index,
    seg_count,
    span_inverse,
    span_couple,
):
    _, nx, ny, nz = right_side.shape
    slots = send_cells.shape[1]
    wells, longest = recv_index.shape
    chunks, width, span_all = span_inverse.shape
    span = width // 3
    blocks = slots // LANES
    tile = round_up(3 * blocks, 16)
    rows = round_up(9 * blocks, 16)
    tall = round_up(chunks, 16)
    live = jnp.arange(longest)[None, :] < seg_count[:, None]
    index = jnp.where(live, recv_index, -1)
    index = index.reshape(wells, chunks, span).transpose(1, 0, 2).reshape(1, wells * longest)
    idx = jnp.concatenate(
        [send_cells // nz, send_cells % nz, index >> 7, index & (LANES - 1)], axis=0
    )
    couple = jnp.pad(span_couple.transpose(1, 0, 2), ((0, 0), (0, tall - chunks), (0, 0)))
    h, e, apart = call(
        prep_kernel,
        [(3, tall, span_all), (9, tall, wells), (3, chunks, span, span_all)],
        [((chunks, width, LANES), F32)],
    )(span_inverse, couple)

    def precondition(vector, picked):
        left, right = shift(picked, "gx", 1), shift(picked, "gx", -1)
        mid = jnp.concatenate([left, picked, right], axis=0)
        low, high = shift(mid, "gy", 1), shift(mid, "gy", -1)
        down, keep, up = call(
            solve_kernel,
            [(3 * tile, LANES)] * 3,
            [
                ((3, rows, LANES), F32),
                ((3, tall, wells * span), F32),
                ((tall, span_all), F32),
                ((3, tall, wells), F32),
                ((3, tall, wells), F32),
                ((tall, span_all), F32),
                ((rows, slots), BF16),
                ((6 * LANES, slots), BF16),
            ],
            flops=4 * 10**9,
        )(idx, low, mid, high, apart, h, e)
        down, up = shift(down, "gx", -1), shift(up, "gx", 1)
        low, keep, high = call(add_kernel, [(tile, LANES)] * 3)(down, keep, up)
        low, high = shift(low, "gy", -1), shift(high, "gy", 1)
        z, xl, xh, yl, yh = call(
            place_kernel,
            [(3, nx, ny, nz), (3, ny, nz), (3, ny, nz), (3, nx, nz), (3, nx, nz)],
            [((6 * nx * ny, slots), BF16), ((nz, slots), BF16)],
            flops=10**9,
        )(idx, vector, cell_inverse, low, keep, high)
        xl, xh = shift(xh, "gx", 1), shift(xl, "gx", -1)
        yl, yh = shift(yh, "gy", 1), shift(yl, "gy", -1)
        return z, (xl, xh, yl, yh)

    field = right_side.shape
    (picked,) = call(first_kernel, [(tile, LANES)], flops=10**9)(idx, right_side, diag_blocks)
    z1, faces = precondition(right_side, picked)
    w1, turned, picked = call(next_kernel, [field, field, (tile, LANES)], flops=10**9)(
        idx, z1, *faces, diag_blocks, off_blocks, right_side
    )
    z2, faces = precondition(turned, picked)
    w2, sums = call(gram_kernel, [field, (8, LANES)])(
        z2, *faces, diag_blocks, off_blocks, right_side, w1
    )
    every = lax.all_gather(sums, ("gx", "gy"))
    return tuple(
        call(final_kernel, [field, field])(every, right_side, z1, z2, w1, w2)
    )


def solution(mesh):
    return jax.shard_map(
        body,
        mesh=mesh,
        in_specs=(
            P(None, "gx", "gy", None),
            P(None, "gx", "gy", None),
            P(None, None, "gx", "gy", None),
            P(None, "gx", "gy", None),
            P(("gx", "gy"), None),
            P(("gx", "gy"), None),
            P(("gx", "gy")),
            P(None, None, ("gx", "gy")),
            P(None, None, ("gx", "gy")),
        ),
        out_specs=(P(None, "gx", "gy", None), P(None, "gx", "gy", None)),
        check_vma=False,
    )
```

time: 811 us -> 165 us (0.20); the launches traced: 801 us -> 164 us
  local copies, waits for them, and re-layouts: 247 us -> 2.7 us
  other arithmetic: 236 us -> 1.65 us
  blocking collectives: 205 us -> 44.4 us
  Pallas kernels: 0 us -> 20.2 us
  between operations: 14.1 us -> 1.08 us
    psum x5 -> x0, blocking collectives: 205 us -> none  [the longest x2 84.4 us: orthogonalize(): lax.psum(jnp.stack([jnp.sum(image * vector) for vector in basis]), ('gx',...]
    scatter-add x4 -> x0, other arithmetic: 102 us -> none  [the longest x2 52.4 us: body(): jnp.zeros((3, 9 * picked.shape[1]), jnp.float32).at[:, recv_list]]
    gather x6 -> x0, local copies, waits for them, and re-layouts: 63.4 us -> none  [the longest x2 23 us: body(): arrived = jnp.take(gather_values(picked), recv_list, axis=1)]
    slice x109 -> x0, local copies, waits for them, and re-layouts: 62.2 us -> none  [the longest x2 38.7 us: block_apply(): vector[0]]
    reduce_sum x57 -> x0, other arithmetic: 59 us -> none  [the longest x50 52.6 us: advance(): solved = jnp.sum(block_inverse * block_rhs[:, :, None], axis=0).T]
    all_gather x0 -> x1, blocking collectives: none -> 44.4 us  [body(): every = lax.all_gather(sums, ('gx', 'gy'))]
    add x70 -> x0, other arithmetic: 40.2 us -> none  [block_apply(): matrix[3 * a] * vector[0] + matrix[3 * a + 1] * vector[1]]
    reshape x11 -> x0, local copies, waits for them, and re-layouts: 36.6 us -> none  [the longest x2 18.7 us: return_values(): slots.reshape(count, 3, 3, -1)]
  transfers between devices with their start and end apart: 28 -> 24, of which waited for: 8 -> 12; matrix products, arithmetic and copies ran while one was open for 11% -> 0% of each run, Pallas kernels for 0% -> 1%
where the time goes in v1:
time: 165 us; the launch traced here: 164 us
  starting transfers between devices  66.6 us (40%)
  blocking collectives  44.4 us (27%)
  waiting for transfers between devices  27.8 us (17%)
  Pallas kernels  20.2 us (12%)
  local copies, waits for them, and re-layouts  2.7 us (2%)
    ppermute x24, starting transfers between devices, shift(): return lax.ppermute(value, axis, pairs)  66.6 us
    all_gather x1, blocking collectives, body(): every = lax.all_gather(sums, ('gx', 'gy'))  44.4 us
    ppermute x24, waiting for transfers between devices, shift(): return lax.ppermute(value, axis, pairs)  27.8 us
    pallas_call x11, Pallas kernels, run(): pl.pallas_call(kernel, out_shape=[jax.ShapeDtypeStruct(o, F32) for o in o...  20.2 us
  transfers between devices with their start and end apart: 24, of which 12 were waited for; matrix products, arithmetic and copies ran while one was open for 0% of the time, Pallas kernels for 1%

profile of v1, /device:TPU:0, one launch (start us, length us, event | category | flops | bytes accessed | tf_op | source)
XLA Modules:
  0.0 164.4 jit_solution(1238862134900637304)
XLA Ops:
  7.1 5.5 %collective-permute-start = (f32[80,128]{1,0:T(8,128)S(1)}, f32[80,128]{1,0:T(8,128)S(1)}, u32[]{:S(2)}, u32[]{:S(2)}) collective-permute-start(f32[80,128]{1,0:T(8,128)S(1)} %shard_map.104), channel_id=1, source_target_pairs={{0,4},{4,8},{8,12},{12,16},{16,20},{20,24},{24,28},{1,5},{5,9},{9,... | collective-permute-start | bytes 122888 | tf_op jit(solution)/shard_map/ppermute | solution.py:382
  12.7 1.6 collective-permute-done
  15.6 3.0 %collective-permute-start.2 = (f32[240,128]{1,0:T(8,128)S(1)}, f32[240,128]{1,0:T(8,128)S(1)}, u32[]{:S(2)}, u32[]{:S(2)}) collective-permute-start(f32[240,128]{1,0:T(8,128)S(1)} %pad_maximum_fusion.mid_ref), channel_id=1, source_target_pairs={{0,1},{1,2},{2,3},{4,5},{5,6},{6,7},{8,9},{9,10},{10,11},{12,13},{... | collective-permute-start | bytes 368648 | tf_op jit(solution)/shard_map/ppermute | solution.py:382
  20.2 6.0 %shard_map.106 = (f32[240,128]{1,0:T(8,128)S(1)}, f32[240,128]{1,0:T(8,128)S(1)}, f32[240,128]{1,0:T(8,128)S(1)}) custom-call(s32[4,3200]{1,0:T(4,128)S(1)} %pad_add_fusion.idx_ref, f32[240,128]{1,0:T(8,128)S(1)} %collective-permute-done.2.low_ref, f32[240,128]{1,0:T(8,128)S(1)} %pad_maximum_fusion.mid_ref, f32[240,128]{1,0:T(8,128)S(1)} %collective-permute-done.3.high_ref, ...), custom_call_target="tpu_custom_call" | custom-call | flops 4000000000 | bytes 2788352 | tf_op jit(solution)/shard_map/pallas_call | solution.py:55
  27.5 5.5 %collective-permute-start.5 = (f32[240,128]{1,0:T(8,128)S(1)}, f32[240,128]{1,0:T(8,128)S(1)}, u32[]{:S(2)}, u32[]{:S(2)}) collective-permute-start(f32[240,128]{1,0:T(8,128)S(1)} %get-tuple-element.37), channel_id=1, source_target_pairs={{0,4},{4,8},{8,12},{12,16},{16,20},{20,24},{24,28},{1,5},{5,9},{9,... | collective-permute-start | bytes 368648 | tf_op jit(solution)/shard_map/ppermute | solution.py:382
  33.0 1.5 collective-permute-done.4.x_ref
  34.5 4.0 %collective-permute-done.5.z_ref = f32[240,128]{1,0:T(8,128)S(1)} collective-permute-done((f32[240,128]{1,0:T(8,128)S(1)}, f32[240,128]{1,0:T(8,128)S(1)}, u32[]{:S(2)}, u32[]{:S(2)}) %collective-permute-start.5) | collective-permute-done | bytes 122912 | tf_op jit(solution)/shard_map/ppermute | solution.py:382
  39.8 3.0 %collective-permute-start.7 = (f32[80,128]{1,0:T(8,128)S(1)}, f32[80,128]{1,0:T(8,128)S(1)}, u32[]{:S(2)}, u32[]{:S(2)}) collective-permute-start(f32[80,128]{1,0:T(8,128)S(1)} %get-tuple-element.40), channel_id=1, source_target_pairs={{0,1},{1,2},{2,3},{4,5},{5,6},{6,7},{8,9},{9,10},{10,11},{12,13},{... | collective-permute-start | bytes 122888 | tf_op jit(solution)/shard_map/ppermute | solution.py:382
  43.7 1.4 shard_map.108
  45.1 4.4 %collective-permute-start.8 = (f32[3,16,256]{2,1,0:T(8,128)S(1)}, f32[3,16,256]{2,1,0:T(8,128)S(1)}, u32[]{:S(2)}, u32[]{:S(2)}) collective-permute-start(f32[3,16,256]{2,1,0:T(8,128)S(1)} %get-tuple-element.42), channel_id=1, source_target_pairs={{0,4},{4,8},{8,12},{12,16},{16,20},{20,24},{24,28},{1,5},{5,9},{9,... | collective-permute-start | bytes 147464 | tf_op jit(solution)/shard_map/ppermute | solution.py:382
  50.8 3.2 %collective-permute-start.10 = (f32[3,4,256]{2,1,0:T(4,128)S(1)}, f32[3,4,256]{2,1,0:T(4,128)S(1)}, u32[]{:S(2)}, u32[]{:S(2)}) collective-permute-start(f32[3,4,256]{2,1,0:T(4,128)S(1)} %get-tuple-element.44), channel_id=1, source_target_pairs={{0,1},{1,2},{2,3},{4,5},{5,6},{6,7},{8,9},{9,10},{10,11},{12,13},{... | collective-permute-start | bytes 36872 | tf_op jit(solution)/shard_map/ppermute | solution.py:382
  55.4 3.9 %collective-permute-done.11.yh_ref = f32[3,4,256]{2,1,0:T(4,128)S(1)} collective-permute-done((f32[3,4,256]{2,1,0:T(4,128)S(1)}, f32[3,4,256]{2,1,0:T(4,128)S(1)}, u32[]{:S(2)}, u32[]{:S(2)}) %collective-permute-start.11) | collective-permute-done | bytes 12320 | tf_op jit(solution)/shard_map/ppermute | solution.py:382
  59.2 1.5 shard_map.109
  60.7 5.5 %collective-permute-start.12 = (f32[80,128]{1,0:T(8,128)S(1)}, f32[80,128]{1,0:T(8,128)S(1)}, u32[]{:S(2)}, u32[]{:S(2)}) collective-permute-start(f32[80,128]{1,0:T(8,128)S(1)} %get-tuple-element.47), channel_id=1, source_target_pairs={{0,4},{4,8},{8,12},{12,16},{16,20},{20,24},{24,28},{1,5},{5,9},{9,... | collective-permute-start | bytes 122888 | tf_op jit(solution)/shard_map/ppermute | solution.py:382
  67.8 5.1 %collective-permute-done.13 = f32[80,128]{1,0:T(8,128)S(1)} collective-permute-done((f32[80,128]{1,0:T(8,128)S(1)}, f32[80,128]{1,0:T(8,128)S(1)}, u32[]{:S(2)}, u32[]{:S(2)}) %collective-permute-start.13) | collective-permute-done | bytes 40992 | tf_op jit(solution)/shard_map/ppermute | solution.py:382
  74.3 4.0 %collective-permute-start.14 = (f32[240,128]{1,0:T(8,128)S(1)}, f32[240,128]{1,0:T(8,128)S(1)}, u32[]{:S(2)}, u32[]{:S(2)}) collective-permute-start(f32[240,128]{1,0:T(8,128)S(1)} %constant_dynamic-update-slice_fusion.mid_ref), channel_id=1, source_target_pairs={{0,1},{1,2},{2,3},{4,5},{5,6},{6,7},{8,9},{9,10},{10,11},{12,13},{... | collective-permute-start | bytes 368648 | tf_op jit(solution)/shard_map/ppermute | solution.py:382
  79.1 6.0 %shard_map.110 = (f32[240,128]{1,0:T(8,128)S(1)}, f32[240,128]{1,0:T(8,128)S(1)}, f32[240,128]{1,0:T(8,128)S(1)}) custom-call(s32[4,3200]{1,0:T(4,128)S(1)} %pad_add_fusion.idx_ref, f32[240,128]{1,0:T(8,128)S(1)} %collective-permute-done.14.low_ref, f32[240,128]{1,0:T(8,128)S(1)} %constant_dynamic-update-slice_fusion.mid_ref, ...), custom_call_target="tpu_custom_call" | custom-call | flops 4000000000 | bytes 2788352 | tf_op jit(solution)/shard_map/pallas_call | solution.py:55
  86.4 5.2 %collective-permute-start.17 = (f32[240,128]{1,0:T(8,128)S(1)}, f32[240,128]{1,0:T(8,128)S(1)}, u32[]{:S(2)}, u32[]{:S(2)}) collective-permute-start(f32[240,128]{1,0:T(8,128)S(1)} %get-tuple-element.50), channel_id=1, source_target_pairs={{0,4},{4,8},{8,12},{12,16},{16,20},{20,24},{24,28},{1,5},{5,9},{9,... | collective-permute-start | bytes 368648 | tf_op jit(solution)/shard_map/ppermute | solution.py:382
  92.4 3.9 %collective-permute-done.17.z_ref = f32[240,128]{1,0:T(8,128)S(1)} collective-permute-done((f32[240,128]{1,0:T(8,128)S(1)}, f32[240,128]{1,0:T(8,128)S(1)}, u32[]{:S(2)}, u32[]{:S(2)}) %collective-permute-start.17) | collective-permute-done | bytes 122912 | tf_op jit(solution)/shard_map/ppermute | solution.py:382
  97.7 3.1 %collective-permute-start.19 = (f32[80,128]{1,0:T(8,128)S(1)}, f32[80,128]{1,0:T(8,128)S(1)}, u32[]{:S(2)}, u32[]{:S(2)}) collective-permute-start(f32[80,128]{1,0:T(8,128)S(1)} %get-tuple-element.53), channel_id=1, source_target_pairs={{0,1},{1,2},{2,3},{4,5},{5,6},{6,7},{8,9},{9,10},{10,11},{12,13},{... | collective-permute-start | bytes 122888 | tf_op jit(solution)/shard_map/ppermute | solution.py:382
  103.0 4.3 %collective-permute-start.20 = (f32[3,16,256]{2,1,0:T(8,128)S(1)}, f32[3,16,256]{2,1,0:T(8,128)S(1)}, u32[]{:S(2)}, u32[]{:S(2)}) collective-permute-start(f32[3,16,256]{2,1,0:T(8,128)S(1)} %get-tuple-element.55), channel_id=1, source_target_pairs={{0,4},{4,8},{8,12},{12,16},{16,20},{20,24},{24,28},{1,5},{5,9},{9,... | collective-permute-start | bytes 147464 | tf_op jit(solution)/shard_map/ppermute | solution.py:382
  108.7 4.4 %collective-permute-start.22 = (f32[3,4,256]{2,1,0:T(4,128)S(1)}, f32[3,4,256]{2,1,0:T(4,128)S(1)}, u32[]{:S(2)}, u32[]{:S(2)}) collective-permute-start(f32[3,4,256]{2,1,0:T(4,128)S(1)} %get-tuple-element.57), channel_id=1, source_target_pairs={{0,1},{1,2},{2,3},{4,5},{5,6},{6,7},{8,9},{9,10},{10,11},{12,13},{... | collective-permute-start | bytes 36872 | tf_op jit(solution)/shard_map/ppermute | solution.py:382
  114.4 3.9 %collective-permute-done.23.yh_ref = f32[3,4,256]{2,1,0:T(4,128)S(1)} collective-permute-done((f32[3,4,256]{2,1,0:T(4,128)S(1)}, f32[3,4,256]{2,1,0:T(4,128)S(1)}, u32[]{:S(2)}, u32[]{:S(2)}) %collective-permute-start.23) | collective-permute-done | bytes 12320 | tf_op jit(solution)/shard_map/ppermute | solution.py:382
  119.1 44.4 %all-gather = f32[256,128]{1,0:T(8,128)S(1)} all-gather(f32[8,128]{1,0:T(8,128)S(1)} %get-tuple-element.60), channel_id=2, replica_groups=mesh['gx'=8,'gy'=4] {'gx','gy'}, dimensions={0}, use_global_device_ids=true | all-gather | bytes 135168 | tf_op jit(solution)/shard_map/all_gather | solution.py:460
  (68 shorter events, 29.0 us)
Async XLA Ops:
  5.8 6.8 %collective-permute-start.1 = (f32[80,128]{1,0:T(8,128)S(1)}, f32[80,128]{1,0:T(8,128)S(1)}, u32[]{:S(2)}, u32[]{:S(2)}) collective-permute-start(f32[80,128]{1,0:T(8,128)S(1)} %shard_map.104), channel_id=1, source_target_pairs={{4,0},{8,4},{12,8},{16,12},{20,16},{24,20},{28,24},{5,1},{9,5},{13... | collective-permute-start | bytes 122888 | tf_op jit(solution)/shard_map/ppermute | solution.py:382
  7.1 7.2 %collective-permute-start = (f32[80,128]{1,0:T(8,128)S(1)}, f32[80,128]{1,0:T(8,128)S(1)}, u32[]{:S(2)}, u32[]{:S(2)}) collective-permute-start(f32[80,128]{1,0:T(8,128)S(1)} %shard_map.104), channel_id=1, source_target_pairs={{0,4},{4,8},{8,12},{12,16},{16,20},{20,24},{24,28},{1,5},{5,9},{9,... | collective-permute-start | bytes 122888 | tf_op jit(solution)/shard_map/ppermute | solution.py:382
  14.3 5.8 %collective-permute-start.3 = (f32[240,128]{1,0:T(8,128)S(1)}, f32[240,128]{1,0:T(8,128)S(1)}, u32[]{:S(2)}, u32[]{:S(2)}) collective-permute-start(f32[240,128]{1,0:T(8,128)S(1)} %pad_maximum_fusion.mid_ref), channel_id=1, source_target_pairs={{1,0},{2,1},{3,2},{5,4},{6,5},{7,6},{9,8},{10,9},{11,10},{13,12},{... | collective-permute-start | bytes 368648 | tf_op jit(solution)/shard_map/ppermute | solution.py:382
  15.6 4.5 %collective-permute-start.2 = (f32[240,128]{1,0:T(8,128)S(1)}, f32[240,128]{1,0:T(8,128)S(1)}, u32[]{:S(2)}, u32[]{:S(2)}) collective-permute-start(f32[240,128]{1,0:T(8,128)S(1)} %pad_maximum_fusion.mid_ref), channel_id=1, source_target_pairs={{0,1},{1,2},{2,3},{4,5},{5,6},{6,7},{8,9},{9,10},{10,11},{12,13},{... | collective-permute-start | bytes 368648 | tf_op jit(solution)/shard_map/ppermute | solution.py:382
  26.2 8.3 %collective-permute-start.4 = (f32[240,128]{1,0:T(8,128)S(1)}, f32[240,128]{1,0:T(8,128)S(1)}, u32[]{:S(2)}, u32[]{:S(2)}) collective-permute-start(f32[240,128]{1,0:T(8,128)S(1)} %get-tuple-element.35), channel_id=1, source_target_pairs={{4,0},{8,4},{12,8},{16,12},{20,16},{24,20},{28,24},{5,1},{9,5},{13... | collective-permute-start | bytes 368648 | tf_op jit(solution)/shard_map/ppermute | solution.py:382
  27.5 11.0 %collective-permute-start.5 = (f32[240,128]{1,0:T(8,128)S(1)}, f32[240,128]{1,0:T(8,128)S(1)}, u32[]{:S(2)}, u32[]{:S(2)}) collective-permute-start(f32[240,128]{1,0:T(8,128)S(1)} %get-tuple-element.37), channel_id=1, source_target_pairs={{0,4},{4,8},{8,12},{12,16},{16,20},{20,24},{24,28},{1,5},{5,9},{9,... | collective-permute-start | bytes 368648 | tf_op jit(solution)/shard_map/ppermute | solution.py:382
  38.5 4.3 %collective-permute-start.6 = (f32[80,128]{1,0:T(8,128)S(1)}, f32[80,128]{1,0:T(8,128)S(1)}, u32[]{:S(2)}, u32[]{:S(2)}) collective-permute-start(f32[80,128]{1,0:T(8,128)S(1)} %get-tuple-element.38), channel_id=1, source_target_pairs={{1,0},{2,1},{3,2},{5,4},{6,5},{7,6},{9,8},{10,9},{11,10},{13,12},{... | collective-permute-start | bytes 122888 | tf_op jit(solution)/shard_map/ppermute | solution.py:382
  39.8 3.9 %collective-permute-start.7 = (f32[80,128]{1,0:T(8,128)S(1)}, f32[80,128]{1,0:T(8,128)S(1)}, u32[]{:S(2)}, u32[]{:S(2)}) collective-permute-start(f32[80,128]{1,0:T(8,128)S(1)} %get-tuple-element.40), channel_id=1, source_target_pairs={{0,1},{1,2},{2,3},{4,5},{5,6},{6,7},{8,9},{9,10},{10,11},{12,13},{... | collective-permute-start | bytes 122888 | tf_op jit(solution)/shard_map/ppermute | solution.py:382
  45.1 14.1 %collective-permute-start.8 = (f32[3,16,256]{2,1,0:T(8,128)S(1)}, f32[3,16,256]{2,1,0:T(8,128)S(1)}, u32[]{:S(2)}, u32[]{:S(2)}) collective-permute-start(f32[3,16,256]{2,1,0:T(8,128)S(1)} %get-tuple-element.42), channel_id=1, source_target_pairs={{0,4},{4,8},{8,12},{12,16},{16,20},{20,24},{24,28},{1,5},{5,9},{9,... | collective-permute-start | bytes 147464 | tf_op jit(solution)/shard_map/ppermute | solution.py:382
  49.5 9.7 %collective-permute-start.9 = (f32[3,16,256]{2,1,0:T(8,128)S(1)}, f32[3,16,256]{2,1,0:T(8,128)S(1)}, u32[]{:S(2)}, u32[]{:S(2)}) collective-permute-start(f32[3,16,256]{2,1,0:T(8,128)S(1)} %get-tuple-element.43), channel_id=1, source_target_pairs={{4,0},{8,4},{12,8},{16,12},{20,16},{24,20},{28,24},{5,1},{9,5},{13... | collective-permute-start | bytes 147464 | tf_op jit(solution)/shard_map/ppermute | solution.py:382
  50.8 4.5 %collective-permute-start.10 = (f32[3,4,256]{2,1,0:T(4,128)S(1)}, f32[3,4,256]{2,1,0:T(4,128)S(1)}, u32[]{:S(2)}, u32[]{:S(2)}) collective-permute-start(f32[3,4,256]{2,1,0:T(4,128)S(1)} %get-tuple-element.44), channel_id=1, source_target_pairs={{0,1},{1,2},{2,3},{4,5},{5,6},{6,7},{8,9},{9,10},{10,11},{12,13},{... | collective-permute-start | bytes 36872 | tf_op jit(solution)/shard_map/ppermute | solution.py:382
  54.0 5.2 %collective-permute-start.11 = (f32[3,4,256]{2,1,0:T(4,128)S(1)}, f32[3,4,256]{2,1,0:T(4,128)S(1)}, u32[]{:S(2)}, u32[]{:S(2)}) collective-permute-start(f32[3,4,256]{2,1,0:T(4,128)S(1)} %get-tuple-element.45), channel_id=1, source_target_pairs={{1,0},{2,1},{3,2},{5,4},{6,5},{7,6},{9,8},{10,9},{11,10},{13,12},{... | collective-permute-start | bytes 36872 | tf_op jit(solution)/shard_map/ppermute | solution.py:382
  60.7 7.1 %collective-permute-start.12 = (f32[80,128]{1,0:T(8,128)S(1)}, f32[80,128]{1,0:T(8,128)S(1)}, u32[]{:S(2)}, u32[]{:S(2)}) collective-permute-start(f32[80,128]{1,0:T(8,128)S(1)} %get-tuple-element.47), channel_id=1, source_target_pairs={{0,4},{4,8},{8,12},{12,16},{16,20},{20,24},{24,28},{1,5},{5,9},{9,... | collective-permute-start | bytes 122888 | tf_op jit(solution)/shard_map/ppermute | solution.py:382
  66.2 6.8 %collective-permute-start.13 = (f32[80,128]{1,0:T(8,128)S(1)}, f32[80,128]{1,0:T(8,128)S(1)}, u32[]{:S(2)}, u32[]{:S(2)}) collective-permute-start(f32[80,128]{1,0:T(8,128)S(1)} %get-tuple-element.47), channel_id=1, source_target_pairs={{4,0},{8,4},{12,8},{16,12},{20,16},{24,20},{28,24},{5,1},{9,5},{13... | collective-permute-start | bytes 122888 | tf_op jit(solution)/shard_map/ppermute | solution.py:382
  73.0 5.3 %collective-permute-start.15 = (f32[240,128]{1,0:T(8,128)S(1)}, f32[240,128]{1,0:T(8,128)S(1)}, u32[]{:S(2)}, u32[]{:S(2)}) collective-permute-start(f32[240,128]{1,0:T(8,128)S(1)} %constant_dynamic-update-slice_fusion.mid_ref), channel_id=1, source_target_pairs={{1,0},{2,1},{3,2},{5,4},{6,5},{7,6},{9,8},{10,9},{11,10},{13,12},{... | collective-permute-start | bytes 368648 | tf_op jit(solution)/shard_map/ppermute | solution.py:382
  74.3 4.8 %collective-permute-start.14 = (f32[240,128]{1,0:T(8,128)S(1)}, f32[240,128]{1,0:T(8,128)S(1)}, u32[]{:S(2)}, u32[]{:S(2)}) collective-permute-start(f32[240,128]{1,0:T(8,128)S(1)} %constant_dynamic-update-slice_fusion.mid_ref), channel_id=1, source_target_pairs={{0,1},{1,2},{2,3},{4,5},{5,6},{6,7},{8,9},{9,10},{10,11},{12,13},{... | collective-permute-start | bytes 368648 | tf_op jit(solution)/shard_map/ppermute | solution.py:382
  85.1 7.4 %collective-permute-start.16 = (f32[240,128]{1,0:T(8,128)S(1)}, f32[240,128]{1,0:T(8,128)S(1)}, u32[]{:S(2)}, u32[]{:S(2)}) collective-permute-start(f32[240,128]{1,0:T(8,128)S(1)} %get-tuple-element.48), channel_id=1, source_target_pairs={{4,0},{8,4},{12,8},{16,12},{20,16},{24,20},{28,24},{5,1},{9,5},{13... | collective-permute-start | bytes 368648 | tf_op jit(solution)/shard_map/ppermute | solution.py:382
  86.4 10.0 %collective-permute-start.17 = (f32[240,128]{1,0:T(8,128)S(1)}, f32[240,128]{1,0:T(8,128)S(1)}, u32[]{:S(2)}, u32[]{:S(2)}) collective-permute-start(f32[240,128]{1,0:T(8,128)S(1)} %get-tuple-element.50), channel_id=1, source_target_pairs={{0,4},{4,8},{8,12},{12,16},{16,20},{20,24},{24,28},{1,5},{5,9},{9,... | collective-permute-start | bytes 368648 | tf_op jit(solution)/shard_map/ppermute | solution.py:382
  96.4 4.4 %collective-permute-start.18 = (f32[80,128]{1,0:T(8,128)S(1)}, f32[80,128]{1,0:T(8,128)S(1)}, u32[]{:S(2)}, u32[]{:S(2)}) collective-permute-start(f32[80,128]{1,0:T(8,128)S(1)} %get-tuple-element.51), channel_id=1, source_target_pairs={{1,0},{2,1},{3,2},{5,4},{6,5},{7,6},{9,8},{10,9},{11,10},{13,12},{... | collective-permute-start | bytes 122888 | tf_op jit(solution)/shard_map/ppermute | solution.py:382
  97.7 4.0 %collective-permute-start.19 = (f32[80,128]{1,0:T(8,128)S(1)}, f32[80,128]{1,0:T(8,128)S(1)}, u32[]{:S(2)}, u32[]{:S(2)}) collective-permute-start(f32[80,128]{1,0:T(8,128)S(1)} %get-tuple-element.53), channel_id=1, source_target_pairs={{0,1},{1,2},{2,3},{4,5},{5,6},{6,7},{8,9},{9,10},{10,11},{12,13},{... | collective-permute-start | bytes 122888 | tf_op jit(solution)/shard_map/ppermute | solution.py:382
  103.0 15.2 %collective-permute-start.20 = (f32[3,16,256]{2,1,0:T(8,128)S(1)}, f32[3,16,256]{2,1,0:T(8,128)S(1)}, u32[]{:S(2)}, u32[]{:S(2)}) collective-permute-start(f32[3,16,256]{2,1,0:T(8,128)S(1)} %get-tuple-element.55), channel_id=1, source_target_pairs={{0,4},{4,8},{8,12},{12,16},{16,20},{20,24},{24,28},{1,5},{5,9},{9,... | collective-permute-start | bytes 147464 | tf_op jit(solution)/shard_map/ppermute | solution.py:382
  107.4 10.9 %collective-permute-start.21 = (f32[3,16,256]{2,1,0:T(8,128)S(1)}, f32[3,16,256]{2,1,0:T(8,128)S(1)}, u32[]{:S(2)}, u32[]{:S(2)}) collective-permute-start(f32[3,16,256]{2,1,0:T(8,128)S(1)} %get-tuple-element.56), channel_id=1, source_target_pairs={{4,0},{8,4},{12,8},{16,12},{20,16},{24,20},{28,24},{5,1},{9,5},{13... | collective-permute-start | bytes 147464 | tf_op jit(solution)/shard_map/ppermute | solution.py:382
  108.7 5.7 %collective-permute-start.22 = (f32[3,4,256]{2,1,0:T(4,128)S(1)}, f32[3,4,256]{2,1,0:T(4,128)S(1)}, u32[]{:S(2)}, u32[]{:S(2)}) collective-permute-start(f32[3,4,256]{2,1,0:T(4,128)S(1)} %get-tuple-element.57), channel_id=1, source_target_pairs={{0,1},{1,2},{2,3},{4,5},{5,6},{6,7},{8,9},{9,10},{10,11},{12,13},{... | collective-permute-start | bytes 36872 | tf_op jit(solution)/shard_map/ppermute | solution.py:382
  113.1 5.2 %collective-permute-start.23 = (f32[3,4,256]{2,1,0:T(4,128)S(1)}, f32[3,4,256]{2,1,0:T(4,128)S(1)}, u32[]{:S(2)}, u32[]{:S(2)}) collective-permute-start(f32[3,4,256]{2,1,0:T(4,128)S(1)} %get-tuple-element.58), channel_id=1, source_target_pairs={{1,0},{2,1},{3,2},{5,4},{6,5},{7,6},{9,8},{10,9},{11,10},{13,12},{... | collective-permute-start | bytes 36872 | tf_op jit(solution)/shard_map/ppermute | solution.py:382
  (8 other events, 131.5 us)

commit v2 on v1

--- a/solution.py
+++ b/solution.py
@@ -47,7 +47,7 @@
     return jnp.where(mask, 1.0, 0.0).astype(BF16)
 
 
-def call(kernel, outs, scratch=(), flops=0):
+def call(kernel, outs, scratch=(), flops=0, scalars=0):
     def run(*args):
         moved = sum(a.size * 4 for a in args) + sum(
             4 * functools.reduce(lambda p, q: p * q, o) for o in outs
@@ -55,7 +55,8 @@
         return pl.pallas_call(
             kernel,
             out_shape=[jax.ShapeDtypeStruct(o, F32) for o in outs],
-            in_specs=[pl.BlockSpec(memory_space=pltpu.VMEM)] * len(args),
+            in_specs=[pl.BlockSpec(memory_space=pltpu.SMEM)] * scalars
+            + [pl.BlockSpec(memory_space=pltpu.VMEM)] * (len(args) - scalars),
             out_specs=[pl.BlockSpec(memory_space=pltpu.VMEM)] * len(outs),
             scratch_shapes=[pltpu.VMEM(s, t) for s, t in scratch],
             cost_estimate=pl.CostEstimate(
@@ -73,16 +74,21 @@
             return groups * LANES
 
 
-def pick(field, idx_ref, out_ref):
+def row_and_depth(cells, nz):
+    if nz & (nz - 1) == 0:
+        return lax.shift_right_logical(cells, nz.bit_length() - 1), cells & (nz - 1)
+    return lax.div(cells, jnp.int32(nz)), lax.rem(cells, jnp.int32(nz))
+
+
+def pick(field, cells_ref, out_ref):
     _, rows, depth = field.shape
-    slots = idx_ref.shape[1]
+    slots = cells_ref.shape[1]
     blocks = slots // LANES
     chunk = chunk_of(slots)
     flat = field.reshape(3 * rows, depth)
     left = jnp.concatenate(split(flat, 2), axis=0)
     for start in range(0, slots, chunk):
-        row = idx_ref[0:1, start : start + chunk]
-        deep = idx_ref[1:2, start : start + chunk]
+        row, deep = row_and_depth(cells_ref[:, start : start + chunk], depth)
         right = ones_where(iota((depth, chunk), 0) == deep)
         found = mm(left, right)
         found = found[: 3 * rows] + found[3 * rows :]
@@ -108,8 +114,8 @@
     )
 
 
-def first_kernel(idx_ref, v_ref, d_ref, out_ref):
-    pick(times_diag(d_ref, [v_ref[b] for b in range(3)]), idx_ref, out_ref)
+def first_kernel(cells_ref, v_ref, d_ref, out_ref):
+    pick(times_diag(d_ref, [v_ref[b] for b in range(3)]), cells_ref, out_ref)
 
 
 def spread_matrix(wells, width):
@@ -147,8 +153,8 @@
 
 
 def solve_kernel(
-    idx_ref, low_ref, mid_ref, high_ref, g_ref, h_ref, e_ref,
-    down_ref, keep_ref, up_ref,
+    odd_ref, idx_ref, own_ref, even_ref, next_ref, g_ref, h_ref, e_ref,
+    keep_ref, to_even_ref, to_next_ref,
     pool_ref, r_ref, q_ref, tail_ref, p_ref, y_ref, ohr_ref, w_ref,
 ):
     _, chunks, span, span_all = g_ref.shape
@@ -157,23 +163,31 @@
     slots = idx_ref.shape[1]
     blocks = slots // LANES
     rows = pool_ref.shape[1]
-    tile = low_ref.shape[0] // 3
+    tile = own_ref.shape[0] // 3
     group = wells * span
+    odd_x, odd_y = odd_ref[0] == 1, odd_ref[1] == 1
     pool_ref[:, 9 * blocks :, :] = jnp.zeros((3, rows - 9 * blocks, LANES), F32)
-    for a in range(3):
-        for b, src in enumerate((low_ref, mid_ref, high_ref)):
+    own, even, following = own_ref[...], even_ref[...], next_ref[...]
+    columns = (
+        jnp.where(odd_y, even, following), own, jnp.where(odd_y, following, even)
+    )
+    for b, column in enumerate(columns):
+        own, even, following = column[:tile], column[tile : 2 * tile], column[2 * tile :]
+        parts = (jnp.where(odd_x, even, following), own, jnp.where(odd_x, following, even))
+        for a, part in enumerate(parts):
             for comp in range(3):
                 at = (a * 3 + b) * blocks
-                pool_ref[comp, at : at + blocks, :] = src[
-                    a * tile + comp * blocks : a * tile + (comp + 1) * blocks, :
+                pool_ref[comp, at : at + blocks, :] = part[
+                    comp * blocks : (comp + 1) * blocks
                 ]
     pooled = pool_ref[...].reshape(3 * rows, LANES)
     left = jnp.concatenate(split(pooled, 2), axis=1)
     size = chunk_of(slots)
     r_ref[...] = jnp.zeros(r_ref.shape, F32)
     for start in range(0, slots, size):
-        high = idx_ref[2:3, start : start + size]
-        low = idx_ref[3:4, start : start + size]
+        place = idx_ref[:, start : start + size]
+        high = lax.shift_right_arithmetic(place, LANES.bit_length() - 1)
+        low = place & (LANES - 1)
         right = ones_where((iota((2 * LANES, size), 0) & (LANES - 1)) == low)
         found = mm(left, right)
         here = iota((rows, size), 0) == high
@@ -226,7 +240,7 @@
     source = width * lax.div(rest, jnp.int32(span)) + 3 * lax.rem(rest, jnp.int32(span)) + comp_of
     y_ref[...] = mm_exact(plain, ones_where(iota(square, 0) == source))
     for c in range(chunks):
-        low = idx_ref[3:4, c * group : (c + 1) * group]
+        low = idx_ref[:, c * group : (c + 1) * group] & (LANES - 1)
         match = iota((LANES, group), 0) == low
         for comp in range(3):
             value = y_ref[c : c + 1, comp * group : (comp + 1) * group]
@@ -240,38 +254,49 @@
     pool_ref[0] = spread_out[:, :LANES]
     pool_ref[1] = spread_out[:, LANES : 2 * LANES]
     pool_ref[2] = spread_out[:, 2 * LANES :]
-    for a, dst in enumerate((down_ref, keep_ref, up_ref)):
+    for dst in (keep_ref, to_even_ref, to_next_ref):
         dst[...] = jnp.zeros(dst.shape, F32)
-        for b in range(3):
-            for comp in range(3):
+    for a in range(3):
+        for comp in range(3):
+            parts = []
+            for b in range(3):
                 at = (a * 3 + b) * blocks
-                dst[b * tile + comp * blocks : b * tile + (comp + 1) * blocks, :] = pool_ref[
-                    comp, at : at + blocks, :
-                ]
-
-
-def add_kernel(x_ref, y_ref, z_ref, low_ref, mid_ref, high_ref):
-    tile = low_ref.shape[0]
-    for place, dst in enumerate((low_ref, mid_ref, high_ref)):
-        part = slice(place * tile, (place + 1) * tile)
-        dst[...] = x_ref[part, :] + y_ref[part, :] + z_ref[part, :]
+                parts.append(pool_ref[comp, at : at + blocks, :])
+            at = slice(a * tile + comp * blocks, a * tile + (comp + 1) * blocks)
+            keep_ref[at, :] = parts[1]
+            to_even_ref[at, :] = jnp.where(odd_y, parts[0], parts[2])
+            to_next_ref[at, :] = jnp.where(odd_y, parts[2], parts[0])
+
+
+def add_kernel(odd_ref, x_ref, y_ref, z_ref, keep_ref, to_even_ref, to_next_ref):
+    tile = keep_ref.shape[0]
+    odd_x = odd_ref[0] == 1
+    low, mid, high = [
+        x_ref[part, :] + y_ref[part, :] + z_ref[part, :]
+        for part in [slice(place * tile, (place + 1) * tile) for place in range(3)]
+    ]
+    keep_ref[...] = mid
+    to_even_ref[...] = jnp.where(odd_x, low, high)
+    to_next_ref[...] = jnp.where(odd_x, high, low)
 
 
 def place_kernel(
-    idx_ref, v_ref, inv_ref, x_ref, y_ref, z_ref,
-    out_ref, xl_ref, xh_ref, yl_ref, yh_ref,
+    odd_ref, cells_ref, v_ref, inv_ref, x_ref, y_ref, z_ref,
+    out_ref, x_even_ref, x_next_ref, y_even_ref, y_next_ref,
     left_ref, right_ref,
 ):
+    odd_x, odd_y = odd_ref[0] == 1, odd_ref[1] == 1
     nx, ny, nz = v_ref.shape[1:]
     rows = nx * ny
-    slots = idx_ref.shape[1]
+    slots = cells_ref.shape[1]
     blocks = slots // LANES
     back = x_ref[...] + y_ref[...] + z_ref[...]
     pieces = [piece.astype(F32) for piece in split(back, 2)]
     for block in range(blocks):
         lanes = slice(block * LANES, (block + 1) * LANES)
-        here = iota((rows, LANES), 0) == idx_ref[0:1, lanes]
-        right_ref[:, lanes] = ones_where(iota((nz, LANES), 0) == idx_ref[1:2, lanes])
+        row, deep = row_and_depth(cells_ref[:, lanes], nz)
+        here = iota((rows, LANES), 0) == row
+        right_ref[:, lanes] = ones_where(iota((nz, LANES), 0) == deep)
         for place, piece in enumerate(pieces):
             for comp in range(3):
                 at = comp * blocks + block
@@ -284,14 +309,20 @@
     for a in range(3):
         own = sum(inv_ref[3 * a + b] * v_ref[b] for b in range(3))
         out_ref[a] = own + placed[a * rows : (a + 1) * rows].reshape(nx, ny, nz)
-        xl_ref[a] = out_ref[a, 0]
-        xh_ref[a] = out_ref[a, nx - 1]
-        yl_ref[a] = out_ref[a, :, 0, :]
-        yh_ref[a] = out_ref[a, :, ny - 1, :]
-
-
-def jacobian(z_ref, xl_ref, xh_ref, yl_ref, yh_ref, d_ref, off_ref, store):
+        low, high = out_ref[a, 0], out_ref[a, nx - 1]
+        x_even_ref[a] = jnp.where(odd_x, low, high)
+        x_next_ref[a] = jnp.where(odd_x, high, low)
+        low, high = out_ref[a, :, 0, :], out_ref[a, :, ny - 1, :]
+        y_even_ref[a] = jnp.where(odd_y, low, high)
+        y_next_ref[a] = jnp.where(odd_y, high, low)
+
+
+def jacobian(odd_ref, z_ref, faces, d_ref, off_ref, store):
     nx, ny, nz = z_ref.shape[1:]
+    odd_x, odd_y = odd_ref[0] == 1, odd_ref[1] == 1
+    x_even, x_next, y_even, y_next = [face[...] for face in faces]
+    xl, xh = jnp.where(odd_x, x_even, x_next), jnp.where(odd_x, x_next, x_even)
+    yl, yh = jnp.where(odd_y, y_even, y_next), jnp.where(odd_y, y_next, y_even)
     row = iota((ny, nz), 0)
     lane = iota((ny, nz), 1)
     for x in range(nx):
@@ -300,10 +331,10 @@
             own = z_ref[b, x]
             beside.append(
                 [
-                    z_ref[b, x - 1] if x else xl_ref[b],
-                    z_ref[b, x + 1] if x < nx - 1 else xh_ref[b],
-                    jnp.where(row == 0, yl_ref[b, x : x + 1, :], pltpu.roll(own, 1, 0)),
-                    jnp.where(row == ny - 1, yh_ref[b, x : x + 1, :], pltpu.roll(own, ny - 1, 0)),
+                    z_ref[b, x - 1] if x else xl[b],
+                    z_ref[b, x + 1] if x < nx - 1 else xh[b],
+                    jnp.where(row == 0, yl[b, x : x + 1, :], pltpu.roll(own, 1, 0)),
+                    jnp.where(row == ny - 1, yh[b, x : x + 1, :], pltpu.roll(own, ny - 1, 0)),
                     jnp.where(lane == 0, 0.0, pltpu.roll(own, 1, 1)),
                     jnp.where(lane == nz - 1, 0.0, pltpu.roll(own, nz - 1, 1)),
                 ]
@@ -317,25 +348,25 @@
 
 
 def next_kernel(
-    idx_ref, z_ref, xl_ref, xh_ref, yl_ref, yh_ref, d_ref, off_ref, v_ref,
+    odd_ref, cells_ref, z_ref, f0_ref, f1_ref, f2_ref, f3_ref, d_ref, off_ref, v_ref,
     w_ref, t_ref, out_ref,
 ):
     def store(a, x, value):
         w_ref[a, x] = value
         t_ref[a, x] = value - v_ref[a, x]
 
-    jacobian(z_ref, xl_ref, xh_ref, yl_ref, yh_ref, d_ref, off_ref, store)
-    pick(times_diag(d_ref, [t_ref[b] for b in range(3)]), idx_ref, out_ref)
+    jacobian(odd_ref, z_ref, (f0_ref, f1_ref, f2_ref, f3_ref), d_ref, off_ref, store)
+    pick(times_diag(d_ref, [t_ref[b] for b in range(3)]), cells_ref, out_ref)
 
 
 def gram_kernel(
-    z_ref, xl_ref, xh_ref, yl_ref, yh_ref, d_ref, off_ref, v_ref, w1_ref,
+    odd_ref, z_ref, f0_ref, f1_ref, f2_ref, f3_ref, d_ref, off_ref, v_ref, w1_ref,
     w_ref, sums_ref,
 ):
     def store(a, x, value):
         w_ref[a, x] = value
 
-    jacobian(z_ref, xl_ref, xh_ref, yl_ref, yh_ref, d_ref, off_ref, store)
+    jacobian(odd_ref, z_ref, (f0_ref, f1_ref, f2_ref, f3_ref), d_ref, off_ref, store)
     one, two, rhs = w1_ref[...], w_ref[...], v_ref[...]
     top_one = jnp.maximum(jnp.max(jnp.abs(one)), 1e-30)
     top_two = jnp.maximum(jnp.max(jnp.abs(two)), 1e-30)
@@ -376,10 +407,15 @@
     res_ref[...] = v_ref[...] - y1 * w1_ref[...] - y2 * w2_ref[...]
 
 
-def shift(value, axis, step):
+def swap(axis, to_even, to_next):
     count = lax.axis_size(axis)
-    pairs = [(i, i + step) for i in range(count) if 0 <= i + step < count]
-    return lax.ppermute(value, axis, pairs)
+    out = []
+    for first, value in ((0, to_even), (1, to_next)):
+        pairs = []
+        for i in range(first, count - 1, 2):
+            pairs += [(i, i + 1), (i + 1, i)]
+        out.append(lax.ppermute(value, axis, pairs))
+    return out
 
 
 def body(
@@ -402,12 +438,14 @@
     tile = round_up(3 * blocks, 16)
     rows = round_up(9 * blocks, 16)
     tall = round_up(chunks, 16)
+    odd = jnp.stack([lax.axis_index("gx") % 2, lax.axis_index("gy") % 2]).astype(jnp.int32)
+    field = right_side.shape
+    (picked,) = call(first_kernel, [(tile, LANES)], flops=10**9)(
+        send_cells, right_side, diag_blocks
+    )
     live = jnp.arange(longest)[None, :] < seg_count[:, None]
     index = jnp.where(live, recv_index, -1)
     index = index.reshape(wells, chunks, span).transpose(1, 0, 2).reshape(1, wells * longest)
-    idx = jnp.concatenate(
-        [send_cells // nz, send_cells % nz, index >> 7, index & (LANES - 1)], axis=0
-    )
     couple = jnp.pad(span_couple.transpose(1, 0, 2), ((0, 0), (0, tall - chunks), (0, 0)))
     h, e, apart = call(
         prep_kernel,
@@ -416,10 +454,9 @@
     )(span_inverse, couple)
 
     def precondition(vector, picked):
-        left, right = shift(picked, "gx", 1), shift(picked, "gx", -1)
-        mid = jnp.concatenate([left, picked, right], axis=0)
-        low, high = shift(mid, "gy", 1), shift(mid, "gy", -1)
-        down, keep, up = call(
+        column = jnp.concatenate([picked, *swap("gx", picked, picked)], axis=0)
+        even, following = swap("gy", column, column)
+        keep, even, following = call(
             solve_kernel,
             [(3 * tile, LANES)] * 3,
             [
@@ -433,31 +470,31 @@
                 ((6 * LANES, slots), BF16),
             ],
             flops=4 * 10**9,
-        )(idx, low, mid, high, apart, h, e)
-        down, up = shift(down, "gx", -1), shift(up, "gx", 1)
-        low, keep, high = call(add_kernel, [(tile, LANES)] * 3)(down, keep, up)
-        low, high = shift(low, "gy", -1), shift(high, "gy", 1)
-        z, xl, xh, yl, yh = call(
+            scalars=1,
+        )(odd, index, column, even, following, apart, h, e)
+        even, following = swap("gy", even, following)
+        keep, even, following = call(add_kernel, [(tile, LANES)] * 3, scalars=1)(
+            odd, keep, even, following
+        )
+        even, following = swap("gx", even, following)
+        z, *faces = call(
             place_kernel,
-            [(3, nx, ny, nz), (3, ny, nz), (3, ny, nz), (3, nx, nz), (3, nx, nz)],
+            [(3, nx, ny, nz)] + [(3, ny, nz)] * 2 + [(3, nx, nz)] * 2,
             [((6 * nx * ny, slots), BF16), ((nz, slots), BF16)],
             flops=10**9,
-        )(idx, vector, cell_inverse, low, keep, high)
-        xl, xh = shift(xh, "gx", 1), shift(xl, "gx", -1)
-        yl, yh = shift(yh, "gy", 1), shift(yl, "gy", -1)
-        return z, (xl, xh, yl, yh)
-
-    field = right_side.shape
-    (picked,) = call(first_kernel, [(tile, LANES)], flops=10**9)(idx, right_side, diag_blocks)
+            scalars=1,
+        )(odd, send_cells, vector, cell_inverse, keep, even, following)
+        return z, swap("gx", *faces[:2]) + swap("gy", *faces[2:])
+
     z1, faces = precondition(right_side, picked)
-    w1, turned, picked = call(next_kernel, [field, field, (tile, LANES)], flops=10**9)(
-        idx, z1, *faces, diag_blocks, off_blocks, right_side
+    w1, turned, picked = call(
+        next_kernel, [field, field, (tile, LANES)], flops=10**9, scalars=1
+    )(odd, send_cells, z1, *faces, diag_blocks, off_blocks, right_side)
+    z2, faces = precondition(turned, picked)
+    w2, sums = call(gram_kernel, [field, (8, LANES)], scalars=1)(
+        odd, z2, *faces, diag_blocks, off_blocks, right_side, w1
     )
-    z2, faces = precondition(turned, picked)
-    w2, sums = call(gram_kernel, [field, (8, LANES)])(
-        z2, *faces, diag_blocks, off_blocks, right_side, w1
-    )
-    every = lax.all_gather(sums, ("gx", "gy"))
+    every = lax.all_gather(lax.all_gather(sums, "gy"), "gx").reshape(-1, 8, LANES)
     return tuple(
         call(final_kernel, [field, field])(every, right_side, z1, z2, w1, w2)
     )

time: 165 us -> 139 us (0.84)
  waiting for transfers between devices: 27.8 us -> 8.59 us
  starting transfers between devices: 66.6 us -> 56.7 us
  Pallas kernels: 20.2 us -> 24.6 us
    ppermute x24, waiting for transfers between devices: 27.8 us -> 8.59 us  [swap(): out.append(lax.ppermute(value, axis, pairs))]
    ppermute x24, starting transfers between devices: 66.6 us -> 56.7 us  [swap(): out.append(lax.ppermute(value, axis, pairs))]
    pallas_call x11, Pallas kernels: 20.2 us -> 24.6 us  [run(): pl.pallas_call(kernel, out_shape=[jax.ShapeDtypeStruct(o, F32) for o in o...]
    all_gather x1 -> x2, blocking collectives: 44.4 us -> 44.4 us  [the longest x1 33.9 us: body(): lax.all_gather(lax.all_gather(sums, 'gy'), 'gx').reshape(-1, 8, LANES)]
  transfers between devices with their start and end apart: 24 -> 24, of which waited for: 12 -> 9; matrix products, arithmetic and copies ran while one was open for 0% -> 0% of each run, Pallas kernels for 1% -> 1%
where the time goes in v2:
time: 139 us
  starting transfers between devices  56.7 us (41%)
  blocking collectives  44.4 us (32%)
  Pallas kernels  24.6 us (18%)
  waiting for transfers between devices  8.59 us (6%)
  local copies, waits for them, and re-layouts  3.16 us (2%)
    ppermute x24, starting transfers between devices, swap(): out.append(lax.ppermute(value, axis, pairs))  56.7 us
    all_gather x1, blocking collectives, body(): lax.all_gather(lax.all_gather(sums, 'gy'), 'gx').reshape(-1, 8, LANES)  33.9 us
    pallas_call x11, Pallas kernels, run(): pl.pallas_call(kernel, out_shape=[jax.ShapeDtypeStruct(o, F32) for o in o...  24.6 us
    all_gather x1, blocking collectives, body(): lax.all_gather(sums, 'gy')  10.5 us
    ppermute x24, waiting for transfers between devices, swap(): out.append(lax.ppermute(value, axis, pairs))  8.59 us
    unnamed x27, local copies, waits for them, and re-layouts  2.88 us
  transfers between devices with their start and end apart: 24, of which 9 were waited for; matrix products, arithmetic and copies ran while one was open for 0% of the time, Pallas kernels for 1%

profile of v2, /device:TPU:0, one launch (start us, length us, event | category | flops | bytes accessed | tf_op | source)
XLA Modules:
  0.0 138.5 jit_solution(590436590987217601)
XLA Ops:
  5.0 5.8 %collective-permute-start = (f32[80,128]{1,0:T(8,128)S(1)}, f32[80,128]{1,0:T(8,128)S(1)}, u32[]{:S(2)}, u32[]{:S(2)}) collective-permute-start(f32[80,128]{1,0:T(8,128)S(1)} %shard_map.104), channel_id=1, source_target_pairs={{0,4},{4,0},{8,12},{12,8},{16,20},{20,16},{24,28},{28,24},{1,5},{5... | collective-permute-start | bytes 122888 | tf_op jit(solution)/shard_map/ppermute | solution.py:417
  10.8 2.0 %collective-permute-done = f32[80,128]{1,0:T(8,128)S(1)} collective-permute-done((f32[80,128]{1,0:T(8,128)S(1)}, f32[80,128]{1,0:T(8,128)S(1)}, u32[]{:S(2)}, u32[]{:S(2)}) %collective-permute-start) | collective-permute-done | bytes 40992 | tf_op jit(solution)/shard_map/ppermute | solution.py:417
  13.5 2.9 %collective-permute-start.2 = (f32[240,128]{1,0:T(8,128)S(1)}, f32[240,128]{1,0:T(8,128)S(1)}, u32[]{:S(2)}, u32[]{:S(2)}) collective-permute-start(f32[240,128]{1,0:T(8,128)S(1)} %pad_maximum_fusion.own_ref), channel_id=1, source_target_pairs={{0,1},{1,0},{2,3},{3,2},{4,5},{5,4},{6,7},{7,6},{8,9},{9,8},{10,11... | collective-permute-start | bytes 368648 | tf_op jit(solution)/shard_map/ppermute | solution.py:417
  16.9 1.3 shard_map.105
  18.4 6.5 %shard_map.106 = (f32[240,128]{1,0:T(8,128)S(1)}, f32[240,128]{1,0:T(8,128)S(1)}, f32[240,128]{1,0:T(8,128)S(1)}) custom-call(s32[2]{0:T(128)S(1)} %pad_add_fusion.odd_ref, s32[1,3200]{1,0:T(1,128)S(1)} %reshape.15.idx_ref, f32[240,128]{1,0:T(8,128)S(1)} %pad_maximum_fusion.own_ref, f32[240,128]{1,0:T(8,128)S(1)} %collective-permute-done.2.even_ref, ...), custom_call_target="tpu_custom_call" | custom-call | flops 4000000000 | bytes 2749960 | tf_op jit(solution)/shard_map/pallas_call | solution.py:55
  27.0 2.1 %collective-permute-start.6 = (f32[80,128]{1,0:T(8,128)S(1)}, f32[80,128]{1,0:T(8,128)S(1)}, u32[]{:S(2)}, u32[]{:S(2)}) collective-permute-start(f32[80,128]{1,0:T(8,128)S(1)} %get-tuple-element.39), channel_id=1, source_target_pairs={{0,4},{4,0},{8,12},{12,8},{16,20},{20,16},{24,28},{28,24},{1,5},{5... | collective-permute-start | bytes 122888 | tf_op jit(solution)/shard_map/ppermute | solution.py:417
  29.7 1.3 collective-permute-done.6.y_ref
  31.1 2.0 %shard_map.108 = (f32[3,4,16,256]{3,2,1,0:T(8,128)S(1)}, f32[3,16,256]{2,1,0:T(8,128)S(1)}, f32[3,16,256]{2,1,0:T(8,128)S(1)}, f32[3,4,256]{2,1,0:T(4,128)S(1)}, f32[3,4,256]{2,1,0:T(4,128)S(1)}) custom-call(s32[2]{0:T(128)S(1)} %pad_add_fusion.odd_ref, s32[1,3200]{1,0:T(1,128)S(1)} %copy-done.7, f32[3,4,16,256]{3,2,1,0:T(8,128)S(1)} %copy-done.5, ...), custom_call_target="tpu_custom_call" | custom-call | flops 1000000000 | bytes 1241608 | tf_op jit(solution)/shard_map/pallas_call | solution.py:55
  33.1 5.0 %collective-permute-start.8 = (f32[3,16,256]{2,1,0:T(8,128)S(1)}, f32[3,16,256]{2,1,0:T(8,128)S(1)}, u32[]{:S(2)}, u32[]{:S(2)}) collective-permute-start(f32[3,16,256]{2,1,0:T(8,128)S(1)} %get-tuple-element.42), channel_id=1, source_target_pairs={{0,4},{4,0},{8,12},{12,8},{16,20},{20,16},{24,28},{28,24},{1,5},{5... | collective-permute-start | bytes 147464 | tf_op jit(solution)/shard_map/ppermute | solution.py:417
  38.7 3.9 %collective-permute-start.10 = (f32[3,4,256]{2,1,0:T(4,128)S(1)}, f32[3,4,256]{2,1,0:T(4,128)S(1)}, u32[]{:S(2)}, u32[]{:S(2)}) collective-permute-start(f32[3,4,256]{2,1,0:T(4,128)S(1)} %get-tuple-element.44), channel_id=1, source_target_pairs={{0,1},{1,0},{2,3},{3,2},{4,5},{5,4},{6,7},{7,6},{8,9},{9,8},{10,11... | collective-permute-start | bytes 36872 | tf_op jit(solution)/shard_map/ppermute | solution.py:417
  43.5 2.0 %shard_map.109 = (f32[3,4,16,256]{3,2,1,0:T(8,128)S(1)}, f32[3,4,16,256]{3,2,1,0:T(8,128)S(1)}, f32[80,128]{1,0:T(8,128)S(1)}) custom-call(s32[2]{0:T(128)S(1)} %pad_add_fusion.odd_ref, s32[1,3200]{1,0:T(1,128)S(1)} %copy-done.7, f32[3,4,16,256]{3,2,1,0:T(8,128)S(1)} %get-tuple-element.41.z_ref.z1_ref, f32[3,16,256]{2,1,0:T(8,128)S(1)} %collective-permute-done.8.f0_ref, ...), custom_call_target="tpu_custom_call" | custom-call | flops 1000000000 | bytes 5091848 | tf_op jit(solution)/shard_map/pallas_call | solution.py:55
  46.2 6.2 %collective-permute-start.12 = (f32[80,128]{1,0:T(8,128)S(1)}, f32[80,128]{1,0:T(8,128)S(1)}, u32[]{:S(2)}, u32[]{:S(2)}) collective-permute-start(f32[80,128]{1,0:T(8,128)S(1)} %get-tuple-element.47), channel_id=1, source_target_pairs={{0,4},{4,0},{8,12},{12,8},{16,20},{20,16},{24,28},{28,24},{1,5},{5... | collective-permute-start | bytes 122888 | tf_op jit(solution)/shard_map/ppermute | solution.py:417
  52.4 2.0 %collective-permute-done.12 = f32[80,128]{1,0:T(8,128)S(1)} collective-permute-done((f32[80,128]{1,0:T(8,128)S(1)}, f32[80,128]{1,0:T(8,128)S(1)}, u32[]{:S(2)}, u32[]{:S(2)}) %collective-permute-start.12) | collective-permute-done | bytes 40992 | tf_op jit(solution)/shard_map/ppermute | solution.py:417
  55.2 8.3 %collective-permute-start.14 = (f32[240,128]{1,0:T(8,128)S(1)}, f32[240,128]{1,0:T(8,128)S(1)}, u32[]{:S(2)}, u32[]{:S(2)}) collective-permute-start(f32[240,128]{1,0:T(8,128)S(1)} %constant_dynamic-update-slice_fusion.own_ref), channel_id=1, source_target_pairs={{0,1},{1,0},{2,3},{3,2},{4,5},{5,4},{6,7},{7,6},{8,9},{9,8},{10,11... | collective-permute-start | bytes 368648 | tf_op jit(solution)/shard_map/ppermute | solution.py:417
  64.5 6.5 %shard_map.110 = (f32[240,128]{1,0:T(8,128)S(1)}, f32[240,128]{1,0:T(8,128)S(1)}, f32[240,128]{1,0:T(8,128)S(1)}) custom-call(s32[2]{0:T(128)S(1)} %pad_add_fusion.odd_ref, s32[1,3200]{1,0:T(1,128)S(1)} %reshape.15.idx_ref, f32[240,128]{1,0:T(8,128)S(1)} %constant_dynamic-update-slice_fusion.own_ref, f32[240,128]{1,0:T(8,128)S(1)} %collective-permute-done.14.even_ref, ...), custom_call_target="tpu_custom_call" | custom-call | flops 4000000000 | bytes 2749960 | tf_op jit(solution)/shard_map/pallas_call | solution.py:55
  71.0 1.4 %collective-permute-start.16 = (f32[240,128]{1,0:T(8,128)S(1)}, f32[240,128]{1,0:T(8,128)S(1)}, u32[]{:S(2)}, u32[]{:S(2)}) collective-permute-start(f32[240,128]{1,0:T(8,128)S(1)} %get-tuple-element.49), channel_id=1, source_target_pairs={{0,1},{1,0},{2,3},{3,2},{4,5},{5,4},{6,7},{7,6},{8,9},{9,8},{10,11... | collective-permute-start | bytes 368648 | tf_op jit(solution)/shard_map/ppermute | solution.py:417
  74.0 2.9 %collective-permute-start.18 = (f32[80,128]{1,0:T(8,128)S(1)}, f32[80,128]{1,0:T(8,128)S(1)}, u32[]{:S(2)}, u32[]{:S(2)}) collective-permute-start(f32[80,128]{1,0:T(8,128)S(1)} %get-tuple-element.52), channel_id=1, source_target_pairs={{0,4},{4,0},{8,12},{12,8},{16,20},{20,16},{24,28},{28,24},{1,5},{5... | collective-permute-start | bytes 122888 | tf_op jit(solution)/shard_map/ppermute | solution.py:417
  77.5 1.3 collective-permute-done.18.y_ref
  78.8 2.0 %shard_map.112 = (f32[3,4,16,256]{3,2,1,0:T(8,128)S(1)}, f32[3,16,256]{2,1,0:T(8,128)S(1)}, f32[3,16,256]{2,1,0:T(8,128)S(1)}, f32[3,4,256]{2,1,0:T(4,128)S(1)}, f32[3,4,256]{2,1,0:T(4,128)S(1)}) custom-call(s32[2]{0:T(128)S(1)} %pad_add_fusion.odd_ref, s32[1,3200]{1,0:T(1,128)S(1)} %copy-done.7, f32[3,4,16,256]{3,2,1,0:T(8,128)S(1)} %get-tuple-element.46.v_ref, ...), custom_call_target="tpu_custom_call" | custom-call | flops 1000000000 | bytes 1241608 | tf_op jit(solution)/shard_map/pallas_call | solution.py:55
  80.8 5.7 %collective-permute-start.20 = (f32[3,16,256]{2,1,0:T(8,128)S(1)}, f32[3,16,256]{2,1,0:T(8,128)S(1)}, u32[]{:S(2)}, u32[]{:S(2)}) collective-permute-start(f32[3,16,256]{2,1,0:T(8,128)S(1)} %get-tuple-element.55), channel_id=1, source_target_pairs={{0,4},{4,0},{8,12},{12,8},{16,20},{20,16},{24,28},{28,24},{1,5},{5... | collective-permute-start | bytes 147464 | tf_op jit(solution)/shard_map/ppermute | solution.py:417
  87.2 3.9 %collective-permute-start.22 = (f32[3,4,256]{2,1,0:T(4,128)S(1)}, f32[3,4,256]{2,1,0:T(4,128)S(1)}, u32[]{:S(2)}, u32[]{:S(2)}) collective-permute-start(f32[3,4,256]{2,1,0:T(4,128)S(1)} %get-tuple-element.57), channel_id=1, source_target_pairs={{0,1},{1,0},{2,3},{3,2},{4,5},{5,4},{6,7},{7,6},{8,9},{9,8},{10,11... | collective-permute-start | bytes 36872 | tf_op jit(solution)/shard_map/ppermute | solution.py:417
  91.9 1.4 shard_map.113
  93.2 10.5 %all-gather = f32[32,128]{1,0:T(8,128)S(1)} all-gather(f32[8,128]{1,0:T(8,128)S(1)} %get-tuple-element.60), channel_id=2, replica_groups=mesh['gx'=8,'gy'=4] {'gy'}, dimensions={0}, use_global_device_ids=true | all-gather | bytes 20480 | tf_op jit(solution)/shard_map/all_gather | solution.py:497
  103.7 33.9 %all-gather.1.all_ref = f32[32,8,128]{2,1,0:T(8,128)S(1)} all-gather(f32[4,8,128]{2,1,0:T(8,128)S(1)} %bitcast.7), channel_id=3, replica_groups=mesh['gx'=8,'gy'=4] {'gx'}, dimensions={0}, use_global_device_ids=true | all-gather | bytes 147456 | tf_op jit(solution)/shard_map/all_gather | solution.py:497
  (72 shorter events, 17.0 us)
Async XLA Ops:
  4.3 6.5 %collective-permute-start.1 = (f32[80,128]{1,0:T(8,128)S(1)}, f32[80,128]{1,0:T(8,128)S(1)}, u32[]{:S(2)}, u32[]{:S(2)}) collective-permute-start(f32[80,128]{1,0:T(8,128)S(1)} %shard_map.104), channel_id=1, source_target_pairs={{4,8},{8,4},{12,16},{16,12},{20,24},{24,20},{5,9},{9,5},{13,17},{1... | collective-permute-start | bytes 122888 | tf_op jit(solution)/shard_map/ppermute | solution.py:417
  5.0 7.8 %collective-permute-start = (f32[80,128]{1,0:T(8,128)S(1)}, f32[80,128]{1,0:T(8,128)S(1)}, u32[]{:S(2)}, u32[]{:S(2)}) collective-permute-start(f32[80,128]{1,0:T(8,128)S(1)} %shard_map.104), channel_id=1, source_target_pairs={{0,4},{4,0},{8,12},{12,8},{16,20},{20,16},{24,28},{28,24},{1,5},{5... | collective-permute-start | bytes 122888 | tf_op jit(solution)/shard_map/ppermute | solution.py:417
  12.8 5.5 %collective-permute-start.3 = (f32[240,128]{1,0:T(8,128)S(1)}, f32[240,128]{1,0:T(8,128)S(1)}, u32[]{:S(2)}, u32[]{:S(2)}) collective-permute-start(f32[240,128]{1,0:T(8,128)S(1)} %pad_maximum_fusion.own_ref), channel_id=1, source_target_pairs={{1,2},{2,1},{5,6},{6,5},{9,10},{10,9},{13,14},{14,13},{17,18},{18,... | collective-permute-start | bytes 368648 | tf_op jit(solution)/shard_map/ppermute | solution.py:417
  13.5 4.8 %collective-permute-start.2 = (f32[240,128]{1,0:T(8,128)S(1)}, f32[240,128]{1,0:T(8,128)S(1)}, u32[]{:S(2)}, u32[]{:S(2)}) collective-permute-start(f32[240,128]{1,0:T(8,128)S(1)} %pad_maximum_fusion.own_ref), channel_id=1, source_target_pairs={{0,1},{1,0},{2,3},{3,2},{4,5},{5,4},{6,7},{7,6},{8,9},{9,8},{10,11... | collective-permute-start | bytes 368648 | tf_op jit(solution)/shard_map/ppermute | solution.py:417
  24.9 1.6 %collective-permute-start.4 = (f32[240,128]{1,0:T(8,128)S(1)}, f32[240,128]{1,0:T(8,128)S(1)}, u32[]{:S(2)}, u32[]{:S(2)}) collective-permute-start(f32[240,128]{1,0:T(8,128)S(1)} %get-tuple-element.36), channel_id=1, source_target_pairs={{0,1},{1,0},{2,3},{3,2},{4,5},{5,4},{6,7},{7,6},{8,9},{9,8},{10,11... | collective-permute-start | bytes 368648 | tf_op jit(solution)/shard_map/ppermute | solution.py:417
  25.4 1.0 collective-permute-start.5
  27.0 4.1 %collective-permute-start.6 = (f32[80,128]{1,0:T(8,128)S(1)}, f32[80,128]{1,0:T(8,128)S(1)}, u32[]{:S(2)}, u32[]{:S(2)}) collective-permute-start(f32[80,128]{1,0:T(8,128)S(1)} %get-tuple-element.39), channel_id=1, source_target_pairs={{0,4},{4,0},{8,12},{12,8},{16,20},{20,16},{24,28},{28,24},{1,5},{5... | collective-permute-start | bytes 122888 | tf_op jit(solution)/shard_map/ppermute | solution.py:417
  29.1 2.0 %collective-permute-start.7 = (f32[80,128]{1,0:T(8,128)S(1)}, f32[80,128]{1,0:T(8,128)S(1)}, u32[]{:S(2)}, u32[]{:S(2)}) collective-permute-start(f32[80,128]{1,0:T(8,128)S(1)} %get-tuple-element.40), channel_id=1, source_target_pairs={{4,8},{8,4},{12,16},{16,12},{20,24},{24,20},{5,9},{9,5},{13,17},{1... | collective-permute-start | bytes 122888 | tf_op jit(solution)/shard_map/ppermute | solution.py:417
  33.1 10.4 %collective-permute-start.8 = (f32[3,16,256]{2,1,0:T(8,128)S(1)}, f32[3,16,256]{2,1,0:T(8,128)S(1)}, u32[]{:S(2)}, u32[]{:S(2)}) collective-permute-start(f32[3,16,256]{2,1,0:T(8,128)S(1)} %get-tuple-element.42), channel_id=1, source_target_pairs={{0,4},{4,0},{8,12},{12,8},{16,20},{20,16},{24,28},{28,24},{1,5},{5... | collective-permute-start | bytes 147464 | tf_op jit(solution)/shard_map/ppermute | solution.py:417
  38.1 5.4 %collective-permute-start.9 = (f32[3,16,256]{2,1,0:T(8,128)S(1)}, f32[3,16,256]{2,1,0:T(8,128)S(1)}, u32[]{:S(2)}, u32[]{:S(2)}) collective-permute-start(f32[3,16,256]{2,1,0:T(8,128)S(1)} %get-tuple-element.43), channel_id=1, source_target_pairs={{4,8},{8,4},{12,16},{16,12},{20,24},{24,20},{5,9},{9,5},{13,17},{1... | collective-permute-start | bytes 147464 | tf_op jit(solution)/shard_map/ppermute | solution.py:417
  38.7 4.7 %collective-permute-start.10 = (f32[3,4,256]{2,1,0:T(4,128)S(1)}, f32[3,4,256]{2,1,0:T(4,128)S(1)}, u32[]{:S(2)}, u32[]{:S(2)}) collective-permute-start(f32[3,4,256]{2,1,0:T(4,128)S(1)} %get-tuple-element.44), channel_id=1, source_target_pairs={{0,1},{1,0},{2,3},{3,2},{4,5},{5,4},{6,7},{7,6},{8,9},{9,8},{10,11... | collective-permute-start | bytes 36872 | tf_op jit(solution)/shard_map/ppermute | solution.py:417
  42.6 0.8 collective-permute-start.11
  45.5 8.9 %collective-permute-start.13 = (f32[80,128]{1,0:T(8,128)S(1)}, f32[80,128]{1,0:T(8,128)S(1)}, u32[]{:S(2)}, u32[]{:S(2)}) collective-permute-start(f32[80,128]{1,0:T(8,128)S(1)} %get-tuple-element.47), channel_id=1, source_target_pairs={{4,8},{8,4},{12,16},{16,12},{20,24},{24,20},{5,9},{9,5},{13,17},{1... | collective-permute-start | bytes 122888 | tf_op jit(solution)/shard_map/ppermute | solution.py:417
  46.2 8.2 %collective-permute-start.12 = (f32[80,128]{1,0:T(8,128)S(1)}, f32[80,128]{1,0:T(8,128)S(1)}, u32[]{:S(2)}, u32[]{:S(2)}) collective-permute-start(f32[80,128]{1,0:T(8,128)S(1)} %get-tuple-element.47), channel_id=1, source_target_pairs={{0,4},{4,0},{8,12},{12,8},{16,20},{20,16},{24,28},{28,24},{1,5},{5... | collective-permute-start | bytes 122888 | tf_op jit(solution)/shard_map/ppermute | solution.py:417
  54.4 9.2 %collective-permute-start.15 = (f32[240,128]{1,0:T(8,128)S(1)}, f32[240,128]{1,0:T(8,128)S(1)}, u32[]{:S(2)}, u32[]{:S(2)}) collective-permute-start(f32[240,128]{1,0:T(8,128)S(1)} %constant_dynamic-update-slice_fusion.own_ref), channel_id=1, source_target_pairs={{1,2},{2,1},{5,6},{6,5},{9,10},{10,9},{13,14},{14,13},{17,18},{18,... | collective-permute-start | bytes 368648 | tf_op jit(solution)/shard_map/ppermute | solution.py:417
  55.2 9.3 %collective-permute-start.14 = (f32[240,128]{1,0:T(8,128)S(1)}, f32[240,128]{1,0:T(8,128)S(1)}, u32[]{:S(2)}, u32[]{:S(2)}) collective-permute-start(f32[240,128]{1,0:T(8,128)S(1)} %constant_dynamic-update-slice_fusion.own_ref), channel_id=1, source_target_pairs={{0,1},{1,0},{2,3},{3,2},{4,5},{5,4},{6,7},{7,6},{8,9},{9,8},{10,11... | collective-permute-start | bytes 368648 | tf_op jit(solution)/shard_map/ppermute | solution.py:417
  71.0 2.4 %collective-permute-start.16 = (f32[240,128]{1,0:T(8,128)S(1)}, f32[240,128]{1,0:T(8,128)S(1)}, u32[]{:S(2)}, u32[]{:S(2)}) collective-permute-start(f32[240,128]{1,0:T(8,128)S(1)} %get-tuple-element.49), channel_id=1, source_target_pairs={{0,1},{1,0},{2,3},{3,2},{4,5},{5,4},{6,7},{7,6},{8,9},{9,8},{10,11... | collective-permute-start | bytes 368648 | tf_op jit(solution)/shard_map/ppermute | solution.py:417
  72.4 1.0 collective-permute-start.17
  74.0 4.8 %collective-permute-start.18 = (f32[80,128]{1,0:T(8,128)S(1)}, f32[80,128]{1,0:T(8,128)S(1)}, u32[]{:S(2)}, u32[]{:S(2)}) collective-permute-start(f32[80,128]{1,0:T(8,128)S(1)} %get-tuple-element.52), channel_id=1, source_target_pairs={{0,4},{4,0},{8,12},{12,8},{16,20},{20,16},{24,28},{28,24},{1,5},{5... | collective-permute-start | bytes 122888 | tf_op jit(solution)/shard_map/ppermute | solution.py:417
  76.8 2.0 %collective-permute-start.19 = (f32[80,128]{1,0:T(8,128)S(1)}, f32[80,128]{1,0:T(8,128)S(1)}, u32[]{:S(2)}, u32[]{:S(2)}) collective-permute-start(f32[80,128]{1,0:T(8,128)S(1)} %get-tuple-element.53), channel_id=1, source_target_pairs={{4,8},{8,4},{12,16},{16,12},{20,24},{24,20},{5,9},{9,5},{13,17},{1... | collective-permute-start | bytes 122888 | tf_op jit(solution)/shard_map/ppermute | solution.py:417
  80.8 11.1 %collective-permute-start.20 = (f32[3,16,256]{2,1,0:T(8,128)S(1)}, f32[3,16,256]{2,1,0:T(8,128)S(1)}, u32[]{:S(2)}, u32[]{:S(2)}) collective-permute-start(f32[3,16,256]{2,1,0:T(8,128)S(1)} %get-tuple-element.55), channel_id=1, source_target_pairs={{0,4},{4,0},{8,12},{12,8},{16,20},{20,16},{24,28},{28,24},{1,5},{5... | collective-permute-start | bytes 147464 | tf_op jit(solution)/shard_map/ppermute | solution.py:417
  86.5 5.4 %collective-permute-start.21 = (f32[3,16,256]{2,1,0:T(8,128)S(1)}, f32[3,16,256]{2,1,0:T(8,128)S(1)}, u32[]{:S(2)}, u32[]{:S(2)}) collective-permute-start(f32[3,16,256]{2,1,0:T(8,128)S(1)} %get-tuple-element.56), channel_id=1, source_target_pairs={{4,8},{8,4},{12,16},{16,12},{20,24},{24,20},{5,9},{9,5},{13,17},{1... | collective-permute-start | bytes 147464 | tf_op jit(solution)/shard_map/ppermute | solution.py:417
  87.2 4.7 %collective-permute-start.22 = (f32[3,4,256]{2,1,0:T(4,128)S(1)}, f32[3,4,256]{2,1,0:T(4,128)S(1)}, u32[]{:S(2)}, u32[]{:S(2)}) collective-permute-start(f32[3,4,256]{2,1,0:T(4,128)S(1)} %get-tuple-element.57), channel_id=1, source_target_pairs={{0,1},{1,0},{2,3},{3,2},{4,5},{5,4},{6,7},{7,6},{8,9},{9,8},{10,11... | collective-permute-start | bytes 36872 | tf_op jit(solution)/shard_map/ppermute | solution.py:417
  91.0 0.8 collective-permute-start.23
  (12 other events, 131.5 us)

commit v3 on v2

--- a/solution.py
+++ b/solution.py
@@ -47,7 +47,7 @@
     return jnp.where(mask, 1.0, 0.0).astype(BF16)
 
 
-def call(kernel, outs, scratch=(), flops=0, scalars=0):
+def call(kernel, outs, scratch=(), flops=0, space=pltpu.VMEM):
     def run(*args):
         moved = sum(a.size * 4 for a in args) + sum(
             4 * functools.reduce(lambda p, q: p * q, o) for o in outs
@@ -55,10 +55,9 @@
         return pl.pallas_call(
             kernel,
             out_shape=[jax.ShapeDtypeStruct(o, F32) for o in outs],
-            in_specs=[pl.BlockSpec(memory_space=pltpu.SMEM)] * scalars
-            + [pl.BlockSpec(memory_space=pltpu.VMEM)] * (len(args) - scalars),
+            in_specs=[pl.BlockSpec(memory_space=space)] * len(args),
             out_specs=[pl.BlockSpec(memory_space=pltpu.VMEM)] * len(outs),
-            scratch_shapes=[pltpu.VMEM(s, t) for s, t in scratch],
+            scratch_shapes=[s if hasattr(s, "dtype") else pltpu.VMEM(*s) for s in scratch],
             cost_estimate=pl.CostEstimate(
                 flops=flops, bytes_accessed=moved, transcendentals=0
             ),
@@ -72,6 +71,10 @@
     for groups in (5, 4, 3, 2, 1):
         if slots % (groups * LANES) == 0:
             return groups * LANES
+
+
+def is_odd(axis):
+    return lax.rem(lax.axis_index(axis), 2) == 1
 
 
 def row_and_depth(cells, nz):
@@ -114,7 +117,16 @@
     )
 
 
-def first_kernel(cells_ref, v_ref, d_ref, out_ref):
+def first_kernel(cells_hbm, v_hbm, d_hbm, out_ref, cells_ref, v_ref, d_ref, sem):
+    pairs = ((cells_hbm, cells_ref), (v_hbm, v_ref), (d_hbm, d_ref))
+    copies = [
+        pltpu.make_async_copy(src, dst, sem.at[place])
+        for place, (src, dst) in enumerate(pairs)
+    ]
+    for copy in copies:
+        copy.start()
+    for copy in copies:
+        copy.wait()
     pick(times_diag(d_ref, [v_ref[b] for b in range(3)]), cells_ref, out_ref)
 
 
@@ -153,7 +165,7 @@
 
 
 def solve_kernel(
-    odd_ref, idx_ref, own_ref, even_ref, next_ref, g_ref, h_ref, e_ref,
+    idx_ref, own_ref, even_ref, next_ref, g_ref, h_ref, e_ref,
     keep_ref, to_even_ref, to_next_ref,
     pool_ref, r_ref, q_ref, tail_ref, p_ref, y_ref, ohr_ref, w_ref,
 ):
@@ -165,7 +177,7 @@
     rows = pool_ref.shape[1]
     tile = own_ref.shape[0] // 3
     group = wells * span
-    odd_x, odd_y = odd_ref[0] == 1, odd_ref[1] == 1
+    odd_x, odd_y = is_odd("gx"), is_odd("gy")
     pool_ref[:, 9 * blocks :, :] = jnp.zeros((3, rows - 9 * blocks, LANES), F32)
     own, even, following = own_ref[...], even_ref[...], next_ref[...]
     columns = (
@@ -268,9 +280,9 @@
             to_next_ref[at, :] = jnp.where(odd_y, parts[2], parts[0])
 
 
-def add_kernel(odd_ref, x_ref, y_ref, z_ref, keep_ref, to_even_ref, to_next_ref):
+def add_kernel(x_ref, y_ref, z_ref, keep_ref, to_even_ref, to_next_ref):
     tile = keep_ref.shape[0]
-    odd_x = odd_ref[0] == 1
+    odd_x = is_odd("gx")
     low, mid, high = [
         x_ref[part, :] + y_ref[part, :] + z_ref[part, :]
         for part in [slice(place * tile, (place + 1) * tile) for place in range(3)]
@@ -281,11 +293,15 @@
 
 
 def place_kernel(
-    odd_ref, cells_ref, v_ref, inv_ref, x_ref, y_ref, z_ref,
+    cells_ref, v_ref, inv_ref, x_ref, y_ref, z_ref,
     out_ref, x_even_ref, x_next_ref, y_even_ref, y_next_ref,
     left_ref, right_ref,
 ):
-    odd_x, odd_y = odd_ref[0] == 1, odd_ref[1] == 1
+    (first_x, last_x), (first_y, last_y) = [
+        (lax.axis_index(axis) == 0, lax.axis_index(axis) == lax.axis_size(axis) - 1)
+        for axis in ("gx", "gy")
+    ]
+    odd_x, odd_y = is_odd("gx"), is_odd("gy")
     nx, ny, nz = v_ref.shape[1:]
     rows = nx * ny
     slots = cells_ref.shape[1]
@@ -309,17 +325,19 @@
     for a in range(3):
         own = sum(inv_ref[3 * a + b] * v_ref[b] for b in range(3))
         out_ref[a] = own + placed[a * rows : (a + 1) * rows].reshape(nx, ny, nz)
-        low, high = out_ref[a, 0], out_ref[a, nx - 1]
+        low = jnp.where(first_x, 0.0, out_ref[a, 0])
+        high = jnp.where(last_x, 0.0, out_ref[a, nx - 1])
         x_even_ref[a] = jnp.where(odd_x, low, high)
         x_next_ref[a] = jnp.where(odd_x, high, low)
-        low, high = out_ref[a, :, 0, :], out_ref[a, :, ny - 1, :]
+        low = jnp.where(first_y, 0.0, out_ref[a, :, 0, :])
+        high = jnp.where(last_y, 0.0, out_ref[a, :, ny - 1, :])
         y_even_ref[a] = jnp.where(odd_y, low, high)
         y_next_ref[a] = jnp.where(odd_y, high, low)
 
 
-def jacobian(odd_ref, z_ref, faces, d_ref, off_ref, store):
+def jacobian(z_ref, faces, d_ref, off_ref, store):
     nx, ny, nz = z_ref.shape[1:]
-    odd_x, odd_y = odd_ref[0] == 1, odd_ref[1] == 1
+    odd_x, odd_y = is_odd("gx"), is_odd("gy")
     x_even, x_next, y_even, y_next = [face[...] for face in faces]
     xl, xh = jnp.where(odd_x, x_even, x_next), jnp.where(odd_x, x_next, x_even)
     yl, yh = jnp.where(odd_y, y_even, y_next), jnp.where(odd_y, y_next, y_even)
@@ -348,25 +366,25 @@
 
 
 def next_kernel(
-    odd_ref, cells_ref, z_ref, f0_ref, f1_ref, f2_ref, f3_ref, d_ref, off_ref, v_ref,
+    cells_ref, z_ref, f0_ref, f1_ref, f2_ref, f3_ref, d_ref, off_ref, v_ref,
     w_ref, t_ref, out_ref,
 ):
     def store(a, x, value):
         w_ref[a, x] = value
         t_ref[a, x] = value - v_ref[a, x]
 
-    jacobian(odd_ref, z_ref, (f0_ref, f1_ref, f2_ref, f3_ref), d_ref, off_ref, store)
+    jacobian(z_ref, (f0_ref, f1_ref, f2_ref, f3_ref), d_ref, off_ref, store)
     pick(times_diag(d_ref, [t_ref[b] for b in range(3)]), cells_ref, out_ref)
 
 
 def gram_kernel(
-    odd_ref, z_ref, f0_ref, f1_ref, f2_ref, f3_ref, d_ref, off_ref, v_ref, w1_ref,
+    z_ref, f0_ref, f1_ref, f2_ref, f3_ref, d_ref, off_ref, v_ref, w1_ref,
     w_ref, sums_ref,
 ):
     def store(a, x, value):
         w_ref[a, x] = value
 
-    jacobian(odd_ref, z_ref, (f0_ref, f1_ref, f2_ref, f3_ref), d_ref, off_ref, store)
+    jacobian(z_ref, (f0_ref, f1_ref, f2_ref, f3_ref), d_ref, off_ref, store)
     one, two, rhs = w1_ref[...], w_ref[...], v_ref[...]
     top_one = jnp.maximum(jnp.max(jnp.abs(one)), 1e-30)
     top_two = jnp.maximum(jnp.max(jnp.abs(two)), 1e-30)
@@ -414,8 +432,22 @@
         pairs = []
         for i in range(first, count - 1, 2):
             pairs += [(i, i + 1), (i + 1, i)]
+        taken = [source for source, _ in pairs]
+        pairs += [(i, i) for i in range(count) if i not in taken]
         out.append(lax.ppermute(value, axis, pairs))
     return out
+
+
+def gather_all(value, axis):
+    count = lax.axis_size(axis)
+    if count & (count - 1):
+        return lax.all_gather(value, axis, tiled=True)
+    step = 1
+    while step < count:
+        other = lax.ppermute(value, axis, [(i, i ^ step) for i in range(count)])
+        value = jnp.concatenate([value, other], axis=0)
+        step *= 2
+    return value
 
 
 def body(
@@ -438,11 +470,19 @@
     tile = round_up(3 * blocks, 16)
     rows = round_up(9 * blocks, 16)
     tall = round_up(chunks, 16)
-    odd = jnp.stack([lax.axis_index("gx") % 2, lax.axis_index("gy") % 2]).astype(jnp.int32)
     field = right_side.shape
-    (picked,) = call(first_kernel, [(tile, LANES)], flops=10**9)(
-        send_cells, right_side, diag_blocks
-    )
+    (picked,) = call(
+        first_kernel,
+        [(tile, LANES)],
+        [
+            (send_cells.shape, jnp.int32),
+            (field, F32),
+            (diag_blocks.shape, F32),
+            pltpu.SemaphoreType.DMA((3,)),
+        ],
+        flops=10**9,
+        space=pltpu.HBM,
+    )(send_cells, right_side, diag_blocks)
     live = jnp.arange(longest)[None, :] < seg_count[:, None]
     index = jnp.where(live, recv_index, -1)
     index = index.reshape(wells, chunks, span).transpose(1, 0, 2).reshape(1, wells * longest)
@@ -470,11 +510,10 @@
                 ((6 * LANES, slots), BF16),
             ],
             flops=4 * 10**9,
-            scalars=1,
-        )(odd, index, column, even, following, apart, h, e)
+        )(index, column, even, following, apart, h, e)
         even, following = swap("gy", even, following)
-        keep, even, following = call(add_kernel, [(tile, LANES)] * 3, scalars=1)(
-            odd, keep, even, following
+        keep, even, following = call(add_kernel, [(tile, LANES)] * 3)(
+            keep, even, following
         )
         even, following = swap("gx", even, following)
         z, *faces = call(
@@ -482,19 +521,18 @@
             [(3, nx, ny, nz)] + [(3, ny, nz)] * 2 + [(3, nx, nz)] * 2,
             [((6 * nx * ny, slots), BF16), ((nz, slots), BF16)],
             flops=10**9,
-            scalars=1,
-        )(odd, send_cells, vector, cell_inverse, keep, even, following)
+        )(send_cells, vector, cell_inverse, keep, even, following)
         return z, swap("gx", *faces[:2]) + swap("gy", *faces[2:])
 
     z1, faces = precondition(right_side, picked)
     w1, turned, picked = call(
-        next_kernel, [field, field, (tile, LANES)], flops=10**9, scalars=1
-    )(odd, send_cells, z1, *faces, diag_blocks, off_blocks, right_side)
+        next_kernel, [field, field, (tile, LANES)], flops=10**9
+    )(send_cells, z1, *faces, diag_blocks, off_blocks, right_side)
     z2, faces = precondition(turned, picked)
-    w2, sums = call(gram_kernel, [field, (8, LANES)], scalars=1)(
-        odd, z2, *faces, diag_blocks, off_blocks, right_side, w1
+    w2, sums = call(gram_kernel, [field, (8, LANES)])(
+        z2, *faces, diag_blocks, off_blocks, right_side, w1
     )
-    every = lax.all_gather(lax.all_gather(sums, "gy"), "gx").reshape(-1, 8, LANES)
+    every = gather_all(gather_all(sums, "gy"), "gx").reshape(-1, 8, LANES)
     return tuple(
         call(final_kernel, [field, field])(every, right_side, z1, z2, w1, w2)
     )

time: 139 us -> 117 us (0.84)
  blocking collectives: 44.4 us -> 0 us
  starting transfers between devices: 56.7 us -> 73.9 us
  waiting for transfers between devices: 8.59 us -> 17.4 us
  Pallas kernels: 24.6 us -> 20.5 us
    all_gather x2 -> x0, blocking collectives: 44.4 us -> none  [the longest x1 33.9 us: body(): lax.all_gather(lax.all_gather(sums, 'gy'), 'gx').reshape(-1, 8, LANES)]
    ppermute x0 -> x5, starting transfers between devices: none -> 17.2 us  [gather_all(): other = lax.ppermute(value, axis, [(i, i ^ step) for i in range(count)])]
    ppermute x0 -> x5, waiting for transfers between devices: none -> 8.81 us  [gather_all(): other = lax.ppermute(value, axis, [(i, i ^ step) for i in range(count)])]
    pallas_call x11, Pallas kernels: 24.6 us -> 20.5 us  [run(): pl.pallas_call(kernel, out_shape=[jax.ShapeDtypeStruct(o, F32) for o in o...]
    unnamed x27 -> x31, local copies, waits for them, and re-layouts: 2.88 us -> 2.89 us
  transfers between devices with their start and end apart: 24 -> 29, of which waited for: 9 -> 14; matrix products, arithmetic and copies ran while one was open for 0% -> 0% of each run, Pallas kernels for 1% -> 1%
where the time goes in v3:
time: 117 us; the launch traced here: 116 us
  starting transfers between devices  73.9 us (63%)
  Pallas kernels  20.5 us (18%)
  waiting for transfers between devices  17.4 us (15%)
  local copies, waits for them, and re-layouts  3.19 us (3%)
    ppermute x24, starting transfers between devices, swap(): out.append(lax.ppermute(value, axis, pairs))  56.7 us
    pallas_call x11, Pallas kernels, run(): pl.pallas_call(kernel, out_shape=[jax.ShapeDtypeStruct(o, F32) for o in o...  20.5 us
    ppermute x5, starting transfers between devices, gather_all(): other = lax.ppermute(value, axis, [(i, i ^ step) for i in range(count)])  17.2 us
    ppermute x5, waiting for transfers between devices, gather_all(): other = lax.ppermute(value, axis, [(i, i ^ step) for i in range(count)])  8.81 us
    ppermute x24, waiting for transfers between devices, swap(): out.append(lax.ppermute(value, axis, pairs))  8.59 us
    unnamed x31, local copies, waits for them, and re-layouts  2.89 us
  transfers between devices with their start and end apart: 29, of which 14 were waited for; matrix products, arithmetic and copies ran while one was open for 0% of the time, Pallas kernels for 1%

profile of v3, /device:TPU:0, one launch (start us, length us, event | category | flops | bytes accessed | tf_op | source)
XLA Modules:
  0.0 116.1 jit_solution(11734614398072859869)
XLA Ops:
  5.4 5.8 %collective-permute-start = (f32[80,128]{1,0:T(8,128)S(1)}, f32[80,128]{1,0:T(8,128)S(1)}, u32[]{:S(2)}, u32[]{:S(2)}) collective-permute-start(f32[80,128]{1,0:T(8,128)S(1)} %shard_map.104), channel_id=1, source_target_pairs={{0,4},{4,0},{8,12},{12,8},{16,20},{20,16},{24,28},{28,24},{1,5},{5... | collective-permute-start | bytes 122888 | tf_op jit(solution)/shard_map/ppermute | solution.py:437
  11.2 2.0 %collective-permute-done = f32[80,128]{1,0:T(8,128)S(1)} collective-permute-done((f32[80,128]{1,0:T(8,128)S(1)}, f32[80,128]{1,0:T(8,128)S(1)}, u32[]{:S(2)}, u32[]{:S(2)}) %collective-permute-start) | collective-permute-done | bytes 40992 | tf_op jit(solution)/shard_map/ppermute | solution.py:437
  13.9 2.9 %collective-permute-start.2 = (f32[240,128]{1,0:T(8,128)S(1)}, f32[240,128]{1,0:T(8,128)S(1)}, u32[]{:S(2)}, u32[]{:S(2)}) collective-permute-start(f32[240,128]{1,0:T(8,128)S(1)} %pad_maximum_fusion.own_ref), channel_id=1, source_target_pairs={{0,1},{1,0},{2,3},{3,2},{4,5},{5,4},{6,7},{7,6},{8,9},{9,8},{10,11... | collective-permute-start | bytes 368648 | tf_op jit(solution)/shard_map/ppermute | solution.py:437
  18.7 5.9 %shard_map.106 = (f32[240,128]{1,0:T(8,128)S(1)}, f32[240,128]{1,0:T(8,128)S(1)}, f32[240,128]{1,0:T(8,128)S(1)}) custom-call(s32[1,3200]{1,0:T(1,128)S(1)} %reshape.15.idx_ref, f32[240,128]{1,0:T(8,128)S(1)} %pad_maximum_fusion.own_ref, f32[240,128]{1,0:T(8,128)S(1)} %collective-permute-done.2.even_ref, f32[240,128]{1,0:T(8,128)S(1)} %collective-permute-done.3.next_ref, ...), custom_call_target="tpu_custom_call" | custom-call | flops 4000000000 | bytes 2749952 | tf_op jit(solution)/shard_map/pallas_call | solution.py:55
  26.3 2.1 %collective-permute-start.6 = (f32[80,128]{1,0:T(8,128)S(1)}, f32[80,128]{1,0:T(8,128)S(1)}, u32[]{:S(2)}, u32[]{:S(2)}) collective-permute-start(f32[80,128]{1,0:T(8,128)S(1)} %get-tuple-element.39), channel_id=1, source_target_pairs={{0,4},{4,0},{8,12},{12,8},{16,20},{20,16},{24,28},{28,24},{1,5},{5... | collective-permute-start | bytes 122888 | tf_op jit(solution)/shard_map/ppermute | solution.py:437
  31.8 5.0 %collective-permute-start.8 = (f32[3,16,256]{2,1,0:T(8,128)S(1)}, f32[3,16,256]{2,1,0:T(8,128)S(1)}, u32[]{:S(2)}, u32[]{:S(2)}) collective-permute-start(f32[3,16,256]{2,1,0:T(8,128)S(1)} %get-tuple-element.42), channel_id=1, source_target_pairs={{0,4},{4,0},{8,12},{12,8},{16,20},{20,16},{24,28},{28,24},{1,5},{5... | collective-permute-start | bytes 147464 | tf_op jit(solution)/shard_map/ppermute | solution.py:437
  37.5 3.9 %collective-permute-start.10 = (f32[3,4,256]{2,1,0:T(4,128)S(1)}, f32[3,4,256]{2,1,0:T(4,128)S(1)}, u32[]{:S(2)}, u32[]{:S(2)}) collective-permute-start(f32[3,4,256]{2,1,0:T(4,128)S(1)} %get-tuple-element.44), channel_id=1, source_target_pairs={{0,1},{1,0},{2,3},{3,2},{4,5},{5,4},{6,7},{7,6},{8,9},{9,8},{10,11... | collective-permute-start | bytes 36872 | tf_op jit(solution)/shard_map/ppermute | solution.py:437
  42.2 1.4 %shard_map.109 = (f32[3,4,16,256]{3,2,1,0:T(8,128)S(1)}, f32[3,4,16,256]{3,2,1,0:T(8,128)S(1)}, f32[80,128]{1,0:T(8,128)S(1)}) custom-call(s32[1,3200]{1,0:T(1,128)S(1)} %copy-done.7, f32[3,4,16,256]{3,2,1,0:T(8,128)S(1)} %get-tuple-element.41.z_ref.z1_ref, f32[3,16,256]{2,1,0:T(8,128)S(1)} %collective-permute-done.8.f0_ref, ...), custom_call_target="tpu_custom_call" | custom-call | flops 1000000000 | bytes 5091840 | tf_op jit(solution)/shard_map/pallas_call | solution.py:55
  44.3 6.2 %collective-permute-start.12 = (f32[80,128]{1,0:T(8,128)S(1)}, f32[80,128]{1,0:T(8,128)S(1)}, u32[]{:S(2)}, u32[]{:S(2)}) collective-permute-start(f32[80,128]{1,0:T(8,128)S(1)} %get-tuple-element.47), channel_id=1, source_target_pairs={{0,4},{4,0},{8,12},{12,8},{16,20},{20,16},{24,28},{28,24},{1,5},{5... | collective-permute-start | bytes 122888 | tf_op jit(solution)/shard_map/ppermute | solution.py:437
  50.5 2.0 %collective-permute-done.12 = f32[80,128]{1,0:T(8,128)S(1)} collective-permute-done((f32[80,128]{1,0:T(8,128)S(1)}, f32[80,128]{1,0:T(8,128)S(1)}, u32[]{:S(2)}, u32[]{:S(2)}) %collective-permute-start.12) | collective-permute-done | bytes 40992 | tf_op jit(solution)/shard_map/ppermute | solution.py:437
  53.4 8.3 %collective-permute-start.14 = (f32[240,128]{1,0:T(8,128)S(1)}, f32[240,128]{1,0:T(8,128)S(1)}, u32[]{:S(2)}, u32[]{:S(2)}) collective-permute-start(f32[240,128]{1,0:T(8,128)S(1)} %constant_dynamic-update-slice_fusion.own_ref), channel_id=1, source_target_pairs={{0,1},{1,0},{2,3},{3,2},{4,5},{5,4},{6,7},{7,6},{8,9},{9,8},{10,11... | collective-permute-start | bytes 368648 | tf_op jit(solution)/shard_map/ppermute | solution.py:437
  62.7 5.9 %shard_map.110 = (f32[240,128]{1,0:T(8,128)S(1)}, f32[240,128]{1,0:T(8,128)S(1)}, f32[240,128]{1,0:T(8,128)S(1)}) custom-call(s32[1,3200]{1,0:T(1,128)S(1)} %reshape.15.idx_ref, f32[240,128]{1,0:T(8,128)S(1)} %constant_dynamic-update-slice_fusion.own_ref, f32[240,128]{1,0:T(8,128)S(1)} %collective-permute-done.14.even_ref, ...), custom_call_target="tpu_custom_call" | custom-call | flops 4000000000 | bytes 2749952 | tf_op jit(solution)/shard_map/pallas_call | solution.py:55
  71.0 2.8 %collective-permute-start.18 = (f32[80,128]{1,0:T(8,128)S(1)}, f32[80,128]{1,0:T(8,128)S(1)}, u32[]{:S(2)}, u32[]{:S(2)}) collective-permute-start(f32[80,128]{1,0:T(8,128)S(1)} %get-tuple-element.52), channel_id=1, source_target_pairs={{0,4},{4,0},{8,12},{12,8},{16,20},{20,16},{24,28},{28,24},{1,5},{5... | collective-permute-start | bytes 122888 | tf_op jit(solution)/shard_map/ppermute | solution.py:437
  77.3 5.7 %collective-permute-start.20 = (f32[3,16,256]{2,1,0:T(8,128)S(1)}, f32[3,16,256]{2,1,0:T(8,128)S(1)}, u32[]{:S(2)}, u32[]{:S(2)}) collective-permute-start(f32[3,16,256]{2,1,0:T(8,128)S(1)} %get-tuple-element.55), channel_id=1, source_target_pairs={{0,4},{4,0},{8,12},{12,8},{16,20},{20,16},{24,28},{28,24},{1,5},{5... | collective-permute-start | bytes 147464 | tf_op jit(solution)/shard_map/ppermute | solution.py:437
  83.7 3.9 %collective-permute-start.22 = (f32[3,4,256]{2,1,0:T(4,128)S(1)}, f32[3,4,256]{2,1,0:T(4,128)S(1)}, u32[]{:S(2)}, u32[]{:S(2)}) collective-permute-start(f32[3,4,256]{2,1,0:T(4,128)S(1)} %get-tuple-element.57), channel_id=1, source_target_pairs={{0,1},{1,0},{2,3},{3,2},{4,5},{5,4},{6,7},{7,6},{8,9},{9,8},{10,11... | collective-permute-start | bytes 36872 | tf_op jit(solution)/shard_map/ppermute | solution.py:437
  89.2 5.7 %collective-permute-start.24 = (f32[8,128]{1,0:T(8,128)S(1)}, f32[8,128]{1,0:T(8,128)S(1)}, u32[]{:S(2)}, u32[]{:S(2)}) collective-permute-start(f32[8,128]{1,0:T(8,128)S(1)} %get-tuple-element.60), channel_id=1, source_target_pairs={{0,1},{1,0},{2,3},{3,2},{4,5},{5,4},{6,7},{7,6},{8,9},{9,8},{10,11... | collective-permute-start | bytes 12296 | tf_op jit(solution)/shard_map/ppermute | solution.py:447
  95.7 2.0 %collective-permute-start.25 = (f32[16,128]{1,0:T(8,128)S(1)}, f32[16,128]{1,0:T(8,128)S(1)}, u32[]{:S(2)}, u32[]{:S(2)}) collective-permute-start(f32[16,128]{1,0:T(8,128)S(1)} %pad_maximum_fusion.3), channel_id=1, source_target_pairs={{0,2},{1,3},{2,0},{3,1},{4,6},{5,7},{6,4},{7,5},{8,10},{9,11},{10,... | collective-permute-start | bytes 24584 | tf_op jit(solution)/shard_map/ppermute | solution.py:447
  97.6 1.7 %collective-permute-done.25 = f32[16,128]{1,0:T(8,128)S(1)} collective-permute-done((f32[16,128]{1,0:T(8,128)S(1)}, f32[16,128]{1,0:T(8,128)S(1)}, u32[]{:S(2)}, u32[]{:S(2)}) %collective-permute-start.25) | collective-permute-done | bytes 8224 | tf_op jit(solution)/shard_map/ppermute | solution.py:447
  99.3 4.5 %collective-permute-start.26 = (f32[32,128]{1,0:T(8,128)S(1)}, f32[32,128]{1,0:T(8,128)S(1)}, u32[]{:S(2)}, u32[]{:S(2)}) collective-permute-start(f32[32,128]{1,0:T(8,128)S(1)} %pad_maximum_fusion.2), channel_id=1, source_target_pairs={{0,4},{4,0},{8,12},{12,8},{16,20},{20,16},{24,28},{28,24},{1,5},{5... | collective-permute-start | bytes 49160 | tf_op jit(solution)/shard_map/ppermute | solution.py:447
  103.9 1.7 %collective-permute-done.26 = f32[32,128]{1,0:T(8,128)S(1)} collective-permute-done((f32[32,128]{1,0:T(8,128)S(1)}, f32[32,128]{1,0:T(8,128)S(1)}, u32[]{:S(2)}, u32[]{:S(2)}) %collective-permute-start.26) | collective-permute-done | bytes 16416 | tf_op jit(solution)/shard_map/ppermute | solution.py:447
  105.6 1.6 %collective-permute-start.27 = (f32[64,128]{1,0:T(8,128)S(1)}, f32[64,128]{1,0:T(8,128)S(1)}, u32[]{:S(2)}, u32[]{:S(2)}) collective-permute-start(f32[64,128]{1,0:T(8,128)S(1)} %pad_maximum_fusion.1), channel_id=1, source_target_pairs={{0,8},{4,12},{8,0},{12,4},{16,24},{20,28},{24,16},{28,20},{1,9},{5... | collective-permute-start | bytes 98312 | tf_op jit(solution)/shard_map/ppermute | solution.py:447
  107.2 2.3 %collective-permute-done.27 = f32[64,128]{1,0:T(8,128)S(1)} collective-permute-done((f32[64,128]{1,0:T(8,128)S(1)}, f32[64,128]{1,0:T(8,128)S(1)}, u32[]{:S(2)}, u32[]{:S(2)}) %collective-permute-start.27) | collective-permute-done | bytes 32800 | tf_op jit(solution)/shard_map/ppermute | solution.py:447
  109.5 3.4 %collective-permute-start.28 = (f32[128,128]{1,0:T(8,128)S(1)}, f32[128,128]{1,0:T(8,128)S(1)}, u32[]{:S(2)}, u32[]{:S(2)}) collective-permute-start(f32[128,128]{1,0:T(8,128)S(1)} %get-tuple-element.62), channel_id=1, source_target_pairs={{0,16},{4,20},{8,24},{12,28},{16,0},{20,4},{24,8},{28,12},{1,17},{... | collective-permute-start | bytes 196616 | tf_op jit(solution)/shard_map/ppermute | solution.py:447
  113.0 2.3 %collective-permute-done.28 = f32[128,128]{1,0:T(8,128)S(1)} collective-permute-done((f32[128,128]{1,0:T(8,128)S(1)}, f32[128,128]{1,0:T(8,128)S(1)}, u32[]{:S(2)}, u32[]{:S(2)}) %collective-permute-start.28) | collective-permute-done | bytes 65568 | tf_op jit(solution)/shard_map/ppermute | solution.py:447
  (88 shorter events, 26.2 us)
Async XLA Ops:
  4.8 6.5 %collective-permute-start.1 = (f32[80,128]{1,0:T(8,128)S(1)}, f32[80,128]{1,0:T(8,128)S(1)}, u32[]{:S(2)}, u32[]{:S(2)}) collective-permute-start(f32[80,128]{1,0:T(8,128)S(1)} %shard_map.104), channel_id=1, source_target_pairs={{4,8},{8,4},{12,16},{16,12},{20,24},{24,20},{0,0},{28,28},{5,9},{9... | collective-permute-start | bytes 122888 | tf_op jit(solution)/shard_map/ppermute | solution.py:437
  5.4 7.8 %collective-permute-start = (f32[80,128]{1,0:T(8,128)S(1)}, f32[80,128]{1,0:T(8,128)S(1)}, u32[]{:S(2)}, u32[]{:S(2)}) collective-permute-start(f32[80,128]{1,0:T(8,128)S(1)} %shard_map.104), channel_id=1, source_target_pairs={{0,4},{4,0},{8,12},{12,8},{16,20},{20,16},{24,28},{28,24},{1,5},{5... | collective-permute-start | bytes 122888 | tf_op jit(solution)/shard_map/ppermute | solution.py:437
  13.2 5.4 %collective-permute-start.3 = (f32[240,128]{1,0:T(8,128)S(1)}, f32[240,128]{1,0:T(8,128)S(1)}, u32[]{:S(2)}, u32[]{:S(2)}) collective-permute-start(f32[240,128]{1,0:T(8,128)S(1)} %pad_maximum_fusion.own_ref), channel_id=1, source_target_pairs={{1,2},{2,1},{0,0},{3,3},{5,6},{6,5},{4,4},{7,7},{9,10},{10,9},{8,8... | collective-permute-start | bytes 368648 | tf_op jit(solution)/shard_map/ppermute | solution.py:437
  13.9 4.8 %collective-permute-start.2 = (f32[240,128]{1,0:T(8,128)S(1)}, f32[240,128]{1,0:T(8,128)S(1)}, u32[]{:S(2)}, u32[]{:S(2)}) collective-permute-start(f32[240,128]{1,0:T(8,128)S(1)} %pad_maximum_fusion.own_ref), channel_id=1, source_target_pairs={{0,1},{1,0},{2,3},{3,2},{4,5},{5,4},{6,7},{7,6},{8,9},{9,8},{10,11... | collective-permute-start | bytes 368648 | tf_op jit(solution)/shard_map/ppermute | solution.py:437
  26.3 4.1 %collective-permute-start.6 = (f32[80,128]{1,0:T(8,128)S(1)}, f32[80,128]{1,0:T(8,128)S(1)}, u32[]{:S(2)}, u32[]{:S(2)}) collective-permute-start(f32[80,128]{1,0:T(8,128)S(1)} %get-tuple-element.39), channel_id=1, source_target_pairs={{0,4},{4,0},{8,12},{12,8},{16,20},{20,16},{24,28},{28,24},{1,5},{5... | collective-permute-start | bytes 122888 | tf_op jit(solution)/shard_map/ppermute | solution.py:437
  28.4 2.0 %collective-permute-start.7 = (f32[80,128]{1,0:T(8,128)S(1)}, f32[80,128]{1,0:T(8,128)S(1)}, u32[]{:S(2)}, u32[]{:S(2)}) collective-permute-start(f32[80,128]{1,0:T(8,128)S(1)} %get-tuple-element.40), channel_id=1, source_target_pairs={{4,8},{8,4},{12,16},{16,12},{20,24},{24,20},{0,0},{28,28},{5,9},{9... | collective-permute-start | bytes 122888 | tf_op jit(solution)/shard_map/ppermute | solution.py:437
  31.8 10.3 %collective-permute-start.8 = (f32[3,16,256]{2,1,0:T(8,128)S(1)}, f32[3,16,256]{2,1,0:T(8,128)S(1)}, u32[]{:S(2)}, u32[]{:S(2)}) collective-permute-start(f32[3,16,256]{2,1,0:T(8,128)S(1)} %get-tuple-element.42), channel_id=1, source_target_pairs={{0,4},{4,0},{8,12},{12,8},{16,20},{20,16},{24,28},{28,24},{1,5},{5... | collective-permute-start | bytes 147464 | tf_op jit(solution)/shard_map/ppermute | solution.py:437
  36.8 5.4 %collective-permute-start.9 = (f32[3,16,256]{2,1,0:T(8,128)S(1)}, f32[3,16,256]{2,1,0:T(8,128)S(1)}, u32[]{:S(2)}, u32[]{:S(2)}) collective-permute-start(f32[3,16,256]{2,1,0:T(8,128)S(1)} %get-tuple-element.43), channel_id=1, source_target_pairs={{4,8},{8,4},{12,16},{16,12},{20,24},{24,20},{0,0},{28,28},{5,9},{9... | collective-permute-start | bytes 147464 | tf_op jit(solution)/shard_map/ppermute | solution.py:437
  37.5 4.7 %collective-permute-start.10 = (f32[3,4,256]{2,1,0:T(4,128)S(1)}, f32[3,4,256]{2,1,0:T(4,128)S(1)}, u32[]{:S(2)}, u32[]{:S(2)}) collective-permute-start(f32[3,4,256]{2,1,0:T(4,128)S(1)} %get-tuple-element.44), channel_id=1, source_target_pairs={{0,1},{1,0},{2,3},{3,2},{4,5},{5,4},{6,7},{7,6},{8,9},{9,8},{10,11... | collective-permute-start | bytes 36872 | tf_op jit(solution)/shard_map/ppermute | solution.py:437
  43.7 8.9 %collective-permute-start.13 = (f32[80,128]{1,0:T(8,128)S(1)}, f32[80,128]{1,0:T(8,128)S(1)}, u32[]{:S(2)}, u32[]{:S(2)}) collective-permute-start(f32[80,128]{1,0:T(8,128)S(1)} %get-tuple-element.47), channel_id=1, source_target_pairs={{4,8},{8,4},{12,16},{16,12},{20,24},{24,20},{0,0},{28,28},{5,9},{9... | collective-permute-start | bytes 122888 | tf_op jit(solution)/shard_map/ppermute | solution.py:437
  44.3 8.2 %collective-permute-start.12 = (f32[80,128]{1,0:T(8,128)S(1)}, f32[80,128]{1,0:T(8,128)S(1)}, u32[]{:S(2)}, u32[]{:S(2)}) collective-permute-start(f32[80,128]{1,0:T(8,128)S(1)} %get-tuple-element.47), channel_id=1, source_target_pairs={{0,4},{4,0},{8,12},{12,8},{16,20},{20,16},{24,28},{28,24},{1,5},{5... | collective-permute-start | bytes 122888 | tf_op jit(solution)/shard_map/ppermute | solution.py:437
  52.5 9.2 %collective-permute-start.15 = (f32[240,128]{1,0:T(8,128)S(1)}, f32[240,128]{1,0:T(8,128)S(1)}, u32[]{:S(2)}, u32[]{:S(2)}) collective-permute-start(f32[240,128]{1,0:T(8,128)S(1)} %constant_dynamic-update-slice_fusion.own_ref), channel_id=1, source_target_pairs={{1,2},{2,1},{0,0},{3,3},{5,6},{6,5},{4,4},{7,7},{9,10},{10,9},{8,8... | collective-permute-start | bytes 368648 | tf_op jit(solution)/shard_map/ppermute | solution.py:437
  53.4 9.3 %collective-permute-start.14 = (f32[240,128]{1,0:T(8,128)S(1)}, f32[240,128]{1,0:T(8,128)S(1)}, u32[]{:S(2)}, u32[]{:S(2)}) collective-permute-start(f32[240,128]{1,0:T(8,128)S(1)} %constant_dynamic-update-slice_fusion.own_ref), channel_id=1, source_target_pairs={{0,1},{1,0},{2,3},{3,2},{4,5},{5,4},{6,7},{7,6},{8,9},{9,8},{10,11... | collective-permute-start | bytes 368648 | tf_op jit(solution)/shard_map/ppermute | solution.py:437
  68.6 2.4 %collective-permute-start.16 = (f32[240,128]{1,0:T(8,128)S(1)}, f32[240,128]{1,0:T(8,128)S(1)}, u32[]{:S(2)}, u32[]{:S(2)}) collective-permute-start(f32[240,128]{1,0:T(8,128)S(1)} %get-tuple-element.49), channel_id=1, source_target_pairs={{0,1},{1,0},{2,3},{3,2},{4,5},{5,4},{6,7},{7,6},{8,9},{9,8},{10,11... | collective-permute-start | bytes 368648 | tf_op jit(solution)/shard_map/ppermute | solution.py:437
  71.0 4.8 %collective-permute-start.18 = (f32[80,128]{1,0:T(8,128)S(1)}, f32[80,128]{1,0:T(8,128)S(1)}, u32[]{:S(2)}, u32[]{:S(2)}) collective-permute-start(f32[80,128]{1,0:T(8,128)S(1)} %get-tuple-element.52), channel_id=1, source_target_pairs={{0,4},{4,0},{8,12},{12,8},{16,20},{20,16},{24,28},{28,24},{1,5},{5... | collective-permute-start | bytes 122888 | tf_op jit(solution)/shard_map/ppermute | solution.py:437
  73.9 2.0 %collective-permute-start.19 = (f32[80,128]{1,0:T(8,128)S(1)}, f32[80,128]{1,0:T(8,128)S(1)}, u32[]{:S(2)}, u32[]{:S(2)}) collective-permute-start(f32[80,128]{1,0:T(8,128)S(1)} %get-tuple-element.53), channel_id=1, source_target_pairs={{4,8},{8,4},{12,16},{16,12},{20,24},{24,20},{0,0},{28,28},{5,9},{9... | collective-permute-start | bytes 122888 | tf_op jit(solution)/shard_map/ppermute | solution.py:437
  77.3 11.1 %collective-permute-start.20 = (f32[3,16,256]{2,1,0:T(8,128)S(1)}, f32[3,16,256]{2,1,0:T(8,128)S(1)}, u32[]{:S(2)}, u32[]{:S(2)}) collective-permute-start(f32[3,16,256]{2,1,0:T(8,128)S(1)} %get-tuple-element.55), channel_id=1, source_target_pairs={{0,4},{4,0},{8,12},{12,8},{16,20},{20,16},{24,28},{28,24},{1,5},{5... | collective-permute-start | bytes 147464 | tf_op jit(solution)/shard_map/ppermute | solution.py:437
  83.0 5.4 %collective-permute-start.21 = (f32[3,16,256]{2,1,0:T(8,128)S(1)}, f32[3,16,256]{2,1,0:T(8,128)S(1)}, u32[]{:S(2)}, u32[]{:S(2)}) collective-permute-start(f32[3,16,256]{2,1,0:T(8,128)S(1)} %get-tuple-element.56), channel_id=1, source_target_pairs={{4,8},{8,4},{12,16},{16,12},{20,24},{24,20},{0,0},{28,28},{5,9},{9... | collective-permute-start | bytes 147464 | tf_op jit(solution)/shard_map/ppermute | solution.py:437
  83.7 4.7 %collective-permute-start.22 = (f32[3,4,256]{2,1,0:T(4,128)S(1)}, f32[3,4,256]{2,1,0:T(4,128)S(1)}, u32[]{:S(2)}, u32[]{:S(2)}) collective-permute-start(f32[3,4,256]{2,1,0:T(4,128)S(1)} %get-tuple-element.57), channel_id=1, source_target_pairs={{0,1},{1,0},{2,3},{3,2},{4,5},{5,4},{6,7},{7,6},{8,9},{9,8},{10,11... | collective-permute-start | bytes 36872 | tf_op jit(solution)/shard_map/ppermute | solution.py:437
  89.2 6.5 %collective-permute-start.24 = (f32[8,128]{1,0:T(8,128)S(1)}, f32[8,128]{1,0:T(8,128)S(1)}, u32[]{:S(2)}, u32[]{:S(2)}) collective-permute-start(f32[8,128]{1,0:T(8,128)S(1)} %get-tuple-element.60), channel_id=1, source_target_pairs={{0,1},{1,0},{2,3},{3,2},{4,5},{5,4},{6,7},{7,6},{8,9},{9,8},{10,11... | collective-permute-start | bytes 12296 | tf_op jit(solution)/shard_map/ppermute | solution.py:447
  95.7 3.7 %collective-permute-start.25 = (f32[16,128]{1,0:T(8,128)S(1)}, f32[16,128]{1,0:T(8,128)S(1)}, u32[]{:S(2)}, u32[]{:S(2)}) collective-permute-start(f32[16,128]{1,0:T(8,128)S(1)} %pad_maximum_fusion.3), channel_id=1, source_target_pairs={{0,2},{1,3},{2,0},{3,1},{4,6},{5,7},{6,4},{7,5},{8,10},{9,11},{10,... | collective-permute-start | bytes 24584 | tf_op jit(solution)/shard_map/ppermute | solution.py:447
  99.3 6.3 %collective-permute-start.26 = (f32[32,128]{1,0:T(8,128)S(1)}, f32[32,128]{1,0:T(8,128)S(1)}, u32[]{:S(2)}, u32[]{:S(2)}) collective-permute-start(f32[32,128]{1,0:T(8,128)S(1)} %pad_maximum_fusion.2), channel_id=1, source_target_pairs={{0,4},{4,0},{8,12},{12,8},{16,20},{20,16},{24,28},{28,24},{1,5},{5... | collective-permute-start | bytes 49160 | tf_op jit(solution)/shard_map/ppermute | solution.py:447
  105.6 3.9 %collective-permute-start.27 = (f32[64,128]{1,0:T(8,128)S(1)}, f32[64,128]{1,0:T(8,128)S(1)}, u32[]{:S(2)}, u32[]{:S(2)}) collective-permute-start(f32[64,128]{1,0:T(8,128)S(1)} %pad_maximum_fusion.1), channel_id=1, source_target_pairs={{0,8},{4,12},{8,0},{12,4},{16,24},{20,28},{24,16},{28,20},{1,9},{5... | collective-permute-start | bytes 98312 | tf_op jit(solution)/shard_map/ppermute | solution.py:447
  109.5 5.7 %collective-permute-start.28 = (f32[128,128]{1,0:T(8,128)S(1)}, f32[128,128]{1,0:T(8,128)S(1)}, u32[]{:S(2)}, u32[]{:S(2)}) collective-permute-start(f32[128,128]{1,0:T(8,128)S(1)} %get-tuple-element.62), channel_id=1, source_target_pairs={{0,16},{4,20},{8,24},{12,28},{16,0},{20,4},{24,8},{28,12},{1,17},{... | collective-permute-start | bytes 196616 | tf_op jit(solution)/shard_map/ppermute | solution.py:447
  (17 other events, 133.1 us)

commit v4 on v3

--- a/solution.py
+++ b/solution.py
@@ -47,7 +47,7 @@
     return jnp.where(mask, 1.0, 0.0).astype(BF16)
 
 
-def call(kernel, outs, scratch=(), flops=0, space=pltpu.VMEM):
+def call(kernel, outs, scratch=(), flops=0, space=pltpu.VMEM, mib=40):
     def run(*args):
         moved = sum(a.size * 4 for a in args) + sum(
             4 * functools.reduce(lambda p, q: p * q, o) for o in outs
@@ -61,7 +61,7 @@
             cost_estimate=pl.CostEstimate(
                 flops=flops, bytes_accessed=moved, transcendentals=0
             ),
-            compiler_params=pltpu.CompilerParams(vmem_limit_bytes=40 * 2**20),
+            compiler_params=pltpu.CompilerParams(vmem_limit_bytes=mib * 2**20),
         )(*args)
 
     return run
@@ -432,6 +432,8 @@
         pairs = []
         for i in range(first, count - 1, 2):
             pairs += [(i, i + 1), (i + 1, i)]
+        if first and count % 2 == 0 and count > 2:
+            pairs += [(0, count - 1), (count - 1, 0)]
         taken = [source for source, _ in pairs]
         pairs += [(i, i) for i in range(count) if i not in taken]
         out.append(lax.ppermute(value, axis, pairs))
@@ -482,6 +484,7 @@
         ],
         flops=10**9,
         space=pltpu.HBM,
+        mib=60,
     )(send_cells, right_side, diag_blocks)
     live = jnp.arange(longest)[None, :] < seg_count[:, None]
     index = jnp.where(live, recv_index, -1)

time: 117 us -> 107 us (0.915)
  starting transfers between devices: 73.9 us -> 28.2 us
  waiting for transfers between devices: 17.4 us -> 54.2 us
  local copies, waits for them, and re-layouts: 3.19 us -> 0.49 us
  Pallas kernels: 20.5 us -> 22.2 us
    ppermute x24, starting transfers between devices: 56.7 us -> 26.6 us  [swap(): out.append(lax.ppermute(value, axis, pairs))]
    ppermute x24, waiting for transfers between devices: 8.59 us -> 37.6 us  [swap(): out.append(lax.ppermute(value, axis, pairs))]
    ppermute x5, starting transfers between devices: 17.2 us -> 1.61 us  [gather_all(): other = lax.ppermute(value, axis, [(i, i ^ step) for i in range(count)])]
    ppermute x5, waiting for transfers between devices: 8.81 us -> 16.5 us  [gather_all(): other = lax.ppermute(value, axis, [(i, i ^ step) for i in range(count)])]
    unnamed x31 -> x25, local copies, waits for them, and re-layouts: 2.89 us -> 0.19 us
    pallas_call x11, Pallas kernels: 20.5 us -> 22.2 us  [run(): pl.pallas_call(kernel, out_shape=[jax.ShapeDtypeStruct(o, F32) for o in o...]
  transfers between devices with their start and end apart: 29 -> 29, of which waited for: 14 -> 22; matrix products, arithmetic and copies ran while one was open for 0% -> 0% of each run, Pallas kernels for 1% -> 1%
where the time goes in v4:
time: 107 us
  waiting for transfers between devices  54.2 us (51%)
  starting transfers between devices  28.2 us (26%)
  Pallas kernels  22.2 us (21%)
    ppermute x24, waiting for transfers between devices, swap(): out.append(lax.ppermute(value, axis, pairs))  37.6 us
    ppermute x24, starting transfers between devices, swap(): out.append(lax.ppermute(value, axis, pairs))  26.6 us
    pallas_call x11, Pallas kernels, run(): pl.pallas_call(kernel, out_shape=[jax.ShapeDtypeStruct(o, F32) for o in o...  22.2 us
    ppermute x5, waiting for transfers between devices, gather_all(): other = lax.ppermute(value, axis, [(i, i ^ step) for i in range(count)])  16.5 us
  transfers between devices with their start and end apart: 29, of which 22 were waited for; matrix products, arithmetic and copies ran while one was open for 0% of the time, Pallas kernels for 1%

profile of v4, /device:TPU:0, one launch (start us, length us, event | category | flops | bytes accessed | tf_op | source)
XLA Modules:
  0.0 106.8 jit_solution(10645114288239170807)
XLA Ops:
  0.7 2.9 %shard_map.104 = f32[80,128]{1,0:T(8,128)} custom-call(s32[1,3200]{1,0:T(1,128)} %cells_ref.5, f32[3,4,16,256]{3,2,1,0:T(8,128)} %v_ref.7, f32[9,4,16,256]{3,2,1,0:T(8,128)} %d_ref.3), custom_call_target="tpu_custom_call" | custom-call | flops 1000000000 | bytes 840192 | tf_op jit(solution)/shard_map/pallas_call | solution.py:55
  3.6 6.1 %collective-permute-start.1 = (f32[80,128]{1,0:T(8,128)}, f32[80,128]{1,0:T(8,128)S(1)}, u32[]{:S(2)}, u32[]{:S(2)}) collective-permute-start(f32[80,128]{1,0:T(8,128)} %shard_map.104), channel_id=1, source_target_pairs={{4,8},{8,4},{12,16},{16,12},{20,24},{24,20},{0,28},{28,0},{5,9},{9... | collective-permute-start | bytes 122888 | tf_op jit(solution)/shard_map/ppermute | solution.py:439
  9.7 2.2 %collective-permute-done.1 = f32[80,128]{1,0:T(8,128)S(1)} collective-permute-done((f32[80,128]{1,0:T(8,128)}, f32[80,128]{1,0:T(8,128)S(1)}, u32[]{:S(2)}, u32[]{:S(2)}) %collective-permute-start.1) | collective-permute-done | bytes 40992 | tf_op jit(solution)/shard_map/ppermute | solution.py:439
  11.9 2.0 %collective-permute-done = f32[80,128]{1,0:T(8,128)S(1)} collective-permute-done((f32[80,128]{1,0:T(8,128)}, f32[80,128]{1,0:T(8,128)S(1)}, u32[]{:S(2)}, u32[]{:S(2)}) %collective-permute-start) | collective-permute-done | bytes 40992 | tf_op jit(solution)/shard_map/ppermute | solution.py:439
  18.2 2.1 %collective-permute-done.3.next_ref = f32[240,128]{1,0:T(8,128)S(1)} collective-permute-done((f32[240,128]{1,0:T(8,128)S(1)}, f32[240,128]{1,0:T(8,128)S(1)}, u32[]{:S(2)}, u32[]{:S(2)}) %collective-permute-start.3) | collective-permute-done | bytes 122912 | tf_op jit(solution)/shard_map/ppermute | solution.py:439
  20.3 5.9 %shard_map.106 = (f32[240,128]{1,0:T(8,128)S(1)}, f32[240,128]{1,0:T(8,128)S(1)}, f32[240,128]{1,0:T(8,128)S(1)}) custom-call(s32[1,3200]{1,0:T(1,128)S(1)} %reshape.15.idx_ref, f32[240,128]{1,0:T(8,128)S(1)} %pad_maximum_fusion.own_ref, f32[240,128]{1,0:T(8,128)S(1)} %collective-permute-done.2.even_ref, f32[240,128]{1,0:T(8,128)S(1)} %collective-permute-done.3.next_ref, ...), custom_call_target="tpu_custom_call" | custom-call | flops 4000000000 | bytes 2749952 | tf_op jit(solution)/shard_map/pallas_call | solution.py:55
  27.7 3.8 %collective-permute-done.5.z_ref = f32[240,128]{1,0:T(8,128)S(1)} collective-permute-done((f32[240,128]{1,0:T(8,128)S(1)}, f32[240,128]{1,0:T(8,128)S(1)}, u32[]{:S(2)}, u32[]{:S(2)}) %collective-permute-start.5) | collective-permute-done | bytes 122912 | tf_op jit(solution)/shard_map/ppermute | solution.py:439
  31.7 2.8 %collective-permute-start.7 = (f32[80,128]{1,0:T(8,128)S(1)}, f32[80,128]{1,0:T(8,128)S(1)}, u32[]{:S(2)}, u32[]{:S(2)}) collective-permute-start(f32[80,128]{1,0:T(8,128)S(1)} %get-tuple-element.40), channel_id=1, source_target_pairs={{4,8},{8,4},{12,16},{16,12},{20,24},{24,20},{0,28},{28,0},{5,9},{9... | collective-permute-start | bytes 122888 | tf_op jit(solution)/shard_map/ppermute | solution.py:439
  35.6 2.8 %collective-permute-done.7.z_ref = f32[80,128]{1,0:T(8,128)S(1)} collective-permute-done((f32[80,128]{1,0:T(8,128)S(1)}, f32[80,128]{1,0:T(8,128)S(1)}, u32[]{:S(2)}, u32[]{:S(2)}) %collective-permute-start.7) | collective-permute-done | bytes 40992 | tf_op jit(solution)/shard_map/ppermute | solution.py:439
  40.1 2.8 %collective-permute-start.9 = (f32[3,16,256]{2,1,0:T(8,128)S(1)}, f32[3,16,256]{2,1,0:T(8,128)S(1)}, u32[]{:S(2)}, u32[]{:S(2)}) collective-permute-start(f32[3,16,256]{2,1,0:T(8,128)S(1)} %get-tuple-element.43), channel_id=1, source_target_pairs={{4,8},{8,4},{12,16},{16,12},{20,24},{24,20},{0,28},{28,0},{5,9},{9... | collective-permute-start | bytes 147464 | tf_op jit(solution)/shard_map/ppermute | solution.py:439
  44.0 1.9 %collective-permute-done.11.f3_ref = f32[3,4,256]{2,1,0:T(4,128)S(1)} collective-permute-done((f32[3,4,256]{2,1,0:T(4,128)S(1)}, f32[3,4,256]{2,1,0:T(4,128)S(1)}, u32[]{:S(2)}, u32[]{:S(2)}) %collective-permute-start.11) | collective-permute-done | bytes 12320 | tf_op jit(solution)/shard_map/ppermute | solution.py:439
  48.3 2.9 %collective-permute-start.13 = (f32[80,128]{1,0:T(8,128)S(1)}, f32[80,128]{1,0:T(8,128)S(1)}, u32[]{:S(2)}, u32[]{:S(2)}) collective-permute-start(f32[80,128]{1,0:T(8,128)S(1)} %get-tuple-element.47), channel_id=1, source_target_pairs={{4,8},{8,4},{12,16},{16,12},{20,24},{24,20},{0,28},{28,0},{5,9},{9... | collective-permute-start | bytes 122888 | tf_op jit(solution)/shard_map/ppermute | solution.py:439
  51.1 4.3 %collective-permute-done.12 = f32[80,128]{1,0:T(8,128)S(1)} collective-permute-done((f32[80,128]{1,0:T(8,128)S(1)}, f32[80,128]{1,0:T(8,128)S(1)}, u32[]{:S(2)}, u32[]{:S(2)}) %collective-permute-start.12) | collective-permute-done | bytes 40992 | tf_op jit(solution)/shard_map/ppermute | solution.py:439
  56.3 4.1 %collective-permute-done.15.next_ref = f32[240,128]{1,0:T(8,128)S(1)} collective-permute-done((f32[240,128]{1,0:T(8,128)S(1)}, f32[240,128]{1,0:T(8,128)S(1)}, u32[]{:S(2)}, u32[]{:S(2)}) %collective-permute-start.15) | collective-permute-done | bytes 122912 | tf_op jit(solution)/shard_map/ppermute | solution.py:439
  60.3 6.1 %shard_map.110 = (f32[240,128]{1,0:T(8,128)S(1)}, f32[240,128]{1,0:T(8,128)S(1)}, f32[240,128]{1,0:T(8,128)S(1)}) custom-call(s32[1,3200]{1,0:T(1,128)S(1)} %reshape.15.idx_ref, f32[240,128]{1,0:T(8,128)S(1)} %constant_dynamic-update-slice_fusion.own_ref, f32[240,128]{1,0:T(8,128)S(1)} %collective-permute-done.14.even_ref, ...), custom_call_target="tpu_custom_call" | custom-call | flops 4000000000 | bytes 2749952 | tf_op jit(solution)/shard_map/pallas_call | solution.py:55
  68.1 3.6 %collective-permute-done.17.z_ref = f32[240,128]{1,0:T(8,128)S(1)} collective-permute-done((f32[240,128]{1,0:T(8,128)S(1)}, f32[240,128]{1,0:T(8,128)S(1)}, u32[]{:S(2)}, u32[]{:S(2)}) %collective-permute-start.17) | collective-permute-done | bytes 122912 | tf_op jit(solution)/shard_map/ppermute | solution.py:439
  71.8 2.3 %collective-permute-start.19 = (f32[80,128]{1,0:T(8,128)S(1)}, f32[80,128]{1,0:T(8,128)S(1)}, u32[]{:S(2)}, u32[]{:S(2)}) collective-permute-start(f32[80,128]{1,0:T(8,128)S(1)} %get-tuple-element.53), channel_id=1, source_target_pairs={{4,8},{8,4},{12,16},{16,12},{20,24},{24,20},{0,28},{28,0},{5,9},{9... | collective-permute-start | bytes 122888 | tf_op jit(solution)/shard_map/ppermute | solution.py:439
  74.0 1.8 %collective-permute-done.18.y_ref = f32[80,128]{1,0:T(8,128)S(1)} collective-permute-done((f32[80,128]{1,0:T(8,128)S(1)}, f32[80,128]{1,0:T(8,128)S(1)}, u32[]{:S(2)}, u32[]{:S(2)}) %collective-permute-start.18) | collective-permute-done | bytes 40992 | tf_op jit(solution)/shard_map/ppermute | solution.py:439
  75.8 2.8 %collective-permute-done.19.z_ref = f32[80,128]{1,0:T(8,128)S(1)} collective-permute-done((f32[80,128]{1,0:T(8,128)S(1)}, f32[80,128]{1,0:T(8,128)S(1)}, u32[]{:S(2)}, u32[]{:S(2)}) %collective-permute-start.19) | collective-permute-done | bytes 40992 | tf_op jit(solution)/shard_map/ppermute | solution.py:439
  80.2 2.2 %collective-permute-start.21 = (f32[3,16,256]{2,1,0:T(8,128)S(1)}, f32[3,16,256]{2,1,0:T(8,128)S(1)}, u32[]{:S(2)}, u32[]{:S(2)}) collective-permute-start(f32[3,16,256]{2,1,0:T(8,128)S(1)} %get-tuple-element.56), channel_id=1, source_target_pairs={{4,8},{8,4},{12,16},{16,12},{20,24},{24,20},{0,28},{28,0},{5,9},{9... | collective-permute-start | bytes 147464 | tf_op jit(solution)/shard_map/ppermute | solution.py:439
  90.4 2.2 %collective-permute-done.25 = f32[16,128]{1,0:T(8,128)S(1)} collective-permute-done((f32[16,128]{1,0:T(8,128)S(1)}, f32[16,128]{1,0:T(8,128)S(1)}, u32[]{:S(2)}, u32[]{:S(2)}) %collective-permute-start.25) | collective-permute-done | bytes 8224 | tf_op jit(solution)/shard_map/ppermute | solution.py:449
  92.7 3.7 %collective-permute-done.26 = f32[32,128]{1,0:T(8,128)S(1)} collective-permute-done((f32[32,128]{1,0:T(8,128)S(1)}, f32[32,128]{1,0:T(8,128)S(1)}, u32[]{:S(2)}, u32[]{:S(2)}) %collective-permute-start.26) | collective-permute-done | bytes 16416 | tf_op jit(solution)/shard_map/ppermute | solution.py:449
  96.4 3.9 %collective-permute-done.27 = f32[64,128]{1,0:T(8,128)S(1)} collective-permute-done((f32[64,128]{1,0:T(8,128)S(1)}, f32[64,128]{1,0:T(8,128)S(1)}, u32[]{:S(2)}, u32[]{:S(2)}) %collective-permute-start.27) | collective-permute-done | bytes 32800 | tf_op jit(solution)/shard_map/ppermute | solution.py:449
  100.3 5.6 %collective-permute-done.28 = f32[128,128]{1,0:T(8,128)S(1)} collective-permute-done((f32[128,128]{1,0:T(8,128)S(1)}, f32[128,128]{1,0:T(8,128)S(1)}, u32[]{:S(2)}, u32[]{:S(2)}) %collective-permute-start.28) | collective-permute-done | bytes 65568 | tf_op jit(solution)/shard_map/ppermute | solution.py:449
  (82 shorter events, 25.2 us)
Async XLA Ops:
  3.6 8.3 %collective-permute-start.1 = (f32[80,128]{1,0:T(8,128)}, f32[80,128]{1,0:T(8,128)S(1)}, u32[]{:S(2)}, u32[]{:S(2)}) collective-permute-start(f32[80,128]{1,0:T(8,128)} %shard_map.104), channel_id=1, source_target_pairs={{4,8},{8,4},{12,16},{16,12},{20,24},{24,20},{0,28},{28,0},{5,9},{9... | collective-permute-start | bytes 122888 | tf_op jit(solution)/shard_map/ppermute | solution.py:439
  9.7 4.2 %collective-permute-start = (f32[80,128]{1,0:T(8,128)}, f32[80,128]{1,0:T(8,128)S(1)}, u32[]{:S(2)}, u32[]{:S(2)}) collective-permute-start(f32[80,128]{1,0:T(8,128)} %shard_map.104), channel_id=1, source_target_pairs={{0,4},{4,0},{8,12},{12,8},{16,20},{20,16},{24,28},{28,24},{1,5},{5... | collective-permute-start | bytes 122888 | tf_op jit(solution)/shard_map/ppermute | solution.py:439
  14.7 5.6 %collective-permute-start.3 = (f32[240,128]{1,0:T(8,128)S(1)}, f32[240,128]{1,0:T(8,128)S(1)}, u32[]{:S(2)}, u32[]{:S(2)}) collective-permute-start(f32[240,128]{1,0:T(8,128)S(1)} %pad_maximum_fusion.own_ref), channel_id=1, source_target_pairs={{1,2},{2,1},{0,3},{3,0},{5,6},{6,5},{4,7},{7,4},{9,10},{10,9},{8,1... | collective-permute-start | bytes 368648 | tf_op jit(solution)/shard_map/ppermute | solution.py:439
  14.8 5.6 %collective-permute-start.2 = (f32[240,128]{1,0:T(8,128)S(1)}, f32[240,128]{1,0:T(8,128)S(1)}, u32[]{:S(2)}, u32[]{:S(2)}) collective-permute-start(f32[240,128]{1,0:T(8,128)S(1)} %pad_maximum_fusion.own_ref), channel_id=1, source_target_pairs={{0,1},{1,0},{2,3},{3,2},{4,5},{5,4},{6,7},{7,6},{8,9},{9,8},{10,11... | collective-permute-start | bytes 368648 | tf_op jit(solution)/shard_map/ppermute | solution.py:439
  26.4 5.1 %collective-permute-start.5 = (f32[240,128]{1,0:T(8,128)S(1)}, f32[240,128]{1,0:T(8,128)S(1)}, u32[]{:S(2)}, u32[]{:S(2)}) collective-permute-start(f32[240,128]{1,0:T(8,128)S(1)} %get-tuple-element.37), channel_id=1, source_target_pairs={{1,2},{2,1},{0,3},{3,0},{5,6},{6,5},{4,7},{7,4},{9,10},{10,9},{8,1... | collective-permute-start | bytes 368648 | tf_op jit(solution)/shard_map/ppermute | solution.py:439
  31.5 4.1 %collective-permute-start.6 = (f32[80,128]{1,0:T(8,128)S(1)}, f32[80,128]{1,0:T(8,128)S(1)}, u32[]{:S(2)}, u32[]{:S(2)}) collective-permute-start(f32[80,128]{1,0:T(8,128)S(1)} %get-tuple-element.39), channel_id=1, source_target_pairs={{0,4},{4,0},{8,12},{12,8},{16,20},{20,16},{24,28},{28,24},{1,5},{5... | collective-permute-start | bytes 122888 | tf_op jit(solution)/shard_map/ppermute | solution.py:439
  31.7 6.7 %collective-permute-start.7 = (f32[80,128]{1,0:T(8,128)S(1)}, f32[80,128]{1,0:T(8,128)S(1)}, u32[]{:S(2)}, u32[]{:S(2)}) collective-permute-start(f32[80,128]{1,0:T(8,128)S(1)} %get-tuple-element.40), channel_id=1, source_target_pairs={{4,8},{8,4},{12,16},{16,12},{20,24},{24,20},{0,28},{28,0},{5,9},{9... | collective-permute-start | bytes 122888 | tf_op jit(solution)/shard_map/ppermute | solution.py:439
  39.8 6.1 %collective-permute-start.8 = (f32[3,16,256]{2,1,0:T(8,128)S(1)}, f32[3,16,256]{2,1,0:T(8,128)S(1)}, u32[]{:S(2)}, u32[]{:S(2)}) collective-permute-start(f32[3,16,256]{2,1,0:T(8,128)S(1)} %get-tuple-element.42), channel_id=1, source_target_pairs={{0,4},{4,0},{8,12},{12,8},{16,20},{20,16},{24,28},{28,24},{1,5},{5... | collective-permute-start | bytes 147464 | tf_op jit(solution)/shard_map/ppermute | solution.py:439
  40.1 6.8 %collective-permute-start.9 = (f32[3,16,256]{2,1,0:T(8,128)S(1)}, f32[3,16,256]{2,1,0:T(8,128)S(1)}, u32[]{:S(2)}, u32[]{:S(2)}) collective-permute-start(f32[3,16,256]{2,1,0:T(8,128)S(1)} %get-tuple-element.43), channel_id=1, source_target_pairs={{4,8},{8,4},{12,16},{16,12},{20,24},{24,20},{0,28},{28,0},{5,9},{9... | collective-permute-start | bytes 147464 | tf_op jit(solution)/shard_map/ppermute | solution.py:439
  42.9 3.1 %collective-permute-start.11 = (f32[3,4,256]{2,1,0:T(4,128)S(1)}, f32[3,4,256]{2,1,0:T(4,128)S(1)}, u32[]{:S(2)}, u32[]{:S(2)}) collective-permute-start(f32[3,4,256]{2,1,0:T(4,128)S(1)} %get-tuple-element.45), channel_id=1, source_target_pairs={{1,2},{2,1},{0,3},{3,0},{5,6},{6,5},{4,7},{7,4},{9,10},{10,9},{8,1... | collective-permute-start | bytes 36872 | tf_op jit(solution)/shard_map/ppermute | solution.py:439
  48.3 7.2 %collective-permute-start.13 = (f32[80,128]{1,0:T(8,128)S(1)}, f32[80,128]{1,0:T(8,128)S(1)}, u32[]{:S(2)}, u32[]{:S(2)}) collective-permute-start(f32[80,128]{1,0:T(8,128)S(1)} %get-tuple-element.47), channel_id=1, source_target_pairs={{4,8},{8,4},{12,16},{16,12},{20,24},{24,20},{0,28},{28,0},{5,9},{9... | collective-permute-start | bytes 122888 | tf_op jit(solution)/shard_map/ppermute | solution.py:439
  51.1 4.3 %collective-permute-start.12 = (f32[80,128]{1,0:T(8,128)S(1)}, f32[80,128]{1,0:T(8,128)S(1)}, u32[]{:S(2)}, u32[]{:S(2)}) collective-permute-start(f32[80,128]{1,0:T(8,128)S(1)} %get-tuple-element.47), channel_id=1, source_target_pairs={{0,4},{4,0},{8,12},{12,8},{16,20},{20,16},{24,28},{28,24},{1,5},{5... | collective-permute-start | bytes 122888 | tf_op jit(solution)/shard_map/ppermute | solution.py:439
  55.5 4.8 %collective-permute-start.15 = (f32[240,128]{1,0:T(8,128)S(1)}, f32[240,128]{1,0:T(8,128)S(1)}, u32[]{:S(2)}, u32[]{:S(2)}) collective-permute-start(f32[240,128]{1,0:T(8,128)S(1)} %constant_dynamic-update-slice_fusion.own_ref), channel_id=1, source_target_pairs={{1,2},{2,1},{0,3},{3,0},{5,6},{6,5},{4,7},{7,4},{9,10},{10,9},{8,1... | collective-permute-start | bytes 368648 | tf_op jit(solution)/shard_map/ppermute | solution.py:439
  55.6 4.8 %collective-permute-start.14 = (f32[240,128]{1,0:T(8,128)S(1)}, f32[240,128]{1,0:T(8,128)S(1)}, u32[]{:S(2)}, u32[]{:S(2)}) collective-permute-start(f32[240,128]{1,0:T(8,128)S(1)} %constant_dynamic-update-slice_fusion.own_ref), channel_id=1, source_target_pairs={{0,1},{1,0},{2,3},{3,2},{4,5},{5,4},{6,7},{7,6},{8,9},{9,8},{10,11... | collective-permute-start | bytes 368648 | tf_op jit(solution)/shard_map/ppermute | solution.py:439
  66.5 5.1 %collective-permute-start.17 = (f32[240,128]{1,0:T(8,128)S(1)}, f32[240,128]{1,0:T(8,128)S(1)}, u32[]{:S(2)}, u32[]{:S(2)}) collective-permute-start(f32[240,128]{1,0:T(8,128)S(1)} %get-tuple-element.50), channel_id=1, source_target_pairs={{1,2},{2,1},{0,3},{3,0},{5,6},{6,5},{4,7},{7,4},{9,10},{10,9},{8,1... | collective-permute-start | bytes 368648 | tf_op jit(solution)/shard_map/ppermute | solution.py:439
  71.7 4.1 %collective-permute-start.18 = (f32[80,128]{1,0:T(8,128)S(1)}, f32[80,128]{1,0:T(8,128)S(1)}, u32[]{:S(2)}, u32[]{:S(2)}) collective-permute-start(f32[80,128]{1,0:T(8,128)S(1)} %get-tuple-element.52), channel_id=1, source_target_pairs={{0,4},{4,0},{8,12},{12,8},{16,20},{20,16},{24,28},{28,24},{1,5},{5... | collective-permute-start | bytes 122888 | tf_op jit(solution)/shard_map/ppermute | solution.py:439
  71.8 6.8 %collective-permute-start.19 = (f32[80,128]{1,0:T(8,128)S(1)}, f32[80,128]{1,0:T(8,128)S(1)}, u32[]{:S(2)}, u32[]{:S(2)}) collective-permute-start(f32[80,128]{1,0:T(8,128)S(1)} %get-tuple-element.53), channel_id=1, source_target_pairs={{4,8},{8,4},{12,16},{16,12},{20,24},{24,20},{0,28},{28,0},{5,9},{9... | collective-permute-start | bytes 122888 | tf_op jit(solution)/shard_map/ppermute | solution.py:439
  80.0 5.5 %collective-permute-start.20 = (f32[3,16,256]{2,1,0:T(8,128)S(1)}, f32[3,16,256]{2,1,0:T(8,128)S(1)}, u32[]{:S(2)}, u32[]{:S(2)}) collective-permute-start(f32[3,16,256]{2,1,0:T(8,128)S(1)} %get-tuple-element.55), channel_id=1, source_target_pairs={{0,4},{4,0},{8,12},{12,8},{16,20},{20,16},{24,28},{28,24},{1,5},{5... | collective-permute-start | bytes 147464 | tf_op jit(solution)/shard_map/ppermute | solution.py:439
  80.2 6.8 %collective-permute-start.21 = (f32[3,16,256]{2,1,0:T(8,128)S(1)}, f32[3,16,256]{2,1,0:T(8,128)S(1)}, u32[]{:S(2)}, u32[]{:S(2)}) collective-permute-start(f32[3,16,256]{2,1,0:T(8,128)S(1)} %get-tuple-element.56), channel_id=1, source_target_pairs={{4,8},{8,4},{12,16},{16,12},{20,24},{24,20},{0,28},{28,0},{5,9},{9... | collective-permute-start | bytes 147464 | tf_op jit(solution)/shard_map/ppermute | solution.py:439
  82.4 3.1 %collective-permute-start.23 = (f32[3,4,256]{2,1,0:T(4,128)S(1)}, f32[3,4,256]{2,1,0:T(4,128)S(1)}, u32[]{:S(2)}, u32[]{:S(2)}) collective-permute-start(f32[3,4,256]{2,1,0:T(4,128)S(1)} %get-tuple-element.58), channel_id=1, source_target_pairs={{1,2},{2,1},{0,3},{3,0},{5,6},{6,5},{4,7},{7,4},{9,10},{10,9},{8,1... | collective-permute-start | bytes 36872 | tf_op jit(solution)/shard_map/ppermute | solution.py:439
  89.0 3.7 %collective-permute-start.25 = (f32[16,128]{1,0:T(8,128)S(1)}, f32[16,128]{1,0:T(8,128)S(1)}, u32[]{:S(2)}, u32[]{:S(2)}) collective-permute-start(f32[16,128]{1,0:T(8,128)S(1)} %pad_maximum_fusion.3), channel_id=1, source_target_pairs={{0,2},{1,3},{2,0},{3,1},{4,6},{5,7},{6,4},{7,5},{8,10},{9,11},{10,... | collective-permute-start | bytes 24584 | tf_op jit(solution)/shard_map/ppermute | solution.py:449
  92.6 3.7 %collective-permute-start.26 = (f32[32,128]{1,0:T(8,128)S(1)}, f32[32,128]{1,0:T(8,128)S(1)}, u32[]{:S(2)}, u32[]{:S(2)}) collective-permute-start(f32[32,128]{1,0:T(8,128)S(1)} %pad_maximum_fusion.2), channel_id=1, source_target_pairs={{0,4},{4,0},{8,12},{12,8},{16,20},{20,16},{24,28},{28,24},{1,5},{5... | collective-permute-start | bytes 49160 | tf_op jit(solution)/shard_map/ppermute | solution.py:449
  96.3 3.9 %collective-permute-start.27 = (f32[64,128]{1,0:T(8,128)S(1)}, f32[64,128]{1,0:T(8,128)S(1)}, u32[]{:S(2)}, u32[]{:S(2)}) collective-permute-start(f32[64,128]{1,0:T(8,128)S(1)} %pad_maximum_fusion.1), channel_id=1, source_target_pairs={{0,8},{4,12},{8,0},{12,4},{16,24},{20,28},{24,16},{28,20},{1,9},{5... | collective-permute-start | bytes 98312 | tf_op jit(solution)/shard_map/ppermute | solution.py:449
  100.3 5.7 %collective-permute-start.28 = (f32[128,128]{1,0:T(8,128)S(1)}, f32[128,128]{1,0:T(8,128)S(1)}, u32[]{:S(2)}, u32[]{:S(2)}) collective-permute-start(f32[128,128]{1,0:T(8,128)S(1)} %get-tuple-element.62), channel_id=1, source_target_pairs={{0,16},{4,20},{8,24},{12,28},{16,0},{20,4},{24,8},{28,12},{1,17},{... | collective-permute-start | bytes 196616 | tf_op jit(solution)/shard_map/ppermute | solution.py:449
  (14 other events, 159.9 us)

commit v5 on v4

--- a/solution.py
+++ b/solution.py
@@ -402,22 +402,9 @@
 
 
 def final_kernel(
-    all_ref, v_ref, z1_ref, z2_ref, w1_ref, w2_ref, sol_ref, res_ref
+    sums_ref, v_ref, z1_ref, z2_ref, w1_ref, w2_ref, sol_ref, res_ref
 ):
-    every = [all_ref[:, place, :] for place in range(7)]
-    top_one = jnp.max(every[5], axis=0, keepdims=True)
-    top_two = jnp.max(every[6], axis=0, keepdims=True)
-    one = every[5] / top_one
-    two = every[6] / top_two
-
-    def add(value):
-        return jnp.sum(value, axis=0, keepdims=True)
-
-    g11 = add(every[0] * one * one)
-    g12 = add(every[1] * one * two)
-    g22 = add(every[2] * two * two)
-    r1 = add(every[3] * one)
-    r2 = add(every[4] * two)
+    g11, g12, g22, r1, r2, top_one, top_two = [sums_ref[i : i + 1, :] for i in range(7)]
     det = g11 * g22 - g12 * g12
     y1 = ((g22 * r1 - g12 * r2) / det / top_one)[:, :1]
     y2 = ((g11 * r2 - g12 * r1) / det / top_two)[:, :1]
@@ -426,29 +413,64 @@
 
 
 def swap(axis, to_even, to_next):
-    count = lax.axis_size(axis)
+    size = {name: lax.axis_size(name) for name in ("gx", "gy")}
+    count, breadth = size[axis], size["gy" if axis == "gx" else "gx"]
+
+    def device(along, across):
+        return along * size["gy"] + across if axis == "gx" else across * size["gy"] + along
+
     out = []
     for first, value in ((0, to_even), (1, to_next)):
         pairs = []
-        for i in range(first, count - 1, 2):
-            pairs += [(i, i + 1), (i + 1, i)]
-        if first and count % 2 == 0 and count > 2:
-            pairs += [(0, count - 1), (count - 1, 0)]
-        taken = [source for source, _ in pairs]
-        pairs += [(i, i) for i in range(count) if i not in taken]
-        out.append(lax.ppermute(value, axis, pairs))
+        for across in range(breadth):
+            for i in range(count):
+                other = i + 1 if i % 2 == first else i - 1
+                if 0 <= other < count:
+                    pairs.append((device(i, across), device(other, across)))
+                elif across ^ 1 < breadth:
+                    pairs.append((device(i, across), device(i, across ^ 1)))
+                else:
+                    pairs.append((device(i, across), device(i, across)))
+        out.append(lax.ppermute(value, ("gx", "gy"), pairs))
     return out
 
 
-def gather_all(value, axis):
+def merge_kernel(*refs):
+    *parts, out_ref = refs
+    parts = [part[...] for part in parts]
+    tops = [[part[place : place + 1] for part in parts] for place in (5, 6)]
+    top_one, top_two = [functools.reduce(jnp.maximum, top) for top in tops]
+    line = iota(out_ref.shape, 0)
+    total = None
+    for part in parts:
+        one, two = part[5:6] / top_one, part[6:7] / top_two
+        scale = jnp.where(
+            line == 0, one * one, jnp.where(
+                line == 1, one * two, jnp.where(
+                    line == 2, two * two, jnp.where(line == 3, one, two)
+                )
+            ),
+        )
+        part = part * scale
+        total = part if total is None else total + part
+    total = jnp.where(line == 5, top_one, jnp.where(line == 6, top_two, total))
+    out_ref[...] = total
+
+
+def merge_all(value, axis):
     count = lax.axis_size(axis)
     if count & (count - 1):
-        return lax.all_gather(value, axis, tiled=True)
+        every = lax.all_gather(value, axis)
+        return call(merge_kernel, [value.shape])(*[every[i] for i in range(count)])[0]
     step = 1
     while step < count:
-        other = lax.ppermute(value, axis, [(i, i ^ step) for i in range(count)])
-        value = jnp.concatenate([value, other], axis=0)
-        step *= 2
+        radix = min(4, count // step)
+        others = [
+            lax.ppermute(value, axis, [(i, i ^ (k * step)) for i in range(count)])
+            for k in range(1, radix)
+        ]
+        (value,) = call(merge_kernel, [value.shape])(value, *others)
+        step *= radix
     return value
 
 
@@ -535,9 +557,9 @@
     w2, sums = call(gram_kernel, [field, (8, LANES)])(
         z2, *faces, diag_blocks, off_blocks, right_side, w1
     )
-    every = gather_all(gather_all(sums, "gy"), "gx").reshape(-1, 8, LANES)
+    sums = merge_all(merge_all(sums, "gy"), "gx")
     return tuple(
-        call(final_kernel, [field, field])(every, right_side, z1, z2, w1, w2)
+        call(final_kernel, [field, field])(sums, right_side, z1, z2, w1, w2)
     )
 
 

time: 107 us -> 94.8 us (0.89)
  waiting for transfers between devices: 54.2 us -> 28.4 us
  starting transfers between devices: 28.2 us -> 41.7 us
    ppermute x29 -> x31, waiting for transfers between devices: 54.2 us -> 28.4 us  [the longest x24 21.2 us: swap(): out.append(lax.ppermute(value, ('gx', 'gy'), pairs))]
    ppermute x29 -> x31, starting transfers between devices: 28.2 us -> 41.7 us  [the longest x24 33.5 us: swap(): out.append(lax.ppermute(value, ('gx', 'gy'), pairs))]
    pallas_call x11 -> x14, Pallas kernels: 22.2 us -> 22.2 us  [run(): pl.pallas_call(kernel, out_shape=[jax.ShapeDtypeStruct(o, F32) for o in o...]
  transfers between devices with their start and end apart: 29 -> 31, of which waited for: 22 -> 16; matrix products, arithmetic and copies ran while one was open for 0% -> 1% of each run, Pallas kernels for 1% -> 1%
where the time goes in v5:
time: 94.8 us; the launch traced here: 94.6 us
  starting transfers between devices  41.7 us (44%)
  waiting for transfers between devices  28.4 us (30%)
  Pallas kernels  22.2 us (23%)
    ppermute x24, starting transfers between devices, swap(): out.append(lax.ppermute(value, ('gx', 'gy'), pairs))  33.5 us
    pallas_call x14, Pallas kernels, run(): pl.pallas_call(kernel, out_shape=[jax.ShapeDtypeStruct(o, F32) for o in o...  22.2 us
    ppermute x24, waiting for transfers between devices, swap(): out.append(lax.ppermute(value, ('gx', 'gy'), pairs))  21.2 us
    ppermute x7, starting transfers between devices, merge_all(): lax.ppermute(value, axis, [(i, i ^ k * step) for i in range(count)])  8.2 us
    ppermute x7, waiting for transfers between devices, merge_all(): lax.ppermute(value, axis, [(i, i ^ k * step) for i in range(count)])  7.27 us
  transfers between devices with their start and end apart: 31, of which 16 were waited for; matrix products, arithmetic and copies ran while one was open for 1% of the time, Pallas kernels for 1%

profile of v5, /device:TPU:0, one launch (start us, length us, event | category | flops | bytes accessed | tf_op | source)
XLA Modules:
  0.0 94.6 jit_solution(5247081815025396189)
XLA Ops:
  0.7 2.9 %shard_map.104 = f32[80,128]{1,0:T(8,128)} custom-call(s32[1,3200]{1,0:T(1,128)} %cells_ref.5, f32[3,4,16,256]{3,2,1,0:T(8,128)} %v_ref.7, f32[9,4,16,256]{3,2,1,0:T(8,128)} %d_ref.3), custom_call_target="tpu_custom_call" | custom-call | flops 1000000000 | bytes 840192 | tf_op jit(solution)/shard_map/pallas_call | solution.py:55
  4.1 4.0 %collective-permute-start = (f32[80,128]{1,0:T(8,128)}, f32[80,128]{1,0:T(8,128)S(1)}, u32[]{:S(2)}, u32[]{:S(2)}) collective-permute-start(f32[80,128]{1,0:T(8,128)} %shard_map.104), channel_id=1, source_target_pairs={{0,4},{4,0},{8,12},{12,8},{16,20},{20,16},{24,28},{28,24},{1,5},{5... | collective-permute-start | bytes 122888 | tf_op jit(solution)/shard_map/ppermute | solution.py:434
  8.2 2.2 %collective-permute-done = f32[80,128]{1,0:T(8,128)S(1)} collective-permute-done((f32[80,128]{1,0:T(8,128)}, f32[80,128]{1,0:T(8,128)S(1)}, u32[]{:S(2)}, u32[]{:S(2)}) %collective-permute-start) | collective-permute-done | bytes 40992 | tf_op jit(solution)/shard_map/ppermute | solution.py:434
  11.2 2.1 %collective-permute-start.3 = (f32[240,128]{1,0:T(8,128)S(1)}, f32[240,128]{1,0:T(8,128)S(1)}, u32[]{:S(2)}, u32[]{:S(2)}) collective-permute-start(f32[240,128]{1,0:T(8,128)S(1)} %pad_maximum_fusion.own_ref), channel_id=1, source_target_pairs={{0,4},{1,2},{2,1},{3,7},{4,0},{5,6},{6,5},{7,3},{8,12},{9,10},{10,... | collective-permute-start | bytes 368648 | tf_op jit(solution)/shard_map/ppermute | solution.py:434
  16.1 5.9 %shard_map.106 = (f32[240,128]{1,0:T(8,128)S(1)}, f32[240,128]{1,0:T(8,128)S(1)}, f32[240,128]{1,0:T(8,128)S(1)}) custom-call(s32[1,3200]{1,0:T(1,128)S(1)} %reshape.12.idx_ref, f32[240,128]{1,0:T(8,128)S(1)} %pad_maximum_fusion.own_ref, f32[240,128]{1,0:T(8,128)S(1)} %collective-permute-done.2.even_ref, f32[240,128]{1,0:T(8,128)S(1)} %collective-permute-done.3.next_ref, ...), custom_call_target="tpu_custom_call" | custom-call | flops 4000000000 | bytes 2749952 | tf_op jit(solution)/shard_map/pallas_call | solution.py:55
  22.1 2.1 %collective-permute-start.5 = (f32[240,128]{1,0:T(8,128)S(1)}, f32[240,128]{1,0:T(8,128)S(1)}, u32[]{:S(2)}, u32[]{:S(2)}) collective-permute-start(f32[240,128]{1,0:T(8,128)S(1)} %get-tuple-element.37), channel_id=1, source_target_pairs={{0,4},{1,2},{2,1},{3,7},{4,0},{5,6},{6,5},{7,3},{8,12},{9,10},{10,... | collective-permute-start | bytes 368648 | tf_op jit(solution)/shard_map/ppermute | solution.py:434
  24.2 2.9 %collective-permute-done.5.z_ref = f32[240,128]{1,0:T(8,128)S(1)} collective-permute-done((f32[240,128]{1,0:T(8,128)S(1)}, f32[240,128]{1,0:T(8,128)S(1)}, u32[]{:S(2)}, u32[]{:S(2)}) %collective-permute-start.5) | collective-permute-done | bytes 122912 | tf_op jit(solution)/shard_map/ppermute | solution.py:434
  27.1 2.1 %collective-permute-start.6 = (f32[80,128]{1,0:T(8,128)S(1)}, f32[80,128]{1,0:T(8,128)S(1)}, u32[]{:S(2)}, u32[]{:S(2)}) collective-permute-start(f32[80,128]{1,0:T(8,128)S(1)} %get-tuple-element.39), channel_id=1, source_target_pairs={{0,4},{4,0},{8,12},{12,8},{16,20},{20,16},{24,28},{28,24},{1,5},{5... | collective-permute-start | bytes 122888 | tf_op jit(solution)/shard_map/ppermute | solution.py:434
  29.2 2.0 %collective-permute-done.6.y_ref = f32[80,128]{1,0:T(8,128)S(1)} collective-permute-done((f32[80,128]{1,0:T(8,128)S(1)}, f32[80,128]{1,0:T(8,128)S(1)}, u32[]{:S(2)}, u32[]{:S(2)}) %collective-permute-start.6) | collective-permute-done | bytes 40992 | tf_op jit(solution)/shard_map/ppermute | solution.py:434
  32.6 3.1 %collective-permute-start.8 = (f32[3,16,256]{2,1,0:T(8,128)S(1)}, f32[3,16,256]{2,1,0:T(8,128)S(1)}, u32[]{:S(2)}, u32[]{:S(2)}) collective-permute-start(f32[3,16,256]{2,1,0:T(8,128)S(1)} %get-tuple-element.42), channel_id=1, source_target_pairs={{0,4},{4,0},{8,12},{12,8},{16,20},{20,16},{24,28},{28,24},{1,5},{5... | collective-permute-start | bytes 147464 | tf_op jit(solution)/shard_map/ppermute | solution.py:434
  36.2 2.8 %collective-permute-start.11 = (f32[3,4,256]{2,1,0:T(4,128)S(1)}, f32[3,4,256]{2,1,0:T(4,128)S(1)}, u32[]{:S(2)}, u32[]{:S(2)}) collective-permute-start(f32[3,4,256]{2,1,0:T(4,128)S(1)} %get-tuple-element.45), channel_id=1, source_target_pairs={{0,4},{1,2},{2,1},{3,7},{4,0},{5,6},{6,5},{7,3},{8,12},{9,10},{10,... | collective-permute-start | bytes 36872 | tf_op jit(solution)/shard_map/ppermute | solution.py:434
  42.2 3.4 %collective-permute-start.12 = (f32[80,128]{1,0:T(8,128)S(1)}, f32[80,128]{1,0:T(8,128)S(1)}, u32[]{:S(2)}, u32[]{:S(2)}) collective-permute-start(f32[80,128]{1,0:T(8,128)S(1)} %get-tuple-element.47), channel_id=1, source_target_pairs={{0,4},{4,0},{8,12},{12,8},{16,20},{20,16},{24,28},{28,24},{1,5},{5... | collective-permute-start | bytes 122888 | tf_op jit(solution)/shard_map/ppermute | solution.py:434
  47.6 2.1 %collective-permute-start.15 = (f32[240,128]{1,0:T(8,128)S(1)}, f32[240,128]{1,0:T(8,128)S(1)}, u32[]{:S(2)}, u32[]{:S(2)}) collective-permute-start(f32[240,128]{1,0:T(8,128)S(1)} %constant_dynamic-update-slice_fusion.own_ref), channel_id=1, source_target_pairs={{0,4},{1,2},{2,1},{3,7},{4,0},{5,6},{6,5},{7,3},{8,12},{9,10},{10,... | collective-permute-start | bytes 368648 | tf_op jit(solution)/shard_map/ppermute | solution.py:434
  49.7 2.9 %collective-permute-done.15.next_ref = f32[240,128]{1,0:T(8,128)S(1)} collective-permute-done((f32[240,128]{1,0:T(8,128)S(1)}, f32[240,128]{1,0:T(8,128)S(1)}, u32[]{:S(2)}, u32[]{:S(2)}) %collective-permute-start.15) | collective-permute-done | bytes 122912 | tf_op jit(solution)/shard_map/ppermute | solution.py:434
  52.6 6.1 %shard_map.110 = (f32[240,128]{1,0:T(8,128)S(1)}, f32[240,128]{1,0:T(8,128)S(1)}, f32[240,128]{1,0:T(8,128)S(1)}) custom-call(s32[1,3200]{1,0:T(1,128)S(1)} %reshape.12.idx_ref, f32[240,128]{1,0:T(8,128)S(1)} %constant_dynamic-update-slice_fusion.own_ref, f32[240,128]{1,0:T(8,128)S(1)} %collective-permute-done.14.even_ref, ...), custom_call_target="tpu_custom_call" | custom-call | flops 4000000000 | bytes 2749952 | tf_op jit(solution)/shard_map/pallas_call | solution.py:55
  58.8 2.1 %collective-permute-start.17 = (f32[240,128]{1,0:T(8,128)S(1)}, f32[240,128]{1,0:T(8,128)S(1)}, u32[]{:S(2)}, u32[]{:S(2)}) collective-permute-start(f32[240,128]{1,0:T(8,128)S(1)} %get-tuple-element.50), channel_id=1, source_target_pairs={{0,4},{1,2},{2,1},{3,7},{4,0},{5,6},{6,5},{7,3},{8,12},{9,10},{10,... | collective-permute-start | bytes 368648 | tf_op jit(solution)/shard_map/ppermute | solution.py:434
  60.9 2.9 %collective-permute-done.17.z_ref = f32[240,128]{1,0:T(8,128)S(1)} collective-permute-done((f32[240,128]{1,0:T(8,128)S(1)}, f32[240,128]{1,0:T(8,128)S(1)}, u32[]{:S(2)}, u32[]{:S(2)}) %collective-permute-start.17) | collective-permute-done | bytes 122912 | tf_op jit(solution)/shard_map/ppermute | solution.py:434
  63.8 2.1 %collective-permute-start.18 = (f32[80,128]{1,0:T(8,128)S(1)}, f32[80,128]{1,0:T(8,128)S(1)}, u32[]{:S(2)}, u32[]{:S(2)}) collective-permute-start(f32[80,128]{1,0:T(8,128)S(1)} %get-tuple-element.52), channel_id=1, source_target_pairs={{0,4},{4,0},{8,12},{12,8},{16,20},{20,16},{24,28},{28,24},{1,5},{5... | collective-permute-start | bytes 122888 | tf_op jit(solution)/shard_map/ppermute | solution.py:434
  69.3 3.2 %collective-permute-start.20 = (f32[3,16,256]{2,1,0:T(8,128)S(1)}, f32[3,16,256]{2,1,0:T(8,128)S(1)}, u32[]{:S(2)}, u32[]{:S(2)}) collective-permute-start(f32[3,16,256]{2,1,0:T(8,128)S(1)} %get-tuple-element.55), channel_id=1, source_target_pairs={{0,4},{4,0},{8,12},{12,8},{16,20},{20,16},{24,28},{28,24},{1,5},{5... | collective-permute-start | bytes 147464 | tf_op jit(solution)/shard_map/ppermute | solution.py:434
  73.0 2.8 %collective-permute-start.23 = (f32[3,4,256]{2,1,0:T(4,128)S(1)}, f32[3,4,256]{2,1,0:T(4,128)S(1)}, u32[]{:S(2)}, u32[]{:S(2)}) collective-permute-start(f32[3,4,256]{2,1,0:T(4,128)S(1)} %get-tuple-element.58), channel_id=1, source_target_pairs={{0,4},{1,2},{2,1},{3,7},{4,0},{5,6},{6,5},{7,3},{8,12},{9,10},{10,... | collective-permute-start | bytes 36872 | tf_op jit(solution)/shard_map/ppermute | solution.py:434
  82.0 3.1 %collective-permute-start.29 = (f32[8,128]{1,0:T(8,128)S(1)}, f32[8,128]{1,0:T(8,128)S(1)}, u32[]{:S(2)}, u32[]{:S(2)}) collective-permute-start(f32[8,128]{1,0:T(8,128)S(1)} %shard_map.114.refs_0_), channel_id=1, source_target_pairs={{0,12},{4,8},{8,4},{12,0},{16,28},{20,24},{24,20},{28,16},{1,13},{... | collective-permute-start | bytes 12296 | tf_op jit(solution)/shard_map/ppermute | solution.py:469
  86.7 2.0 %collective-permute-done.28.refs_2_ = f32[8,128]{1,0:T(8,128)S(1)} collective-permute-done((f32[8,128]{1,0:T(8,128)S(1)}, f32[8,128]{1,0:T(8,128)S(1)}, u32[]{:S(2)}, u32[]{:S(2)}) %collective-permute-start.28) | collective-permute-done | bytes 4128 | tf_op jit(solution)/shard_map/ppermute | solution.py:469
  89.2 2.5 %collective-permute-start.30 = (f32[8,128]{1,0:T(8,128)S(1)}, f32[8,128]{1,0:T(8,128)S(1)}, u32[]{:S(2)}, u32[]{:S(2)}) collective-permute-start(f32[8,128]{1,0:T(8,128)S(1)} %shard_map.115.refs_0_), channel_id=1, source_target_pairs={{0,16},{4,20},{8,24},{12,28},{16,0},{20,4},{24,8},{28,12},{1,17},{... | collective-permute-start | bytes 12296 | tf_op jit(solution)/shard_map/ppermute | solution.py:469
  91.7 2.0 %collective-permute-done.30.refs_1_ = f32[8,128]{1,0:T(8,128)S(1)} collective-permute-done((f32[8,128]{1,0:T(8,128)S(1)}, f32[8,128]{1,0:T(8,128)S(1)}, u32[]{:S(2)}, u32[]{:S(2)}) %collective-permute-start.30) | collective-permute-done | bytes 4128 | tf_op jit(solution)/shard_map/ppermute | solution.py:469
  (80 shorter events, 24.4 us)
Async XLA Ops:
  3.6 4.6 %collective-permute-start.1 = (f32[80,128]{1,0:T(8,128)}, f32[80,128]{1,0:T(8,128)S(1)}, u32[]{:S(2)}, u32[]{:S(2)}) collective-permute-start(f32[80,128]{1,0:T(8,128)} %shard_map.104), channel_id=1, source_target_pairs={{0,1},{4,8},{8,4},{12,16},{16,12},{20,24},{24,20},{28,29},{1,0},{5... | collective-permute-start | bytes 122888 | tf_op jit(solution)/shard_map/ppermute | solution.py:434
  4.1 6.3 %collective-permute-start = (f32[80,128]{1,0:T(8,128)}, f32[80,128]{1,0:T(8,128)S(1)}, u32[]{:S(2)}, u32[]{:S(2)}) collective-permute-start(f32[80,128]{1,0:T(8,128)} %shard_map.104), channel_id=1, source_target_pairs={{0,4},{4,0},{8,12},{12,8},{16,20},{20,16},{24,28},{28,24},{1,5},{5... | collective-permute-start | bytes 122888 | tf_op jit(solution)/shard_map/ppermute | solution.py:434
  11.2 4.9 %collective-permute-start.3 = (f32[240,128]{1,0:T(8,128)S(1)}, f32[240,128]{1,0:T(8,128)S(1)}, u32[]{:S(2)}, u32[]{:S(2)}) collective-permute-start(f32[240,128]{1,0:T(8,128)S(1)} %pad_maximum_fusion.own_ref), channel_id=1, source_target_pairs={{0,4},{1,2},{2,1},{3,7},{4,0},{5,6},{6,5},{7,3},{8,12},{9,10},{10,... | collective-permute-start | bytes 368648 | tf_op jit(solution)/shard_map/ppermute | solution.py:434
  22.1 4.9 %collective-permute-start.5 = (f32[240,128]{1,0:T(8,128)S(1)}, f32[240,128]{1,0:T(8,128)S(1)}, u32[]{:S(2)}, u32[]{:S(2)}) collective-permute-start(f32[240,128]{1,0:T(8,128)S(1)} %get-tuple-element.37), channel_id=1, source_target_pairs={{0,4},{1,2},{2,1},{3,7},{4,0},{5,6},{6,5},{7,3},{8,12},{9,10},{10,... | collective-permute-start | bytes 368648 | tf_op jit(solution)/shard_map/ppermute | solution.py:434
  27.1 4.1 %collective-permute-start.6 = (f32[80,128]{1,0:T(8,128)S(1)}, f32[80,128]{1,0:T(8,128)S(1)}, u32[]{:S(2)}, u32[]{:S(2)}) collective-permute-start(f32[80,128]{1,0:T(8,128)S(1)} %get-tuple-element.39), channel_id=1, source_target_pairs={{0,4},{4,0},{8,12},{12,8},{16,20},{20,16},{24,28},{28,24},{1,5},{5... | collective-permute-start | bytes 122888 | tf_op jit(solution)/shard_map/ppermute | solution.py:434
  32.6 8.1 %collective-permute-start.8 = (f32[3,16,256]{2,1,0:T(8,128)S(1)}, f32[3,16,256]{2,1,0:T(8,128)S(1)}, u32[]{:S(2)}, u32[]{:S(2)}) collective-permute-start(f32[3,16,256]{2,1,0:T(8,128)S(1)} %get-tuple-element.42), channel_id=1, source_target_pairs={{0,4},{4,0},{8,12},{12,8},{16,20},{20,16},{24,28},{28,24},{1,5},{5... | collective-permute-start | bytes 147464 | tf_op jit(solution)/shard_map/ppermute | solution.py:434
  35.7 5.0 %collective-permute-start.9 = (f32[3,16,256]{2,1,0:T(8,128)S(1)}, f32[3,16,256]{2,1,0:T(8,128)S(1)}, u32[]{:S(2)}, u32[]{:S(2)}) collective-permute-start(f32[3,16,256]{2,1,0:T(8,128)S(1)} %get-tuple-element.43), channel_id=1, source_target_pairs={{0,1},{4,8},{8,4},{12,16},{16,12},{20,24},{24,20},{28,29},{1,0},{5... | collective-permute-start | bytes 147464 | tf_op jit(solution)/shard_map/ppermute | solution.py:434
  35.7 3.3 %collective-permute-start.10 = (f32[3,4,256]{2,1,0:T(4,128)S(1)}, f32[3,4,256]{2,1,0:T(4,128)S(1)}, u32[]{:S(2)}, u32[]{:S(2)}) collective-permute-start(f32[3,4,256]{2,1,0:T(4,128)S(1)} %get-tuple-element.44), channel_id=1, source_target_pairs={{0,1},{1,0},{2,3},{3,2},{4,5},{5,4},{6,7},{7,6},{8,9},{9,8},{10,11... | collective-permute-start | bytes 36872 | tf_op jit(solution)/shard_map/ppermute | solution.py:434
  36.2 4.5 %collective-permute-start.11 = (f32[3,4,256]{2,1,0:T(4,128)S(1)}, f32[3,4,256]{2,1,0:T(4,128)S(1)}, u32[]{:S(2)}, u32[]{:S(2)}) collective-permute-start(f32[3,4,256]{2,1,0:T(4,128)S(1)} %get-tuple-element.45), channel_id=1, source_target_pairs={{0,4},{1,2},{2,1},{3,7},{4,0},{5,6},{6,5},{7,3},{8,12},{9,10},{10,... | collective-permute-start | bytes 36872 | tf_op jit(solution)/shard_map/ppermute | solution.py:434
  42.1 5.5 %collective-permute-start.13 = (f32[80,128]{1,0:T(8,128)S(1)}, f32[80,128]{1,0:T(8,128)S(1)}, u32[]{:S(2)}, u32[]{:S(2)}) collective-permute-start(f32[80,128]{1,0:T(8,128)S(1)} %get-tuple-element.47), channel_id=1, source_target_pairs={{0,1},{4,8},{8,4},{12,16},{16,12},{20,24},{24,20},{28,29},{1,0},{5... | collective-permute-start | bytes 122888 | tf_op jit(solution)/shard_map/ppermute | solution.py:434
  42.2 5.4 %collective-permute-start.12 = (f32[80,128]{1,0:T(8,128)S(1)}, f32[80,128]{1,0:T(8,128)S(1)}, u32[]{:S(2)}, u32[]{:S(2)}) collective-permute-start(f32[80,128]{1,0:T(8,128)S(1)} %get-tuple-element.47), channel_id=1, source_target_pairs={{0,4},{4,0},{8,12},{12,8},{16,20},{20,16},{24,28},{28,24},{1,5},{5... | collective-permute-start | bytes 122888 | tf_op jit(solution)/shard_map/ppermute | solution.py:434
  47.6 4.9 %collective-permute-start.15 = (f32[240,128]{1,0:T(8,128)S(1)}, f32[240,128]{1,0:T(8,128)S(1)}, u32[]{:S(2)}, u32[]{:S(2)}) collective-permute-start(f32[240,128]{1,0:T(8,128)S(1)} %constant_dynamic-update-slice_fusion.own_ref), channel_id=1, source_target_pairs={{0,4},{1,2},{2,1},{3,7},{4,0},{5,6},{6,5},{7,3},{8,12},{9,10},{10,... | collective-permute-start | bytes 368648 | tf_op jit(solution)/shard_map/ppermute | solution.py:434
  58.8 4.9 %collective-permute-start.17 = (f32[240,128]{1,0:T(8,128)S(1)}, f32[240,128]{1,0:T(8,128)S(1)}, u32[]{:S(2)}, u32[]{:S(2)}) collective-permute-start(f32[240,128]{1,0:T(8,128)S(1)} %get-tuple-element.50), channel_id=1, source_target_pairs={{0,4},{1,2},{2,1},{3,7},{4,0},{5,6},{6,5},{7,3},{8,12},{9,10},{10,... | collective-permute-start | bytes 368648 | tf_op jit(solution)/shard_map/ppermute | solution.py:434
  63.8 4.1 %collective-permute-start.18 = (f32[80,128]{1,0:T(8,128)S(1)}, f32[80,128]{1,0:T(8,128)S(1)}, u32[]{:S(2)}, u32[]{:S(2)}) collective-permute-start(f32[80,128]{1,0:T(8,128)S(1)} %get-tuple-element.52), channel_id=1, source_target_pairs={{0,4},{4,0},{8,12},{12,8},{16,20},{20,16},{24,28},{28,24},{1,5},{5... | collective-permute-start | bytes 122888 | tf_op jit(solution)/shard_map/ppermute | solution.py:434
  69.3 8.2 %collective-permute-start.20 = (f32[3,16,256]{2,1,0:T(8,128)S(1)}, f32[3,16,256]{2,1,0:T(8,128)S(1)}, u32[]{:S(2)}, u32[]{:S(2)}) collective-permute-start(f32[3,16,256]{2,1,0:T(8,128)S(1)} %get-tuple-element.55), channel_id=1, source_target_pairs={{0,4},{4,0},{8,12},{12,8},{16,20},{20,16},{24,28},{28,24},{1,5},{5... | collective-permute-start | bytes 147464 | tf_op jit(solution)/shard_map/ppermute | solution.py:434
  72.5 5.0 %collective-permute-start.21 = (f32[3,16,256]{2,1,0:T(8,128)S(1)}, f32[3,16,256]{2,1,0:T(8,128)S(1)}, u32[]{:S(2)}, u32[]{:S(2)}) collective-permute-start(f32[3,16,256]{2,1,0:T(8,128)S(1)} %get-tuple-element.56), channel_id=1, source_target_pairs={{0,1},{4,8},{8,4},{12,16},{16,12},{20,24},{24,20},{28,29},{1,0},{5... | collective-permute-start | bytes 147464 | tf_op jit(solution)/shard_map/ppermute | solution.py:434
  72.5 3.3 %collective-permute-start.22 = (f32[3,4,256]{2,1,0:T(4,128)S(1)}, f32[3,4,256]{2,1,0:T(4,128)S(1)}, u32[]{:S(2)}, u32[]{:S(2)}) collective-permute-start(f32[3,4,256]{2,1,0:T(4,128)S(1)} %get-tuple-element.57), channel_id=1, source_target_pairs={{0,1},{1,0},{2,3},{3,2},{4,5},{5,4},{6,7},{7,6},{8,9},{9,8},{10,11... | collective-permute-start | bytes 36872 | tf_op jit(solution)/shard_map/ppermute | solution.py:434
  73.0 4.5 %collective-permute-start.23 = (f32[3,4,256]{2,1,0:T(4,128)S(1)}, f32[3,4,256]{2,1,0:T(4,128)S(1)}, u32[]{:S(2)}, u32[]{:S(2)}) collective-permute-start(f32[3,4,256]{2,1,0:T(4,128)S(1)} %get-tuple-element.58), channel_id=1, source_target_pairs={{0,4},{1,2},{2,1},{3,7},{4,0},{5,6},{6,5},{7,3},{8,12},{9,10},{10,... | collective-permute-start | bytes 36872 | tf_op jit(solution)/shard_map/ppermute | solution.py:434
  78.3 3.7 %collective-permute-start.25 = (f32[8,128]{1,0:T(8,128)S(1)}, f32[8,128]{1,0:T(8,128)S(1)}, u32[]{:S(2)}, u32[]{:S(2)}) collective-permute-start(f32[8,128]{1,0:T(8,128)S(1)} %get-tuple-element.60.refs_0_), channel_id=1, source_target_pairs={{0,2},{1,3},{2,0},{3,1},{4,6},{5,7},{6,4},{7,5},{8,10},{9,11},{10,... | collective-permute-start | bytes 12296 | tf_op jit(solution)/shard_map/ppermute | solution.py:469
  78.5 3.4 %collective-permute-start.24 = (f32[8,128]{1,0:T(8,128)S(1)}, f32[8,128]{1,0:T(8,128)S(1)}, u32[]{:S(2)}, u32[]{:S(2)}) collective-permute-start(f32[8,128]{1,0:T(8,128)S(1)} %get-tuple-element.60.refs_0_), channel_id=1, source_target_pairs={{0,1},{1,0},{2,3},{3,2},{4,5},{5,4},{6,7},{7,6},{8,9},{9,8},{10,11... | collective-permute-start | bytes 12296 | tf_op jit(solution)/shard_map/ppermute | solution.py:469
  82.0 4.7 %collective-permute-start.29 = (f32[8,128]{1,0:T(8,128)S(1)}, f32[8,128]{1,0:T(8,128)S(1)}, u32[]{:S(2)}, u32[]{:S(2)}) collective-permute-start(f32[8,128]{1,0:T(8,128)S(1)} %shard_map.114.refs_0_), channel_id=1, source_target_pairs={{0,12},{4,8},{8,4},{12,0},{16,28},{20,24},{24,20},{28,16},{1,13},{... | collective-permute-start | bytes 12296 | tf_op jit(solution)/shard_map/ppermute | solution.py:469
  85.1 3.6 %collective-permute-start.28 = (f32[8,128]{1,0:T(8,128)S(1)}, f32[8,128]{1,0:T(8,128)S(1)}, u32[]{:S(2)}, u32[]{:S(2)}) collective-permute-start(f32[8,128]{1,0:T(8,128)S(1)} %shard_map.114.refs_0_), channel_id=1, source_target_pairs={{0,8},{4,12},{8,0},{12,4},{16,24},{20,28},{24,16},{28,20},{1,9},{5... | collective-permute-start | bytes 12296 | tf_op jit(solution)/shard_map/ppermute | solution.py:469
  85.5 3.6 %collective-permute-start.27 = (f32[8,128]{1,0:T(8,128)S(1)}, f32[8,128]{1,0:T(8,128)S(1)}, u32[]{:S(2)}, u32[]{:S(2)}) collective-permute-start(f32[8,128]{1,0:T(8,128)S(1)} %shard_map.114.refs_0_), channel_id=1, source_target_pairs={{0,4},{4,0},{8,12},{12,8},{16,20},{20,16},{24,28},{28,24},{1,5},{5... | collective-permute-start | bytes 12296 | tf_op jit(solution)/shard_map/ppermute | solution.py:469
  89.2 4.6 %collective-permute-start.30 = (f32[8,128]{1,0:T(8,128)S(1)}, f32[8,128]{1,0:T(8,128)S(1)}, u32[]{:S(2)}, u32[]{:S(2)}) collective-permute-start(f32[8,128]{1,0:T(8,128)S(1)} %shard_map.115.refs_0_), channel_id=1, source_target_pairs={{0,16},{4,20},{8,24},{12,28},{16,0},{20,4},{24,8},{28,12},{1,17},{... | collective-permute-start | bytes 12296 | tf_op jit(solution)/shard_map/ppermute | solution.py:469
  (16 other events, 147.7 us)

commit v6 on v5

--- a/solution.py
+++ b/solution.py
@@ -49,12 +49,13 @@
 
 def call(kernel, outs, scratch=(), flops=0, space=pltpu.VMEM, mib=40):
     def run(*args):
-        moved = sum(a.size * 4 for a in args) + sum(
-            4 * functools.reduce(lambda p, q: p * q, o) for o in outs
-        )
+        shapes = [
+            o if hasattr(o, "dtype") else jax.ShapeDtypeStruct(o, F32) for o in outs
+        ]
+        moved = sum(a.size * a.dtype.itemsize for a in (*args, *shapes))
         return pl.pallas_call(
             kernel,
-            out_shape=[jax.ShapeDtypeStruct(o, F32) for o in outs],
+            out_shape=shapes,
             in_specs=[pl.BlockSpec(memory_space=space)] * len(args),
             out_specs=[pl.BlockSpec(memory_space=pltpu.VMEM)] * len(outs),
             scratch_shapes=[s if hasattr(s, "dtype") else pltpu.VMEM(*s) for s in scratch],
@@ -83,18 +84,16 @@
     return lax.div(cells, jnp.int32(nz)), lax.rem(cells, jnp.int32(nz))
 
 
-def pick(field, cells_ref, out_ref):
+def pick(field, cells_ref, deep_ref, out_ref):
     _, rows, depth = field.shape
     slots = cells_ref.shape[1]
     blocks = slots // LANES
     chunk = chunk_of(slots)
-    flat = field.reshape(3 * rows, depth)
-    left = jnp.concatenate(split(flat, 2), axis=0)
+    left = jnp.concatenate(split(field.reshape(3 * rows, depth), 2), axis=1)
     for start in range(0, slots, chunk):
-        row, deep = row_and_depth(cells_ref[:, start : start + chunk], depth)
-        right = ones_where(iota((depth, chunk), 0) == deep)
-        found = mm(left, right)
-        found = found[: 3 * rows] + found[3 * rows :]
+        row, _ = row_and_depth(cells_ref[:, start : start + chunk], depth)
+        right = deep_ref[:, start : start + chunk]
+        found = mm(left, jnp.concatenate([right, right], axis=0))
         here = iota((rows, chunk), 0) == row
         for comp in range(3):
             part = jnp.where(here, found[comp * rows : (comp + 1) * rows], 0.0)
@@ -107,6 +106,26 @@
         out_ref[3 * blocks :, :] = jnp.zeros((pad, LANES), F32)
 
 
+def one_hot(out_ref, values):
+    chunk = chunk_of(out_ref.shape[1])
+    for start in range(0, out_ref.shape[1], chunk):
+        lanes = slice(start, start + chunk)
+        out_ref[:, lanes] = ones_where(
+            iota((out_ref.shape[0], chunk), 0) == values(lanes)
+        )
+
+
+def scaled(hot, lines):
+    rows = hot.shape[0]
+    out = []
+    for place in range(2):
+        for line in lines:
+            piece = split(line, 2)[place].astype(F32)
+            few = jnp.broadcast_to(piece, (16, piece.shape[1])).astype(BF16)
+            out += [few * hot[at : at + 16] for at in range(0, rows, 16)]
+    return jnp.concatenate(out, axis=0)
+
+
 def times_diag(d_ref, field):
     nx, ny, nz = d_ref.shape[1:]
     return jnp.stack(
@@ -117,7 +136,9 @@
     )
 
 
-def first_kernel(cells_hbm, v_hbm, d_hbm, out_ref, cells_ref, v_ref, d_ref, sem):
+def first_kernel(
+    cells_hbm, v_hbm, d_hbm, out_ref, cells_ref, v_ref, d_ref, deep_ref, sem
+):
     pairs = ((cells_hbm, cells_ref), (v_hbm, v_ref), (d_hbm, d_ref))
     copies = [
         pltpu.make_async_copy(src, dst, sem.at[place])
@@ -125,9 +146,12 @@
     ]
     for copy in copies:
         copy.start()
-    for copy in copies:
-        copy.wait()
-    pick(times_diag(d_ref, [v_ref[b] for b in range(3)]), cells_ref, out_ref)
+    copies[0].wait()
+    depth = v_ref.shape[3]
+    one_hot(deep_ref, lambda lanes: row_and_depth(cells_ref[:, lanes], depth)[1])
+    copies[1].wait()
+    copies[2].wait()
+    pick(times_diag(d_ref, [v_ref[b] for b in range(3)]), cells_ref, deep_ref, out_ref)
 
 
 def spread_matrix(wells, width):
@@ -141,7 +165,20 @@
     return ones_where(iota(shape, 0) == width * iota(shape, 1) + (width - 3 + comp))
 
 
-def prep_kernel(g_ref, couple_ref, h_ref, e_ref, apart_ref, part_ref):
+def prep_kernel(
+    idx_ref, cells_ref, g_ref, couple_ref,
+    h_ref, e_ref, apart_ref, low_ref, high_ref, deep_ref, row_ref,
+    part_ref,
+):
+    wide = low_ref.shape[0]
+    depth = deep_ref.shape[0]
+    one_hot(low_ref, lambda lanes: idx_ref[:, lanes] & (wide - 1))
+    one_hot(
+        high_ref,
+        lambda lanes: lax.shift_right_arithmetic(idx_ref[:, lanes], wide.bit_length() - 1),
+    )
+    one_hot(row_ref, lambda lanes: row_and_depth(cells_ref[:, lanes], depth)[0])
+    one_hot(deep_ref, lambda lanes: row_and_depth(cells_ref[:, lanes], depth)[1])
     chunks, width, span_all = g_ref.shape
     wells = couple_ref.shape[2]
     span = width // 3
@@ -165,9 +202,9 @@
 
 
 def solve_kernel(
-    idx_ref, own_ref, even_ref, next_ref, g_ref, h_ref, e_ref,
+    idx_ref, own_ref, even_ref, next_ref, g_ref, h_ref, e_ref, low_ref, high_ref,
     keep_ref, to_even_ref, to_next_ref,
-    pool_ref, r_ref, q_ref, tail_ref, p_ref, y_ref, ohr_ref, w_ref,
+    pool_ref, r_ref, q_ref, tail_ref, p_ref, y_ref,
 ):
     _, chunks, span, span_all = g_ref.shape
     width = 3 * span
@@ -192,20 +229,27 @@
                 pool_ref[comp, at : at + blocks, :] = part[
                     comp * blocks : (comp + 1) * blocks
                 ]
-    pooled = pool_ref[...].reshape(3 * rows, LANES)
+    half = rows // 2
+    wide = 2 * LANES
+    pooled = jnp.concatenate(
+        [
+            jnp.concatenate(
+                [pool_ref[comp, pl.ds(odd, half, stride=2), :] for odd in range(2)], axis=1
+            )
+            for comp in range(3)
+        ],
+        axis=0,
+    )
     left = jnp.concatenate(split(pooled, 2), axis=1)
     size = chunk_of(slots)
     r_ref[...] = jnp.zeros(r_ref.shape, F32)
     for start in range(0, slots, size):
         place = idx_ref[:, start : start + size]
-        high = lax.shift_right_arithmetic(place, LANES.bit_length() - 1)
-        low = place & (LANES - 1)
-        right = ones_where((iota((2 * LANES, size), 0) & (LANES - 1)) == low)
-        found = mm(left, right)
-        here = iota((rows, size), 0) == high
-        ohr_ref[:, start : start + size] = ones_where(here)
+        right = low_ref[:, start : start + size]
+        found = mm(left, jnp.concatenate([right, right], axis=0))
+        here = iota((half, size), 0) == lax.shift_right_arithmetic(place, wide.bit_length() - 1)
         for comp in range(3):
-            part = jnp.where(here, found[comp * rows : (comp + 1) * rows], 0.0)
+            part = jnp.where(here, found[comp * half : (comp + 1) * half], 0.0)
             line = jnp.sum(part, axis=0, keepdims=True)
             for piece in range(size // group):
                 at = start // group + piece
@@ -251,21 +295,25 @@
     rest = lax.rem(lane, jnp.int32(group))
     source = width * lax.div(rest, jnp.int32(span)) + 3 * lax.rem(rest, jnp.int32(span)) + comp_of
     y_ref[...] = mm_exact(plain, ones_where(iota(square, 0) == source))
-    for c in range(chunks):
-        low = idx_ref[:, c * group : (c + 1) * group] & (LANES - 1)
-        match = iota((LANES, group), 0) == low
-        for comp in range(3):
-            value = y_ref[c : c + 1, comp * group : (comp + 1) * group]
-            for place, piece in enumerate(split(value, 2)):
-                at = (place * 3 + comp) * LANES
-                w_ref[at : at + LANES, c * group : (c + 1) * group] = jnp.where(
-                    match, piece.astype(F32), 0.0
-                ).astype(BF16)
-    spread_out = mm(ohr_ref[...], w_ref[...], trans=True)
-    spread_out = spread_out[:, : 3 * LANES] + spread_out[:, 3 * LANES :]
-    pool_ref[0] = spread_out[:, :LANES]
-    pool_ref[1] = spread_out[:, LANES : 2 * LANES]
-    pool_ref[2] = spread_out[:, 2 * LANES :]
+    spread_out = None
+    for start in range(0, slots, size):
+        lanes = slice(start, start + size)
+        steps = range(start // group, (start + size) // group)
+        lines = [
+            jnp.concatenate(
+                [y_ref[c : c + 1, comp * group : (comp + 1) * group] for c in steps], axis=1
+            )
+            for comp in range(3)
+        ]
+        part = mm(scaled(high_ref[:, lanes], lines), low_ref[:, lanes], trans=True)
+        spread_out = part if spread_out is None else spread_out + part
+    spread_out = spread_out[: 3 * half] + spread_out[3 * half :]
+    for comp in range(3):
+        block = spread_out[comp * half : (comp + 1) * half]
+        for odd in range(2):
+            pool_ref[comp, pl.ds(odd, half, stride=2), :] = block[
+                :, odd * LANES : (odd + 1) * LANES
+            ]
     for dst in (keep_ref, to_even_ref, to_next_ref):
         dst[...] = jnp.zeros(dst.shape, F32)
     for a in range(3):
@@ -293,9 +341,8 @@
 
 
 def place_kernel(
-    cells_ref, v_ref, inv_ref, x_ref, y_ref, z_ref,
+    row_ref, deep_ref, v_ref, inv_ref, x_ref, y_ref, z_ref,
     out_ref, x_even_ref, x_next_ref, y_even_ref, y_next_ref,
-    left_ref, right_ref,
 ):
     (first_x, last_x), (first_y, last_y) = [
         (lax.axis_index(axis) == 0, lax.axis_index(axis) == lax.axis_size(axis) - 1)
@@ -304,23 +351,22 @@
     odd_x, odd_y = is_odd("gx"), is_odd("gy")
     nx, ny, nz = v_ref.shape[1:]
     rows = nx * ny
-    slots = cells_ref.shape[1]
+    slots = row_ref.shape[1]
     blocks = slots // LANES
     back = x_ref[...] + y_ref[...] + z_ref[...]
-    pieces = [piece.astype(F32) for piece in split(back, 2)]
-    for block in range(blocks):
-        lanes = slice(block * LANES, (block + 1) * LANES)
-        row, deep = row_and_depth(cells_ref[:, lanes], nz)
-        here = iota((rows, LANES), 0) == row
-        right_ref[:, lanes] = ones_where(iota((nz, LANES), 0) == deep)
-        for place, piece in enumerate(pieces):
-            for comp in range(3):
-                at = comp * blocks + block
-                group = (place * 3 + comp) * rows
-                left_ref[group : group + rows, lanes] = jnp.where(
-                    here, piece[at : at + 1, :], 0.0
-                ).astype(BF16)
-    placed = mm(left_ref[...], right_ref[...], trans=True)
+    size = chunk_of(slots)
+    placed = None
+    for start in range(0, slots, size):
+        lanes = slice(start, start + size)
+        steps = range(start // LANES, (start + size) // LANES)
+        lines = [
+            jnp.concatenate(
+                [back[comp * blocks + at : comp * blocks + at + 1] for at in steps], axis=1
+            )
+            for comp in range(3)
+        ]
+        part = mm(scaled(row_ref[:, lanes], lines), deep_ref[:, lanes], trans=True)
+        placed = part if placed is None else placed + part
     placed = placed[: 3 * rows] + placed[3 * rows :]
     for a in range(3):
         own = sum(inv_ref[3 * a + b] * v_ref[b] for b in range(3))
@@ -335,12 +381,8 @@
         y_next_ref[a] = jnp.where(odd_y, high, low)
 
 
-def jacobian(z_ref, faces, d_ref, off_ref, store):
+def inner_kernel(z_ref, d_ref, off_ref, w_ref):
     nx, ny, nz = z_ref.shape[1:]
-    odd_x, odd_y = is_odd("gx"), is_odd("gy")
-    x_even, x_next, y_even, y_next = [face[...] for face in faces]
-    xl, xh = jnp.where(odd_x, x_even, x_next), jnp.where(odd_x, x_next, x_even)
-    yl, yh = jnp.where(odd_y, y_even, y_next), jnp.where(odd_y, y_next, y_even)
     row = iota((ny, nz), 0)
     lane = iota((ny, nz), 1)
     for x in range(nx):
@@ -349,10 +391,10 @@
             own = z_ref[b, x]
             beside.append(
                 [
-                    z_ref[b, x - 1] if x else xl[b],
-                    z_ref[b, x + 1] if x < nx - 1 else xh[b],
-                    jnp.where(row == 0, yl[b, x : x + 1, :], pltpu.roll(own, 1, 0)),
-                    jnp.where(row == ny - 1, yh[b, x : x + 1, :], pltpu.roll(own, ny - 1, 0)),
+                    z_ref[b, x - 1] if x else None,
+                    z_ref[b, x + 1] if x < nx - 1 else None,
+                    jnp.where(row == 0, 0.0, pltpu.roll(own, 1, 0)),
+                    jnp.where(row == ny - 1, 0.0, pltpu.roll(own, ny - 1, 0)),
                     jnp.where(lane == 0, 0.0, pltpu.roll(own, 1, 1)),
                     jnp.where(lane == nz - 1, 0.0, pltpu.roll(own, nz - 1, 1)),
                 ]
@@ -361,30 +403,41 @@
             total = sum(d_ref[3 * a + b, x] * z_ref[b, x] for b in range(3))
             for face in range(6):
                 for b in range(3):
-                    total = total + off_ref[face, 3 * a + b, x] * beside[b][face]
-            store(a, x, total)
+                    if beside[b][face] is not None:
+                        total = total + off_ref[face, 3 * a + b, x] * beside[b][face]
+            w_ref[a, x] = total
+
+
+def add_faces(part_ref, faces, off_ref, w_ref):
+    nx, ny, nz = part_ref.shape[1:]
+    odd_x, odd_y = is_odd("gx"), is_odd("gy")
+    x_even, x_next, y_even, y_next = [face[...] for face in faces]
+    xl, xh = jnp.where(odd_x, x_even, x_next), jnp.where(odd_x, x_next, x_even)
+    yl, yh = jnp.where(odd_y, y_even, y_next), jnp.where(odd_y, y_next, y_even)
+    for a in range(3):
+        w_ref[a] = part_ref[a]
+        for x, face, beside in ((0, 0, xl), (nx - 1, 1, xh)):
+            w_ref[a, x] += sum(off_ref[face, 3 * a + b, x] * beside[b] for b in range(3))
+        for y, face, beside in ((0, 2, yl), (ny - 1, 3, yh)):
+            w_ref[a, :, y, :] += sum(
+                off_ref[face, 3 * a + b, :, y, :] * beside[b] for b in range(3)
+            )
 
 
 def next_kernel(
-    cells_ref, z_ref, f0_ref, f1_ref, f2_ref, f3_ref, d_ref, off_ref, v_ref,
+    cells_ref, deep_ref, part_ref, f0_ref, f1_ref, f2_ref, f3_ref, d_ref, off_ref, v_ref,
     w_ref, t_ref, out_ref,
 ):
-    def store(a, x, value):
-        w_ref[a, x] = value
-        t_ref[a, x] = value - v_ref[a, x]
-
-    jacobian(z_ref, (f0_ref, f1_ref, f2_ref, f3_ref), d_ref, off_ref, store)
-    pick(times_diag(d_ref, [t_ref[b] for b in range(3)]), cells_ref, out_ref)
+    add_faces(part_ref, (f0_ref, f1_ref, f2_ref, f3_ref), off_ref, w_ref)
+    t_ref[...] = w_ref[...] - v_ref[...]
+    pick(times_diag(d_ref, [t_ref[b] for b in range(3)]), cells_ref, deep_ref, out_ref)
 
 
 def gram_kernel(
-    z_ref, f0_ref, f1_ref, f2_ref, f3_ref, d_ref, off_ref, v_ref, w1_ref,
+    part_ref, f0_ref, f1_ref, f2_ref, f3_ref, off_ref, v_ref, w1_ref,
     w_ref, sums_ref,
 ):
-    def store(a, x, value):
-        w_ref[a, x] = value
-
-    jacobian(z_ref, (f0_ref, f1_ref, f2_ref, f3_ref), d_ref, off_ref, store)
+    add_faces(part_ref, (f0_ref, f1_ref, f2_ref, f3_ref), off_ref, w_ref)
     one, two, rhs = w1_ref[...], w_ref[...], v_ref[...]
     top_one = jnp.maximum(jnp.max(jnp.abs(one)), 1e-30)
     top_two = jnp.maximum(jnp.max(jnp.abs(two)), 1e-30)
@@ -420,7 +473,9 @@
         return along * size["gy"] + across if axis == "gx" else across * size["gy"] + along
 
     out = []
-    for first, value in ((0, to_even), (1, to_next)):
+    order = [(0, to_even), (1, to_next)]
+    same = to_even is to_next
+    for first, value in order if same else order[::-1]:
         pairs = []
         for across in range(breadth):
             for i in range(count):
@@ -432,7 +487,7 @@
                 else:
                     pairs.append((device(i, across), device(i, across)))
         out.append(lax.ppermute(value, ("gx", "gy"), pairs))
-    return out
+    return out if same else out[::-1]
 
 
 def merge_kernel(*refs):
@@ -492,7 +547,7 @@
     span = width // 3
     blocks = slots // LANES
     tile = round_up(3 * blocks, 16)
-    rows = round_up(9 * blocks, 16)
+    rows = round_up(9 * blocks, 32)
     tall = round_up(chunks, 16)
     field = right_side.shape
     (picked,) = call(
@@ -502,6 +557,7 @@
             (send_cells.shape, jnp.int32),
             (field, F32),
             (diag_blocks.shape, F32),
+            ((nz, slots), BF16),
             pltpu.SemaphoreType.DMA((3,)),
         ],
         flops=10**9,
@@ -512,11 +568,15 @@
     index = jnp.where(live, recv_index, -1)
     index = index.reshape(wells, chunks, span).transpose(1, 0, 2).reshape(1, wells * longest)
     couple = jnp.pad(span_couple.transpose(1, 0, 2), ((0, 0), (0, tall - chunks), (0, 0)))
-    h, e, apart = call(
+    h, e, apart, low, high, deep, row = call(
         prep_kernel,
-        [(3, tall, span_all), (9, tall, wells), (3, chunks, span, span_all)],
+        [(3, tall, span_all), (9, tall, wells), (3, chunks, span, span_all)]
+        + [
+            jax.ShapeDtypeStruct((height, slots), BF16)
+            for height in (2 * LANES, rows // 2, nz, nx * ny)
+        ],
         [((chunks, width, LANES), F32)],
-    )(span_inverse, couple)
+    )(index, send_cells, span_inverse, couple)
 
     def precondition(vector, picked):
         column = jnp.concatenate([picked, *swap("gx", picked, picked)], axis=0)
@@ -531,11 +591,9 @@
                 ((3, tall, wells), F32),
                 ((3, tall, wells), F32),
                 ((tall, span_all), F32),
-                ((rows, slots), BF16),
-                ((6 * LANES, slots), BF16),
             ],
             flops=4 * 10**9,
-        )(index, column, even, following, apart, h, e)
+        )(index, column, even, following, apart, h, e, low, high)
         even, following = swap("gy", even, following)
         keep, even, following = call(add_kernel, [(tile, LANES)] * 3)(
             keep, even, following
@@ -544,18 +602,19 @@
         z, *faces = call(
             place_kernel,
             [(3, nx, ny, nz)] + [(3, ny, nz)] * 2 + [(3, nx, nz)] * 2,
-            [((6 * nx * ny, slots), BF16), ((nz, slots), BF16)],
             flops=10**9,
-        )(send_cells, vector, cell_inverse, keep, even, following)
-        return z, swap("gx", *faces[:2]) + swap("gy", *faces[2:])
-
-    z1, faces = precondition(right_side, picked)
+        )(row, deep, vector, cell_inverse, keep, even, following)
+        faces = swap("gx", *faces[:2]) + swap("gy", *faces[2:])
+        (part,) = call(inner_kernel, [field], flops=10**7)(z, diag_blocks, off_blocks)
+        return z, part, faces
+
+    z1, part, faces = precondition(right_side, picked)
     w1, turned, picked = call(
         next_kernel, [field, field, (tile, LANES)], flops=10**9
-    )(send_cells, z1, *faces, diag_blocks, off_blocks, right_side)
-    z2, faces = precondition(turned, picked)
+    )(send_cells, deep, part, *faces, diag_blocks, off_blocks, right_side)
+    z2, part, faces = precondition(turned, picked)
     w2, sums = call(gram_kernel, [field, (8, LANES)])(
-        z2, *faces, diag_blocks, off_blocks, right_side, w1
+        part, *faces, off_blocks, right_side, w1
     )
     sums = merge_all(merge_all(sums, "gy"), "gx")
     return tuple(

time: 94.8 us -> 91.5 us (0.965)
  starting transfers between devices: 41.7 us -> 40 us
  Pallas kernels: 22.2 us -> 20.6 us
    pallas_call x14 -> x16, Pallas kernels: 22.2 us -> 20.6 us  [run(): pl.pallas_call(kernel, out_shape=shapes, in_specs=[pl.BlockSpec(memory_sp...]
    ppermute x24, starting transfers between devices: 33.5 us -> 32.2 us  [swap(): out.append(lax.ppermute(value, ('gx', 'gy'), pairs))]
  transfers between devices with their start and end apart: 31 -> 31, of which waited for: 16 -> 15; matrix products, arithmetic and copies ran while one was open for 1% -> 1% of each run, Pallas kernels for 1% -> 4%
where the time goes in v6:
time: 91.5 us; the launch traced here: 91.3 us
  starting transfers between devices  40 us (44%)
  waiting for transfers between devices  28.4 us (31%)
  Pallas kernels  20.6 us (23%)
  between operations  0.94 us (1%)
    ppermute x24, starting transfers between devices, swap(): out.append(lax.ppermute(value, ('gx', 'gy'), pairs))  32.2 us
    ppermute x24, waiting for transfers between devices, swap(): out.append(lax.ppermute(value, ('gx', 'gy'), pairs))  20.8 us
    pallas_call x16, Pallas kernels, run(): pl.pallas_call(kernel, out_shape=shapes, in_specs=[pl.BlockSpec(memory_sp...  20.6 us
    ppermute x7, starting transfers between devices, merge_all(): lax.ppermute(value, axis, [(i, i ^ k * step) for i in range(count)])  7.85 us
    ppermute x7, waiting for transfers between devices, merge_all(): lax.ppermute(value, axis, [(i, i ^ k * step) for i in range(count)])  7.62 us
  transfers between devices with their start and end apart: 31, of which 15 were waited for; matrix products, arithmetic and copies ran while one was open for 1% of the time, Pallas kernels for 4%

profile of v6, /device:TPU:0, one launch (start us, length us, event | category | flops | bytes accessed | tf_op | source)
XLA Modules:
  0.0 91.3 jit_solution(13830837870991635433)
XLA Ops:
  0.7 2.9 %shard_map.105 = f32[80,128]{1,0:T(8,128)} custom-call(s32[1,3200]{1,0:T(1,128)} %cells_ref.3, f32[3,4,16,256]{3,2,1,0:T(8,128)} %v_ref.7, f32[9,4,16,256]{3,2,1,0:T(8,128)} %d_ref.5), custom_call_target="tpu_custom_call" | custom-call | flops 1000000000 | bytes 840192 | tf_op jit(solution)/shard_map/pallas_call | solution.py:56
  4.1 4.0 %collective-permute-start = (f32[80,128]{1,0:T(8,128)}, f32[80,128]{1,0:T(8,128)S(1)}, u32[]{:S(2)}, u32[]{:S(2)}) collective-permute-start(f32[80,128]{1,0:T(8,128)} %shard_map.105), channel_id=1, source_target_pairs={{0,4},{4,0},{8,12},{12,8},{16,20},{20,16},{24,28},{28,24},{1,5},{5... | collective-permute-start | bytes 122888 | tf_op jit(solution)/shard_map/ppermute | solution.py:489
  8.2 2.2 %collective-permute-done = f32[80,128]{1,0:T(8,128)S(1)} collective-permute-done((f32[80,128]{1,0:T(8,128)}, f32[80,128]{1,0:T(8,128)S(1)}, u32[]{:S(2)}, u32[]{:S(2)}) %collective-permute-start) | collective-permute-done | bytes 40992 | tf_op jit(solution)/shard_map/ppermute | solution.py:489
  11.2 2.1 %collective-permute-start.3 = (f32[240,128]{1,0:T(8,128)S(1)}, f32[240,128]{1,0:T(8,128)S(1)}, u32[]{:S(2)}, u32[]{:S(2)}) collective-permute-start(f32[240,128]{1,0:T(8,128)S(1)} %pad_maximum_fusion.own_ref), channel_id=1, source_target_pairs={{0,4},{1,2},{2,1},{3,7},{4,0},{5,6},{6,5},{7,3},{8,12},{9,10},{10,... | collective-permute-start | bytes 368648 | tf_op jit(solution)/shard_map/ppermute | solution.py:489
  13.8 2.6 %shard_map.104 = (f32[3,32,384]{2,1,0:T(8,128)S(1)}, f32[9,32,8]{2,1,0:T(8,128)S(1)}, f32[3,25,16,384]{3,2,1,0:T(8,128)S(1)}, bf16[256,3200]{1,0:T(8,128)(2,1)S(...) custom-call(s32[1,3200]{1,0:T(1,128)S(1)} %reshape.12.idx_ref, ...), custom_call_target="tpu_custom_call" | custom-call | bytes 8383488 | tf_op jit(solution)/shard_map/pallas_call | solution.py:56
  16.4 4.9 %shard_map.106 = (f32[240,128]{1,0:T(8,128)S(1)}, f32[240,128]{1,0:T(8,128)S(1)}, f32[240,128]{1,0:T(8,128)S(1)}) custom-call(s32[1,3200]{1,0:T(1,128)S(1)} %reshape.12.idx_ref, f32[240,128]{1,0:T(8,128)S(1)} %pad_maximum_fusion.own_ref, f32[240,128]{1,0:T(8,128)S(1)} %collective-permute-done.2.even_ref, f32[240,128]{1,0:T(8,128)S(1)} %collective-permute-done.3.next_ref, ...), custom_call_target="tpu_custom_call" | custom-call | flops 4000000000 | bytes 5207552 | tf_op jit(solution)/shard_map/pallas_call | solution.py:56
  23.2 3.6 %collective-permute-done.5.z_ref = f32[240,128]{1,0:T(8,128)S(1)} collective-permute-done((f32[240,128]{1,0:T(8,128)S(1)}, f32[240,128]{1,0:T(8,128)S(1)}, u32[]{:S(2)}, u32[]{:S(2)}) %collective-permute-start.5) | collective-permute-done | bytes 122912 | tf_op jit(solution)/shard_map/ppermute | solution.py:489
  28.1 2.7 %collective-permute-done.6.y_ref = f32[80,128]{1,0:T(8,128)S(1)} collective-permute-done((f32[80,128]{1,0:T(8,128)S(1)}, f32[80,128]{1,0:T(8,128)S(1)}, u32[]{:S(2)}, u32[]{:S(2)}) %collective-permute-start.6) | collective-permute-done | bytes 40992 | tf_op jit(solution)/shard_map/ppermute | solution.py:489
  31.9 3.0 %collective-permute-start.8 = (f32[3,16,256]{2,1,0:T(8,128)S(1)}, f32[3,16,256]{2,1,0:T(8,128)S(1)}, u32[]{:S(2)}, u32[]{:S(2)}) collective-permute-start(f32[3,16,256]{2,1,0:T(8,128)S(1)} %get-tuple-element.50), channel_id=1, source_target_pairs={{0,4},{4,0},{8,12},{12,8},{16,20},{20,16},{24,28},{28,24},{1,5},{5... | collective-permute-start | bytes 147464 | tf_op jit(solution)/shard_map/ppermute | solution.py:489
  35.3 2.5 %collective-permute-start.11 = (f32[3,4,256]{2,1,0:T(4,128)S(1)}, f32[3,4,256]{2,1,0:T(4,128)S(1)}, u32[]{:S(2)}, u32[]{:S(2)}) collective-permute-start(f32[3,4,256]{2,1,0:T(4,128)S(1)} %get-tuple-element.53), channel_id=1, source_target_pairs={{0,4},{1,2},{2,1},{3,7},{4,0},{5,6},{6,5},{7,3},{8,12},{9,10},{10,... | collective-permute-start | bytes 36872 | tf_op jit(solution)/shard_map/ppermute | solution.py:489
  40.7 3.4 %collective-permute-start.12 = (f32[80,128]{1,0:T(8,128)S(1)}, f32[80,128]{1,0:T(8,128)S(1)}, u32[]{:S(2)}, u32[]{:S(2)}) collective-permute-start(f32[80,128]{1,0:T(8,128)S(1)} %get-tuple-element.55), channel_id=1, source_target_pairs={{0,4},{4,0},{8,12},{12,8},{16,20},{20,16},{24,28},{28,24},{1,5},{5... | collective-permute-start | bytes 122888 | tf_op jit(solution)/shard_map/ppermute | solution.py:489
  46.1 2.1 %collective-permute-start.15 = (f32[240,128]{1,0:T(8,128)S(1)}, f32[240,128]{1,0:T(8,128)S(1)}, u32[]{:S(2)}, u32[]{:S(2)}) collective-permute-start(f32[240,128]{1,0:T(8,128)S(1)} %constant_dynamic-update-slice_fusion.own_ref), channel_id=1, source_target_pairs={{0,4},{1,2},{2,1},{3,7},{4,0},{5,6},{6,5},{7,3},{8,12},{9,10},{10,... | collective-permute-start | bytes 368648 | tf_op jit(solution)/shard_map/ppermute | solution.py:489
  48.2 2.9 %collective-permute-done.15.next_ref = f32[240,128]{1,0:T(8,128)S(1)} collective-permute-done((f32[240,128]{1,0:T(8,128)S(1)}, f32[240,128]{1,0:T(8,128)S(1)}, u32[]{:S(2)}, u32[]{:S(2)}) %collective-permute-start.15) | collective-permute-done | bytes 122912 | tf_op jit(solution)/shard_map/ppermute | solution.py:489
  51.1 5.1 %shard_map.111 = (f32[240,128]{1,0:T(8,128)S(1)}, f32[240,128]{1,0:T(8,128)S(1)}, f32[240,128]{1,0:T(8,128)S(1)}) custom-call(s32[1,3200]{1,0:T(1,128)S(1)} %reshape.12.idx_ref, f32[240,128]{1,0:T(8,128)S(1)} %constant_dynamic-update-slice_fusion.own_ref, f32[240,128]{1,0:T(8,128)S(1)} %collective-permute-done.14.even_ref, ...), custom_call_target="tpu_custom_call" | custom-call | flops 4000000000 | bytes 5207552 | tf_op jit(solution)/shard_map/pallas_call | solution.py:56
  56.3 2.1 %collective-permute-start.17 = (f32[240,128]{1,0:T(8,128)S(1)}, f32[240,128]{1,0:T(8,128)S(1)}, u32[]{:S(2)}, u32[]{:S(2)}) collective-permute-start(f32[240,128]{1,0:T(8,128)S(1)} %get-tuple-element.58), channel_id=1, source_target_pairs={{0,4},{1,2},{2,1},{3,7},{4,0},{5,6},{6,5},{7,3},{8,12},{9,10},{10,... | collective-permute-start | bytes 368648 | tf_op jit(solution)/shard_map/ppermute | solution.py:489
  58.4 2.9 %collective-permute-done.17.z_ref = f32[240,128]{1,0:T(8,128)S(1)} collective-permute-done((f32[240,128]{1,0:T(8,128)S(1)}, f32[240,128]{1,0:T(8,128)S(1)}, u32[]{:S(2)}, u32[]{:S(2)}) %collective-permute-start.17) | collective-permute-done | bytes 122912 | tf_op jit(solution)/shard_map/ppermute | solution.py:489
  61.3 2.1 %collective-permute-start.18 = (f32[80,128]{1,0:T(8,128)S(1)}, f32[80,128]{1,0:T(8,128)S(1)}, u32[]{:S(2)}, u32[]{:S(2)}) collective-permute-start(f32[80,128]{1,0:T(8,128)S(1)} %get-tuple-element.60), channel_id=1, source_target_pairs={{0,4},{4,0},{8,12},{12,8},{16,20},{20,16},{24,28},{28,24},{1,5},{5... | collective-permute-start | bytes 122888 | tf_op jit(solution)/shard_map/ppermute | solution.py:489
  63.4 2.0 %collective-permute-done.18.y_ref = f32[80,128]{1,0:T(8,128)S(1)} collective-permute-done((f32[80,128]{1,0:T(8,128)S(1)}, f32[80,128]{1,0:T(8,128)S(1)}, u32[]{:S(2)}, u32[]{:S(2)}) %collective-permute-start.18) | collective-permute-done | bytes 40992 | tf_op jit(solution)/shard_map/ppermute | solution.py:489
  66.3 3.1 %collective-permute-start.20 = (f32[3,16,256]{2,1,0:T(8,128)S(1)}, f32[3,16,256]{2,1,0:T(8,128)S(1)}, u32[]{:S(2)}, u32[]{:S(2)}) collective-permute-start(f32[3,16,256]{2,1,0:T(8,128)S(1)} %get-tuple-element.63), channel_id=1, source_target_pairs={{0,4},{4,0},{8,12},{12,8},{16,20},{20,16},{24,28},{28,24},{1,5},{5... | collective-permute-start | bytes 147464 | tf_op jit(solution)/shard_map/ppermute | solution.py:489
  69.9 2.9 %collective-permute-start.23 = (f32[3,4,256]{2,1,0:T(4,128)S(1)}, f32[3,4,256]{2,1,0:T(4,128)S(1)}, u32[]{:S(2)}, u32[]{:S(2)}) collective-permute-start(f32[3,4,256]{2,1,0:T(4,128)S(1)} %get-tuple-element.66), channel_id=1, source_target_pairs={{0,4},{1,2},{2,1},{3,7},{4,0},{5,6},{6,5},{7,3},{8,12},{9,10},{10,... | collective-permute-start | bytes 36872 | tf_op jit(solution)/shard_map/ppermute | solution.py:489
  78.7 3.1 %collective-permute-start.29 = (f32[8,128]{1,0:T(8,128)S(1)}, f32[8,128]{1,0:T(8,128)S(1)}, u32[]{:S(2)}, u32[]{:S(2)}) collective-permute-start(f32[8,128]{1,0:T(8,128)S(1)} %shard_map.116.refs_0_), channel_id=1, source_target_pairs={{0,12},{4,8},{8,4},{12,0},{16,28},{20,24},{24,20},{28,16},{1,13},{... | collective-permute-start | bytes 12296 | tf_op jit(solution)/shard_map/ppermute | solution.py:524
  83.4 2.0 %collective-permute-done.28.refs_2_ = f32[8,128]{1,0:T(8,128)S(1)} collective-permute-done((f32[8,128]{1,0:T(8,128)S(1)}, f32[8,128]{1,0:T(8,128)S(1)}, u32[]{:S(2)}, u32[]{:S(2)}) %collective-permute-start.28) | collective-permute-done | bytes 4128 | tf_op jit(solution)/shard_map/ppermute | solution.py:524
  85.9 2.2 %collective-permute-start.30 = (f32[8,128]{1,0:T(8,128)S(1)}, f32[8,128]{1,0:T(8,128)S(1)}, u32[]{:S(2)}, u32[]{:S(2)}) collective-permute-start(f32[8,128]{1,0:T(8,128)S(1)} %shard_map.117.refs_0_), channel_id=1, source_target_pairs={{0,16},{4,20},{8,24},{12,28},{16,0},{20,4},{24,8},{28,12},{1,17},{... | collective-permute-start | bytes 12296 | tf_op jit(solution)/shard_map/ppermute | solution.py:524
  88.1 2.4 %collective-permute-done.30.refs_1_ = f32[8,128]{1,0:T(8,128)S(1)} collective-permute-done((f32[8,128]{1,0:T(8,128)S(1)}, f32[8,128]{1,0:T(8,128)S(1)}, u32[]{:S(2)}, u32[]{:S(2)}) %collective-permute-start.30) | collective-permute-done | bytes 4128 | tf_op jit(solution)/shard_map/ppermute | solution.py:524
  (82 shorter events, 21.7 us)
Async XLA Ops:
  3.6 4.6 %collective-permute-start.1 = (f32[80,128]{1,0:T(8,128)}, f32[80,128]{1,0:T(8,128)S(1)}, u32[]{:S(2)}, u32[]{:S(2)}) collective-permute-start(f32[80,128]{1,0:T(8,128)} %shard_map.105), channel_id=1, source_target_pairs={{0,1},{4,8},{8,4},{12,16},{16,12},{20,24},{24,20},{28,29},{1,0},{5... | collective-permute-start | bytes 122888 | tf_op jit(solution)/shard_map/ppermute | solution.py:489
  4.1 6.3 %collective-permute-start = (f32[80,128]{1,0:T(8,128)}, f32[80,128]{1,0:T(8,128)S(1)}, u32[]{:S(2)}, u32[]{:S(2)}) collective-permute-start(f32[80,128]{1,0:T(8,128)} %shard_map.105), channel_id=1, source_target_pairs={{0,4},{4,0},{8,12},{12,8},{16,20},{20,16},{24,28},{28,24},{1,5},{5... | collective-permute-start | bytes 122888 | tf_op jit(solution)/shard_map/ppermute | solution.py:489
  11.2 5.2 %collective-permute-start.3 = (f32[240,128]{1,0:T(8,128)S(1)}, f32[240,128]{1,0:T(8,128)S(1)}, u32[]{:S(2)}, u32[]{:S(2)}) collective-permute-start(f32[240,128]{1,0:T(8,128)S(1)} %pad_maximum_fusion.own_ref), channel_id=1, source_target_pairs={{0,4},{1,2},{2,1},{3,7},{4,0},{5,6},{6,5},{7,3},{8,12},{9,10},{10,... | collective-permute-start | bytes 368648 | tf_op jit(solution)/shard_map/ppermute | solution.py:489
  21.9 4.9 %collective-permute-start.5 = (f32[240,128]{1,0:T(8,128)S(1)}, f32[240,128]{1,0:T(8,128)S(1)}, u32[]{:S(2)}, u32[]{:S(2)}) collective-permute-start(f32[240,128]{1,0:T(8,128)S(1)} %get-tuple-element.45), channel_id=1, source_target_pairs={{0,4},{1,2},{2,1},{3,7},{4,0},{5,6},{6,5},{7,3},{8,12},{9,10},{10,... | collective-permute-start | bytes 368648 | tf_op jit(solution)/shard_map/ppermute | solution.py:489
  26.8 4.1 %collective-permute-start.6 = (f32[80,128]{1,0:T(8,128)S(1)}, f32[80,128]{1,0:T(8,128)S(1)}, u32[]{:S(2)}, u32[]{:S(2)}) collective-permute-start(f32[80,128]{1,0:T(8,128)S(1)} %get-tuple-element.47), channel_id=1, source_target_pairs={{0,4},{4,0},{8,12},{12,8},{16,20},{20,16},{24,28},{28,24},{1,5},{5... | collective-permute-start | bytes 122888 | tf_op jit(solution)/shard_map/ppermute | solution.py:489
  31.9 7.7 %collective-permute-start.8 = (f32[3,16,256]{2,1,0:T(8,128)S(1)}, f32[3,16,256]{2,1,0:T(8,128)S(1)}, u32[]{:S(2)}, u32[]{:S(2)}) collective-permute-start(f32[3,16,256]{2,1,0:T(8,128)S(1)} %get-tuple-element.50), channel_id=1, source_target_pairs={{0,4},{4,0},{8,12},{12,8},{16,20},{20,16},{24,28},{28,24},{1,5},{5... | collective-permute-start | bytes 147464 | tf_op jit(solution)/shard_map/ppermute | solution.py:489
  34.8 4.7 %collective-permute-start.9 = (f32[3,16,256]{2,1,0:T(8,128)S(1)}, f32[3,16,256]{2,1,0:T(8,128)S(1)}, u32[]{:S(2)}, u32[]{:S(2)}) collective-permute-start(f32[3,16,256]{2,1,0:T(8,128)S(1)} %get-tuple-element.51), channel_id=1, source_target_pairs={{0,1},{4,8},{8,4},{12,16},{16,12},{20,24},{24,20},{28,29},{1,0},{5... | collective-permute-start | bytes 147464 | tf_op jit(solution)/shard_map/ppermute | solution.py:489
  34.8 3.4 %collective-permute-start.10 = (f32[3,4,256]{2,1,0:T(4,128)S(1)}, f32[3,4,256]{2,1,0:T(4,128)S(1)}, u32[]{:S(2)}, u32[]{:S(2)}) collective-permute-start(f32[3,4,256]{2,1,0:T(4,128)S(1)} %get-tuple-element.52), channel_id=1, source_target_pairs={{0,1},{1,0},{2,3},{3,2},{4,5},{5,4},{6,7},{7,6},{8,9},{9,8},{10,11... | collective-permute-start | bytes 36872 | tf_op jit(solution)/shard_map/ppermute | solution.py:489
  35.3 4.2 %collective-permute-start.11 = (f32[3,4,256]{2,1,0:T(4,128)S(1)}, f32[3,4,256]{2,1,0:T(4,128)S(1)}, u32[]{:S(2)}, u32[]{:S(2)}) collective-permute-start(f32[3,4,256]{2,1,0:T(4,128)S(1)} %get-tuple-element.53), channel_id=1, source_target_pairs={{0,4},{1,2},{2,1},{3,7},{4,0},{5,6},{6,5},{7,3},{8,12},{9,10},{10,... | collective-permute-start | bytes 36872 | tf_op jit(solution)/shard_map/ppermute | solution.py:489
  40.6 5.5 %collective-permute-start.13 = (f32[80,128]{1,0:T(8,128)S(1)}, f32[80,128]{1,0:T(8,128)S(1)}, u32[]{:S(2)}, u32[]{:S(2)}) collective-permute-start(f32[80,128]{1,0:T(8,128)S(1)} %get-tuple-element.55), channel_id=1, source_target_pairs={{0,1},{4,8},{8,4},{12,16},{16,12},{20,24},{24,20},{28,29},{1,0},{5... | collective-permute-start | bytes 122888 | tf_op jit(solution)/shard_map/ppermute | solution.py:489
  40.7 5.4 %collective-permute-start.12 = (f32[80,128]{1,0:T(8,128)S(1)}, f32[80,128]{1,0:T(8,128)S(1)}, u32[]{:S(2)}, u32[]{:S(2)}) collective-permute-start(f32[80,128]{1,0:T(8,128)S(1)} %get-tuple-element.55), channel_id=1, source_target_pairs={{0,4},{4,0},{8,12},{12,8},{16,20},{20,16},{24,28},{28,24},{1,5},{5... | collective-permute-start | bytes 122888 | tf_op jit(solution)/shard_map/ppermute | solution.py:489
  46.1 4.9 %collective-permute-start.15 = (f32[240,128]{1,0:T(8,128)S(1)}, f32[240,128]{1,0:T(8,128)S(1)}, u32[]{:S(2)}, u32[]{:S(2)}) collective-permute-start(f32[240,128]{1,0:T(8,128)S(1)} %constant_dynamic-update-slice_fusion.own_ref), channel_id=1, source_target_pairs={{0,4},{1,2},{2,1},{3,7},{4,0},{5,6},{6,5},{7,3},{8,12},{9,10},{10,... | collective-permute-start | bytes 368648 | tf_op jit(solution)/shard_map/ppermute | solution.py:489
  56.3 4.9 %collective-permute-start.17 = (f32[240,128]{1,0:T(8,128)S(1)}, f32[240,128]{1,0:T(8,128)S(1)}, u32[]{:S(2)}, u32[]{:S(2)}) collective-permute-start(f32[240,128]{1,0:T(8,128)S(1)} %get-tuple-element.58), channel_id=1, source_target_pairs={{0,4},{1,2},{2,1},{3,7},{4,0},{5,6},{6,5},{7,3},{8,12},{9,10},{10,... | collective-permute-start | bytes 368648 | tf_op jit(solution)/shard_map/ppermute | solution.py:489
  61.3 4.1 %collective-permute-start.18 = (f32[80,128]{1,0:T(8,128)S(1)}, f32[80,128]{1,0:T(8,128)S(1)}, u32[]{:S(2)}, u32[]{:S(2)}) collective-permute-start(f32[80,128]{1,0:T(8,128)S(1)} %get-tuple-element.60), channel_id=1, source_target_pairs={{0,4},{4,0},{8,12},{12,8},{16,20},{20,16},{24,28},{28,24},{1,5},{5... | collective-permute-start | bytes 122888 | tf_op jit(solution)/shard_map/ppermute | solution.py:489
  66.3 8.2 %collective-permute-start.20 = (f32[3,16,256]{2,1,0:T(8,128)S(1)}, f32[3,16,256]{2,1,0:T(8,128)S(1)}, u32[]{:S(2)}, u32[]{:S(2)}) collective-permute-start(f32[3,16,256]{2,1,0:T(8,128)S(1)} %get-tuple-element.63), channel_id=1, source_target_pairs={{0,4},{4,0},{8,12},{12,8},{16,20},{20,16},{24,28},{28,24},{1,5},{5... | collective-permute-start | bytes 147464 | tf_op jit(solution)/shard_map/ppermute | solution.py:489
  69.4 5.1 %collective-permute-start.21 = (f32[3,16,256]{2,1,0:T(8,128)S(1)}, f32[3,16,256]{2,1,0:T(8,128)S(1)}, u32[]{:S(2)}, u32[]{:S(2)}) collective-permute-start(f32[3,16,256]{2,1,0:T(8,128)S(1)} %get-tuple-element.64), channel_id=1, source_target_pairs={{0,1},{4,8},{8,4},{12,16},{16,12},{20,24},{24,20},{28,29},{1,0},{5... | collective-permute-start | bytes 147464 | tf_op jit(solution)/shard_map/ppermute | solution.py:489
  69.4 3.8 %collective-permute-start.22 = (f32[3,4,256]{2,1,0:T(4,128)S(1)}, f32[3,4,256]{2,1,0:T(4,128)S(1)}, u32[]{:S(2)}, u32[]{:S(2)}) collective-permute-start(f32[3,4,256]{2,1,0:T(4,128)S(1)} %get-tuple-element.65), channel_id=1, source_target_pairs={{0,1},{1,0},{2,3},{3,2},{4,5},{5,4},{6,7},{7,6},{8,9},{9,8},{10,11... | collective-permute-start | bytes 36872 | tf_op jit(solution)/shard_map/ppermute | solution.py:489
  69.9 4.6 %collective-permute-start.23 = (f32[3,4,256]{2,1,0:T(4,128)S(1)}, f32[3,4,256]{2,1,0:T(4,128)S(1)}, u32[]{:S(2)}, u32[]{:S(2)}) collective-permute-start(f32[3,4,256]{2,1,0:T(4,128)S(1)} %get-tuple-element.66), channel_id=1, source_target_pairs={{0,4},{1,2},{2,1},{3,7},{4,0},{5,6},{6,5},{7,3},{8,12},{9,10},{10,... | collective-permute-start | bytes 36872 | tf_op jit(solution)/shard_map/ppermute | solution.py:489
  75.0 3.7 %collective-permute-start.25 = (f32[8,128]{1,0:T(8,128)S(1)}, f32[8,128]{1,0:T(8,128)S(1)}, u32[]{:S(2)}, u32[]{:S(2)}) collective-permute-start(f32[8,128]{1,0:T(8,128)S(1)} %get-tuple-element.68.refs_0_), channel_id=1, source_target_pairs={{0,2},{1,3},{2,0},{3,1},{4,6},{5,7},{6,4},{7,5},{8,10},{9,11},{10,... | collective-permute-start | bytes 12296 | tf_op jit(solution)/shard_map/ppermute | solution.py:524
  75.2 3.5 %collective-permute-start.24 = (f32[8,128]{1,0:T(8,128)S(1)}, f32[8,128]{1,0:T(8,128)S(1)}, u32[]{:S(2)}, u32[]{:S(2)}) collective-permute-start(f32[8,128]{1,0:T(8,128)S(1)} %get-tuple-element.68.refs_0_), channel_id=1, source_target_pairs={{0,1},{1,0},{2,3},{3,2},{4,5},{5,4},{6,7},{7,6},{8,9},{9,8},{10,11... | collective-permute-start | bytes 12296 | tf_op jit(solution)/shard_map/ppermute | solution.py:524
  78.7 4.7 %collective-permute-start.29 = (f32[8,128]{1,0:T(8,128)S(1)}, f32[8,128]{1,0:T(8,128)S(1)}, u32[]{:S(2)}, u32[]{:S(2)}) collective-permute-start(f32[8,128]{1,0:T(8,128)S(1)} %shard_map.116.refs_0_), channel_id=1, source_target_pairs={{0,12},{4,8},{8,4},{12,0},{16,28},{20,24},{24,20},{28,16},{1,13},{... | collective-permute-start | bytes 12296 | tf_op jit(solution)/shard_map/ppermute | solution.py:524
  81.8 3.6 %collective-permute-start.28 = (f32[8,128]{1,0:T(8,128)S(1)}, f32[8,128]{1,0:T(8,128)S(1)}, u32[]{:S(2)}, u32[]{:S(2)}) collective-permute-start(f32[8,128]{1,0:T(8,128)S(1)} %shard_map.116.refs_0_), channel_id=1, source_target_pairs={{0,8},{4,12},{8,0},{12,4},{16,24},{20,28},{24,16},{28,20},{1,9},{5... | collective-permute-start | bytes 12296 | tf_op jit(solution)/shard_map/ppermute | solution.py:524
  82.3 3.6 %collective-permute-start.27 = (f32[8,128]{1,0:T(8,128)S(1)}, f32[8,128]{1,0:T(8,128)S(1)}, u32[]{:S(2)}, u32[]{:S(2)}) collective-permute-start(f32[8,128]{1,0:T(8,128)S(1)} %shard_map.116.refs_0_), channel_id=1, source_target_pairs={{0,4},{4,0},{8,12},{12,8},{16,20},{20,16},{24,28},{28,24},{1,5},{5... | collective-permute-start | bytes 12296 | tf_op jit(solution)/shard_map/ppermute | solution.py:524
  85.9 4.6 %collective-permute-start.30 = (f32[8,128]{1,0:T(8,128)S(1)}, f32[8,128]{1,0:T(8,128)S(1)}, u32[]{:S(2)}, u32[]{:S(2)}) collective-permute-start(f32[8,128]{1,0:T(8,128)S(1)} %shard_map.117.refs_0_), channel_id=1, source_target_pairs={{0,16},{4,20},{8,24},{12,28},{16,0},{20,4},{24,8},{28,12},{1,17},{... | collective-permute-start | bytes 12296 | tf_op jit(solution)/shard_map/ppermute | solution.py:524
  (16 other events, 139.6 us)

commit v7 on v6

--- a/solution.py
+++ b/solution.py
@@ -139,7 +139,8 @@
 def first_kernel(
     cells_hbm, v_hbm, d_hbm, out_ref, cells_ref, v_ref, d_ref, deep_ref, sem
 ):
-    pairs = ((cells_hbm, cells_ref), (v_hbm, v_ref), (d_hbm, d_ref))
+    pairs = [(cells_hbm, cells_ref), (v_hbm, v_ref)]
+    pairs += [(d_hbm.at[entry], d_ref.at[entry]) for entry in range(9)]
     copies = [
         pltpu.make_async_copy(src, dst, sem.at[place])
         for place, (src, dst) in enumerate(pairs)
@@ -149,9 +150,13 @@
     copies[0].wait()
     depth = v_ref.shape[3]
     one_hot(deep_ref, lambda lanes: row_and_depth(cells_ref[:, lanes], depth)[1])
-    copies[1].wait()
-    copies[2].wait()
+    for copy in copies[1:]:
+        copy.wait()
     pick(times_diag(d_ref, [v_ref[b] for b in range(3)]), cells_ref, deep_ref, out_ref)
+
+
+def hold_kernel(value_ref, out_ref):
+    out_ref[...] = value_ref[...]
 
 
 def spread_matrix(wells, width):
@@ -203,7 +208,7 @@
 
 def solve_kernel(
     idx_ref, own_ref, even_ref, next_ref, g_ref, h_ref, e_ref, low_ref, high_ref,
-    keep_ref, to_even_ref, to_next_ref,
+    keep_ref, to_next_ref, to_even_ref,
     pool_ref, r_ref, q_ref, tail_ref, p_ref, y_ref,
 ):
     _, chunks, span, span_all = g_ref.shape
@@ -328,7 +333,7 @@
             to_next_ref[at, :] = jnp.where(odd_y, parts[2], parts[0])
 
 
-def add_kernel(x_ref, y_ref, z_ref, keep_ref, to_even_ref, to_next_ref):
+def add_kernel(x_ref, y_ref, z_ref, keep_ref, to_next_ref, to_even_ref):
     tile = keep_ref.shape[0]
     odd_x = is_odd("gx")
     low, mid, high = [
@@ -342,7 +347,7 @@
 
 def place_kernel(
     row_ref, deep_ref, v_ref, inv_ref, x_ref, y_ref, z_ref,
-    out_ref, x_even_ref, x_next_ref, y_even_ref, y_next_ref,
+    out_ref, x_next_ref, x_even_ref, y_next_ref, y_even_ref,
 ):
     (first_x, last_x), (first_y, last_y) = [
         (lax.axis_index(axis) == 0, lax.axis_index(axis) == lax.axis_size(axis) - 1)
@@ -411,7 +416,7 @@
 def add_faces(part_ref, faces, off_ref, w_ref):
     nx, ny, nz = part_ref.shape[1:]
     odd_x, odd_y = is_odd("gx"), is_odd("gy")
-    x_even, x_next, y_even, y_next = [face[...] for face in faces]
+    x_next, x_even, y_next, y_even = [face[...] for face in faces]
     xl, xh = jnp.where(odd_x, x_even, x_next), jnp.where(odd_x, x_next, x_even)
     yl, yh = jnp.where(odd_y, y_even, y_next), jnp.where(odd_y, y_next, y_even)
     for a in range(3):
@@ -473,9 +478,9 @@
         return along * size["gy"] + across if axis == "gx" else across * size["gy"] + along
 
     out = []
-    order = [(0, to_even), (1, to_next)]
+    order = [(1, to_next), (0, to_even)]
     same = to_even is to_next
-    for first, value in order if same else order[::-1]:
+    for first, value in order:
         pairs = []
         for across in range(breadth):
             for i in range(count):
@@ -487,7 +492,7 @@
                 else:
                     pairs.append((device(i, across), device(i, across)))
         out.append(lax.ppermute(value, ("gx", "gy"), pairs))
-    return out if same else out[::-1]
+    return out[::-1]
 
 
 def merge_kernel(*refs):
@@ -512,20 +517,20 @@
     out_ref[...] = total
 
 
-def merge_all(value, axis):
-    count = lax.axis_size(axis)
+def merge_all(value):
+    axes = ("gx", "gy")
+    count = lax.axis_size(axes)
     if count & (count - 1):
-        every = lax.all_gather(value, axis)
+        every = lax.all_gather(value, axes)
         return call(merge_kernel, [value.shape])(*[every[i] for i in range(count)])[0]
-    step = 1
+    step, radix = 1, 2 if count.bit_length() % 2 == 0 else 4
     while step < count:
-        radix = min(4, count // step)
         others = [
-            lax.ppermute(value, axis, [(i, i ^ (k * step)) for i in range(count)])
+            lax.ppermute(value, axes, [(i, i ^ (k * step)) for i in range(count)])
             for k in range(1, radix)
         ]
         (value,) = call(merge_kernel, [value.shape])(value, *others)
-        step *= radix
+        step, radix = step * radix, 4
     return value
 
 
@@ -558,7 +563,7 @@
             (field, F32),
             (diag_blocks.shape, F32),
             ((nz, slots), BF16),
-            pltpu.SemaphoreType.DMA((3,)),
+            pltpu.SemaphoreType.DMA((11,)),
         ],
         flops=10**9,
         space=pltpu.HBM,
@@ -579,9 +584,12 @@
     )(index, send_cells, span_inverse, couple)
 
     def precondition(vector, picked):
-        column = jnp.concatenate([picked, *swap("gx", picked, picked)], axis=0)
+        beside = swap("gx", picked, picked)
+        if vector is right_side:
+            (picked,) = call(hold_kernel, [picked.shape])(picked)
+        column = jnp.concatenate([picked, *beside], axis=0)
         even, following = swap("gy", column, column)
-        keep, even, following = call(
+        keep, following, even = call(
             solve_kernel,
             [(3 * tile, LANES)] * 3,
             [
@@ -595,16 +603,16 @@
             flops=4 * 10**9,
         )(index, column, even, following, apart, h, e, low, high)
         even, following = swap("gy", even, following)
-        keep, even, following = call(add_kernel, [(tile, LANES)] * 3)(
-            keep, even, following
+        keep, following, even = call(add_kernel, [(tile, LANES)] * 3)(
+            keep, following, even
         )
         even, following = swap("gx", even, following)
         z, *faces = call(
             place_kernel,
             [(3, nx, ny, nz)] + [(3, ny, nz)] * 2 + [(3, nx, nz)] * 2,
             flops=10**9,
-        )(row, deep, vector, cell_inverse, keep, even, following)
-        faces = swap("gx", *faces[:2]) + swap("gy", *faces[2:])
+        )(row, deep, vector, cell_inverse, keep, following, even)
+        faces = swap("gx", *faces[1::-1])[::-1] + swap("gy", *faces[:1:-1])[::-1]
         (part,) = call(inner_kernel, [field], flops=10**7)(z, diag_blocks, off_blocks)
         return z, part, faces
 
@@ -616,7 +624,7 @@
     w2, sums = call(gram_kernel, [field, (8, LANES)])(
         part, *faces, off_blocks, right_side, w1
     )
-    sums = merge_all(merge_all(sums, "gy"), "gx")
+    sums = merge_all(sums)
     return tuple(
         call(final_kernel, [field, field])(sums, right_side, z1, z2, w1, w2)
     )

time: 91.5 us -> 88.6 us (0.968)
  starting transfers between devices: 40 us -> 38.1 us
  waiting for transfers between devices: 28.4 us -> 27.4 us
    ppermute x7, waiting for transfers between devices: 7.62 us -> 4.99 us  [merge_all(): lax.ppermute(value, axes, [(i, i ^ k * step) for i in range(count)])]
    ppermute x24, starting transfers between devices: 32.2 us -> 30 us  [swap(): out.append(lax.ppermute(value, ('gx', 'gy'), pairs))]
    ppermute x24, waiting for transfers between devices: 20.8 us -> 22.4 us  [swap(): out.append(lax.ppermute(value, ('gx', 'gy'), pairs))]
    pallas_call x16 -> x17, Pallas kernels: 20.6 us -> 20.7 us  [run(): pl.pallas_call(kernel, out_shape=shapes, in_specs=[pl.BlockSpec(memory_sp...]
where the time goes in v7:
time: 88.6 us; the launch traced here: 88.4 us
  starting transfers between devices  38.1 us (43%)
  waiting for transfers between devices  27.4 us (31%)
  Pallas kernels  20.7 us (23%)
  local copies, waits for them, and re-layouts  1.29 us (1%)
  between operations  0.95 us (1%)
    ppermute x24, starting transfers between devices, swap(): out.append(lax.ppermute(value, ('gx', 'gy'), pairs))  30 us
    ppermute x24, waiting for transfers between devices, swap(): out.append(lax.ppermute(value, ('gx', 'gy'), pairs))  22.4 us
    pallas_call x17, Pallas kernels, run(): pl.pallas_call(kernel, out_shape=shapes, in_specs=[pl.BlockSpec(memory_sp...  20.7 us
    ppermute x7, starting transfers between devices, merge_all(): lax.ppermute(value, axes, [(i, i ^ k * step) for i in range(count)])  8.07 us
    ppermute x7, waiting for transfers between devices, merge_all(): lax.ppermute(value, axes, [(i, i ^ k * step) for i in range(count)])  4.99 us
  transfers between devices with their start and end apart: 31, of which 15 were waited for; matrix products, arithmetic and copies ran while one was open for 1% of the time, Pallas kernels for 4%

profile of v7, /device:TPU:0, one launch (start us, length us, event | category | flops | bytes accessed | tf_op | source)
XLA Modules:
  0.0 88.4 jit_solution(12596911014890003716)
XLA Ops:
  0.7 3.0 %shard_map.105.value_ref = f32[80,128]{1,0:T(8,128)} custom-call(s32[1,3200]{1,0:T(1,128)} %cells_ref.3, f32[3,4,16,256]{3,2,1,0:T(8,128)} %v_ref.7, f32[9,4,16,256]{3,2,1,0:T(8,128)} %d_ref.5), custom_call_target="tpu_custom_call" | custom-call | flops 1000000000 | bytes 840192 | tf_op jit(solution)/shard_map/pallas_call | solution.py:56
  4.2 4.0 %collective-permute-start = (f32[80,128]{1,0:T(8,128)}, f32[80,128]{1,0:T(8,128)S(1)}, u32[]{:S(2)}, u32[]{:S(2)}) collective-permute-start(f32[80,128]{1,0:T(8,128)} %shard_map.105.value_ref), channel_id=1, source_target_pairs={{0,4},{4,0},{8,12},{12,8},{16,20},{20,16},{24,28},{28,24},{1,5},{5... | collective-permute-start | bytes 122888 | tf_op jit(solution)/shard_map/ppermute | solution.py:494
  10.4 2.1 %collective-permute-start.3 = (f32[240,128]{1,0:T(8,128)S(1)}, f32[240,128]{1,0:T(8,128)S(1)}, u32[]{:S(2)}, u32[]{:S(2)}) collective-permute-start(f32[240,128]{1,0:T(8,128)S(1)} %pad_maximum_fusion.own_ref), channel_id=1, source_target_pairs={{0,4},{1,2},{2,1},{3,7},{4,0},{5,6},{6,5},{7,3},{8,12},{9,10},{10,... | collective-permute-start | bytes 368648 | tf_op jit(solution)/shard_map/ppermute | solution.py:494
  13.1 2.6 %shard_map.104 = (f32[3,32,384]{2,1,0:T(8,128)S(1)}, f32[9,32,8]{2,1,0:T(8,128)S(1)}, f32[3,25,16,384]{3,2,1,0:T(8,128)S(1)}, bf16[256,3200]{1,0:T(8,128)(2,1)S(...) custom-call(s32[1,3200]{1,0:T(1,128)S(1)} %reshape.12.idx_ref, ...), custom_call_target="tpu_custom_call" | custom-call | bytes 8383488 | tf_op jit(solution)/shard_map/pallas_call | solution.py:56
  15.7 4.9 %shard_map.107 = (f32[240,128]{1,0:T(8,128)S(1)}, f32[240,128]{1,0:T(8,128)S(1)}, f32[240,128]{1,0:T(8,128)S(1)}) custom-call(s32[1,3200]{1,0:T(1,128)S(1)} %reshape.12.idx_ref, f32[240,128]{1,0:T(8,128)S(1)} %pad_maximum_fusion.own_ref, f32[240,128]{1,0:T(8,128)S(1)} %collective-permute-done.2.even_ref, f32[240,128]{1,0:T(8,128)S(1)} %collective-permute-done.3.next_ref, ...), custom_call_target="tpu_custom_call" | custom-call | flops 4000000000 | bytes 5207552 | tf_op jit(solution)/shard_map/pallas_call | solution.py:56
  20.6 1.8 %collective-permute-start.4 = (f32[240,128]{1,0:T(8,128)S(1)}, f32[240,128]{1,0:T(8,128)S(1)}, u32[]{:S(2)}, u32[]{:S(2)}) collective-permute-start(f32[240,128]{1,0:T(8,128)S(1)} %get-tuple-element.44), channel_id=1, source_target_pairs={{0,4},{1,2},{2,1},{3,7},{4,0},{5,6},{6,5},{7,3},{8,12},{9,10},{10,... | collective-permute-start | bytes 368648 | tf_op jit(solution)/shard_map/ppermute | solution.py:494
  22.4 3.2 %collective-permute-done.4.y_ref = f32[240,128]{1,0:T(8,128)S(1)} collective-permute-done((f32[240,128]{1,0:T(8,128)S(1)}, f32[240,128]{1,0:T(8,128)S(1)}, u32[]{:S(2)}, u32[]{:S(2)}) %collective-permute-start.4) | collective-permute-done | bytes 122912 | tf_op jit(solution)/shard_map/ppermute | solution.py:494
  25.8 3.0 %collective-permute-start.7 = (f32[80,128]{1,0:T(8,128)S(1)}, f32[80,128]{1,0:T(8,128)S(1)}, u32[]{:S(2)}, u32[]{:S(2)}) collective-permute-start(f32[80,128]{1,0:T(8,128)S(1)} %get-tuple-element.48), channel_id=1, source_target_pairs={{0,4},{4,0},{8,12},{12,8},{16,20},{20,16},{24,28},{28,24},{1,5},{5... | collective-permute-start | bytes 122888 | tf_op jit(solution)/shard_map/ppermute | solution.py:494
  28.8 2.0 %collective-permute-done.7.z_ref = f32[80,128]{1,0:T(8,128)S(1)} collective-permute-done((f32[80,128]{1,0:T(8,128)S(1)}, f32[80,128]{1,0:T(8,128)S(1)}, u32[]{:S(2)}, u32[]{:S(2)}) %collective-permute-start.7) | collective-permute-done | bytes 40992 | tf_op jit(solution)/shard_map/ppermute | solution.py:494
  31.8 3.5 %collective-permute-start.9 = (f32[3,16,256]{2,1,0:T(8,128)S(1)}, f32[3,16,256]{2,1,0:T(8,128)S(1)}, u32[]{:S(2)}, u32[]{:S(2)}) collective-permute-start(f32[3,16,256]{2,1,0:T(8,128)S(1)} %get-tuple-element.51), channel_id=1, source_target_pairs={{0,4},{4,0},{8,12},{12,8},{16,20},{20,16},{24,28},{28,24},{1,5},{5... | collective-permute-start | bytes 147464 | tf_op jit(solution)/shard_map/ppermute | solution.py:494
  36.2 2.9 %collective-permute-done.10.f2_ref = f32[3,4,256]{2,1,0:T(4,128)S(1)} collective-permute-done((f32[3,4,256]{2,1,0:T(4,128)S(1)}, f32[3,4,256]{2,1,0:T(4,128)S(1)}, u32[]{:S(2)}, u32[]{:S(2)}) %collective-permute-start.10) | collective-permute-done | bytes 12320 | tf_op jit(solution)/shard_map/ppermute | solution.py:494
  40.2 3.0 %collective-permute-start.12 = (f32[80,128]{1,0:T(8,128)S(1)}, f32[80,128]{1,0:T(8,128)S(1)}, u32[]{:S(2)}, u32[]{:S(2)}) collective-permute-start(f32[80,128]{1,0:T(8,128)S(1)} %get-tuple-element.55), channel_id=1, source_target_pairs={{0,4},{4,0},{8,12},{12,8},{16,20},{20,16},{24,28},{28,24},{1,5},{5... | collective-permute-start | bytes 122888 | tf_op jit(solution)/shard_map/ppermute | solution.py:494
  43.2 2.0 %collective-permute-done.12 = f32[80,128]{1,0:T(8,128)S(1)} collective-permute-done((f32[80,128]{1,0:T(8,128)S(1)}, f32[80,128]{1,0:T(8,128)S(1)}, u32[]{:S(2)}, u32[]{:S(2)}) %collective-permute-start.12) | collective-permute-done | bytes 40992 | tf_op jit(solution)/shard_map/ppermute | solution.py:494
  45.2 2.1 %collective-permute-start.15 = (f32[240,128]{1,0:T(8,128)S(1)}, f32[240,128]{1,0:T(8,128)S(1)}, u32[]{:S(2)}, u32[]{:S(2)}) collective-permute-start(f32[240,128]{1,0:T(8,128)S(1)} %constant_dynamic-update-slice_fusion.own_ref), channel_id=1, source_target_pairs={{0,4},{1,2},{2,1},{3,7},{4,0},{5,6},{6,5},{7,3},{8,12},{9,10},{10,... | collective-permute-start | bytes 368648 | tf_op jit(solution)/shard_map/ppermute | solution.py:494
  47.3 2.9 %collective-permute-done.15.next_ref = f32[240,128]{1,0:T(8,128)S(1)} collective-permute-done((f32[240,128]{1,0:T(8,128)S(1)}, f32[240,128]{1,0:T(8,128)S(1)}, u32[]{:S(2)}, u32[]{:S(2)}) %collective-permute-start.15) | collective-permute-done | bytes 122912 | tf_op jit(solution)/shard_map/ppermute | solution.py:494
  50.2 5.1 %shard_map.112 = (f32[240,128]{1,0:T(8,128)S(1)}, f32[240,128]{1,0:T(8,128)S(1)}, f32[240,128]{1,0:T(8,128)S(1)}) custom-call(s32[1,3200]{1,0:T(1,128)S(1)} %reshape.12.idx_ref, f32[240,128]{1,0:T(8,128)S(1)} %constant_dynamic-update-slice_fusion.own_ref, f32[240,128]{1,0:T(8,128)S(1)} %collective-permute-done.14.even_ref, ...), custom_call_target="tpu_custom_call" | custom-call | flops 4000000000 | bytes 5207552 | tf_op jit(solution)/shard_map/pallas_call | solution.py:56
  55.3 2.1 %collective-permute-start.16 = (f32[240,128]{1,0:T(8,128)S(1)}, f32[240,128]{1,0:T(8,128)S(1)}, u32[]{:S(2)}, u32[]{:S(2)}) collective-permute-start(f32[240,128]{1,0:T(8,128)S(1)} %get-tuple-element.57), channel_id=1, source_target_pairs={{0,4},{1,2},{2,1},{3,7},{4,0},{5,6},{6,5},{7,3},{8,12},{9,10},{10,... | collective-permute-start | bytes 368648 | tf_op jit(solution)/shard_map/ppermute | solution.py:494
  57.4 2.9 %collective-permute-done.16.y_ref = f32[240,128]{1,0:T(8,128)S(1)} collective-permute-done((f32[240,128]{1,0:T(8,128)S(1)}, f32[240,128]{1,0:T(8,128)S(1)}, u32[]{:S(2)}, u32[]{:S(2)}) %collective-permute-start.16) | collective-permute-done | bytes 122912 | tf_op jit(solution)/shard_map/ppermute | solution.py:494
  60.4 3.3 %collective-permute-start.19 = (f32[80,128]{1,0:T(8,128)S(1)}, f32[80,128]{1,0:T(8,128)S(1)}, u32[]{:S(2)}, u32[]{:S(2)}) collective-permute-start(f32[80,128]{1,0:T(8,128)S(1)} %get-tuple-element.61), channel_id=1, source_target_pairs={{0,4},{4,0},{8,12},{12,8},{16,20},{20,16},{24,28},{28,24},{1,5},{5... | collective-permute-start | bytes 122888 | tf_op jit(solution)/shard_map/ppermute | solution.py:494
  63.7 2.0 %collective-permute-done.19.z_ref = f32[80,128]{1,0:T(8,128)S(1)} collective-permute-done((f32[80,128]{1,0:T(8,128)S(1)}, f32[80,128]{1,0:T(8,128)S(1)}, u32[]{:S(2)}, u32[]{:S(2)}) %collective-permute-start.19) | collective-permute-done | bytes 40992 | tf_op jit(solution)/shard_map/ppermute | solution.py:494
  66.7 3.6 %collective-permute-start.21 = (f32[3,16,256]{2,1,0:T(8,128)S(1)}, f32[3,16,256]{2,1,0:T(8,128)S(1)}, u32[]{:S(2)}, u32[]{:S(2)}) collective-permute-start(f32[3,16,256]{2,1,0:T(8,128)S(1)} %get-tuple-element.64), channel_id=1, source_target_pairs={{0,4},{4,0},{8,12},{12,8},{16,20},{20,16},{24,28},{28,24},{1,5},{5... | collective-permute-start | bytes 147464 | tf_op jit(solution)/shard_map/ppermute | solution.py:494
  70.7 3.3 %collective-permute-done.22.f2_ref = f32[3,4,256]{2,1,0:T(4,128)S(1)} collective-permute-done((f32[3,4,256]{2,1,0:T(4,128)S(1)}, f32[3,4,256]{2,1,0:T(4,128)S(1)}, u32[]{:S(2)}, u32[]{:S(2)}) %collective-permute-start.22) | collective-permute-done | bytes 12320 | tf_op jit(solution)/shard_map/ppermute | solution.py:494
  76.4 2.9 %collective-permute-start.25 = (f32[8,128]{1,0:T(8,128)S(1)}, f32[8,128]{1,0:T(8,128)S(1)}, u32[]{:S(2)}, u32[]{:S(2)}) collective-permute-start(f32[8,128]{1,0:T(8,128)S(1)} %shard_map.117.refs_0_), channel_id=1, source_target_pairs={{0,2},{1,3},{2,0},{3,1},{4,6},{5,7},{6,4},{7,5},{8,10},{9,11},{10,... | collective-permute-start | bytes 12296 | tf_op jit(solution)/shard_map/ppermute | solution.py:529
  80.9 1.7 %collective-permute-start.30 = (f32[8,128]{1,0:T(8,128)S(1)}, f32[8,128]{1,0:T(8,128)S(1)}, u32[]{:S(2)}, u32[]{:S(2)}) collective-permute-start(f32[8,128]{1,0:T(8,128)S(1)} %shard_map.118.refs_0_), channel_id=1, source_target_pairs={{0,24},{1,25},{2,26},{3,27},{4,28},{5,29},{6,30},{7,31},{8,16},{9,... | collective-permute-start | bytes 12296 | tf_op jit(solution)/shard_map/ppermute | solution.py:529
  (85 shorter events, 17.9 us)
Async XLA Ops:
  3.7 5.4 %collective-permute-start.1 = (f32[80,128]{1,0:T(8,128)}, f32[80,128]{1,0:T(8,128)S(1)}, u32[]{:S(2)}, u32[]{:S(2)}) collective-permute-start(f32[80,128]{1,0:T(8,128)} %shard_map.105.value_ref), channel_id=1, source_target_pairs={{0,1},{4,8},{8,4},{12,16},{16,12},{20,24},{24,20},{28,29},{1,0},{5... | collective-permute-start | bytes 122888 | tf_op jit(solution)/shard_map/ppermute | solution.py:494
  4.2 6.3 %collective-permute-start = (f32[80,128]{1,0:T(8,128)}, f32[80,128]{1,0:T(8,128)S(1)}, u32[]{:S(2)}, u32[]{:S(2)}) collective-permute-start(f32[80,128]{1,0:T(8,128)} %shard_map.105.value_ref), channel_id=1, source_target_pairs={{0,4},{4,0},{8,12},{12,8},{16,20},{20,16},{24,28},{28,24},{1,5},{5... | collective-permute-start | bytes 122888 | tf_op jit(solution)/shard_map/ppermute | solution.py:494
  10.4 5.2 %collective-permute-start.3 = (f32[240,128]{1,0:T(8,128)S(1)}, f32[240,128]{1,0:T(8,128)S(1)}, u32[]{:S(2)}, u32[]{:S(2)}) collective-permute-start(f32[240,128]{1,0:T(8,128)S(1)} %pad_maximum_fusion.own_ref), channel_id=1, source_target_pairs={{0,4},{1,2},{2,1},{3,7},{4,0},{5,6},{6,5},{7,3},{8,12},{9,10},{10,... | collective-permute-start | bytes 368648 | tf_op jit(solution)/shard_map/ppermute | solution.py:494
  20.6 4.9 %collective-permute-start.4 = (f32[240,128]{1,0:T(8,128)S(1)}, f32[240,128]{1,0:T(8,128)S(1)}, u32[]{:S(2)}, u32[]{:S(2)}) collective-permute-start(f32[240,128]{1,0:T(8,128)S(1)} %get-tuple-element.44), channel_id=1, source_target_pairs={{0,4},{1,2},{2,1},{3,7},{4,0},{5,6},{6,5},{7,3},{8,12},{9,10},{10,... | collective-permute-start | bytes 368648 | tf_op jit(solution)/shard_map/ppermute | solution.py:494
  25.8 5.0 %collective-permute-start.7 = (f32[80,128]{1,0:T(8,128)S(1)}, f32[80,128]{1,0:T(8,128)S(1)}, u32[]{:S(2)}, u32[]{:S(2)}) collective-permute-start(f32[80,128]{1,0:T(8,128)S(1)} %get-tuple-element.48), channel_id=1, source_target_pairs={{0,4},{4,0},{8,12},{12,8},{16,20},{20,16},{24,28},{28,24},{1,5},{5... | collective-permute-start | bytes 122888 | tf_op jit(solution)/shard_map/ppermute | solution.py:494
  31.7 7.3 %collective-permute-start.8 = (f32[3,16,256]{2,1,0:T(8,128)S(1)}, f32[3,16,256]{2,1,0:T(8,128)S(1)}, u32[]{:S(2)}, u32[]{:S(2)}) collective-permute-start(f32[3,16,256]{2,1,0:T(8,128)S(1)} %get-tuple-element.50), channel_id=1, source_target_pairs={{0,1},{4,8},{8,4},{12,16},{16,12},{20,24},{24,20},{28,29},{1,0},{5... | collective-permute-start | bytes 147464 | tf_op jit(solution)/shard_map/ppermute | solution.py:494
  31.8 7.2 %collective-permute-start.9 = (f32[3,16,256]{2,1,0:T(8,128)S(1)}, f32[3,16,256]{2,1,0:T(8,128)S(1)}, u32[]{:S(2)}, u32[]{:S(2)}) collective-permute-start(f32[3,16,256]{2,1,0:T(8,128)S(1)} %get-tuple-element.51), channel_id=1, source_target_pairs={{0,4},{4,0},{8,12},{12,8},{16,20},{20,16},{24,28},{28,24},{1,5},{5... | collective-permute-start | bytes 147464 | tf_op jit(solution)/shard_map/ppermute | solution.py:494
  35.3 3.7 %collective-permute-start.10 = (f32[3,4,256]{2,1,0:T(4,128)S(1)}, f32[3,4,256]{2,1,0:T(4,128)S(1)}, u32[]{:S(2)}, u32[]{:S(2)}) collective-permute-start(f32[3,4,256]{2,1,0:T(4,128)S(1)} %get-tuple-element.52), channel_id=1, source_target_pairs={{0,4},{1,2},{2,1},{3,7},{4,0},{5,6},{6,5},{7,3},{8,12},{9,10},{10,... | collective-permute-start | bytes 36872 | tf_op jit(solution)/shard_map/ppermute | solution.py:494
  35.4 3.7 %collective-permute-start.11 = (f32[3,4,256]{2,1,0:T(4,128)S(1)}, f32[3,4,256]{2,1,0:T(4,128)S(1)}, u32[]{:S(2)}, u32[]{:S(2)}) collective-permute-start(f32[3,4,256]{2,1,0:T(4,128)S(1)} %get-tuple-element.53), channel_id=1, source_target_pairs={{0,1},{1,0},{2,3},{3,2},{4,5},{5,4},{6,7},{7,6},{8,9},{9,8},{10,11... | collective-permute-start | bytes 36872 | tf_op jit(solution)/shard_map/ppermute | solution.py:494
  40.1 5.1 %collective-permute-start.13 = (f32[80,128]{1,0:T(8,128)S(1)}, f32[80,128]{1,0:T(8,128)S(1)}, u32[]{:S(2)}, u32[]{:S(2)}) collective-permute-start(f32[80,128]{1,0:T(8,128)S(1)} %get-tuple-element.55), channel_id=1, source_target_pairs={{0,1},{4,8},{8,4},{12,16},{16,12},{20,24},{24,20},{28,29},{1,0},{5... | collective-permute-start | bytes 122888 | tf_op jit(solution)/shard_map/ppermute | solution.py:494
  40.2 5.0 %collective-permute-start.12 = (f32[80,128]{1,0:T(8,128)S(1)}, f32[80,128]{1,0:T(8,128)S(1)}, u32[]{:S(2)}, u32[]{:S(2)}) collective-permute-start(f32[80,128]{1,0:T(8,128)S(1)} %get-tuple-element.55), channel_id=1, source_target_pairs={{0,4},{4,0},{8,12},{12,8},{16,20},{20,16},{24,28},{28,24},{1,5},{5... | collective-permute-start | bytes 122888 | tf_op jit(solution)/shard_map/ppermute | solution.py:494
  45.2 4.9 %collective-permute-start.15 = (f32[240,128]{1,0:T(8,128)S(1)}, f32[240,128]{1,0:T(8,128)S(1)}, u32[]{:S(2)}, u32[]{:S(2)}) collective-permute-start(f32[240,128]{1,0:T(8,128)S(1)} %constant_dynamic-update-slice_fusion.own_ref), channel_id=1, source_target_pairs={{0,4},{1,2},{2,1},{3,7},{4,0},{5,6},{6,5},{7,3},{8,12},{9,10},{10,... | collective-permute-start | bytes 368648 | tf_op jit(solution)/shard_map/ppermute | solution.py:494
  55.3 4.9 %collective-permute-start.16 = (f32[240,128]{1,0:T(8,128)S(1)}, f32[240,128]{1,0:T(8,128)S(1)}, u32[]{:S(2)}, u32[]{:S(2)}) collective-permute-start(f32[240,128]{1,0:T(8,128)S(1)} %get-tuple-element.57), channel_id=1, source_target_pairs={{0,4},{1,2},{2,1},{3,7},{4,0},{5,6},{6,5},{7,3},{8,12},{9,10},{10,... | collective-permute-start | bytes 368648 | tf_op jit(solution)/shard_map/ppermute | solution.py:494
  60.4 5.3 %collective-permute-start.19 = (f32[80,128]{1,0:T(8,128)S(1)}, f32[80,128]{1,0:T(8,128)S(1)}, u32[]{:S(2)}, u32[]{:S(2)}) collective-permute-start(f32[80,128]{1,0:T(8,128)S(1)} %get-tuple-element.61), channel_id=1, source_target_pairs={{0,4},{4,0},{8,12},{12,8},{16,20},{20,16},{24,28},{28,24},{1,5},{5... | collective-permute-start | bytes 122888 | tf_op jit(solution)/shard_map/ppermute | solution.py:494
  66.6 7.4 %collective-permute-start.20 = (f32[3,16,256]{2,1,0:T(8,128)S(1)}, f32[3,16,256]{2,1,0:T(8,128)S(1)}, u32[]{:S(2)}, u32[]{:S(2)}) collective-permute-start(f32[3,16,256]{2,1,0:T(8,128)S(1)} %get-tuple-element.63), channel_id=1, source_target_pairs={{0,1},{4,8},{8,4},{12,16},{16,12},{20,24},{24,20},{28,29},{1,0},{5... | collective-permute-start | bytes 147464 | tf_op jit(solution)/shard_map/ppermute | solution.py:494
  66.7 7.3 %collective-permute-start.21 = (f32[3,16,256]{2,1,0:T(8,128)S(1)}, f32[3,16,256]{2,1,0:T(8,128)S(1)}, u32[]{:S(2)}, u32[]{:S(2)}) collective-permute-start(f32[3,16,256]{2,1,0:T(8,128)S(1)} %get-tuple-element.64), channel_id=1, source_target_pairs={{0,4},{4,0},{8,12},{12,8},{16,20},{20,16},{24,28},{28,24},{1,5},{5... | collective-permute-start | bytes 147464 | tf_op jit(solution)/shard_map/ppermute | solution.py:494
  70.3 3.7 %collective-permute-start.22 = (f32[3,4,256]{2,1,0:T(4,128)S(1)}, f32[3,4,256]{2,1,0:T(4,128)S(1)}, u32[]{:S(2)}, u32[]{:S(2)}) collective-permute-start(f32[3,4,256]{2,1,0:T(4,128)S(1)} %get-tuple-element.65), channel_id=1, source_target_pairs={{0,4},{1,2},{2,1},{3,7},{4,0},{5,6},{6,5},{7,3},{8,12},{9,10},{10,... | collective-permute-start | bytes 36872 | tf_op jit(solution)/shard_map/ppermute | solution.py:494
  70.4 3.7 %collective-permute-start.23 = (f32[3,4,256]{2,1,0:T(4,128)S(1)}, f32[3,4,256]{2,1,0:T(4,128)S(1)}, u32[]{:S(2)}, u32[]{:S(2)}) collective-permute-start(f32[3,4,256]{2,1,0:T(4,128)S(1)} %get-tuple-element.66), channel_id=1, source_target_pairs={{0,1},{1,0},{2,3},{3,2},{4,5},{5,4},{6,7},{7,6},{8,9},{9,8},{10,11... | collective-permute-start | bytes 36872 | tf_op jit(solution)/shard_map/ppermute | solution.py:494
  75.7 4.6 %collective-permute-start.27 = (f32[8,128]{1,0:T(8,128)S(1)}, f32[8,128]{1,0:T(8,128)S(1)}, u32[]{:S(2)}, u32[]{:S(2)}) collective-permute-start(f32[8,128]{1,0:T(8,128)S(1)} %shard_map.117.refs_0_), channel_id=1, source_target_pairs={{0,6},{1,7},{2,4},{3,5},{4,2},{5,3},{6,0},{7,1},{8,14},{9,15},{10,... | collective-permute-start | bytes 12296 | tf_op jit(solution)/shard_map/ppermute | solution.py:529
  75.8 4.5 %collective-permute-start.26 = (f32[8,128]{1,0:T(8,128)S(1)}, f32[8,128]{1,0:T(8,128)S(1)}, u32[]{:S(2)}, u32[]{:S(2)}) collective-permute-start(f32[8,128]{1,0:T(8,128)S(1)} %shard_map.117.refs_0_), channel_id=1, source_target_pairs={{0,4},{1,5},{2,6},{3,7},{4,0},{5,1},{6,2},{7,3},{8,12},{9,13},{10,... | collective-permute-start | bytes 12296 | tf_op jit(solution)/shard_map/ppermute | solution.py:529
  76.4 4.5 %collective-permute-start.25 = (f32[8,128]{1,0:T(8,128)S(1)}, f32[8,128]{1,0:T(8,128)S(1)}, u32[]{:S(2)}, u32[]{:S(2)}) collective-permute-start(f32[8,128]{1,0:T(8,128)S(1)} %shard_map.117.refs_0_), channel_id=1, source_target_pairs={{0,2},{1,3},{2,0},{3,1},{4,6},{5,7},{6,4},{7,5},{8,10},{9,11},{10,... | collective-permute-start | bytes 12296 | tf_op jit(solution)/shard_map/ppermute | solution.py:529
  80.9 5.5 %collective-permute-start.30 = (f32[8,128]{1,0:T(8,128)S(1)}, f32[8,128]{1,0:T(8,128)S(1)}, u32[]{:S(2)}, u32[]{:S(2)}) collective-permute-start(f32[8,128]{1,0:T(8,128)S(1)} %shard_map.118.refs_0_), channel_id=1, source_target_pairs={{0,24},{1,25},{2,26},{3,27},{4,28},{5,29},{6,30},{7,31},{8,16},{9,... | collective-permute-start | bytes 12296 | tf_op jit(solution)/shard_map/ppermute | solution.py:529
  82.5 4.5 %collective-permute-start.29 = (f32[8,128]{1,0:T(8,128)S(1)}, f32[8,128]{1,0:T(8,128)S(1)}, u32[]{:S(2)}, u32[]{:S(2)}) collective-permute-start(f32[8,128]{1,0:T(8,128)S(1)} %shard_map.118.refs_0_), channel_id=1, source_target_pairs={{0,16},{1,17},{2,18},{3,19},{4,20},{5,21},{6,22},{7,23},{8,24},{9,... | collective-permute-start | bytes 12296 | tf_op jit(solution)/shard_map/ppermute | solution.py:529
  84.0 3.6 %collective-permute-start.28 = (f32[8,128]{1,0:T(8,128)S(1)}, f32[8,128]{1,0:T(8,128)S(1)}, u32[]{:S(2)}, u32[]{:S(2)}) collective-permute-start(f32[8,128]{1,0:T(8,128)S(1)} %shard_map.118.refs_0_), channel_id=1, source_target_pairs={{0,8},{1,9},{2,10},{3,11},{4,12},{5,13},{6,14},{7,15},{8,0},{9,1},... | collective-permute-start | bytes 12296 | tf_op jit(solution)/shard_map/ppermute | solution.py:529
  (17 other events, 136.8 us)

commit v8 on v7

--- a/solution.py
+++ b/solution.py
@@ -206,35 +206,23 @@
             e_ref[3 * a + b] = mm_exact(full, last_matrix(wells, width, a))
 
 
-def solve_kernel(
-    idx_ref, own_ref, even_ref, next_ref, g_ref, h_ref, e_ref, low_ref, high_ref,
-    keep_ref, to_next_ref, to_even_ref,
-    pool_ref, r_ref, q_ref, tail_ref, p_ref, y_ref,
-):
-    _, chunks, span, span_all = g_ref.shape
-    width = 3 * span
-    wells = span_all // width
-    slots = idx_ref.shape[1]
-    blocks = slots // LANES
-    rows = pool_ref.shape[1]
-    tile = own_ref.shape[0] // 3
-    group = wells * span
-    odd_x, odd_y = is_odd("gx"), is_odd("gy")
-    pool_ref[:, 9 * blocks :, :] = jnp.zeros((3, rows - 9 * blocks, LANES), F32)
-    own, even, following = own_ref[...], even_ref[...], next_ref[...]
-    columns = (
-        jnp.where(odd_y, even, following), own, jnp.where(odd_y, following, even)
-    )
-    for b, column in enumerate(columns):
-        own, even, following = column[:tile], column[tile : 2 * tile], column[2 * tile :]
-        parts = (jnp.where(odd_x, even, following), own, jnp.where(odd_x, following, even))
-        for a, part in enumerate(parts):
-            for comp in range(3):
-                at = (a * 3 + b) * blocks
-                pool_ref[comp, at : at + blocks, :] = part[
-                    comp * blocks : (comp + 1) * blocks
-                ]
-    half = rows // 2
+def pool_column(pool_ref, column, first, blocks):
+    odd_x = is_odd("gx")
+    tile = column.shape[0] // 3
+    own, even, following = column[:tile], column[tile : 2 * tile], column[2 * tile :]
+    parts = (jnp.where(odd_x, even, following), own, jnp.where(odd_x, following, even))
+    for a, part in enumerate(parts):
+        for comp in range(3):
+            at = (first + a) * blocks
+            pool_ref[comp, at : at + blocks, :] = part[comp * blocks : (comp + 1) * blocks]
+
+
+def clear_tail(pool_ref, used):
+    pool_ref[:, used:, :] = jnp.zeros((3, pool_ref.shape[1] - used, LANES), F32)
+
+
+def gather_lines(pool_ref, idx_ref, low_ref, first_row):
+    half = pool_ref.shape[1] // 2
     wide = 2 * LANES
     pooled = jnp.concatenate(
         [
@@ -246,19 +234,93 @@
         axis=0,
     )
     left = jnp.concatenate(split(pooled, 2), axis=1)
+    slots = idx_ref.shape[1]
     size = chunk_of(slots)
-    r_ref[...] = jnp.zeros(r_ref.shape, F32)
     for start in range(0, slots, size):
         place = idx_ref[:, start : start + size]
         right = low_ref[:, start : start + size]
         found = mm(left, jnp.concatenate([right, right], axis=0))
-        here = iota((half, size), 0) == lax.shift_right_arithmetic(place, wide.bit_length() - 1)
+        block = lax.shift_right_arithmetic(place, wide.bit_length() - 1) - first_row
+        here = iota((half, size), 0) == block
         for comp in range(3):
             part = jnp.where(here, found[comp * half : (comp + 1) * half], 0.0)
-            line = jnp.sum(part, axis=0, keepdims=True)
-            for piece in range(size // group):
-                at = start // group + piece
-                r_ref[comp, at : at + 1, :] = line[:, piece * group : (piece + 1) * group]
+            yield start, comp, jnp.sum(part, axis=0, keepdims=True)
+
+
+def scatter_lines(pool_ref, y_ref, low_ref, high_ref, first_row, group):
+    half = pool_ref.shape[1] // 2
+    slots = low_ref.shape[1]
+    size = chunk_of(slots)
+    spread_out = None
+    for start in range(0, slots, size):
+        lanes = slice(start, start + size)
+        steps = range(start // group, (start + size) // group)
+        lines = [
+            jnp.concatenate(
+                [y_ref[c : c + 1, comp * group : (comp + 1) * group] for c in steps], axis=1
+            )
+            for comp in range(3)
+        ]
+        hot = high_ref[first_row : first_row + half, lanes]
+        part = mm(scaled(hot, lines), low_ref[:, lanes], trans=True)
+        spread_out = part if spread_out is None else spread_out + part
+    spread_out = spread_out[: 3 * half] + spread_out[3 * half :]
+    for comp in range(3):
+        block = spread_out[comp * half : (comp + 1) * half]
+        for odd in range(2):
+            pool_ref[comp, pl.ds(odd, half, stride=2), :] = block[
+                :, odd * LANES : (odd + 1) * LANES
+            ]
+
+
+def own_gather_kernel(idx_ref, own_ref, low_ref, r_ref, pool_ref):
+    group = r_ref.shape[2]
+    blocks = idx_ref.shape[1] // LANES
+    clear_tail(pool_ref, 3 * blocks)
+    pool_column(pool_ref, own_ref[...], 0, blocks)
+    r_ref[...] = jnp.zeros(r_ref.shape, F32)
+    first_row = round_up(3 * blocks, 16)
+    for start, comp, line in gather_lines(pool_ref, idx_ref, low_ref, first_row):
+        for piece in range(line.shape[1] // group):
+            at = start // group + piece
+            r_ref[comp, at : at + 1, :] = line[:, piece * group : (piece + 1) * group]
+
+
+def own_scatter_kernel(y_ref, low_ref, high_ref, keep_ref, pool_ref):
+    blocks = low_ref.shape[1] // LANES
+    tile = keep_ref.shape[0] // 3
+    first_row = round_up(3 * blocks, 16)
+    scatter_lines(pool_ref, y_ref, low_ref, high_ref, first_row, y_ref.shape[1] // 3)
+    keep_ref[...] = jnp.zeros(keep_ref.shape, F32)
+    for a in range(3):
+        for comp in range(3):
+            at = slice(a * tile + comp * blocks, a * tile + (comp + 1) * blocks)
+            keep_ref[at, :] = pool_ref[comp, a * blocks : (a + 1) * blocks, :]
+
+
+def solve_kernel(
+    idx_ref, even_ref, next_ref, part_ref, g_ref, h_ref, e_ref, low_ref, high_ref,
+    y_ref, to_next_ref, to_even_ref,
+    pool_ref, r_ref, q_ref, tail_ref, p_ref,
+):
+    _, chunks, span, span_all = g_ref.shape
+    width = 3 * span
+    wells = span_all // width
+    blocks = idx_ref.shape[1] // LANES
+    tile = even_ref.shape[0] // 3
+    group = wells * span
+    odd_y = is_odd("gy")
+    clear_tail(pool_ref, 6 * blocks)
+    even, following = even_ref[...], next_ref[...]
+    pool_column(pool_ref, jnp.where(odd_y, even, following), 0, blocks)
+    pool_column(pool_ref, jnp.where(odd_y, following, even), 3, blocks)
+    r_ref[...] = jnp.zeros(r_ref.shape, F32)
+    for start, comp, line in gather_lines(pool_ref, idx_ref, low_ref, 0):
+        for piece in range(line.shape[1] // group):
+            at = start // group + piece
+            r_ref[comp, at : at + 1, :] = (
+                line[:, piece * group : (piece + 1) * group] + part_ref[comp, at : at + 1, :]
+            )
     two = (2 * group, span_all)
     well_of = lax.shift_right_logical(iota(two, 0) & (group - 1), (span - 1).bit_length())
     gap = iota(two, 1) - width * well_of
@@ -300,37 +362,17 @@
     rest = lax.rem(lane, jnp.int32(group))
     source = width * lax.div(rest, jnp.int32(span)) + 3 * lax.rem(rest, jnp.int32(span)) + comp_of
     y_ref[...] = mm_exact(plain, ones_where(iota(square, 0) == source))
-    spread_out = None
-    for start in range(0, slots, size):
-        lanes = slice(start, start + size)
-        steps = range(start // group, (start + size) // group)
-        lines = [
-            jnp.concatenate(
-                [y_ref[c : c + 1, comp * group : (comp + 1) * group] for c in steps], axis=1
-            )
-            for comp in range(3)
-        ]
-        part = mm(scaled(high_ref[:, lanes], lines), low_ref[:, lanes], trans=True)
-        spread_out = part if spread_out is None else spread_out + part
-    spread_out = spread_out[: 3 * half] + spread_out[3 * half :]
-    for comp in range(3):
-        block = spread_out[comp * half : (comp + 1) * half]
-        for odd in range(2):
-            pool_ref[comp, pl.ds(odd, half, stride=2), :] = block[
-                :, odd * LANES : (odd + 1) * LANES
-            ]
-    for dst in (keep_ref, to_even_ref, to_next_ref):
+    scatter_lines(pool_ref, y_ref, low_ref, high_ref, 0, group)
+    for dst in (to_even_ref, to_next_ref):
         dst[...] = jnp.zeros(dst.shape, F32)
     for a in range(3):
         for comp in range(3):
-            parts = []
-            for b in range(3):
-                at = (a * 3 + b) * blocks
-                parts.append(pool_ref[comp, at : at + blocks, :])
+            before, after = [
+                pool_ref[comp, (b + a) * blocks : (b + a + 1) * blocks, :] for b in (0, 3)
+            ]
             at = slice(a * tile + comp * blocks, a * tile + (comp + 1) * blocks)
-            keep_ref[at, :] = parts[1]
-            to_even_ref[at, :] = jnp.where(odd_y, parts[0], parts[2])
-            to_next_ref[at, :] = jnp.where(odd_y, parts[2], parts[0])
+            to_even_ref[at, :] = jnp.where(odd_y, before, after)
+            to_next_ref[at, :] = jnp.where(odd_y, after, before)
 
 
 def add_kernel(x_ref, y_ref, z_ref, keep_ref, to_next_ref, to_even_ref):
@@ -552,7 +594,8 @@
     span = width // 3
     blocks = slots // LANES
     tile = round_up(3 * blocks, 16)
-    rows = round_up(9 * blocks, 32)
+    beside_rows = round_up(6 * blocks, 32)
+    own_rows = round_up(3 * blocks, 32)
     tall = round_up(chunks, 16)
     field = right_side.shape
     (picked,) = call(
@@ -570,7 +613,10 @@
         mib=60,
     )(send_cells, right_side, diag_blocks)
     live = jnp.arange(longest)[None, :] < seg_count[:, None]
-    index = jnp.where(live, recv_index, -1)
+    along, column = recv_index // slots // 3, recv_index // slots % 3
+    index = recv_index % slots + slots * along
+    index = index + jnp.where(column == 1, beside_rows * LANES, slots * 3 * (column // 2))
+    index = jnp.where(live, index, -1)
     index = index.reshape(wells, chunks, span).transpose(1, 0, 2).reshape(1, wells * longest)
     couple = jnp.pad(span_couple.transpose(1, 0, 2), ((0, 0), (0, tall - chunks), (0, 0)))
     h, e, apart, low, high, deep, row = call(
@@ -578,7 +624,7 @@
         [(3, tall, span_all), (9, tall, wells), (3, chunks, span, span_all)]
         + [
             jax.ShapeDtypeStruct((height, slots), BF16)
-            for height in (2 * LANES, rows // 2, nz, nx * ny)
+            for height in (2 * LANES, (beside_rows + own_rows) // 2, nz, nx * ny)
         ],
         [((chunks, width, LANES), F32)],
     )(index, send_cells, span_inverse, couple)
@@ -589,20 +635,31 @@
             (picked,) = call(hold_kernel, [picked.shape])(picked)
         column = jnp.concatenate([picked, *beside], axis=0)
         even, following = swap("gy", column, column)
-        keep, following, even = call(
+        (part,) = call(
+            own_gather_kernel,
+            [(3, tall, wells * span)],
+            [((3, own_rows, LANES), F32)],
+            flops=10**9,
+        )(index, column, low)
+        y, following, even = call(
             solve_kernel,
-            [(3 * tile, LANES)] * 3,
+            [(tall, span_all)] + [(3 * tile, LANES)] * 2,
             [
-                ((3, rows, LANES), F32),
+                ((3, beside_rows, LANES), F32),
                 ((3, tall, wells * span), F32),
                 ((tall, span_all), F32),
                 ((3, tall, wells), F32),
                 ((3, tall, wells), F32),
-                ((tall, span_all), F32),
             ],
-            flops=4 * 10**9,
-        )(index, column, even, following, apart, h, e, low, high)
+            flops=3 * 10**9,
+        )(index, even, following, part, apart, h, e, low, high)
         even, following = swap("gy", even, following)
+        (keep,) = call(
+            own_scatter_kernel,
+            [(3 * tile, LANES)],
+            [((3, own_rows, LANES), F32)],
+            flops=10**9,
+        )(y, low, high)
         keep, following, even = call(add_kernel, [(tile, LANES)] * 3)(
             keep, following, even
         )

time: 88.6 us -> 86.6 us (0.977)
  waiting for transfers between devices: 27.4 us -> 25.4 us
    ppermute x24, waiting for transfers between devices: 22.4 us -> 20.4 us  [swap(): out.append(lax.ppermute(value, ('gx', 'gy'), pairs))]
    pallas_call x17 -> x21, Pallas kernels: 20.7 us -> 21.2 us  [run(): pl.pallas_call(kernel, out_shape=shapes, in_specs=[pl.BlockSpec(memory_sp...]
  transfers between devices with their start and end apart: 31 -> 31, of which waited for: 15 -> 15; matrix products, arithmetic and copies ran while one was open for 1% -> 1% of each run, Pallas kernels for 4% -> 8%
where the time goes in v8:
time: 86.6 us; the launch traced here: 86.4 us
  starting transfers between devices  37.5 us (43%)
  waiting for transfers between devices  25.4 us (29%)
  Pallas kernels  21.2 us (24%)
  local copies, waits for them, and re-layouts  1.28 us (1%)
  between operations  0.95 us (1%)
    ppermute x24, starting transfers between devices, swap(): out.append(lax.ppermute(value, ('gx', 'gy'), pairs))  29.4 us
    pallas_call x21, Pallas kernels, run(): pl.pallas_call(kernel, out_shape=shapes, in_specs=[pl.BlockSpec(memory_sp...  21.2 us
    ppermute x24, waiting for transfers between devices, swap(): out.append(lax.ppermute(value, ('gx', 'gy'), pairs))  20.4 us
    ppermute x7, starting transfers between devices, merge_all(): lax.ppermute(value, axes, [(i, i ^ k * step) for i in range(count)])  8.07 us
    ppermute x7, waiting for transfers between devices, merge_all(): lax.ppermute(value, axes, [(i, i ^ k * step) for i in range(count)])  4.99 us
  transfers between devices with their start and end apart: 31, of which 15 were waited for; matrix products, arithmetic and copies ran while one was open for 1% of the time, Pallas kernels for 8%

profile of v8, /device:TPU:0, one launch (start us, length us, event | category | flops | bytes accessed | tf_op | source)
XLA Modules:
  0.0 86.4 jit_solution(13537854214400034405)
XLA Ops:
  0.7 3.0 %shard_map.105.value_ref = f32[80,128]{1,0:T(8,128)} custom-call(s32[1,3200]{1,0:T(1,128)} %cells_ref.3, f32[3,4,16,256]{3,2,1,0:T(8,128)} %v_ref.7, f32[9,4,16,256]{3,2,1,0:T(8,128)} %d_ref.5), custom_call_target="tpu_custom_call" | custom-call | flops 1000000000 | bytes 840192 | tf_op jit(solution)/shard_map/pallas_call | solution.py:56
  4.2 4.0 %collective-permute-start = (f32[80,128]{1,0:T(8,128)}, f32[80,128]{1,0:T(8,128)S(1)}, u32[]{:S(2)}, u32[]{:S(2)}) collective-permute-start(f32[80,128]{1,0:T(8,128)} %shard_map.105.value_ref), channel_id=1, source_target_pairs={{0,4},{4,0},{8,12},{12,8},{16,20},{20,16},{24,28},{28,24},{1,5},{5... | collective-permute-start | bytes 122888 | tf_op jit(solution)/shard_map/ppermute | solution.py:536
  10.4 2.1 %collective-permute-start.3 = (f32[240,128]{1,0:T(8,128)S(1)}, f32[240,128]{1,0:T(8,128)S(1)}, u32[]{:S(2)}, u32[]{:S(2)}) collective-permute-start(f32[240,128]{1,0:T(8,128)S(1)} %pad_maximum_fusion.own_ref), channel_id=1, source_target_pairs={{0,4},{1,2},{2,1},{3,7},{4,0},{5,6},{6,5},{7,3},{8,12},{9,10},{10,... | collective-permute-start | bytes 368648 | tf_op jit(solution)/shard_map/ppermute | solution.py:536
  13.1 2.6 %shard_map.104 = (f32[3,32,384]{2,1,0:T(8,128)S(1)}, f32[9,32,8]{2,1,0:T(8,128)S(1)}, f32[3,25,16,384]{3,2,1,0:T(8,128)S(1)}, bf16[256,3200]{1,0:T(8,128)(2,1)S(...) custom-call(s32[1,3200]{1,0:T(1,128)S(1)} %reshape.12.idx_ref, ...), custom_call_target="tpu_custom_call" | custom-call | bytes 8383488 | tf_op jit(solution)/shard_map/pallas_call | solution.py:56
  16.4 3.7 %shard_map.108 = (f32[32,384]{1,0:T(8,128)S(1)}, f32[240,128]{1,0:T(8,128)S(1)}, f32[240,128]{1,0:T(8,128)S(1)}) custom-call(s32[1,3200]{1,0:T(1,128)S(1)} %reshape.12.idx_ref, f32[240,128]{1,0:T(8,128)S(1)} %collective-permute-done.2.even_ref, f32[240,128]{1,0:T(8,128)S(1)} %collective-permute-done.3.next_ref, f32[3,32,128]{2,1,0:T(8,128)S(1)} %shard_map.107.part_ref, ...), custom_call_target="tpu_custom_call" | custom-call | flops 3000000000 | bytes 5060096 | tf_op jit(solution)/shard_map/pallas_call | solution.py:56
  20.1 1.7 %collective-permute-start.4 = (f32[240,128]{1,0:T(8,128)S(1)}, f32[240,128]{1,0:T(8,128)S(1)}, u32[]{:S(2)}, u32[]{:S(2)}) collective-permute-start(f32[240,128]{1,0:T(8,128)S(1)} %get-tuple-element.44), channel_id=1, source_target_pairs={{0,4},{1,2},{2,1},{3,7},{4,0},{5,6},{6,5},{7,3},{8,12},{9,10},{10,... | collective-permute-start | bytes 368648 | tf_op jit(solution)/shard_map/ppermute | solution.py:536
  22.6 2.5 %collective-permute-done.4.y_ref = f32[240,128]{1,0:T(8,128)S(1)} collective-permute-done((f32[240,128]{1,0:T(8,128)S(1)}, f32[240,128]{1,0:T(8,128)S(1)}, u32[]{:S(2)}, u32[]{:S(2)}) %collective-permute-start.4) | collective-permute-done | bytes 122912 | tf_op jit(solution)/shard_map/ppermute | solution.py:536
  25.3 2.9 %collective-permute-start.7 = (f32[80,128]{1,0:T(8,128)S(1)}, f32[80,128]{1,0:T(8,128)S(1)}, u32[]{:S(2)}, u32[]{:S(2)}) collective-permute-start(f32[80,128]{1,0:T(8,128)S(1)} %get-tuple-element.48), channel_id=1, source_target_pairs={{0,4},{4,0},{8,12},{12,8},{16,20},{20,16},{24,28},{28,24},{1,5},{5... | collective-permute-start | bytes 122888 | tf_op jit(solution)/shard_map/ppermute | solution.py:536
  28.2 2.0 %collective-permute-done.7.z_ref = f32[80,128]{1,0:T(8,128)S(1)} collective-permute-done((f32[80,128]{1,0:T(8,128)S(1)}, f32[80,128]{1,0:T(8,128)S(1)}, u32[]{:S(2)}, u32[]{:S(2)}) %collective-permute-start.7) | collective-permute-done | bytes 40992 | tf_op jit(solution)/shard_map/ppermute | solution.py:536
  31.2 3.5 %collective-permute-start.9 = (f32[3,16,256]{2,1,0:T(8,128)S(1)}, f32[3,16,256]{2,1,0:T(8,128)S(1)}, u32[]{:S(2)}, u32[]{:S(2)}) collective-permute-start(f32[3,16,256]{2,1,0:T(8,128)S(1)} %get-tuple-element.51), channel_id=1, source_target_pairs={{0,4},{4,0},{8,12},{12,8},{16,20},{20,16},{24,28},{28,24},{1,5},{5... | collective-permute-start | bytes 147464 | tf_op jit(solution)/shard_map/ppermute | solution.py:536
  35.1 3.3 %collective-permute-done.10.f2_ref = f32[3,4,256]{2,1,0:T(4,128)S(1)} collective-permute-done((f32[3,4,256]{2,1,0:T(4,128)S(1)}, f32[3,4,256]{2,1,0:T(4,128)S(1)}, u32[]{:S(2)}, u32[]{:S(2)}) %collective-permute-start.10) | collective-permute-done | bytes 12320 | tf_op jit(solution)/shard_map/ppermute | solution.py:536
  39.6 3.0 %collective-permute-start.12 = (f32[80,128]{1,0:T(8,128)S(1)}, f32[80,128]{1,0:T(8,128)S(1)}, u32[]{:S(2)}, u32[]{:S(2)}) collective-permute-start(f32[80,128]{1,0:T(8,128)S(1)} %get-tuple-element.55), channel_id=1, source_target_pairs={{0,4},{4,0},{8,12},{12,8},{16,20},{20,16},{24,28},{28,24},{1,5},{5... | collective-permute-start | bytes 122888 | tf_op jit(solution)/shard_map/ppermute | solution.py:536
  42.6 2.0 %collective-permute-done.12 = f32[80,128]{1,0:T(8,128)S(1)} collective-permute-done((f32[80,128]{1,0:T(8,128)S(1)}, f32[80,128]{1,0:T(8,128)S(1)}, u32[]{:S(2)}, u32[]{:S(2)}) %collective-permute-start.12) | collective-permute-done | bytes 40992 | tf_op jit(solution)/shard_map/ppermute | solution.py:536
  44.6 2.1 %collective-permute-start.15 = (f32[240,128]{1,0:T(8,128)S(1)}, f32[240,128]{1,0:T(8,128)S(1)}, u32[]{:S(2)}, u32[]{:S(2)}) collective-permute-start(f32[240,128]{1,0:T(8,128)S(1)} %constant_dynamic-update-slice_fusion.own_ref), channel_id=1, source_target_pairs={{0,4},{1,2},{2,1},{3,7},{4,0},{5,6},{6,5},{7,3},{8,12},{9,10},{10,... | collective-permute-start | bytes 368648 | tf_op jit(solution)/shard_map/ppermute | solution.py:536
  47.7 1.9 %collective-permute-done.15.next_ref = f32[240,128]{1,0:T(8,128)S(1)} collective-permute-done((f32[240,128]{1,0:T(8,128)S(1)}, f32[240,128]{1,0:T(8,128)S(1)}, u32[]{:S(2)}, u32[]{:S(2)}) %collective-permute-start.15) | collective-permute-done | bytes 122912 | tf_op jit(solution)/shard_map/ppermute | solution.py:536
  49.6 3.7 %shard_map.115 = (f32[32,384]{1,0:T(8,128)S(1)}, f32[240,128]{1,0:T(8,128)S(1)}, f32[240,128]{1,0:T(8,128)S(1)}) custom-call(s32[1,3200]{1,0:T(1,128)S(1)} %reshape.12.idx_ref, f32[240,128]{1,0:T(8,128)S(1)} %collective-permute-done.14.even_ref, f32[240,128]{1,0:T(8,128)S(1)} %collective-permute-done.15.next_ref, f32[3,32,128]{2,1,0:T(8,128)S(1)} %shard_map.114.part_ref, ...), custom_call_target="tpu_custom_call" | custom-call | flops 3000000000 | bytes 5060096 | tf_op jit(solution)/shard_map/pallas_call | solution.py:56
  53.2 2.1 %collective-permute-start.16 = (f32[240,128]{1,0:T(8,128)S(1)}, f32[240,128]{1,0:T(8,128)S(1)}, u32[]{:S(2)}, u32[]{:S(2)}) collective-permute-start(f32[240,128]{1,0:T(8,128)S(1)} %get-tuple-element.57), channel_id=1, source_target_pairs={{0,4},{1,2},{2,1},{3,7},{4,0},{5,6},{6,5},{7,3},{8,12},{9,10},{10,... | collective-permute-start | bytes 368648 | tf_op jit(solution)/shard_map/ppermute | solution.py:536
  56.1 2.1 %collective-permute-done.16.y_ref = f32[240,128]{1,0:T(8,128)S(1)} collective-permute-done((f32[240,128]{1,0:T(8,128)S(1)}, f32[240,128]{1,0:T(8,128)S(1)}, u32[]{:S(2)}, u32[]{:S(2)}) %collective-permute-start.16) | collective-permute-done | bytes 122912 | tf_op jit(solution)/shard_map/ppermute | solution.py:536
  58.3 3.3 %collective-permute-start.19 = (f32[80,128]{1,0:T(8,128)S(1)}, f32[80,128]{1,0:T(8,128)S(1)}, u32[]{:S(2)}, u32[]{:S(2)}) collective-permute-start(f32[80,128]{1,0:T(8,128)S(1)} %get-tuple-element.61), channel_id=1, source_target_pairs={{0,4},{4,0},{8,12},{12,8},{16,20},{20,16},{24,28},{28,24},{1,5},{5... | collective-permute-start | bytes 122888 | tf_op jit(solution)/shard_map/ppermute | solution.py:536
  61.6 2.0 %collective-permute-done.19.z_ref = f32[80,128]{1,0:T(8,128)S(1)} collective-permute-done((f32[80,128]{1,0:T(8,128)S(1)}, f32[80,128]{1,0:T(8,128)S(1)}, u32[]{:S(2)}, u32[]{:S(2)}) %collective-permute-start.19) | collective-permute-done | bytes 40992 | tf_op jit(solution)/shard_map/ppermute | solution.py:536
  64.7 3.6 %collective-permute-start.21 = (f32[3,16,256]{2,1,0:T(8,128)S(1)}, f32[3,16,256]{2,1,0:T(8,128)S(1)}, u32[]{:S(2)}, u32[]{:S(2)}) collective-permute-start(f32[3,16,256]{2,1,0:T(8,128)S(1)} %get-tuple-element.64), channel_id=1, source_target_pairs={{0,4},{4,0},{8,12},{12,8},{16,20},{20,16},{24,28},{28,24},{1,5},{5... | collective-permute-start | bytes 147464 | tf_op jit(solution)/shard_map/ppermute | solution.py:536
  68.7 3.3 %collective-permute-done.22.f2_ref = f32[3,4,256]{2,1,0:T(4,128)S(1)} collective-permute-done((f32[3,4,256]{2,1,0:T(4,128)S(1)}, f32[3,4,256]{2,1,0:T(4,128)S(1)}, u32[]{:S(2)}, u32[]{:S(2)}) %collective-permute-start.22) | collective-permute-done | bytes 12320 | tf_op jit(solution)/shard_map/ppermute | solution.py:536
  74.3 2.9 %collective-permute-start.25 = (f32[8,128]{1,0:T(8,128)S(1)}, f32[8,128]{1,0:T(8,128)S(1)}, u32[]{:S(2)}, u32[]{:S(2)}) collective-permute-start(f32[8,128]{1,0:T(8,128)S(1)} %shard_map.121.refs_0_), channel_id=1, source_target_pairs={{0,2},{1,3},{2,0},{3,1},{4,6},{5,7},{6,4},{7,5},{8,10},{9,11},{10,... | collective-permute-start | bytes 12296 | tf_op jit(solution)/shard_map/ppermute | solution.py:571
  78.8 1.7 %collective-permute-start.30 = (f32[8,128]{1,0:T(8,128)S(1)}, f32[8,128]{1,0:T(8,128)S(1)}, u32[]{:S(2)}, u32[]{:S(2)}) collective-permute-start(f32[8,128]{1,0:T(8,128)S(1)} %shard_map.122.refs_0_), channel_id=1, source_target_pairs={{0,24},{1,25},{2,26},{3,27},{4,28},{5,29},{6,30},{7,31},{8,16},{9,... | collective-permute-start | bytes 12296 | tf_op jit(solution)/shard_map/ppermute | solution.py:571
  (89 shorter events, 20.8 us)
Async XLA Ops:
  3.7 5.4 %collective-permute-start.1 = (f32[80,128]{1,0:T(8,128)}, f32[80,128]{1,0:T(8,128)S(1)}, u32[]{:S(2)}, u32[]{:S(2)}) collective-permute-start(f32[80,128]{1,0:T(8,128)} %shard_map.105.value_ref), channel_id=1, source_target_pairs={{0,1},{4,8},{8,4},{12,16},{16,12},{20,24},{24,20},{28,29},{1,0},{5... | collective-permute-start | bytes 122888 | tf_op jit(solution)/shard_map/ppermute | solution.py:536
  4.2 6.3 %collective-permute-start = (f32[80,128]{1,0:T(8,128)}, f32[80,128]{1,0:T(8,128)S(1)}, u32[]{:S(2)}, u32[]{:S(2)}) collective-permute-start(f32[80,128]{1,0:T(8,128)} %shard_map.105.value_ref), channel_id=1, source_target_pairs={{0,4},{4,0},{8,12},{12,8},{16,20},{20,16},{24,28},{28,24},{1,5},{5... | collective-permute-start | bytes 122888 | tf_op jit(solution)/shard_map/ppermute | solution.py:536
  10.4 6.0 %collective-permute-start.3 = (f32[240,128]{1,0:T(8,128)S(1)}, f32[240,128]{1,0:T(8,128)S(1)}, u32[]{:S(2)}, u32[]{:S(2)}) collective-permute-start(f32[240,128]{1,0:T(8,128)S(1)} %pad_maximum_fusion.own_ref), channel_id=1, source_target_pairs={{0,4},{1,2},{2,1},{3,7},{4,0},{5,6},{6,5},{7,3},{8,12},{9,10},{10,... | collective-permute-start | bytes 368648 | tf_op jit(solution)/shard_map/ppermute | solution.py:536
  12.5 3.9 %collective-permute-start.2 = (f32[240,128]{1,0:T(8,128)S(1)}, f32[240,128]{1,0:T(8,128)S(1)}, u32[]{:S(2)}, u32[]{:S(2)}) collective-permute-start(f32[240,128]{1,0:T(8,128)S(1)} %pad_maximum_fusion.own_ref), channel_id=1, source_target_pairs={{0,1},{1,0},{2,3},{3,2},{4,5},{5,4},{6,7},{7,6},{8,9},{9,8},{10,11... | collective-permute-start | bytes 368648 | tf_op jit(solution)/shard_map/ppermute | solution.py:536
  20.1 4.9 %collective-permute-start.4 = (f32[240,128]{1,0:T(8,128)S(1)}, f32[240,128]{1,0:T(8,128)S(1)}, u32[]{:S(2)}, u32[]{:S(2)}) collective-permute-start(f32[240,128]{1,0:T(8,128)S(1)} %get-tuple-element.44), channel_id=1, source_target_pairs={{0,4},{1,2},{2,1},{3,7},{4,0},{5,6},{6,5},{7,3},{8,12},{9,10},{10,... | collective-permute-start | bytes 368648 | tf_op jit(solution)/shard_map/ppermute | solution.py:536
  25.3 4.9 %collective-permute-start.7 = (f32[80,128]{1,0:T(8,128)S(1)}, f32[80,128]{1,0:T(8,128)S(1)}, u32[]{:S(2)}, u32[]{:S(2)}) collective-permute-start(f32[80,128]{1,0:T(8,128)S(1)} %get-tuple-element.48), channel_id=1, source_target_pairs={{0,4},{4,0},{8,12},{12,8},{16,20},{20,16},{24,28},{28,24},{1,5},{5... | collective-permute-start | bytes 122888 | tf_op jit(solution)/shard_map/ppermute | solution.py:536
  31.1 7.3 %collective-permute-start.8 = (f32[3,16,256]{2,1,0:T(8,128)S(1)}, f32[3,16,256]{2,1,0:T(8,128)S(1)}, u32[]{:S(2)}, u32[]{:S(2)}) collective-permute-start(f32[3,16,256]{2,1,0:T(8,128)S(1)} %get-tuple-element.50), channel_id=1, source_target_pairs={{0,1},{4,8},{8,4},{12,16},{16,12},{20,24},{24,20},{28,29},{1,0},{5... | collective-permute-start | bytes 147464 | tf_op jit(solution)/shard_map/ppermute | solution.py:536
  31.2 7.2 %collective-permute-start.9 = (f32[3,16,256]{2,1,0:T(8,128)S(1)}, f32[3,16,256]{2,1,0:T(8,128)S(1)}, u32[]{:S(2)}, u32[]{:S(2)}) collective-permute-start(f32[3,16,256]{2,1,0:T(8,128)S(1)} %get-tuple-element.51), channel_id=1, source_target_pairs={{0,4},{4,0},{8,12},{12,8},{16,20},{20,16},{24,28},{28,24},{1,5},{5... | collective-permute-start | bytes 147464 | tf_op jit(solution)/shard_map/ppermute | solution.py:536
  34.7 3.7 %collective-permute-start.10 = (f32[3,4,256]{2,1,0:T(4,128)S(1)}, f32[3,4,256]{2,1,0:T(4,128)S(1)}, u32[]{:S(2)}, u32[]{:S(2)}) collective-permute-start(f32[3,4,256]{2,1,0:T(4,128)S(1)} %get-tuple-element.52), channel_id=1, source_target_pairs={{0,4},{1,2},{2,1},{3,7},{4,0},{5,6},{6,5},{7,3},{8,12},{9,10},{10,... | collective-permute-start | bytes 36872 | tf_op jit(solution)/shard_map/ppermute | solution.py:536
  34.7 3.7 %collective-permute-start.11 = (f32[3,4,256]{2,1,0:T(4,128)S(1)}, f32[3,4,256]{2,1,0:T(4,128)S(1)}, u32[]{:S(2)}, u32[]{:S(2)}) collective-permute-start(f32[3,4,256]{2,1,0:T(4,128)S(1)} %get-tuple-element.53), channel_id=1, source_target_pairs={{0,1},{1,0},{2,3},{3,2},{4,5},{5,4},{6,7},{7,6},{8,9},{9,8},{10,11... | collective-permute-start | bytes 36872 | tf_op jit(solution)/shard_map/ppermute | solution.py:536
  39.5 5.1 %collective-permute-start.13 = (f32[80,128]{1,0:T(8,128)S(1)}, f32[80,128]{1,0:T(8,128)S(1)}, u32[]{:S(2)}, u32[]{:S(2)}) collective-permute-start(f32[80,128]{1,0:T(8,128)S(1)} %get-tuple-element.55), channel_id=1, source_target_pairs={{0,1},{4,8},{8,4},{12,16},{16,12},{20,24},{24,20},{28,29},{1,0},{5... | collective-permute-start | bytes 122888 | tf_op jit(solution)/shard_map/ppermute | solution.py:536
  39.6 5.0 %collective-permute-start.12 = (f32[80,128]{1,0:T(8,128)S(1)}, f32[80,128]{1,0:T(8,128)S(1)}, u32[]{:S(2)}, u32[]{:S(2)}) collective-permute-start(f32[80,128]{1,0:T(8,128)S(1)} %get-tuple-element.55), channel_id=1, source_target_pairs={{0,4},{4,0},{8,12},{12,8},{16,20},{20,16},{24,28},{28,24},{1,5},{5... | collective-permute-start | bytes 122888 | tf_op jit(solution)/shard_map/ppermute | solution.py:536
  44.6 4.9 %collective-permute-start.15 = (f32[240,128]{1,0:T(8,128)S(1)}, f32[240,128]{1,0:T(8,128)S(1)}, u32[]{:S(2)}, u32[]{:S(2)}) collective-permute-start(f32[240,128]{1,0:T(8,128)S(1)} %constant_dynamic-update-slice_fusion.own_ref), channel_id=1, source_target_pairs={{0,4},{1,2},{2,1},{3,7},{4,0},{5,6},{6,5},{7,3},{8,12},{9,10},{10,... | collective-permute-start | bytes 368648 | tf_op jit(solution)/shard_map/ppermute | solution.py:536
  53.2 4.9 %collective-permute-start.16 = (f32[240,128]{1,0:T(8,128)S(1)}, f32[240,128]{1,0:T(8,128)S(1)}, u32[]{:S(2)}, u32[]{:S(2)}) collective-permute-start(f32[240,128]{1,0:T(8,128)S(1)} %get-tuple-element.57), channel_id=1, source_target_pairs={{0,4},{1,2},{2,1},{3,7},{4,0},{5,6},{6,5},{7,3},{8,12},{9,10},{10,... | collective-permute-start | bytes 368648 | tf_op jit(solution)/shard_map/ppermute | solution.py:536
  58.3 5.3 %collective-permute-start.19 = (f32[80,128]{1,0:T(8,128)S(1)}, f32[80,128]{1,0:T(8,128)S(1)}, u32[]{:S(2)}, u32[]{:S(2)}) collective-permute-start(f32[80,128]{1,0:T(8,128)S(1)} %get-tuple-element.61), channel_id=1, source_target_pairs={{0,4},{4,0},{8,12},{12,8},{16,20},{20,16},{24,28},{28,24},{1,5},{5... | collective-permute-start | bytes 122888 | tf_op jit(solution)/shard_map/ppermute | solution.py:536
  64.6 7.4 %collective-permute-start.20 = (f32[3,16,256]{2,1,0:T(8,128)S(1)}, f32[3,16,256]{2,1,0:T(8,128)S(1)}, u32[]{:S(2)}, u32[]{:S(2)}) collective-permute-start(f32[3,16,256]{2,1,0:T(8,128)S(1)} %get-tuple-element.63), channel_id=1, source_target_pairs={{0,1},{4,8},{8,4},{12,16},{16,12},{20,24},{24,20},{28,29},{1,0},{5... | collective-permute-start | bytes 147464 | tf_op jit(solution)/shard_map/ppermute | solution.py:536
  64.7 7.3 %collective-permute-start.21 = (f32[3,16,256]{2,1,0:T(8,128)S(1)}, f32[3,16,256]{2,1,0:T(8,128)S(1)}, u32[]{:S(2)}, u32[]{:S(2)}) collective-permute-start(f32[3,16,256]{2,1,0:T(8,128)S(1)} %get-tuple-element.64), channel_id=1, source_target_pairs={{0,4},{4,0},{8,12},{12,8},{16,20},{20,16},{24,28},{28,24},{1,5},{5... | collective-permute-start | bytes 147464 | tf_op jit(solution)/shard_map/ppermute | solution.py:536
  68.3 3.7 %collective-permute-start.22 = (f32[3,4,256]{2,1,0:T(4,128)S(1)}, f32[3,4,256]{2,1,0:T(4,128)S(1)}, u32[]{:S(2)}, u32[]{:S(2)}) collective-permute-start(f32[3,4,256]{2,1,0:T(4,128)S(1)} %get-tuple-element.65), channel_id=1, source_target_pairs={{0,4},{1,2},{2,1},{3,7},{4,0},{5,6},{6,5},{7,3},{8,12},{9,10},{10,... | collective-permute-start | bytes 36872 | tf_op jit(solution)/shard_map/ppermute | solution.py:536
  68.3 3.7 %collective-permute-start.23 = (f32[3,4,256]{2,1,0:T(4,128)S(1)}, f32[3,4,256]{2,1,0:T(4,128)S(1)}, u32[]{:S(2)}, u32[]{:S(2)}) collective-permute-start(f32[3,4,256]{2,1,0:T(4,128)S(1)} %get-tuple-element.66), channel_id=1, source_target_pairs={{0,1},{1,0},{2,3},{3,2},{4,5},{5,4},{6,7},{7,6},{8,9},{9,8},{10,11... | collective-permute-start | bytes 36872 | tf_op jit(solution)/shard_map/ppermute | solution.py:536
  73.6 4.6 %collective-permute-start.27 = (f32[8,128]{1,0:T(8,128)S(1)}, f32[8,128]{1,0:T(8,128)S(1)}, u32[]{:S(2)}, u32[]{:S(2)}) collective-permute-start(f32[8,128]{1,0:T(8,128)S(1)} %shard_map.121.refs_0_), channel_id=1, source_target_pairs={{0,6},{1,7},{2,4},{3,5},{4,2},{5,3},{6,0},{7,1},{8,14},{9,15},{10,... | collective-permute-start | bytes 12296 | tf_op jit(solution)/shard_map/ppermute | solution.py:571
  73.7 4.5 %collective-permute-start.26 = (f32[8,128]{1,0:T(8,128)S(1)}, f32[8,128]{1,0:T(8,128)S(1)}, u32[]{:S(2)}, u32[]{:S(2)}) collective-permute-start(f32[8,128]{1,0:T(8,128)S(1)} %shard_map.121.refs_0_), channel_id=1, source_target_pairs={{0,4},{1,5},{2,6},{3,7},{4,0},{5,1},{6,2},{7,3},{8,12},{9,13},{10,... | collective-permute-start | bytes 12296 | tf_op jit(solution)/shard_map/ppermute | solution.py:571
  74.3 4.5 %collective-permute-start.25 = (f32[8,128]{1,0:T(8,128)S(1)}, f32[8,128]{1,0:T(8,128)S(1)}, u32[]{:S(2)}, u32[]{:S(2)}) collective-permute-start(f32[8,128]{1,0:T(8,128)S(1)} %shard_map.121.refs_0_), channel_id=1, source_target_pairs={{0,2},{1,3},{2,0},{3,1},{4,6},{5,7},{6,4},{7,5},{8,10},{9,11},{10,... | collective-permute-start | bytes 12296 | tf_op jit(solution)/shard_map/ppermute | solution.py:571
  78.8 5.5 %collective-permute-start.30 = (f32[8,128]{1,0:T(8,128)S(1)}, f32[8,128]{1,0:T(8,128)S(1)}, u32[]{:S(2)}, u32[]{:S(2)}) collective-permute-start(f32[8,128]{1,0:T(8,128)S(1)} %shard_map.122.refs_0_), channel_id=1, source_target_pairs={{0,24},{1,25},{2,26},{3,27},{4,28},{5,29},{6,30},{7,31},{8,16},{9,... | collective-permute-start | bytes 12296 | tf_op jit(solution)/shard_map/ppermute | solution.py:571
  80.5 4.5 %collective-permute-start.29 = (f32[8,128]{1,0:T(8,128)S(1)}, f32[8,128]{1,0:T(8,128)S(1)}, u32[]{:S(2)}, u32[]{:S(2)}) collective-permute-start(f32[8,128]{1,0:T(8,128)S(1)} %shard_map.122.refs_0_), channel_id=1, source_target_pairs={{0,16},{1,17},{2,18},{3,19},{4,20},{5,21},{6,22},{7,23},{8,24},{9,... | collective-permute-start | bytes 12296 | tf_op jit(solution)/shard_map/ppermute | solution.py:571
  (17 other events, 116.3 us)

commit v9 on v8

--- a/solution.py
+++ b/solution.py
@@ -155,10 +155,6 @@
     pick(times_diag(d_ref, [v_ref[b] for b in range(3)]), cells_ref, deep_ref, out_ref)
 
 
-def hold_kernel(value_ref, out_ref):
-    out_ref[...] = value_ref[...]
-
-
 def spread_matrix(wells, width):
     shape = (wells, wells * width)
     gap = iota(shape, 1) - width * iota(shape, 0)
@@ -170,11 +166,7 @@
     return ones_where(iota(shape, 0) == width * iota(shape, 1) + (width - 3 + comp))
 
 
-def prep_kernel(
-    idx_ref, cells_ref, g_ref, couple_ref,
-    h_ref, e_ref, apart_ref, low_ref, high_ref, deep_ref, row_ref,
-    part_ref,
-):
+def prep_kernel(idx_ref, cells_ref, low_ref, high_ref, deep_ref, row_ref):
     wide = low_ref.shape[0]
     depth = deep_ref.shape[0]
     one_hot(low_ref, lambda lanes: idx_ref[:, lanes] & (wide - 1))
@@ -184,6 +176,12 @@
     )
     one_hot(row_ref, lambda lanes: row_and_depth(cells_ref[:, lanes], depth)[0])
     one_hot(deep_ref, lambda lanes: row_and_depth(cells_ref[:, lanes], depth)[1])
+
+
+def chain_kernel(
+    value_ref, g_ref, couple_ref, out_ref, h_ref, e_ref, apart_ref, part_ref
+):
+    out_ref[...] = value_ref[...]
     chunks, width, span_all = g_ref.shape
     wells = couple_ref.shape[2]
     span = width // 3
@@ -494,17 +492,25 @@
         jnp.sum(one * one), jnp.sum(one * two), jnp.sum(two * two),
         jnp.sum(one * rhs), jnp.sum(two * rhs), top_one, top_two,
     ]
-    line = iota(sums_ref.shape, 0)
-    total = jnp.zeros(sums_ref.shape, F32)
+    line = iota(sums_ref.shape[1:], 0)
+    total = jnp.zeros(sums_ref.shape[1:], F32)
     for place, value in enumerate(sums):
         total = jnp.where(line == place, value, total)
-    sums_ref[...] = total
+    sums_ref[...] = jnp.broadcast_to(total[None], sums_ref.shape)
 
 
 def final_kernel(
-    sums_ref, v_ref, z1_ref, z2_ref, w1_ref, w2_ref, sol_ref, res_ref
-):
-    g11, g12, g22, r1, r2, top_one, top_two = [sums_ref[i : i + 1, :] for i in range(7)]
+    all_ref, v_ref, z1_ref, z2_ref, w1_ref, w2_ref, sol_ref, res_ref
+):
+    every = [all_ref[:, place, :] for place in range(7)]
+    top_one = jnp.max(every[5], axis=0, keepdims=True)
+    top_two = jnp.max(every[6], axis=0, keepdims=True)
+    one = every[5] / top_one
+    two = every[6] / top_two
+    scales = (one * one, one * two, two * two, one, two)
+    g11, g12, g22, r1, r2 = [
+        jnp.sum(value * scale, axis=0, keepdims=True) for value, scale in zip(every, scales)
+    ]
     det = g11 * g22 - g12 * g12
     y1 = ((g22 * r1 - g12 * r2) / det / top_one)[:, :1]
     y2 = ((g11 * r2 - g12 * r1) / det / top_two)[:, :1]
@@ -535,45 +541,6 @@
                     pairs.append((device(i, across), device(i, across)))
         out.append(lax.ppermute(value, ("gx", "gy"), pairs))
     return out[::-1]
-
-
-def merge_kernel(*refs):
-    *parts, out_ref = refs
-    parts = [part[...] for part in parts]
-    tops = [[part[place : place + 1] for part in parts] for place in (5, 6)]
-    top_one, top_two = [functools.reduce(jnp.maximum, top) for top in tops]
-    line = iota(out_ref.shape, 0)
-    total = None
-    for part in parts:
-        one, two = part[5:6] / top_one, part[6:7] / top_two
-        scale = jnp.where(
-            line == 0, one * one, jnp.where(
-                line == 1, one * two, jnp.where(
-                    line == 2, two * two, jnp.where(line == 3, one, two)
-                )
-            ),
-        )
-        part = part * scale
-        total = part if total is None else total + part
-    total = jnp.where(line == 5, top_one, jnp.where(line == 6, top_two, total))
-    out_ref[...] = total
-
-
-def merge_all(value):
-    axes = ("gx", "gy")
-    count = lax.axis_size(axes)
-    if count & (count - 1):
-        every = lax.all_gather(value, axes)
-        return call(merge_kernel, [value.shape])(*[every[i] for i in range(count)])[0]
-    step, radix = 1, 2 if count.bit_length() % 2 == 0 else 4
-    while step < count:
-        others = [
-            lax.ppermute(value, axes, [(i, i ^ (k * step)) for i in range(count)])
-            for k in range(1, radix)
-        ]
-        (value,) = call(merge_kernel, [value.shape])(value, *others)
-        step, radix = step * radix, 4
-    return value
 
 
 def body(
@@ -619,21 +586,28 @@
     index = jnp.where(live, index, -1)
     index = index.reshape(wells, chunks, span).transpose(1, 0, 2).reshape(1, wells * longest)
     couple = jnp.pad(span_couple.transpose(1, 0, 2), ((0, 0), (0, tall - chunks), (0, 0)))
-    h, e, apart, low, high, deep, row = call(
+    low, high, deep, row = call(
         prep_kernel,
-        [(3, tall, span_all), (9, tall, wells), (3, chunks, span, span_all)]
-        + [
+        [
             jax.ShapeDtypeStruct((height, slots), BF16)
             for height in (2 * LANES, (beside_rows + own_rows) // 2, nz, nx * ny)
         ],
+    )(index, send_cells)
+    held, h, e, apart = call(
+        chain_kernel,
+        [
+            picked.shape,
+            (3, tall, span_all),
+            (9, tall, wells),
+            (3, chunks, span, span_all),
+        ],
         [((chunks, width, LANES), F32)],
-    )(index, send_cells, span_inverse, couple)
+    )(picked, span_inverse, couple)
 
     def precondition(vector, picked):
         beside = swap("gx", picked, picked)
-        if vector is right_side:
-            (picked,) = call(hold_kernel, [picked.shape])(picked)
-        column = jnp.concatenate([picked, *beside], axis=0)
+        own = held if vector is right_side else picked
+        column = jnp.concatenate([own, *beside], axis=0)
         even, following = swap("gy", column, column)
         (part,) = call(
             own_gather_kernel,
@@ -678,10 +652,11 @@
         next_kernel, [field, field, (tile, LANES)], flops=10**9
     )(send_cells, deep, part, *faces, diag_blocks, off_blocks, right_side)
     z2, part, faces = precondition(turned, picked)
-    w2, sums = call(gram_kernel, [field, (8, LANES)])(
+    count = lax.axis_size(("gx", "gy"))
+    w2, sums = call(gram_kernel, [field, (count, 8, LANES)])(
         part, *faces, off_blocks, right_side, w1
     )
-    sums = merge_all(sums)
+    sums = lax.all_to_all(sums, ("gx", "gy"), 0, 0)
     return tuple(
         call(final_kernel, [field, field])(sums, right_side, z1, z2, w1, w2)
     )

time: 86.6 us -> 84.8 us (0.979)
  blocking collectives: 0 us -> 11.2 us
  starting transfers between devices: 37.5 us -> 28.4 us
  waiting for transfers between devices: 25.4 us -> 20.6 us
  local copies, waits for them, and re-layouts: 1.28 us -> 2.54 us
    all_to_all x0 -> x1, blocking collectives: none -> 11.2 us  [body(): sums = lax.all_to_all(sums, ('gx', 'gy'), 0, 0)]
    ppermute x7 -> x0, starting transfers between devices: 8.07 us -> none  [merge_all(): lax.ppermute(value, axes, [(i, i ^ k * step) for i in range(count)])]
    ppermute x7 -> x0, waiting for transfers between devices: 4.99 us -> none  [merge_all(): lax.ppermute(value, axes, [(i, i ^ k * step) for i in range(count)])]
    unnamed x23 -> x29, local copies, waits for them, and re-layouts: 0.99 us -> 2.24 us
    ppermute x24, starting transfers between devices: 29.4 us -> 28.4 us  [swap(): out.append(lax.ppermute(value, ('gx', 'gy'), pairs))]
    pallas_call x21 -> x18, Pallas kernels: 21.2 us -> 20.9 us  [run(): pl.pallas_call(kernel, out_shape=shapes, in_specs=[pl.BlockSpec(memory_sp...]
  transfers between devices with their start and end apart: 31 -> 24, of which waited for: 15 -> 9; matrix products, arithmetic and copies ran while one was open for 1% -> 1% of each run, Pallas kernels for 8% -> 7%
where the time goes in v9:
time: 84.8 us; the launch traced here: 84.6 us
  starting transfers between devices  28.4 us (33%)
  Pallas kernels  20.9 us (25%)
  waiting for transfers between devices  20.6 us (24%)
  blocking collectives  11.2 us (13%)
  local copies, waits for them, and re-layouts  2.54 us (3%)
  between operations  0.93 us (1%)
    ppermute x24, starting transfers between devices, swap(): out.append(lax.ppermute(value, ('gx', 'gy'), pairs))  28.4 us
    pallas_call x18, Pallas kernels, run(): pl.pallas_call(kernel, out_shape=shapes, in_specs=[pl.BlockSpec(memory_sp...  20.9 us
    ppermute x24, waiting for transfers between devices, swap(): out.append(lax.ppermute(value, ('gx', 'gy'), pairs))  20.6 us
    all_to_all x1, blocking collectives, body(): sums = lax.all_to_all(sums, ('gx', 'gy'), 0, 0)  11.2 us
    unnamed x29, local copies, waits for them, and re-layouts  2.24 us
  transfers between devices with their start and end apart: 24, of which 9 were waited for; matrix products, arithmetic and copies ran while one was open for 1% of the time, Pallas kernels for 7%

profile of v9, /device:TPU:0, one launch (start us, length us, event | category | flops | bytes accessed | tf_op | source)
XLA Modules:
  0.0 84.6 jit_solution(4112236873131184352)
XLA Ops:
  0.6 3.0 %shard_map.105.value_ref = f32[80,128]{1,0:T(8,128)} custom-call(s32[1,3200]{1,0:T(1,128)} %cells_ref.3, f32[3,4,16,256]{3,2,1,0:T(8,128)} %v_ref.7, f32[9,4,16,256]{3,2,1,0:T(8,128)} %d_ref.5), custom_call_target="tpu_custom_call" | custom-call | flops 1000000000 | bytes 840192 | tf_op jit(solution)/shard_map/pallas_call | solution.py:56
  4.2 4.0 %collective-permute-start = (f32[80,128]{1,0:T(8,128)}, f32[80,128]{1,0:T(8,128)S(1)}, u32[]{:S(2)}, u32[]{:S(2)}) collective-permute-start(f32[80,128]{1,0:T(8,128)} %shard_map.105.value_ref), channel_id=1, source_target_pairs={{0,4},{4,0},{8,12},{12,8},{16,20},{20,16},{24,28},{28,24},{1,5},{5... | collective-permute-start | bytes 122888 | tf_op jit(solution)/shard_map/ppermute | solution.py:542
  9.2 1.3 %shard_map.106 = (f32[80,128]{1,0:T(8,128)S(1)}, f32[3,32,384]{2,1,0:T(8,128)S(1)}, f32[9,32,8]{2,1,0:T(8,128)S(1)}, f32[3,25,16,384]{3,2,1,0:T(8,128)S(1)}) custom-call(f32[80,128]{1,0:T(8,128)S(1)} %copy-done.5, f32[25,48,384]{2,1,0:T(8,128)S(1)} %copy-done.2, f32[9,32,8]{2,1,0:T(8,128)S(1)} %pad.4.couple_ref), custom_call_target="tpu_custom_call" | custom-call | bytes 3934208 | tf_op jit(solution)/shard_map/pallas_call | solution.py:56
  10.5 1.3 %copy-done.6 = f32[3,25,16,384]{3,2,1,0:T(8,128)} copy-done((f32[3,25,16,384]{3,2,1,0:T(8,128)}, f32[3,25,16,384]{3,2,1,0:T(8,128)S(1)}, u32[]{:S(2)}) %copy-start.6) | copy-done | bytes 1843224
  15.5 1.3 %collective-permute-done.3.next_ref = f32[240,128]{1,0:T(8,128)S(1)} collective-permute-done((f32[240,128]{1,0:T(8,128)S(1)}, f32[240,128]{1,0:T(8,128)S(1)}, u32[]{:S(2)}, u32[]{:S(2)}) %collective-permute-start.3) | collective-permute-done | bytes 122912 | tf_op jit(solution)/shard_map/ppermute | solution.py:542
  16.8 3.7 %shard_map.108 = (f32[32,384]{1,0:T(8,128)S(1)}, f32[240,128]{1,0:T(8,128)S(1)}, f32[240,128]{1,0:T(8,128)S(1)}) custom-call(s32[1,3200]{1,0:T(1,128)S(1)} %reshape.12.idx_ref, f32[240,128]{1,0:T(8,128)S(1)} %collective-permute-done.2.even_ref, f32[240,128]{1,0:T(8,128)S(1)} %collective-permute-done.3.next_ref, f32[3,32,128]{2,1,0:T(8,128)S(1)} %shard_map.107.part_ref, ...), custom_call_target="tpu_custom_call" | custom-call | flops 3000000000 | bytes 5060096 | tf_op jit(solution)/shard_map/pallas_call | solution.py:56
  22.3 3.1 %collective-permute-done.4.y_ref = f32[240,128]{1,0:T(8,128)S(1)} collective-permute-done((f32[240,128]{1,0:T(8,128)S(1)}, f32[240,128]{1,0:T(8,128)S(1)}, u32[]{:S(2)}, u32[]{:S(2)}) %collective-permute-start.4) | collective-permute-done | bytes 122912 | tf_op jit(solution)/shard_map/ppermute | solution.py:542
  25.5 3.0 %collective-permute-start.7 = (f32[80,128]{1,0:T(8,128)S(1)}, f32[80,128]{1,0:T(8,128)S(1)}, u32[]{:S(2)}, u32[]{:S(2)}) collective-permute-start(f32[80,128]{1,0:T(8,128)S(1)} %get-tuple-element.50), channel_id=1, source_target_pairs={{0,4},{4,0},{8,12},{12,8},{16,20},{20,16},{24,28},{28,24},{1,5},{5... | collective-permute-start | bytes 122888 | tf_op jit(solution)/shard_map/ppermute | solution.py:542
  28.5 2.0 %collective-permute-done.7.z_ref = f32[80,128]{1,0:T(8,128)S(1)} collective-permute-done((f32[80,128]{1,0:T(8,128)S(1)}, f32[80,128]{1,0:T(8,128)S(1)}, u32[]{:S(2)}, u32[]{:S(2)}) %collective-permute-start.7) | collective-permute-done | bytes 40992 | tf_op jit(solution)/shard_map/ppermute | solution.py:542
  31.5 3.3 %collective-permute-start.9 = (f32[3,16,256]{2,1,0:T(8,128)S(1)}, f32[3,16,256]{2,1,0:T(8,128)S(1)}, u32[]{:S(2)}, u32[]{:S(2)}) collective-permute-start(f32[3,16,256]{2,1,0:T(8,128)S(1)} %get-tuple-element.53), channel_id=1, source_target_pairs={{0,4},{4,0},{8,12},{12,8},{16,20},{20,16},{24,28},{28,24},{1,5},{5... | collective-permute-start | bytes 147464 | tf_op jit(solution)/shard_map/ppermute | solution.py:542
  35.7 2.8 %collective-permute-done.10.f2_ref = f32[3,4,256]{2,1,0:T(4,128)S(1)} collective-permute-done((f32[3,4,256]{2,1,0:T(4,128)S(1)}, f32[3,4,256]{2,1,0:T(4,128)S(1)}, u32[]{:S(2)}, u32[]{:S(2)}) %collective-permute-start.10) | collective-permute-done | bytes 12320 | tf_op jit(solution)/shard_map/ppermute | solution.py:542
  38.6 1.1 %shard_map.113 = (f32[3,4,16,256]{3,2,1,0:T(8,128)S(1)}, f32[3,4,16,256]{3,2,1,0:T(8,128)S(1)}, f32[80,128]{1,0:T(8,128)S(1)}) custom-call(s32[1,3200]{1,0:T(1,128)S(1)} %copy-done.4, bf16[256,3200]{1,0:T(8,128)(2,1)S(1)} %get-tuple-element.38.deep_ref, f32[3,4,16,256]{3,2,1,0:T(8,128)S(1)} %shard_map.112.part_ref, ...), custom_call_target="tpu_custom_call" | custom-call | flops 1000000000 | bytes 6730240 | tf_op jit(solution)/shard_map/pallas_call | solution.py:56
  39.8 2.7 %collective-permute-start.12 = (f32[80,128]{1,0:T(8,128)S(1)}, f32[80,128]{1,0:T(8,128)S(1)}, u32[]{:S(2)}, u32[]{:S(2)}) collective-permute-start(f32[80,128]{1,0:T(8,128)S(1)} %get-tuple-element.57), channel_id=1, source_target_pairs={{0,4},{4,0},{8,12},{12,8},{16,20},{20,16},{24,28},{28,24},{1,5},{5... | collective-permute-start | bytes 122888 | tf_op jit(solution)/shard_map/ppermute | solution.py:542
  42.4 2.0 %collective-permute-done.12 = f32[80,128]{1,0:T(8,128)S(1)} collective-permute-done((f32[80,128]{1,0:T(8,128)S(1)}, f32[80,128]{1,0:T(8,128)S(1)}, u32[]{:S(2)}, u32[]{:S(2)}) %collective-permute-start.12) | collective-permute-done | bytes 40992 | tf_op jit(solution)/shard_map/ppermute | solution.py:542
  44.4 2.1 %collective-permute-start.15 = (f32[240,128]{1,0:T(8,128)S(1)}, f32[240,128]{1,0:T(8,128)S(1)}, u32[]{:S(2)}, u32[]{:S(2)}) collective-permute-start(f32[240,128]{1,0:T(8,128)S(1)} %constant_dynamic-update-slice_fusion.3.own_ref), channel_id=1, source_target_pairs={{0,4},{1,2},{2,1},{3,7},{4,0},{5,6},{6,5},{7,3},{8,12},{9,10},{10,... | collective-permute-start | bytes 368648 | tf_op jit(solution)/shard_map/ppermute | solution.py:542
  47.3 2.1 %collective-permute-done.15.next_ref = f32[240,128]{1,0:T(8,128)S(1)} collective-permute-done((f32[240,128]{1,0:T(8,128)S(1)}, f32[240,128]{1,0:T(8,128)S(1)}, u32[]{:S(2)}, u32[]{:S(2)}) %collective-permute-start.15) | collective-permute-done | bytes 122912 | tf_op jit(solution)/shard_map/ppermute | solution.py:542
  49.4 3.9 %shard_map.115 = (f32[32,384]{1,0:T(8,128)S(1)}, f32[240,128]{1,0:T(8,128)S(1)}, f32[240,128]{1,0:T(8,128)S(1)}) custom-call(s32[1,3200]{1,0:T(1,128)S(1)} %reshape.12.idx_ref, f32[240,128]{1,0:T(8,128)S(1)} %collective-permute-done.14.even_ref, f32[240,128]{1,0:T(8,128)S(1)} %collective-permute-done.15.next_ref, f32[3,32,128]{2,1,0:T(8,128)S(1)} %shard_map.114.part_ref, ...), custom_call_target="tpu_custom_call" | custom-call | flops 3000000000 | bytes 5060096 | tf_op jit(solution)/shard_map/pallas_call | solution.py:56
  53.3 2.1 %collective-permute-start.16 = (f32[240,128]{1,0:T(8,128)S(1)}, f32[240,128]{1,0:T(8,128)S(1)}, u32[]{:S(2)}, u32[]{:S(2)}) collective-permute-start(f32[240,128]{1,0:T(8,128)S(1)} %get-tuple-element.59), channel_id=1, source_target_pairs={{0,4},{1,2},{2,1},{3,7},{4,0},{5,6},{6,5},{7,3},{8,12},{9,10},{10,... | collective-permute-start | bytes 368648 | tf_op jit(solution)/shard_map/ppermute | solution.py:542
  56.1 2.1 %collective-permute-done.16.y_ref = f32[240,128]{1,0:T(8,128)S(1)} collective-permute-done((f32[240,128]{1,0:T(8,128)S(1)}, f32[240,128]{1,0:T(8,128)S(1)}, u32[]{:S(2)}, u32[]{:S(2)}) %collective-permute-start.16) | collective-permute-done | bytes 122912 | tf_op jit(solution)/shard_map/ppermute | solution.py:542
  58.3 3.3 %collective-permute-start.19 = (f32[80,128]{1,0:T(8,128)S(1)}, f32[80,128]{1,0:T(8,128)S(1)}, u32[]{:S(2)}, u32[]{:S(2)}) collective-permute-start(f32[80,128]{1,0:T(8,128)S(1)} %get-tuple-element.63), channel_id=1, source_target_pairs={{0,4},{4,0},{8,12},{12,8},{16,20},{20,16},{24,28},{28,24},{1,5},{5... | collective-permute-start | bytes 122888 | tf_op jit(solution)/shard_map/ppermute | solution.py:542
  61.6 2.0 %collective-permute-done.19.z_ref = f32[80,128]{1,0:T(8,128)S(1)} collective-permute-done((f32[80,128]{1,0:T(8,128)S(1)}, f32[80,128]{1,0:T(8,128)S(1)}, u32[]{:S(2)}, u32[]{:S(2)}) %collective-permute-start.19) | collective-permute-done | bytes 40992 | tf_op jit(solution)/shard_map/ppermute | solution.py:542
  64.6 3.7 %collective-permute-start.21 = (f32[3,16,256]{2,1,0:T(8,128)S(1)}, f32[3,16,256]{2,1,0:T(8,128)S(1)}, u32[]{:S(2)}, u32[]{:S(2)}) collective-permute-start(f32[3,16,256]{2,1,0:T(8,128)S(1)} %get-tuple-element.66), channel_id=1, source_target_pairs={{0,4},{4,0},{8,12},{12,8},{16,20},{20,16},{24,28},{28,24},{1,5},{5... | collective-permute-start | bytes 147464 | tf_op jit(solution)/shard_map/ppermute | solution.py:542
  68.7 3.3 %collective-permute-done.22.f2_ref = f32[3,4,256]{2,1,0:T(4,128)S(1)} collective-permute-done((f32[3,4,256]{2,1,0:T(4,128)S(1)}, f32[3,4,256]{2,1,0:T(4,128)S(1)}, u32[]{:S(2)}, u32[]{:S(2)}) %collective-permute-start.22) | collective-permute-done | bytes 12320 | tf_op jit(solution)/shard_map/ppermute | solution.py:542
  72.4 11.2 %all_to_all.5.all_ref = f32[32,8,128]{2,1,0:T(8,128)S(1)} all-to-all(f32[32,8,128]{2,1,0:T(8,128)S(1)} %get-tuple-element.70), channel_id=1, replica_groups=mesh['gx'=8,'gy'=4] {'gx','gy'}, dimensions={0} | all-to-all | bytes 262144 | tf_op jit(solution)/shard_map/all_to_all | solution.py:659
  (79 shorter events, 13.5 us)
Async XLA Ops:
  3.7 8.1 %collective-permute-start.1 = (f32[80,128]{1,0:T(8,128)}, f32[80,128]{1,0:T(8,128)S(1)}, u32[]{:S(2)}, u32[]{:S(2)}) collective-permute-start(f32[80,128]{1,0:T(8,128)} %shard_map.105.value_ref), channel_id=1, source_target_pairs={{0,1},{4,8},{8,4},{12,16},{16,12},{20,24},{24,20},{28,29},{1,0},{5... | collective-permute-start | bytes 122888 | tf_op jit(solution)/shard_map/ppermute | solution.py:542
  4.2 7.6 %collective-permute-start = (f32[80,128]{1,0:T(8,128)}, f32[80,128]{1,0:T(8,128)S(1)}, u32[]{:S(2)}, u32[]{:S(2)}) collective-permute-start(f32[80,128]{1,0:T(8,128)} %shard_map.105.value_ref), channel_id=1, source_target_pairs={{0,4},{4,0},{8,12},{12,8},{16,20},{20,16},{24,28},{28,24},{1,5},{5... | collective-permute-start | bytes 122888 | tf_op jit(solution)/shard_map/ppermute | solution.py:542
  11.8 4.9 %collective-permute-start.3 = (f32[240,128]{1,0:T(8,128)S(1)}, f32[240,128]{1,0:T(8,128)S(1)}, u32[]{:S(2)}, u32[]{:S(2)}) collective-permute-start(f32[240,128]{1,0:T(8,128)S(1)} %constant_dynamic-update-slice_fusion.own_ref), channel_id=1, source_target_pairs={{0,4},{1,2},{2,1},{3,7},{4,0},{5,6},{6,5},{7,3},{8,12},{9,10},{10,... | collective-permute-start | bytes 368648 | tf_op jit(solution)/shard_map/ppermute | solution.py:542
  12.5 4.2 %collective-permute-start.2 = (f32[240,128]{1,0:T(8,128)S(1)}, f32[240,128]{1,0:T(8,128)S(1)}, u32[]{:S(2)}, u32[]{:S(2)}) collective-permute-start(f32[240,128]{1,0:T(8,128)S(1)} %constant_dynamic-update-slice_fusion.own_ref), channel_id=1, source_target_pairs={{0,1},{1,0},{2,3},{3,2},{4,5},{5,4},{6,7},{7,6},{8,9},{9,8},{10,11... | collective-permute-start | bytes 368648 | tf_op jit(solution)/shard_map/ppermute | solution.py:542
  20.4 4.9 %collective-permute-start.4 = (f32[240,128]{1,0:T(8,128)S(1)}, f32[240,128]{1,0:T(8,128)S(1)}, u32[]{:S(2)}, u32[]{:S(2)}) collective-permute-start(f32[240,128]{1,0:T(8,128)S(1)} %get-tuple-element.46), channel_id=1, source_target_pairs={{0,4},{1,2},{2,1},{3,7},{4,0},{5,6},{6,5},{7,3},{8,12},{9,10},{10,... | collective-permute-start | bytes 368648 | tf_op jit(solution)/shard_map/ppermute | solution.py:542
  21.1 4.2 %collective-permute-start.5 = (f32[240,128]{1,0:T(8,128)S(1)}, f32[240,128]{1,0:T(8,128)S(1)}, u32[]{:S(2)}, u32[]{:S(2)}) collective-permute-start(f32[240,128]{1,0:T(8,128)S(1)} %get-tuple-element.47), channel_id=1, source_target_pairs={{0,1},{1,0},{2,3},{3,2},{4,5},{5,4},{6,7},{7,6},{8,9},{9,8},{10,11... | collective-permute-start | bytes 368648 | tf_op jit(solution)/shard_map/ppermute | solution.py:542
  25.4 3.1 %collective-permute-start.6 = (f32[80,128]{1,0:T(8,128)S(1)}, f32[80,128]{1,0:T(8,128)S(1)}, u32[]{:S(2)}, u32[]{:S(2)}) collective-permute-start(f32[80,128]{1,0:T(8,128)S(1)} %get-tuple-element.49), channel_id=1, source_target_pairs={{0,1},{4,8},{8,4},{12,16},{16,12},{20,24},{24,20},{28,29},{1,0},{5... | collective-permute-start | bytes 122888 | tf_op jit(solution)/shard_map/ppermute | solution.py:542
  25.5 5.0 %collective-permute-start.7 = (f32[80,128]{1,0:T(8,128)S(1)}, f32[80,128]{1,0:T(8,128)S(1)}, u32[]{:S(2)}, u32[]{:S(2)}) collective-permute-start(f32[80,128]{1,0:T(8,128)S(1)} %get-tuple-element.50), channel_id=1, source_target_pairs={{0,4},{4,0},{8,12},{12,8},{16,20},{20,16},{24,28},{28,24},{1,5},{5... | collective-permute-start | bytes 122888 | tf_op jit(solution)/shard_map/ppermute | solution.py:542
  31.5 7.1 %collective-permute-start.8 = (f32[3,16,256]{2,1,0:T(8,128)S(1)}, f32[3,16,256]{2,1,0:T(8,128)S(1)}, u32[]{:S(2)}, u32[]{:S(2)}) collective-permute-start(f32[3,16,256]{2,1,0:T(8,128)S(1)} %get-tuple-element.52), channel_id=1, source_target_pairs={{0,1},{4,8},{8,4},{12,16},{16,12},{20,24},{24,20},{28,29},{1,0},{5... | collective-permute-start | bytes 147464 | tf_op jit(solution)/shard_map/ppermute | solution.py:542
  31.5 7.1 %collective-permute-start.9 = (f32[3,16,256]{2,1,0:T(8,128)S(1)}, f32[3,16,256]{2,1,0:T(8,128)S(1)}, u32[]{:S(2)}, u32[]{:S(2)}) collective-permute-start(f32[3,16,256]{2,1,0:T(8,128)S(1)} %get-tuple-element.53), channel_id=1, source_target_pairs={{0,4},{4,0},{8,12},{12,8},{16,20},{20,16},{24,28},{28,24},{1,5},{5... | collective-permute-start | bytes 147464 | tf_op jit(solution)/shard_map/ppermute | solution.py:542
  34.9 3.7 %collective-permute-start.10 = (f32[3,4,256]{2,1,0:T(4,128)S(1)}, f32[3,4,256]{2,1,0:T(4,128)S(1)}, u32[]{:S(2)}, u32[]{:S(2)}) collective-permute-start(f32[3,4,256]{2,1,0:T(4,128)S(1)} %get-tuple-element.54), channel_id=1, source_target_pairs={{0,4},{1,2},{2,1},{3,7},{4,0},{5,6},{6,5},{7,3},{8,12},{9,10},{10,... | collective-permute-start | bytes 36872 | tf_op jit(solution)/shard_map/ppermute | solution.py:542
  34.9 3.7 %collective-permute-start.11 = (f32[3,4,256]{2,1,0:T(4,128)S(1)}, f32[3,4,256]{2,1,0:T(4,128)S(1)}, u32[]{:S(2)}, u32[]{:S(2)}) collective-permute-start(f32[3,4,256]{2,1,0:T(4,128)S(1)} %get-tuple-element.55), channel_id=1, source_target_pairs={{0,1},{1,0},{2,3},{3,2},{4,5},{5,4},{6,7},{7,6},{8,9},{9,8},{10,11... | collective-permute-start | bytes 36872 | tf_op jit(solution)/shard_map/ppermute | solution.py:542
  39.7 4.8 %collective-permute-start.13 = (f32[80,128]{1,0:T(8,128)S(1)}, f32[80,128]{1,0:T(8,128)S(1)}, u32[]{:S(2)}, u32[]{:S(2)}) collective-permute-start(f32[80,128]{1,0:T(8,128)S(1)} %get-tuple-element.57), channel_id=1, source_target_pairs={{0,1},{4,8},{8,4},{12,16},{16,12},{20,24},{24,20},{28,29},{1,0},{5... | collective-permute-start | bytes 122888 | tf_op jit(solution)/shard_map/ppermute | solution.py:542
  39.8 4.7 %collective-permute-start.12 = (f32[80,128]{1,0:T(8,128)S(1)}, f32[80,128]{1,0:T(8,128)S(1)}, u32[]{:S(2)}, u32[]{:S(2)}) collective-permute-start(f32[80,128]{1,0:T(8,128)S(1)} %get-tuple-element.57), channel_id=1, source_target_pairs={{0,4},{4,0},{8,12},{12,8},{16,20},{20,16},{24,28},{28,24},{1,5},{5... | collective-permute-start | bytes 122888 | tf_op jit(solution)/shard_map/ppermute | solution.py:542
  44.4 4.9 %collective-permute-start.15 = (f32[240,128]{1,0:T(8,128)S(1)}, f32[240,128]{1,0:T(8,128)S(1)}, u32[]{:S(2)}, u32[]{:S(2)}) collective-permute-start(f32[240,128]{1,0:T(8,128)S(1)} %constant_dynamic-update-slice_fusion.3.own_ref), channel_id=1, source_target_pairs={{0,4},{1,2},{2,1},{3,7},{4,0},{5,6},{6,5},{7,3},{8,12},{9,10},{10,... | collective-permute-start | bytes 368648 | tf_op jit(solution)/shard_map/ppermute | solution.py:542
  46.5 2.9 %collective-permute-start.14 = (f32[240,128]{1,0:T(8,128)S(1)}, f32[240,128]{1,0:T(8,128)S(1)}, u32[]{:S(2)}, u32[]{:S(2)}) collective-permute-start(f32[240,128]{1,0:T(8,128)S(1)} %constant_dynamic-update-slice_fusion.3.own_ref), channel_id=1, source_target_pairs={{0,1},{1,0},{2,3},{3,2},{4,5},{5,4},{6,7},{7,6},{8,9},{9,8},{10,11... | collective-permute-start | bytes 368648 | tf_op jit(solution)/shard_map/ppermute | solution.py:542
  53.3 4.9 %collective-permute-start.16 = (f32[240,128]{1,0:T(8,128)S(1)}, f32[240,128]{1,0:T(8,128)S(1)}, u32[]{:S(2)}, u32[]{:S(2)}) collective-permute-start(f32[240,128]{1,0:T(8,128)S(1)} %get-tuple-element.59), channel_id=1, source_target_pairs={{0,4},{1,2},{2,1},{3,7},{4,0},{5,6},{6,5},{7,3},{8,12},{9,10},{10,... | collective-permute-start | bytes 368648 | tf_op jit(solution)/shard_map/ppermute | solution.py:542
  55.4 2.9 %collective-permute-start.17 = (f32[240,128]{1,0:T(8,128)S(1)}, f32[240,128]{1,0:T(8,128)S(1)}, u32[]{:S(2)}, u32[]{:S(2)}) collective-permute-start(f32[240,128]{1,0:T(8,128)S(1)} %get-tuple-element.60), channel_id=1, source_target_pairs={{0,1},{1,0},{2,3},{3,2},{4,5},{5,4},{6,7},{7,6},{8,9},{9,8},{10,11... | collective-permute-start | bytes 368648 | tf_op jit(solution)/shard_map/ppermute | solution.py:542
  58.2 3.4 %collective-permute-start.18 = (f32[80,128]{1,0:T(8,128)S(1)}, f32[80,128]{1,0:T(8,128)S(1)}, u32[]{:S(2)}, u32[]{:S(2)}) collective-permute-start(f32[80,128]{1,0:T(8,128)S(1)} %get-tuple-element.62), channel_id=1, source_target_pairs={{0,1},{4,8},{8,4},{12,16},{16,12},{20,24},{24,20},{28,29},{1,0},{5... | collective-permute-start | bytes 122888 | tf_op jit(solution)/shard_map/ppermute | solution.py:542
  58.3 5.3 %collective-permute-start.19 = (f32[80,128]{1,0:T(8,128)S(1)}, f32[80,128]{1,0:T(8,128)S(1)}, u32[]{:S(2)}, u32[]{:S(2)}) collective-permute-start(f32[80,128]{1,0:T(8,128)S(1)} %get-tuple-element.63), channel_id=1, source_target_pairs={{0,4},{4,0},{8,12},{12,8},{16,20},{20,16},{24,28},{28,24},{1,5},{5... | collective-permute-start | bytes 122888 | tf_op jit(solution)/shard_map/ppermute | solution.py:542
  64.5 7.4 %collective-permute-start.20 = (f32[3,16,256]{2,1,0:T(8,128)S(1)}, f32[3,16,256]{2,1,0:T(8,128)S(1)}, u32[]{:S(2)}, u32[]{:S(2)}) collective-permute-start(f32[3,16,256]{2,1,0:T(8,128)S(1)} %get-tuple-element.65), channel_id=1, source_target_pairs={{0,1},{4,8},{8,4},{12,16},{16,12},{20,24},{24,20},{28,29},{1,0},{5... | collective-permute-start | bytes 147464 | tf_op jit(solution)/shard_map/ppermute | solution.py:542
  64.6 7.4 %collective-permute-start.21 = (f32[3,16,256]{2,1,0:T(8,128)S(1)}, f32[3,16,256]{2,1,0:T(8,128)S(1)}, u32[]{:S(2)}, u32[]{:S(2)}) collective-permute-start(f32[3,16,256]{2,1,0:T(8,128)S(1)} %get-tuple-element.66), channel_id=1, source_target_pairs={{0,4},{4,0},{8,12},{12,8},{16,20},{20,16},{24,28},{28,24},{1,5},{5... | collective-permute-start | bytes 147464 | tf_op jit(solution)/shard_map/ppermute | solution.py:542
  68.3 3.7 %collective-permute-start.22 = (f32[3,4,256]{2,1,0:T(4,128)S(1)}, f32[3,4,256]{2,1,0:T(4,128)S(1)}, u32[]{:S(2)}, u32[]{:S(2)}) collective-permute-start(f32[3,4,256]{2,1,0:T(4,128)S(1)} %get-tuple-element.67), channel_id=1, source_target_pairs={{0,4},{1,2},{2,1},{3,7},{4,0},{5,6},{6,5},{7,3},{8,12},{9,10},{10,... | collective-permute-start | bytes 36872 | tf_op jit(solution)/shard_map/ppermute | solution.py:542
  68.3 3.7 %collective-permute-start.23 = (f32[3,4,256]{2,1,0:T(4,128)S(1)}, f32[3,4,256]{2,1,0:T(4,128)S(1)}, u32[]{:S(2)}, u32[]{:S(2)}) collective-permute-start(f32[3,4,256]{2,1,0:T(4,128)S(1)} %get-tuple-element.68), channel_id=1, source_target_pairs={{0,1},{1,0},{2,3},{3,2},{4,5},{5,4},{6,7},{7,6},{8,9},{9,8},{10,11... | collective-permute-start | bytes 36872 | tf_op jit(solution)/shard_map/ppermute | solution.py:542
  (12 other events, 86.0 us)

commit v10 on v9

--- a/solution.py
+++ b/solution.py
@@ -47,7 +47,7 @@
     return jnp.where(mask, 1.0, 0.0).astype(BF16)
 
 
-def call(kernel, outs, scratch=(), flops=0, space=pltpu.VMEM, mib=40):
+def call(kernel, outs, scratch=(), flops=0, space=pltpu.VMEM, mib=20):
     def run(*args):
         shapes = [
             o if hasattr(o, "dtype") else jax.ShapeDtypeStruct(o, F32) for o in outs
@@ -492,7 +492,7 @@
         jnp.sum(one * one), jnp.sum(one * two), jnp.sum(two * two),
         jnp.sum(one * rhs), jnp.sum(two * rhs), top_one, top_two,
     ]
-    line = iota(sums_ref.shape[1:], 0)
+    line = iota(sums_ref.shape[1:], 1)
     total = jnp.zeros(sums_ref.shape[1:], F32)
     for place, value in enumerate(sums):
         total = jnp.where(line == place, value, total)
@@ -502,7 +502,7 @@
 def final_kernel(
     all_ref, v_ref, z1_ref, z2_ref, w1_ref, w2_ref, sol_ref, res_ref
 ):
-    every = [all_ref[:, place, :] for place in range(7)]
+    every = [all_ref[:, 0, place : place + 1] for place in range(7)]
     top_one = jnp.max(every[5], axis=0, keepdims=True)
     top_two = jnp.max(every[6], axis=0, keepdims=True)
     one = every[5] / top_one
@@ -512,8 +512,8 @@
         jnp.sum(value * scale, axis=0, keepdims=True) for value, scale in zip(every, scales)
     ]
     det = g11 * g22 - g12 * g12
-    y1 = ((g22 * r1 - g12 * r2) / det / top_one)[:, :1]
-    y2 = ((g11 * r2 - g12 * r1) / det / top_two)[:, :1]
+    y1 = (g22 * r1 - g12 * r2) / det / top_one
+    y2 = (g11 * r2 - g12 * r1) / det / top_two
     sol_ref[...] = y1 * z1_ref[...] + y2 * z2_ref[...]
     res_ref[...] = v_ref[...] - y1 * w1_ref[...] - y2 * w2_ref[...]
 
@@ -653,7 +653,7 @@
     )(send_cells, deep, part, *faces, diag_blocks, off_blocks, right_side)
     z2, part, faces = precondition(turned, picked)
     count = lax.axis_size(("gx", "gy"))
-    w2, sums = call(gram_kernel, [field, (count, 8, LANES)])(
+    w2, sums = call(gram_kernel, [field, (count, 1, LANES)])(
         part, *faces, off_blocks, right_side, w1
     )
     sums = lax.all_to_all(sums, ("gx", "gy"), 0, 0)

time: 84.8 us -> 83.9 us (0.989)
  blocking collectives: 11.2 us -> 10.1 us
    all_to_all x1, blocking collectives: 11.2 us -> 10.1 us  [body(): sums = lax.all_to_all(sums, ('gx', 'gy'), 0, 0)]
where the time goes in v10:
time: 83.9 us; the launch traced here: 83.7 us
  starting transfers between devices  28.4 us (34%)
  Pallas kernels  21.1 us (25%)
  waiting for transfers between devices  20.6 us (25%)
  blocking collectives  10.1 us (12%)
  local copies, waits for them, and re-layouts  2.54 us (3%)
  between operations  0.93 us (1%)
    ppermute x24, starting transfers between devices, swap(): out.append(lax.ppermute(value, ('gx', 'gy'), pairs))  28.4 us
    pallas_call x18, Pallas kernels, run(): pl.pallas_call(kernel, out_shape=shapes, in_specs=[pl.BlockSpec(memory_sp...  21.1 us
    ppermute x24, waiting for transfers between devices, swap(): out.append(lax.ppermute(value, ('gx', 'gy'), pairs))  20.6 us
    all_to_all x1, blocking collectives, body(): sums = lax.all_to_all(sums, ('gx', 'gy'), 0, 0)  10.1 us
    unnamed x29, local copies, waits for them, and re-layouts  2.24 us
  transfers between devices with their start and end apart: 24, of which 9 were waited for; matrix products, arithmetic and copies ran while one was open for 1% of the time, Pallas kernels for 7%

profile of v10, /device:TPU:0, one launch (start us, length us, event | category | flops | bytes accessed | tf_op | source)
XLA Modules:
  0.0 83.7 jit_solution(11121710041605134361)
XLA Ops:
  0.6 3.0 %shard_map.105.value_ref = f32[80,128]{1,0:T(8,128)} custom-call(s32[1,3200]{1,0:T(1,128)} %cells_ref.3, f32[3,4,16,256]{3,2,1,0:T(8,128)} %v_ref.7, f32[9,4,16,256]{3,2,1,0:T(8,128)} %d_ref.5), custom_call_target="tpu_custom_call" | custom-call | flops 1000000000 | bytes 840192 | tf_op jit(solution)/shard_map/pallas_call | solution.py:56
  4.2 4.0 %collective-permute-start = (f32[80,128]{1,0:T(8,128)}, f32[80,128]{1,0:T(8,128)S(1)}, u32[]{:S(2)}, u32[]{:S(2)}) collective-permute-start(f32[80,128]{1,0:T(8,128)} %shard_map.105.value_ref), channel_id=1, source_target_pairs={{0,4},{4,0},{8,12},{12,8},{16,20},{20,16},{24,28},{28,24},{1,5},{5... | collective-permute-start | bytes 122888 | tf_op jit(solution)/shard_map/ppermute | solution.py:542
  9.2 1.3 %shard_map.106 = (f32[80,128]{1,0:T(8,128)S(1)}, f32[3,32,384]{2,1,0:T(8,128)S(1)}, f32[9,32,8]{2,1,0:T(8,128)S(1)}, f32[3,25,16,384]{3,2,1,0:T(8,128)S(1)}) custom-call(f32[80,128]{1,0:T(8,128)S(1)} %copy-done.5, f32[25,48,384]{2,1,0:T(8,128)S(1)} %copy-done.2, f32[9,32,8]{2,1,0:T(8,128)S(1)} %pad.4.couple_ref), custom_call_target="tpu_custom_call" | custom-call | bytes 3934208 | tf_op jit(solution)/shard_map/pallas_call | solution.py:56
  10.5 1.3 %copy-done.6 = f32[3,25,16,384]{3,2,1,0:T(8,128)} copy-done((f32[3,25,16,384]{3,2,1,0:T(8,128)}, f32[3,25,16,384]{3,2,1,0:T(8,128)S(1)}, u32[]{:S(2)}) %copy-start.6) | copy-done | bytes 1843224
  15.5 1.3 %collective-permute-done.3.next_ref = f32[240,128]{1,0:T(8,128)S(1)} collective-permute-done((f32[240,128]{1,0:T(8,128)S(1)}, f32[240,128]{1,0:T(8,128)S(1)}, u32[]{:S(2)}, u32[]{:S(2)}) %collective-permute-start.3) | collective-permute-done | bytes 122912 | tf_op jit(solution)/shard_map/ppermute | solution.py:542
  16.8 3.7 %shard_map.108 = (f32[32,384]{1,0:T(8,128)S(1)}, f32[240,128]{1,0:T(8,128)S(1)}, f32[240,128]{1,0:T(8,128)S(1)}) custom-call(s32[1,3200]{1,0:T(1,128)S(1)} %reshape.12.idx_ref, f32[240,128]{1,0:T(8,128)S(1)} %collective-permute-done.2.even_ref, f32[240,128]{1,0:T(8,128)S(1)} %collective-permute-done.3.next_ref, f32[3,32,128]{2,1,0:T(8,128)S(1)} %shard_map.107.part_ref, ...), custom_call_target="tpu_custom_call" | custom-call | flops 3000000000 | bytes 5060096 | tf_op jit(solution)/shard_map/pallas_call | solution.py:56
  22.3 3.1 %collective-permute-done.4.y_ref = f32[240,128]{1,0:T(8,128)S(1)} collective-permute-done((f32[240,128]{1,0:T(8,128)S(1)}, f32[240,128]{1,0:T(8,128)S(1)}, u32[]{:S(2)}, u32[]{:S(2)}) %collective-permute-start.4) | collective-permute-done | bytes 122912 | tf_op jit(solution)/shard_map/ppermute | solution.py:542
  25.5 3.0 %collective-permute-start.7 = (f32[80,128]{1,0:T(8,128)S(1)}, f32[80,128]{1,0:T(8,128)S(1)}, u32[]{:S(2)}, u32[]{:S(2)}) collective-permute-start(f32[80,128]{1,0:T(8,128)S(1)} %get-tuple-element.50), channel_id=1, source_target_pairs={{0,4},{4,0},{8,12},{12,8},{16,20},{20,16},{24,28},{28,24},{1,5},{5... | collective-permute-start | bytes 122888 | tf_op jit(solution)/shard_map/ppermute | solution.py:542
  28.5 2.0 %collective-permute-done.7.z_ref = f32[80,128]{1,0:T(8,128)S(1)} collective-permute-done((f32[80,128]{1,0:T(8,128)S(1)}, f32[80,128]{1,0:T(8,128)S(1)}, u32[]{:S(2)}, u32[]{:S(2)}) %collective-permute-start.7) | collective-permute-done | bytes 40992 | tf_op jit(solution)/shard_map/ppermute | solution.py:542
  31.5 3.3 %collective-permute-start.9 = (f32[3,16,256]{2,1,0:T(8,128)S(1)}, f32[3,16,256]{2,1,0:T(8,128)S(1)}, u32[]{:S(2)}, u32[]{:S(2)}) collective-permute-start(f32[3,16,256]{2,1,0:T(8,128)S(1)} %get-tuple-element.53), channel_id=1, source_target_pairs={{0,4},{4,0},{8,12},{12,8},{16,20},{20,16},{24,28},{28,24},{1,5},{5... | collective-permute-start | bytes 147464 | tf_op jit(solution)/shard_map/ppermute | solution.py:542
  35.7 2.8 %collective-permute-done.10.f2_ref = f32[3,4,256]{2,1,0:T(4,128)S(1)} collective-permute-done((f32[3,4,256]{2,1,0:T(4,128)S(1)}, f32[3,4,256]{2,1,0:T(4,128)S(1)}, u32[]{:S(2)}, u32[]{:S(2)}) %collective-permute-start.10) | collective-permute-done | bytes 12320 | tf_op jit(solution)/shard_map/ppermute | solution.py:542
  39.8 2.7 %collective-permute-start.12 = (f32[80,128]{1,0:T(8,128)S(1)}, f32[80,128]{1,0:T(8,128)S(1)}, u32[]{:S(2)}, u32[]{:S(2)}) collective-permute-start(f32[80,128]{1,0:T(8,128)S(1)} %get-tuple-element.57), channel_id=1, source_target_pairs={{0,4},{4,0},{8,12},{12,8},{16,20},{20,16},{24,28},{28,24},{1,5},{5... | collective-permute-start | bytes 122888 | tf_op jit(solution)/shard_map/ppermute | solution.py:542
  42.4 2.0 %collective-permute-done.12 = f32[80,128]{1,0:T(8,128)S(1)} collective-permute-done((f32[80,128]{1,0:T(8,128)S(1)}, f32[80,128]{1,0:T(8,128)S(1)}, u32[]{:S(2)}, u32[]{:S(2)}) %collective-permute-start.12) | collective-permute-done | bytes 40992 | tf_op jit(solution)/shard_map/ppermute | solution.py:542
  44.4 2.1 %collective-permute-start.15 = (f32[240,128]{1,0:T(8,128)S(1)}, f32[240,128]{1,0:T(8,128)S(1)}, u32[]{:S(2)}, u32[]{:S(2)}) collective-permute-start(f32[240,128]{1,0:T(8,128)S(1)} %constant_dynamic-update-slice_fusion.3.own_ref), channel_id=1, source_target_pairs={{0,4},{1,2},{2,1},{3,7},{4,0},{5,6},{6,5},{7,3},{8,12},{9,10},{10,... | collective-permute-start | bytes 368648 | tf_op jit(solution)/shard_map/ppermute | solution.py:542
  47.3 2.1 %collective-permute-done.15.next_ref = f32[240,128]{1,0:T(8,128)S(1)} collective-permute-done((f32[240,128]{1,0:T(8,128)S(1)}, f32[240,128]{1,0:T(8,128)S(1)}, u32[]{:S(2)}, u32[]{:S(2)}) %collective-permute-start.15) | collective-permute-done | bytes 122912 | tf_op jit(solution)/shard_map/ppermute | solution.py:542
  49.4 3.9 %shard_map.115 = (f32[32,384]{1,0:T(8,128)S(1)}, f32[240,128]{1,0:T(8,128)S(1)}, f32[240,128]{1,0:T(8,128)S(1)}) custom-call(s32[1,3200]{1,0:T(1,128)S(1)} %reshape.12.idx_ref, f32[240,128]{1,0:T(8,128)S(1)} %collective-permute-done.14.even_ref, f32[240,128]{1,0:T(8,128)S(1)} %collective-permute-done.15.next_ref, f32[3,32,128]{2,1,0:T(8,128)S(1)} %shard_map.114.part_ref, ...), custom_call_target="tpu_custom_call" | custom-call | flops 3000000000 | bytes 5060096 | tf_op jit(solution)/shard_map/pallas_call | solution.py:56
  53.3 2.1 %collective-permute-start.16 = (f32[240,128]{1,0:T(8,128)S(1)}, f32[240,128]{1,0:T(8,128)S(1)}, u32[]{:S(2)}, u32[]{:S(2)}) collective-permute-start(f32[240,128]{1,0:T(8,128)S(1)} %get-tuple-element.59), channel_id=1, source_target_pairs={{0,4},{1,2},{2,1},{3,7},{4,0},{5,6},{6,5},{7,3},{8,12},{9,10},{10,... | collective-permute-start | bytes 368648 | tf_op jit(solution)/shard_map/ppermute | solution.py:542
  56.1 2.1 %collective-permute-done.16.y_ref = f32[240,128]{1,0:T(8,128)S(1)} collective-permute-done((f32[240,128]{1,0:T(8,128)S(1)}, f32[240,128]{1,0:T(8,128)S(1)}, u32[]{:S(2)}, u32[]{:S(2)}) %collective-permute-start.16) | collective-permute-done | bytes 122912 | tf_op jit(solution)/shard_map/ppermute | solution.py:542
  58.3 3.3 %collective-permute-start.19 = (f32[80,128]{1,0:T(8,128)S(1)}, f32[80,128]{1,0:T(8,128)S(1)}, u32[]{:S(2)}, u32[]{:S(2)}) collective-permute-start(f32[80,128]{1,0:T(8,128)S(1)} %get-tuple-element.63), channel_id=1, source_target_pairs={{0,4},{4,0},{8,12},{12,8},{16,20},{20,16},{24,28},{28,24},{1,5},{5... | collective-permute-start | bytes 122888 | tf_op jit(solution)/shard_map/ppermute | solution.py:542
  61.6 2.0 %collective-permute-done.19.z_ref = f32[80,128]{1,0:T(8,128)S(1)} collective-permute-done((f32[80,128]{1,0:T(8,128)S(1)}, f32[80,128]{1,0:T(8,128)S(1)}, u32[]{:S(2)}, u32[]{:S(2)}) %collective-permute-start.19) | collective-permute-done | bytes 40992 | tf_op jit(solution)/shard_map/ppermute | solution.py:542
  64.6 3.7 %collective-permute-start.21 = (f32[3,16,256]{2,1,0:T(8,128)S(1)}, f32[3,16,256]{2,1,0:T(8,128)S(1)}, u32[]{:S(2)}, u32[]{:S(2)}) collective-permute-start(f32[3,16,256]{2,1,0:T(8,128)S(1)} %get-tuple-element.66), channel_id=1, source_target_pairs={{0,4},{4,0},{8,12},{12,8},{16,20},{20,16},{24,28},{28,24},{1,5},{5... | collective-permute-start | bytes 147464 | tf_op jit(solution)/shard_map/ppermute | solution.py:542
  68.7 3.3 %collective-permute-done.22.f2_ref = f32[3,4,256]{2,1,0:T(4,128)S(1)} collective-permute-done((f32[3,4,256]{2,1,0:T(4,128)S(1)}, f32[3,4,256]{2,1,0:T(4,128)S(1)}, u32[]{:S(2)}, u32[]{:S(2)}) %collective-permute-start.22) | collective-permute-done | bytes 12320 | tf_op jit(solution)/shard_map/ppermute | solution.py:542
  72.4 10.1 %all_to_all.5.all_ref = f32[32,1,128]{2,1,0:T(1,128)S(1)} all-to-all(f32[32,1,128]{2,1,0:T(1,128)S(1)} %get-tuple-element.70), channel_id=1, replica_groups=mesh['gx'=8,'gy'=4] {'gx','gy'}, dimensions={0} | all-to-all | bytes 32768 | tf_op jit(solution)/shard_map/all_to_all | solution.py:659
  82.6 1.1 %shard_map.121 = (f32[3,4,16,256]{3,2,1,0:T(8,128)}, f32[3,4,16,256]{3,2,1,0:T(8,128)}) custom-call(f32[32,1,128]{2,1,0:T(1,128)S(1)} %all_to_all.5.all_ref, f32[3,4,16,256]{3,2,1,0:T(8,128)S(1)} %copy-done.3, f32[3,4,16,256]{3,2,1,0:T(8,128)S(1)} %get-tuple-element.51.z_ref.z1_ref, f32[3,4,16,256]{3,2,1,0:T(8,128)S(1)} %get-tuple-element.64.z_ref.z2_ref, ...), custom_call_target="tpu_custom_call" | custom-call | bytes 1392640 | tf_op jit(solution)/shard_map/pallas_call | solution.py:56
  (79 shorter events, 13.7 us)
Async XLA Ops:
  3.7 8.1 %collective-permute-start.1 = (f32[80,128]{1,0:T(8,128)}, f32[80,128]{1,0:T(8,128)S(1)}, u32[]{:S(2)}, u32[]{:S(2)}) collective-permute-start(f32[80,128]{1,0:T(8,128)} %shard_map.105.value_ref), channel_id=1, source_target_pairs={{0,1},{4,8},{8,4},{12,16},{16,12},{20,24},{24,20},{28,29},{1,0},{5... | collective-permute-start | bytes 122888 | tf_op jit(solution)/shard_map/ppermute | solution.py:542
  4.2 7.6 %collective-permute-start = (f32[80,128]{1,0:T(8,128)}, f32[80,128]{1,0:T(8,128)S(1)}, u32[]{:S(2)}, u32[]{:S(2)}) collective-permute-start(f32[80,128]{1,0:T(8,128)} %shard_map.105.value_ref), channel_id=1, source_target_pairs={{0,4},{4,0},{8,12},{12,8},{16,20},{20,16},{24,28},{28,24},{1,5},{5... | collective-permute-start | bytes 122888 | tf_op jit(solution)/shard_map/ppermute | solution.py:542
  11.8 4.9 %collective-permute-start.3 = (f32[240,128]{1,0:T(8,128)S(1)}, f32[240,128]{1,0:T(8,128)S(1)}, u32[]{:S(2)}, u32[]{:S(2)}) collective-permute-start(f32[240,128]{1,0:T(8,128)S(1)} %constant_dynamic-update-slice_fusion.own_ref), channel_id=1, source_target_pairs={{0,4},{1,2},{2,1},{3,7},{4,0},{5,6},{6,5},{7,3},{8,12},{9,10},{10,... | collective-permute-start | bytes 368648 | tf_op jit(solution)/shard_map/ppermute | solution.py:542
  12.5 4.2 %collective-permute-start.2 = (f32[240,128]{1,0:T(8,128)S(1)}, f32[240,128]{1,0:T(8,128)S(1)}, u32[]{:S(2)}, u32[]{:S(2)}) collective-permute-start(f32[240,128]{1,0:T(8,128)S(1)} %constant_dynamic-update-slice_fusion.own_ref), channel_id=1, source_target_pairs={{0,1},{1,0},{2,3},{3,2},{4,5},{5,4},{6,7},{7,6},{8,9},{9,8},{10,11... | collective-permute-start | bytes 368648 | tf_op jit(solution)/shard_map/ppermute | solution.py:542
  20.4 4.9 %collective-permute-start.4 = (f32[240,128]{1,0:T(8,128)S(1)}, f32[240,128]{1,0:T(8,128)S(1)}, u32[]{:S(2)}, u32[]{:S(2)}) collective-permute-start(f32[240,128]{1,0:T(8,128)S(1)} %get-tuple-element.46), channel_id=1, source_target_pairs={{0,4},{1,2},{2,1},{3,7},{4,0},{5,6},{6,5},{7,3},{8,12},{9,10},{10,... | collective-permute-start | bytes 368648 | tf_op jit(solution)/shard_map/ppermute | solution.py:542
  21.1 4.2 %collective-permute-start.5 = (f32[240,128]{1,0:T(8,128)S(1)}, f32[240,128]{1,0:T(8,128)S(1)}, u32[]{:S(2)}, u32[]{:S(2)}) collective-permute-start(f32[240,128]{1,0:T(8,128)S(1)} %get-tuple-element.47), channel_id=1, source_target_pairs={{0,1},{1,0},{2,3},{3,2},{4,5},{5,4},{6,7},{7,6},{8,9},{9,8},{10,11... | collective-permute-start | bytes 368648 | tf_op jit(solution)/shard_map/ppermute | solution.py:542
  25.4 3.1 %collective-permute-start.6 = (f32[80,128]{1,0:T(8,128)S(1)}, f32[80,128]{1,0:T(8,128)S(1)}, u32[]{:S(2)}, u32[]{:S(2)}) collective-permute-start(f32[80,128]{1,0:T(8,128)S(1)} %get-tuple-element.49), channel_id=1, source_target_pairs={{0,1},{4,8},{8,4},{12,16},{16,12},{20,24},{24,20},{28,29},{1,0},{5... | collective-permute-start | bytes 122888 | tf_op jit(solution)/shard_map/ppermute | solution.py:542
  25.5 5.0 %collective-permute-start.7 = (f32[80,128]{1,0:T(8,128)S(1)}, f32[80,128]{1,0:T(8,128)S(1)}, u32[]{:S(2)}, u32[]{:S(2)}) collective-permute-start(f32[80,128]{1,0:T(8,128)S(1)} %get-tuple-element.50), channel_id=1, source_target_pairs={{0,4},{4,0},{8,12},{12,8},{16,20},{20,16},{24,28},{28,24},{1,5},{5... | collective-permute-start | bytes 122888 | tf_op jit(solution)/shard_map/ppermute | solution.py:542
  31.5 7.1 %collective-permute-start.8 = (f32[3,16,256]{2,1,0:T(8,128)S(1)}, f32[3,16,256]{2,1,0:T(8,128)S(1)}, u32[]{:S(2)}, u32[]{:S(2)}) collective-permute-start(f32[3,16,256]{2,1,0:T(8,128)S(1)} %get-tuple-element.52), channel_id=1, source_target_pairs={{0,1},{4,8},{8,4},{12,16},{16,12},{20,24},{24,20},{28,29},{1,0},{5... | collective-permute-start | bytes 147464 | tf_op jit(solution)/shard_map/ppermute | solution.py:542
  31.5 7.1 %collective-permute-start.9 = (f32[3,16,256]{2,1,0:T(8,128)S(1)}, f32[3,16,256]{2,1,0:T(8,128)S(1)}, u32[]{:S(2)}, u32[]{:S(2)}) collective-permute-start(f32[3,16,256]{2,1,0:T(8,128)S(1)} %get-tuple-element.53), channel_id=1, source_target_pairs={{0,4},{4,0},{8,12},{12,8},{16,20},{20,16},{24,28},{28,24},{1,5},{5... | collective-permute-start | bytes 147464 | tf_op jit(solution)/shard_map/ppermute | solution.py:542
  34.9 3.7 %collective-permute-start.10 = (f32[3,4,256]{2,1,0:T(4,128)S(1)}, f32[3,4,256]{2,1,0:T(4,128)S(1)}, u32[]{:S(2)}, u32[]{:S(2)}) collective-permute-start(f32[3,4,256]{2,1,0:T(4,128)S(1)} %get-tuple-element.54), channel_id=1, source_target_pairs={{0,4},{1,2},{2,1},{3,7},{4,0},{5,6},{6,5},{7,3},{8,12},{9,10},{10,... | collective-permute-start | bytes 36872 | tf_op jit(solution)/shard_map/ppermute | solution.py:542
  34.9 3.7 %collective-permute-start.11 = (f32[3,4,256]{2,1,0:T(4,128)S(1)}, f32[3,4,256]{2,1,0:T(4,128)S(1)}, u32[]{:S(2)}, u32[]{:S(2)}) collective-permute-start(f32[3,4,256]{2,1,0:T(4,128)S(1)} %get-tuple-element.55), channel_id=1, source_target_pairs={{0,1},{1,0},{2,3},{3,2},{4,5},{5,4},{6,7},{7,6},{8,9},{9,8},{10,11... | collective-permute-start | bytes 36872 | tf_op jit(solution)/shard_map/ppermute | solution.py:542
  39.7 4.8 %collective-permute-start.13 = (f32[80,128]{1,0:T(8,128)S(1)}, f32[80,128]{1,0:T(8,128)S(1)}, u32[]{:S(2)}, u32[]{:S(2)}) collective-permute-start(f32[80,128]{1,0:T(8,128)S(1)} %get-tuple-element.57), channel_id=1, source_target_pairs={{0,1},{4,8},{8,4},{12,16},{16,12},{20,24},{24,20},{28,29},{1,0},{5... | collective-permute-start | bytes 122888 | tf_op jit(solution)/shard_map/ppermute | solution.py:542
  39.8 4.7 %collective-permute-start.12 = (f32[80,128]{1,0:T(8,128)S(1)}, f32[80,128]{1,0:T(8,128)S(1)}, u32[]{:S(2)}, u32[]{:S(2)}) collective-permute-start(f32[80,128]{1,0:T(8,128)S(1)} %get-tuple-element.57), channel_id=1, source_target_pairs={{0,4},{4,0},{8,12},{12,8},{16,20},{20,16},{24,28},{28,24},{1,5},{5... | collective-permute-start | bytes 122888 | tf_op jit(solution)/shard_map/ppermute | solution.py:542
  44.4 4.9 %collective-permute-start.15 = (f32[240,128]{1,0:T(8,128)S(1)}, f32[240,128]{1,0:T(8,128)S(1)}, u32[]{:S(2)}, u32[]{:S(2)}) collective-permute-start(f32[240,128]{1,0:T(8,128)S(1)} %constant_dynamic-update-slice_fusion.3.own_ref), channel_id=1, source_target_pairs={{0,4},{1,2},{2,1},{3,7},{4,0},{5,6},{6,5},{7,3},{8,12},{9,10},{10,... | collective-permute-start | bytes 368648 | tf_op jit(solution)/shard_map/ppermute | solution.py:542
  46.5 2.9 %collective-permute-start.14 = (f32[240,128]{1,0:T(8,128)S(1)}, f32[240,128]{1,0:T(8,128)S(1)}, u32[]{:S(2)}, u32[]{:S(2)}) collective-permute-start(f32[240,128]{1,0:T(8,128)S(1)} %constant_dynamic-update-slice_fusion.3.own_ref), channel_id=1, source_target_pairs={{0,1},{1,0},{2,3},{3,2},{4,5},{5,4},{6,7},{7,6},{8,9},{9,8},{10,11... | collective-permute-start | bytes 368648 | tf_op jit(solution)/shard_map/ppermute | solution.py:542
  53.3 4.9 %collective-permute-start.16 = (f32[240,128]{1,0:T(8,128)S(1)}, f32[240,128]{1,0:T(8,128)S(1)}, u32[]{:S(2)}, u32[]{:S(2)}) collective-permute-start(f32[240,128]{1,0:T(8,128)S(1)} %get-tuple-element.59), channel_id=1, source_target_pairs={{0,4},{1,2},{2,1},{3,7},{4,0},{5,6},{6,5},{7,3},{8,12},{9,10},{10,... | collective-permute-start | bytes 368648 | tf_op jit(solution)/shard_map/ppermute | solution.py:542
  55.4 2.9 %collective-permute-start.17 = (f32[240,128]{1,0:T(8,128)S(1)}, f32[240,128]{1,0:T(8,128)S(1)}, u32[]{:S(2)}, u32[]{:S(2)}) collective-permute-start(f32[240,128]{1,0:T(8,128)S(1)} %get-tuple-element.60), channel_id=1, source_target_pairs={{0,1},{1,0},{2,3},{3,2},{4,5},{5,4},{6,7},{7,6},{8,9},{9,8},{10,11... | collective-permute-start | bytes 368648 | tf_op jit(solution)/shard_map/ppermute | solution.py:542
  58.2 3.4 %collective-permute-start.18 = (f32[80,128]{1,0:T(8,128)S(1)}, f32[80,128]{1,0:T(8,128)S(1)}, u32[]{:S(2)}, u32[]{:S(2)}) collective-permute-start(f32[80,128]{1,0:T(8,128)S(1)} %get-tuple-element.62), channel_id=1, source_target_pairs={{0,1},{4,8},{8,4},{12,16},{16,12},{20,24},{24,20},{28,29},{1,0},{5... | collective-permute-start | bytes 122888 | tf_op jit(solution)/shard_map/ppermute | solution.py:542
  58.3 5.3 %collective-permute-start.19 = (f32[80,128]{1,0:T(8,128)S(1)}, f32[80,128]{1,0:T(8,128)S(1)}, u32[]{:S(2)}, u32[]{:S(2)}) collective-permute-start(f32[80,128]{1,0:T(8,128)S(1)} %get-tuple-element.63), channel_id=1, source_target_pairs={{0,4},{4,0},{8,12},{12,8},{16,20},{20,16},{24,28},{28,24},{1,5},{5... | collective-permute-start | bytes 122888 | tf_op jit(solution)/shard_map/ppermute | solution.py:542
  64.5 7.4 %collective-permute-start.20 = (f32[3,16,256]{2,1,0:T(8,128)S(1)}, f32[3,16,256]{2,1,0:T(8,128)S(1)}, u32[]{:S(2)}, u32[]{:S(2)}) collective-permute-start(f32[3,16,256]{2,1,0:T(8,128)S(1)} %get-tuple-element.65), channel_id=1, source_target_pairs={{0,1},{4,8},{8,4},{12,16},{16,12},{20,24},{24,20},{28,29},{1,0},{5... | collective-permute-start | bytes 147464 | tf_op jit(solution)/shard_map/ppermute | solution.py:542
  64.6 7.4 %collective-permute-start.21 = (f32[3,16,256]{2,1,0:T(8,128)S(1)}, f32[3,16,256]{2,1,0:T(8,128)S(1)}, u32[]{:S(2)}, u32[]{:S(2)}) collective-permute-start(f32[3,16,256]{2,1,0:T(8,128)S(1)} %get-tuple-element.66), channel_id=1, source_target_pairs={{0,4},{4,0},{8,12},{12,8},{16,20},{20,16},{24,28},{28,24},{1,5},{5... | collective-permute-start | bytes 147464 | tf_op jit(solution)/shard_map/ppermute | solution.py:542
  68.3 3.7 %collective-permute-start.22 = (f32[3,4,256]{2,1,0:T(4,128)S(1)}, f32[3,4,256]{2,1,0:T(4,128)S(1)}, u32[]{:S(2)}, u32[]{:S(2)}) collective-permute-start(f32[3,4,256]{2,1,0:T(4,128)S(1)} %get-tuple-element.67), channel_id=1, source_target_pairs={{0,4},{1,2},{2,1},{3,7},{4,0},{5,6},{6,5},{7,3},{8,12},{9,10},{10,... | collective-permute-start | bytes 36872 | tf_op jit(solution)/shard_map/ppermute | solution.py:542
  68.3 3.7 %collective-permute-start.23 = (f32[3,4,256]{2,1,0:T(4,128)S(1)}, f32[3,4,256]{2,1,0:T(4,128)S(1)}, u32[]{:S(2)}, u32[]{:S(2)}) collective-permute-start(f32[3,4,256]{2,1,0:T(4,128)S(1)} %get-tuple-element.68), channel_id=1, source_target_pairs={{0,1},{1,0},{2,3},{3,2},{4,5},{5,4},{6,7},{7,6},{8,9},{9,8},{10,11... | collective-permute-start | bytes 36872 | tf_op jit(solution)/shard_map/ppermute | solution.py:542
  (12 other events, 86.0 us)

commit v11 on v10

--- a/solution.py
+++ b/solution.py
@@ -179,7 +179,7 @@
 
 
 def chain_kernel(
-    value_ref, g_ref, couple_ref, out_ref, h_ref, e_ref, apart_ref, part_ref
+    value_ref, _, g_ref, couple_ref, out_ref, h_ref, e_ref, apart_ref, part_ref
 ):
     out_ref[...] = value_ref[...]
     chunks, width, span_all = g_ref.shape
@@ -602,7 +602,7 @@
             (3, chunks, span, span_all),
         ],
         [((chunks, width, LANES), F32)],
-    )(picked, span_inverse, couple)
+    )(picked, index, span_inverse, couple)
 
     def precondition(vector, picked):
         beside = swap("gx", picked, picked)

time: 83.9 us -> 83.1 us (level)
  local copies, waits for them, and re-layouts: 2.54 us -> 1.26 us
  starting transfers between devices: 28.4 us -> 29.3 us
    unnamed x29 -> x25, local copies, waits for them, and re-layouts: 2.24 us -> 0.96 us
    ppermute x24, starting transfers between devices: 28.4 us -> 29.3 us  [swap(): out.append(lax.ppermute(value, ('gx', 'gy'), pairs))]
where the time goes in v11:
time: 83.1 us; the launch traced here: 82.9 us
  starting transfers between devices  29.3 us (35%)
  Pallas kernels  21.1 us (25%)
  waiting for transfers between devices  20.5 us (25%)
  blocking collectives  9.76 us (12%)
  local copies, waits for them, and re-layouts  1.26 us (2%)
  between operations  0.93 us (1%)
    ppermute x24, starting transfers between devices, swap(): out.append(lax.ppermute(value, ('gx', 'gy'), pairs))  29.3 us
    pallas_call x18, Pallas kernels, run(): pl.pallas_call(kernel, out_shape=shapes, in_specs=[pl.BlockSpec(memory_sp...  21.1 us
    ppermute x24, waiting for transfers between devices, swap(): out.append(lax.ppermute(value, ('gx', 'gy'), pairs))  20.5 us
    all_to_all x1, blocking collectives, body(): sums = lax.all_to_all(sums, ('gx', 'gy'), 0, 0)  9.76 us
  transfers between devices with their start and end apart: 24, of which 9 were waited for; matrix products, arithmetic and copies ran while one was open for 1% of the time, Pallas kernels for 7%

profile of v11, /device:TPU:0, one launch (start us, length us, event | category | flops | bytes accessed | tf_op | source)
XLA Modules:
  0.0 82.9 jit_solution(17623305491084945208)
XLA Ops:
  0.7 3.0 %shard_map.105.value_ref = f32[80,128]{1,0:T(8,128)} custom-call(s32[1,3200]{1,0:T(1,128)} %cells_ref.3, f32[3,4,16,256]{3,2,1,0:T(8,128)} %v_ref.7, f32[9,4,16,256]{3,2,1,0:T(8,128)} %d_ref.5), custom_call_target="tpu_custom_call" | custom-call | flops 1000000000 | bytes 840192 | tf_op jit(solution)/shard_map/pallas_call | solution.py:56
  4.2 4.0 %collective-permute-start = (f32[80,128]{1,0:T(8,128)}, f32[80,128]{1,0:T(8,128)S(1)}, u32[]{:S(2)}, u32[]{:S(2)}) collective-permute-start(f32[80,128]{1,0:T(8,128)} %shard_map.105.value_ref), channel_id=1, source_target_pairs={{0,4},{4,0},{8,12},{12,8},{16,20},{20,16},{24,28},{28,24},{1,5},{5... | collective-permute-start | bytes 122888 | tf_op jit(solution)/shard_map/ppermute | solution.py:542
  9.5 1.3 %shard_map.106 = (f32[80,128]{1,0:T(8,128)S(1)}, f32[3,32,384]{2,1,0:T(8,128)S(1)}, f32[9,32,8]{2,1,0:T(8,128)S(1)}, f32[3,25,16,384]{3,2,1,0:T(8,128)S(1)}) custom-call(f32[80,128]{1,0:T(8,128)S(1)} %copy-done.5, s32[1,3200]{1,0:T(1,128)S(1)} %reshape.12.idx_ref._, f32[25,48,384]{2,1,0:T(8,128)S(1)} %copy-done.2, f32[9,32,8]{2,1,0:T(8,128)S(1)} %pad.4.couple_ref), custom_call_target="tpu_custom_call" | custom-call | bytes 3947008 | tf_op jit(solution)/shard_map/pallas_call | solution.py:56
  10.9 1.6 %collective-permute-start.3 = (f32[240,128]{1,0:T(8,128)S(1)}, f32[240,128]{1,0:T(8,128)S(1)}, u32[]{:S(2)}, u32[]{:S(2)}) collective-permute-start(f32[240,128]{1,0:T(8,128)S(1)} %constant_dynamic-update-slice_fusion.own_ref), channel_id=1, source_target_pairs={{0,4},{1,2},{2,1},{3,7},{4,0},{5,6},{6,5},{7,3},{8,12},{9,10},{10,... | collective-permute-start | bytes 368648 | tf_op jit(solution)/shard_map/ppermute | solution.py:542
  14.2 1.6 %collective-permute-done.3.next_ref = f32[240,128]{1,0:T(8,128)S(1)} collective-permute-done((f32[240,128]{1,0:T(8,128)S(1)}, f32[240,128]{1,0:T(8,128)S(1)}, u32[]{:S(2)}, u32[]{:S(2)}) %collective-permute-start.3) | collective-permute-done | bytes 122912 | tf_op jit(solution)/shard_map/ppermute | solution.py:542
  15.9 3.7 %shard_map.108 = (f32[32,384]{1,0:T(8,128)S(1)}, f32[240,128]{1,0:T(8,128)S(1)}, f32[240,128]{1,0:T(8,128)S(1)}) custom-call(s32[1,3200]{1,0:T(1,128)S(1)} %reshape.12.idx_ref._, f32[240,128]{1,0:T(8,128)S(1)} %collective-permute-done.2.even_ref, f32[240,128]{1,0:T(8,128)S(1)} %collective-permute-done.3.next_ref, f32[3,32,128]{2,1,0:T(8,128)S(1)} %shard_map.107.part_ref, ...), custom_call_target="tpu_custom_call" | custom-call | flops 3000000000 | bytes 5060096 | tf_op jit(solution)/shard_map/pallas_call | solution.py:56
  19.5 1.6 %collective-permute-start.4 = (f32[240,128]{1,0:T(8,128)S(1)}, f32[240,128]{1,0:T(8,128)S(1)}, u32[]{:S(2)}, u32[]{:S(2)}) collective-permute-start(f32[240,128]{1,0:T(8,128)S(1)} %get-tuple-element.46), channel_id=1, source_target_pairs={{0,4},{1,2},{2,1},{3,7},{4,0},{5,6},{6,5},{7,3},{8,12},{9,10},{10,... | collective-permute-start | bytes 368648 | tf_op jit(solution)/shard_map/ppermute | solution.py:542
  21.9 2.6 %collective-permute-done.4.y_ref = f32[240,128]{1,0:T(8,128)S(1)} collective-permute-done((f32[240,128]{1,0:T(8,128)S(1)}, f32[240,128]{1,0:T(8,128)S(1)}, u32[]{:S(2)}, u32[]{:S(2)}) %collective-permute-start.4) | collective-permute-done | bytes 122912 | tf_op jit(solution)/shard_map/ppermute | solution.py:542
  24.6 3.0 %collective-permute-start.7 = (f32[80,128]{1,0:T(8,128)S(1)}, f32[80,128]{1,0:T(8,128)S(1)}, u32[]{:S(2)}, u32[]{:S(2)}) collective-permute-start(f32[80,128]{1,0:T(8,128)S(1)} %get-tuple-element.50), channel_id=1, source_target_pairs={{0,4},{4,0},{8,12},{12,8},{16,20},{20,16},{24,28},{28,24},{1,5},{5... | collective-permute-start | bytes 122888 | tf_op jit(solution)/shard_map/ppermute | solution.py:542
  27.6 2.0 %collective-permute-done.7.z_ref = f32[80,128]{1,0:T(8,128)S(1)} collective-permute-done((f32[80,128]{1,0:T(8,128)S(1)}, f32[80,128]{1,0:T(8,128)S(1)}, u32[]{:S(2)}, u32[]{:S(2)}) %collective-permute-start.7) | collective-permute-done | bytes 40992 | tf_op jit(solution)/shard_map/ppermute | solution.py:542
  30.7 3.4 %collective-permute-start.9 = (f32[3,16,256]{2,1,0:T(8,128)S(1)}, f32[3,16,256]{2,1,0:T(8,128)S(1)}, u32[]{:S(2)}, u32[]{:S(2)}) collective-permute-start(f32[3,16,256]{2,1,0:T(8,128)S(1)} %get-tuple-element.53), channel_id=1, source_target_pairs={{0,4},{4,0},{8,12},{12,8},{16,20},{20,16},{24,28},{28,24},{1,5},{5... | collective-permute-start | bytes 147464 | tf_op jit(solution)/shard_map/ppermute | solution.py:542
  34.9 2.9 %collective-permute-done.10.f2_ref = f32[3,4,256]{2,1,0:T(4,128)S(1)} collective-permute-done((f32[3,4,256]{2,1,0:T(4,128)S(1)}, f32[3,4,256]{2,1,0:T(4,128)S(1)}, u32[]{:S(2)}, u32[]{:S(2)}) %collective-permute-start.10) | collective-permute-done | bytes 12320 | tf_op jit(solution)/shard_map/ppermute | solution.py:542
  39.0 3.0 %collective-permute-start.12 = (f32[80,128]{1,0:T(8,128)S(1)}, f32[80,128]{1,0:T(8,128)S(1)}, u32[]{:S(2)}, u32[]{:S(2)}) collective-permute-start(f32[80,128]{1,0:T(8,128)S(1)} %get-tuple-element.57), channel_id=1, source_target_pairs={{0,4},{4,0},{8,12},{12,8},{16,20},{20,16},{24,28},{28,24},{1,5},{5... | collective-permute-start | bytes 122888 | tf_op jit(solution)/shard_map/ppermute | solution.py:542
  42.0 2.0 %collective-permute-done.12 = f32[80,128]{1,0:T(8,128)S(1)} collective-permute-done((f32[80,128]{1,0:T(8,128)S(1)}, f32[80,128]{1,0:T(8,128)S(1)}, u32[]{:S(2)}, u32[]{:S(2)}) %collective-permute-start.12) | collective-permute-done | bytes 40992 | tf_op jit(solution)/shard_map/ppermute | solution.py:542
  44.0 2.1 %collective-permute-start.15 = (f32[240,128]{1,0:T(8,128)S(1)}, f32[240,128]{1,0:T(8,128)S(1)}, u32[]{:S(2)}, u32[]{:S(2)}) collective-permute-start(f32[240,128]{1,0:T(8,128)S(1)} %constant_dynamic-update-slice_fusion.3.own_ref), channel_id=1, source_target_pairs={{0,4},{1,2},{2,1},{3,7},{4,0},{5,6},{6,5},{7,3},{8,12},{9,10},{10,... | collective-permute-start | bytes 368648 | tf_op jit(solution)/shard_map/ppermute | solution.py:542
  46.9 2.1 %collective-permute-done.15.next_ref = f32[240,128]{1,0:T(8,128)S(1)} collective-permute-done((f32[240,128]{1,0:T(8,128)S(1)}, f32[240,128]{1,0:T(8,128)S(1)}, u32[]{:S(2)}, u32[]{:S(2)}) %collective-permute-start.15) | collective-permute-done | bytes 122912 | tf_op jit(solution)/shard_map/ppermute | solution.py:542
  48.9 3.9 %shard_map.115 = (f32[32,384]{1,0:T(8,128)S(1)}, f32[240,128]{1,0:T(8,128)S(1)}, f32[240,128]{1,0:T(8,128)S(1)}) custom-call(s32[1,3200]{1,0:T(1,128)S(1)} %reshape.12.idx_ref._, f32[240,128]{1,0:T(8,128)S(1)} %collective-permute-done.14.even_ref, f32[240,128]{1,0:T(8,128)S(1)} %collective-permute-done.15.next_ref, f32[3,32,128]{2,1,0:T(8,128)S(1)} %shard_map.114.part_ref, ...), custom_call_target="tpu_custom_call" | custom-call | flops 3000000000 | bytes 5060096 | tf_op jit(solution)/shard_map/pallas_call | solution.py:56
  52.8 2.1 %collective-permute-start.16 = (f32[240,128]{1,0:T(8,128)S(1)}, f32[240,128]{1,0:T(8,128)S(1)}, u32[]{:S(2)}, u32[]{:S(2)}) collective-permute-start(f32[240,128]{1,0:T(8,128)S(1)} %get-tuple-element.59), channel_id=1, source_target_pairs={{0,4},{1,2},{2,1},{3,7},{4,0},{5,6},{6,5},{7,3},{8,12},{9,10},{10,... | collective-permute-start | bytes 368648 | tf_op jit(solution)/shard_map/ppermute | solution.py:542
  55.7 2.1 %collective-permute-done.16.y_ref = f32[240,128]{1,0:T(8,128)S(1)} collective-permute-done((f32[240,128]{1,0:T(8,128)S(1)}, f32[240,128]{1,0:T(8,128)S(1)}, u32[]{:S(2)}, u32[]{:S(2)}) %collective-permute-start.16) | collective-permute-done | bytes 122912 | tf_op jit(solution)/shard_map/ppermute | solution.py:542
  57.9 3.3 %collective-permute-start.19 = (f32[80,128]{1,0:T(8,128)S(1)}, f32[80,128]{1,0:T(8,128)S(1)}, u32[]{:S(2)}, u32[]{:S(2)}) collective-permute-start(f32[80,128]{1,0:T(8,128)S(1)} %get-tuple-element.63), channel_id=1, source_target_pairs={{0,4},{4,0},{8,12},{12,8},{16,20},{20,16},{24,28},{28,24},{1,5},{5... | collective-permute-start | bytes 122888 | tf_op jit(solution)/shard_map/ppermute | solution.py:542
  61.2 2.0 %collective-permute-done.19.z_ref = f32[80,128]{1,0:T(8,128)S(1)} collective-permute-done((f32[80,128]{1,0:T(8,128)S(1)}, f32[80,128]{1,0:T(8,128)S(1)}, u32[]{:S(2)}, u32[]{:S(2)}) %collective-permute-start.19) | collective-permute-done | bytes 40992 | tf_op jit(solution)/shard_map/ppermute | solution.py:542
  64.2 3.6 %collective-permute-start.21 = (f32[3,16,256]{2,1,0:T(8,128)S(1)}, f32[3,16,256]{2,1,0:T(8,128)S(1)}, u32[]{:S(2)}, u32[]{:S(2)}) collective-permute-start(f32[3,16,256]{2,1,0:T(8,128)S(1)} %get-tuple-element.66), channel_id=1, source_target_pairs={{0,4},{4,0},{8,12},{12,8},{16,20},{20,16},{24,28},{28,24},{1,5},{5... | collective-permute-start | bytes 147464 | tf_op jit(solution)/shard_map/ppermute | solution.py:542
  68.3 3.3 %collective-permute-done.22.f2_ref = f32[3,4,256]{2,1,0:T(4,128)S(1)} collective-permute-done((f32[3,4,256]{2,1,0:T(4,128)S(1)}, f32[3,4,256]{2,1,0:T(4,128)S(1)}, u32[]{:S(2)}, u32[]{:S(2)}) %collective-permute-start.22) | collective-permute-done | bytes 12320 | tf_op jit(solution)/shard_map/ppermute | solution.py:542
  72.0 9.8 %all_to_all.5.all_ref = f32[32,1,128]{2,1,0:T(1,128)S(1)} all-to-all(f32[32,1,128]{2,1,0:T(1,128)S(1)} %get-tuple-element.70), channel_id=1, replica_groups=mesh['gx'=8,'gy'=4] {'gx','gy'}, dimensions={0} | all-to-all | bytes 32768 | tf_op jit(solution)/shard_map/all_to_all | solution.py:659
  (75 shorter events, 12.1 us)
Async XLA Ops:
  3.7 7.2 %collective-permute-start.1 = (f32[80,128]{1,0:T(8,128)}, f32[80,128]{1,0:T(8,128)S(1)}, u32[]{:S(2)}, u32[]{:S(2)}) collective-permute-start(f32[80,128]{1,0:T(8,128)} %shard_map.105.value_ref), channel_id=1, source_target_pairs={{0,1},{4,8},{8,4},{12,16},{16,12},{20,24},{24,20},{28,29},{1,0},{5... | collective-permute-start | bytes 122888 | tf_op jit(solution)/shard_map/ppermute | solution.py:542
  4.2 6.7 %collective-permute-start = (f32[80,128]{1,0:T(8,128)}, f32[80,128]{1,0:T(8,128)S(1)}, u32[]{:S(2)}, u32[]{:S(2)}) collective-permute-start(f32[80,128]{1,0:T(8,128)} %shard_map.105.value_ref), channel_id=1, source_target_pairs={{0,4},{4,0},{8,12},{12,8},{16,20},{20,16},{24,28},{28,24},{1,5},{5... | collective-permute-start | bytes 122888 | tf_op jit(solution)/shard_map/ppermute | solution.py:542
  10.9 4.9 %collective-permute-start.3 = (f32[240,128]{1,0:T(8,128)S(1)}, f32[240,128]{1,0:T(8,128)S(1)}, u32[]{:S(2)}, u32[]{:S(2)}) collective-permute-start(f32[240,128]{1,0:T(8,128)S(1)} %constant_dynamic-update-slice_fusion.own_ref), channel_id=1, source_target_pairs={{0,4},{1,2},{2,1},{3,7},{4,0},{5,6},{6,5},{7,3},{8,12},{9,10},{10,... | collective-permute-start | bytes 368648 | tf_op jit(solution)/shard_map/ppermute | solution.py:542
  12.5 3.3 %collective-permute-start.2 = (f32[240,128]{1,0:T(8,128)S(1)}, f32[240,128]{1,0:T(8,128)S(1)}, u32[]{:S(2)}, u32[]{:S(2)}) collective-permute-start(f32[240,128]{1,0:T(8,128)S(1)} %constant_dynamic-update-slice_fusion.own_ref), channel_id=1, source_target_pairs={{0,1},{1,0},{2,3},{3,2},{4,5},{5,4},{6,7},{7,6},{8,9},{9,8},{10,11... | collective-permute-start | bytes 368648 | tf_op jit(solution)/shard_map/ppermute | solution.py:542
  19.5 4.9 %collective-permute-start.4 = (f32[240,128]{1,0:T(8,128)S(1)}, f32[240,128]{1,0:T(8,128)S(1)}, u32[]{:S(2)}, u32[]{:S(2)}) collective-permute-start(f32[240,128]{1,0:T(8,128)S(1)} %get-tuple-element.46), channel_id=1, source_target_pairs={{0,4},{1,2},{2,1},{3,7},{4,0},{5,6},{6,5},{7,3},{8,12},{9,10},{10,... | collective-permute-start | bytes 368648 | tf_op jit(solution)/shard_map/ppermute | solution.py:542
  21.1 3.3 %collective-permute-start.5 = (f32[240,128]{1,0:T(8,128)S(1)}, f32[240,128]{1,0:T(8,128)S(1)}, u32[]{:S(2)}, u32[]{:S(2)}) collective-permute-start(f32[240,128]{1,0:T(8,128)S(1)} %get-tuple-element.47), channel_id=1, source_target_pairs={{0,1},{1,0},{2,3},{3,2},{4,5},{5,4},{6,7},{7,6},{8,9},{9,8},{10,11... | collective-permute-start | bytes 368648 | tf_op jit(solution)/shard_map/ppermute | solution.py:542
  24.5 3.1 %collective-permute-start.6 = (f32[80,128]{1,0:T(8,128)S(1)}, f32[80,128]{1,0:T(8,128)S(1)}, u32[]{:S(2)}, u32[]{:S(2)}) collective-permute-start(f32[80,128]{1,0:T(8,128)S(1)} %get-tuple-element.49), channel_id=1, source_target_pairs={{0,1},{4,8},{8,4},{12,16},{16,12},{20,24},{24,20},{28,29},{1,0},{5... | collective-permute-start | bytes 122888 | tf_op jit(solution)/shard_map/ppermute | solution.py:542
  24.6 5.0 %collective-permute-start.7 = (f32[80,128]{1,0:T(8,128)S(1)}, f32[80,128]{1,0:T(8,128)S(1)}, u32[]{:S(2)}, u32[]{:S(2)}) collective-permute-start(f32[80,128]{1,0:T(8,128)S(1)} %get-tuple-element.50), channel_id=1, source_target_pairs={{0,4},{4,0},{8,12},{12,8},{16,20},{20,16},{24,28},{28,24},{1,5},{5... | collective-permute-start | bytes 122888 | tf_op jit(solution)/shard_map/ppermute | solution.py:542
  30.6 7.2 %collective-permute-start.8 = (f32[3,16,256]{2,1,0:T(8,128)S(1)}, f32[3,16,256]{2,1,0:T(8,128)S(1)}, u32[]{:S(2)}, u32[]{:S(2)}) collective-permute-start(f32[3,16,256]{2,1,0:T(8,128)S(1)} %get-tuple-element.52), channel_id=1, source_target_pairs={{0,1},{4,8},{8,4},{12,16},{16,12},{20,24},{24,20},{28,29},{1,0},{5... | collective-permute-start | bytes 147464 | tf_op jit(solution)/shard_map/ppermute | solution.py:542
  30.7 7.1 %collective-permute-start.9 = (f32[3,16,256]{2,1,0:T(8,128)S(1)}, f32[3,16,256]{2,1,0:T(8,128)S(1)}, u32[]{:S(2)}, u32[]{:S(2)}) collective-permute-start(f32[3,16,256]{2,1,0:T(8,128)S(1)} %get-tuple-element.53), channel_id=1, source_target_pairs={{0,4},{4,0},{8,12},{12,8},{16,20},{20,16},{24,28},{28,24},{1,5},{5... | collective-permute-start | bytes 147464 | tf_op jit(solution)/shard_map/ppermute | solution.py:542
  34.1 3.7 %collective-permute-start.10 = (f32[3,4,256]{2,1,0:T(4,128)S(1)}, f32[3,4,256]{2,1,0:T(4,128)S(1)}, u32[]{:S(2)}, u32[]{:S(2)}) collective-permute-start(f32[3,4,256]{2,1,0:T(4,128)S(1)} %get-tuple-element.54), channel_id=1, source_target_pairs={{0,4},{1,2},{2,1},{3,7},{4,0},{5,6},{6,5},{7,3},{8,12},{9,10},{10,... | collective-permute-start | bytes 36872 | tf_op jit(solution)/shard_map/ppermute | solution.py:542
  34.1 3.7 %collective-permute-start.11 = (f32[3,4,256]{2,1,0:T(4,128)S(1)}, f32[3,4,256]{2,1,0:T(4,128)S(1)}, u32[]{:S(2)}, u32[]{:S(2)}) collective-permute-start(f32[3,4,256]{2,1,0:T(4,128)S(1)} %get-tuple-element.55), channel_id=1, source_target_pairs={{0,1},{1,0},{2,3},{3,2},{4,5},{5,4},{6,7},{7,6},{8,9},{9,8},{10,11... | collective-permute-start | bytes 36872 | tf_op jit(solution)/shard_map/ppermute | solution.py:542
  38.9 5.1 %collective-permute-start.13 = (f32[80,128]{1,0:T(8,128)S(1)}, f32[80,128]{1,0:T(8,128)S(1)}, u32[]{:S(2)}, u32[]{:S(2)}) collective-permute-start(f32[80,128]{1,0:T(8,128)S(1)} %get-tuple-element.57), channel_id=1, source_target_pairs={{0,1},{4,8},{8,4},{12,16},{16,12},{20,24},{24,20},{28,29},{1,0},{5... | collective-permute-start | bytes 122888 | tf_op jit(solution)/shard_map/ppermute | solution.py:542
  39.0 5.0 %collective-permute-start.12 = (f32[80,128]{1,0:T(8,128)S(1)}, f32[80,128]{1,0:T(8,128)S(1)}, u32[]{:S(2)}, u32[]{:S(2)}) collective-permute-start(f32[80,128]{1,0:T(8,128)S(1)} %get-tuple-element.57), channel_id=1, source_target_pairs={{0,4},{4,0},{8,12},{12,8},{16,20},{20,16},{24,28},{28,24},{1,5},{5... | collective-permute-start | bytes 122888 | tf_op jit(solution)/shard_map/ppermute | solution.py:542
  44.0 4.9 %collective-permute-start.15 = (f32[240,128]{1,0:T(8,128)S(1)}, f32[240,128]{1,0:T(8,128)S(1)}, u32[]{:S(2)}, u32[]{:S(2)}) collective-permute-start(f32[240,128]{1,0:T(8,128)S(1)} %constant_dynamic-update-slice_fusion.3.own_ref), channel_id=1, source_target_pairs={{0,4},{1,2},{2,1},{3,7},{4,0},{5,6},{6,5},{7,3},{8,12},{9,10},{10,... | collective-permute-start | bytes 368648 | tf_op jit(solution)/shard_map/ppermute | solution.py:542
  46.1 2.9 %collective-permute-start.14 = (f32[240,128]{1,0:T(8,128)S(1)}, f32[240,128]{1,0:T(8,128)S(1)}, u32[]{:S(2)}, u32[]{:S(2)}) collective-permute-start(f32[240,128]{1,0:T(8,128)S(1)} %constant_dynamic-update-slice_fusion.3.own_ref), channel_id=1, source_target_pairs={{0,1},{1,0},{2,3},{3,2},{4,5},{5,4},{6,7},{7,6},{8,9},{9,8},{10,11... | collective-permute-start | bytes 368648 | tf_op jit(solution)/shard_map/ppermute | solution.py:542
  52.8 4.9 %collective-permute-start.16 = (f32[240,128]{1,0:T(8,128)S(1)}, f32[240,128]{1,0:T(8,128)S(1)}, u32[]{:S(2)}, u32[]{:S(2)}) collective-permute-start(f32[240,128]{1,0:T(8,128)S(1)} %get-tuple-element.59), channel_id=1, source_target_pairs={{0,4},{1,2},{2,1},{3,7},{4,0},{5,6},{6,5},{7,3},{8,12},{9,10},{10,... | collective-permute-start | bytes 368648 | tf_op jit(solution)/shard_map/ppermute | solution.py:542
  54.9 2.9 %collective-permute-start.17 = (f32[240,128]{1,0:T(8,128)S(1)}, f32[240,128]{1,0:T(8,128)S(1)}, u32[]{:S(2)}, u32[]{:S(2)}) collective-permute-start(f32[240,128]{1,0:T(8,128)S(1)} %get-tuple-element.60), channel_id=1, source_target_pairs={{0,1},{1,0},{2,3},{3,2},{4,5},{5,4},{6,7},{7,6},{8,9},{9,8},{10,11... | collective-permute-start | bytes 368648 | tf_op jit(solution)/shard_map/ppermute | solution.py:542
  57.8 3.4 %collective-permute-start.18 = (f32[80,128]{1,0:T(8,128)S(1)}, f32[80,128]{1,0:T(8,128)S(1)}, u32[]{:S(2)}, u32[]{:S(2)}) collective-permute-start(f32[80,128]{1,0:T(8,128)S(1)} %get-tuple-element.62), channel_id=1, source_target_pairs={{0,1},{4,8},{8,4},{12,16},{16,12},{20,24},{24,20},{28,29},{1,0},{5... | collective-permute-start | bytes 122888 | tf_op jit(solution)/shard_map/ppermute | solution.py:542
  57.9 5.3 %collective-permute-start.19 = (f32[80,128]{1,0:T(8,128)S(1)}, f32[80,128]{1,0:T(8,128)S(1)}, u32[]{:S(2)}, u32[]{:S(2)}) collective-permute-start(f32[80,128]{1,0:T(8,128)S(1)} %get-tuple-element.63), channel_id=1, source_target_pairs={{0,4},{4,0},{8,12},{12,8},{16,20},{20,16},{24,28},{28,24},{1,5},{5... | collective-permute-start | bytes 122888 | tf_op jit(solution)/shard_map/ppermute | solution.py:542
  64.2 7.4 %collective-permute-start.20 = (f32[3,16,256]{2,1,0:T(8,128)S(1)}, f32[3,16,256]{2,1,0:T(8,128)S(1)}, u32[]{:S(2)}, u32[]{:S(2)}) collective-permute-start(f32[3,16,256]{2,1,0:T(8,128)S(1)} %get-tuple-element.65), channel_id=1, source_target_pairs={{0,1},{4,8},{8,4},{12,16},{16,12},{20,24},{24,20},{28,29},{1,0},{5... | collective-permute-start | bytes 147464 | tf_op jit(solution)/shard_map/ppermute | solution.py:542
  64.2 7.3 %collective-permute-start.21 = (f32[3,16,256]{2,1,0:T(8,128)S(1)}, f32[3,16,256]{2,1,0:T(8,128)S(1)}, u32[]{:S(2)}, u32[]{:S(2)}) collective-permute-start(f32[3,16,256]{2,1,0:T(8,128)S(1)} %get-tuple-element.66), channel_id=1, source_target_pairs={{0,4},{4,0},{8,12},{12,8},{16,20},{20,16},{24,28},{28,24},{1,5},{5... | collective-permute-start | bytes 147464 | tf_op jit(solution)/shard_map/ppermute | solution.py:542
  67.8 3.7 %collective-permute-start.22 = (f32[3,4,256]{2,1,0:T(4,128)S(1)}, f32[3,4,256]{2,1,0:T(4,128)S(1)}, u32[]{:S(2)}, u32[]{:S(2)}) collective-permute-start(f32[3,4,256]{2,1,0:T(4,128)S(1)} %get-tuple-element.67), channel_id=1, source_target_pairs={{0,4},{1,2},{2,1},{3,7},{4,0},{5,6},{6,5},{7,3},{8,12},{9,10},{10,... | collective-permute-start | bytes 36872 | tf_op jit(solution)/shard_map/ppermute | solution.py:542
  67.9 3.7 %collective-permute-start.23 = (f32[3,4,256]{2,1,0:T(4,128)S(1)}, f32[3,4,256]{2,1,0:T(4,128)S(1)}, u32[]{:S(2)}, u32[]{:S(2)}) collective-permute-start(f32[3,4,256]{2,1,0:T(4,128)S(1)} %get-tuple-element.68), channel_id=1, source_target_pairs={{0,1},{1,0},{2,3},{3,2},{4,5},{5,4},{6,7},{7,6},{8,9},{9,8},{10,11... | collective-permute-start | bytes 36872 | tf_op jit(solution)/shard_map/ppermute | solution.py:542
  (10 other events, 76.2 us)
